TPU v7x, 32 devices: a whole 2x2x4 slice. The times are simulated.
32 devices in a mesh: seq: 8 (over y, x, core), hid: 4 (over z).
Axes of the slice: x: 2, y: 2, z: 4, core: 2. Of those that a mesh axis runs over, the one named last changes fastest.
Arguments:
- hidden: bfloat16 [2048, 4096], P('seq', 'hid'), may hold values from -6 to 6
- w_in: bfloat16 [2, 4096, 1024], P(None, 'hid'), may hold values from -0.09863281 to 0.09863281
- embedding: bfloat16 [1, 2048, 1024], replicated, may hold values from -6 to 6
- depth_gain: float32 [2, 1024], replicated, may hold values from 0.25 to 1.75
- w_out: bfloat16 [1024, 2, 2048], P(('seq', 'hid')), may hold values from -0.43554688 to 0.43554688
- codebook_ids: int32 [2, 2048], P(None, ('seq', 'hid')), may hold values from 0 to 2047
Outputs:
- grad_hidden: bfloat16 [2048, 4096], P('seq', 'hid')
- grad_in: float32 [2, 4096, 1024], P(None, 'hid', 'seq')
- grad_out: float32 [1024, 2, 2048], P(('seq', 'hid'))
All inputs are finite; a program needn't handle non-finite values.
Results may differ from a plain program's by a relative error of at most 0.01.
Values may be sent and summed in bfloat16 or wider, within the bound.
No kernel may reach another device: no remote copies, remote signals or barrier semaphores. Data moves between devices by JAX's collectives and lax.ppermute only.
A program may use at most 128 MiB of HBM per device.

v0:
```python
import jax
import jax.numpy as jnp
from jax import lax
from jax.experimental import pallas as pl
from jax.experimental.pallas import tpu as pltpu
from jax.sharding import PartitionSpec as P

F32 = jnp.float32
BF16 = jnp.bfloat16


def pick(values, index):
    return lax.dynamic_index_in_dim(values, index, axis=0, keepdims=False)


def matmul(a, b, contract):
    return lax.dot_general(a, b, (contract, ((), ())), preferred_element_type=F32)


def after(value, *others):
    return lax.optimization_barrier((value, *others))[0]


VMEM = pltpu.CompilerParams(vmem_limit_bytes=16 * 2**20)


def whole(shape):
    return pl.BlockSpec(shape, lambda n, place: (0,) * len(shape))


def call(kernel, place, grid, in_specs, out_specs, out_shape, scratch, flops, args):
    moved = sum(a.size * a.dtype.itemsize for a in args)
    return pl.pallas_call(
        kernel,
        grid_spec=pltpu.PrefetchScalarGridSpec(
            num_scalar_prefetch=1,
            grid=(grid,),
            in_specs=in_specs,
            out_specs=out_specs,
            scratch_shapes=scratch,
        ),
        out_shape=out_shape,
        compiler_params=VMEM,
        cost_estimate=pl.CostEstimate(flops=flops, bytes_accessed=moved, transcendentals=0),
    )(place, *args)


EXACT = 3


def parts_of(values):
    out = []
    for _ in range(EXACT):
        piece = lax.reduce_precision(values, 8, 7)
        values = values - piece
        out.append(piece.astype(BF16))
    return out


def head_gradient(place, pieces, halves):
    hids = len(pieces)
    steps, rows, block = pieces[0].shape

    def kernel(place_ref, *refs):
        pieces, out = refs[:-1], refs[-1]
        for r in range(halves):
            which = lax.rem(place_ref[1] - r + hids, halves)
            columns = pl.ds(pl.multiple_of(which * block, block), block)
            for s in range(steps):
                total = pieces[r][s].astype(F32)
                for k in range(r + halves, hids, halves):
                    total = total + pieces[k][s].astype(F32)
                out[:, s, columns] = total

    return call(
        kernel,
        place,
        1,
        [whole((steps, rows, block))] * hids,
        whole((rows, steps, halves * block)),
        jax.ShapeDtypeStruct((rows, steps, halves * block), F32),
        [],
        hids * steps * rows * block,
        tuple(pieces),
    )


def shards(hidden, w_in, embedding, depth_gain, w_out, codebook_ids):
    hids = lax.axis_size("hid")
    seqs = lax.axis_size("seq")
    steps, units, depth = w_in.shape
    entries = w_out.shape[2]
    rows = hidden.shape[0]
    part = rows // hids
    width_in = units * hids
    frames = rows * seqs
    halves = 2 if hids % 2 == 0 else 1
    block = entries // halves
    head_rows = w_out.shape[0]
    groups = seqs // steps
    i = lax.axis_index("seq")
    j = lax.axis_index("hid")
    step = i % steps
    half = j % halves
    owned = steps * part

    def along_hid(values, shift):
        return lax.ppermute(values, "hid", [(a, (a + shift) % hids) for a in range(hids)])

    def turn_hid(values, shift):
        return lax.ppermute(
            values,
            "hid",
            [(a, a - a % halves + (a % halves + shift) % halves) for a in range(hids)],
        )

    def flip_seq(values, flip):
        return lax.ppermute(
            values,
            "seq",
            [(a, a - a % steps + (a % steps + flip) % steps) for a in range(seqs)],
        )

    place = jnp.stack([step, j]).astype(jnp.int32)
    relations = range(1, steps)

    squares_part = jnp.sum(jnp.square(hidden.astype(F32)), axis=1)
    tail = 8 * block
    small = jnp.concatenate(parts_of(squares_part))
    small = jnp.pad(small, (0, tail - small.size)).reshape(1, 1, 8, block)
    head_send = w_out.reshape(head_rows, steps, halves, block).transpose(2, 1, 0, 3)
    head_send = head_send.reshape(1, halves, steps * head_rows, block)
    small = jnp.broadcast_to(small, (1, halves, 8, block))
    head_send = jnp.concatenate([head_send, small], axis=2)
    head_send = jnp.broadcast_to(head_send, (hids // halves,) + head_send.shape[1:])
    head_send = head_send.reshape(hids, steps * head_rows + 8, block)
    head_got = lax.all_to_all(head_send, "hid", 0, 0)
    head_mid = head_got[:, : steps * head_rows].reshape(hids, steps, head_rows, block)
    squares = head_got[:, steps * head_rows :].reshape(hids, tail)[:, : EXACT * rows]
    squares = jnp.sum(squares.astype(F32).reshape(hids * EXACT, rows), axis=0)

    ids = jnp.concatenate([codebook_ids] + [flip_seq(codebook_ids, -m) for m in relations], axis=1)
    ids_rows = [ids] + [turn_hid(ids, -k) for k in range(1, halves)]
    before = jnp.maximum(step - 1, 0)
    looked = jnp.take(pick(embedding, before), pick(ids, before), axis=0)

    group = [hidden] + [after(flip_seq(hidden, -m), looked) for m in relations]
    w_own = pick(w_in, step)
    proj_parts = matmul(jnp.concatenate(group), w_own, ((1,), (0,)))
    proj_parts = proj_parts.reshape(steps, hids, part, depth)

    def owner_block(index):
        return lax.dynamic_index_in_dim(proj_parts, index, 1, False).reshape(owned, depth)

    send = [owner_block((j + shift) % hids).astype(BF16) for shift in range(1, hids)]
    received = [along_hid(send[shift - 1], shift) for shift in range(1, hids)]

    head_send = after(head_mid, *send).transpose(1, 0, 2, 3)
    head_send = head_send.reshape(steps, hids * head_rows, block)
    head_send = jnp.broadcast_to(head_send, (groups,) + head_send.shape)
    head_send = head_send.reshape(seqs, hids * head_rows, block)
    head = lax.all_to_all(head_send, "seq", 0, 0).reshape(depth, block)

    squares = jnp.stack([squares] + [flip_seq(squares, -m) for m in relations])
    ratio_group = lax.rsqrt(squares / width_in + 1e-06).reshape(steps, hids, part)
    order = [(j - shift) % hids for shift in range(hids)]

    ratio = lax.dynamic_index_in_dim(ratio_group, j, 1, False).reshape(owned, 1)
    proj = owner_block(j)
    for r in received:
        proj += r.astype(F32)
    x_rows = ratio * proj + jnp.where(step > 0, looked.astype(F32), 0.0)
    scale = lax.rsqrt(jnp.mean(x_rows * x_rows, axis=1, keepdims=True) + 1e-06)
    gain = pick(depth_gain, step)[None, :]
    normed = (x_rows * scale * gain).astype(BF16)

    normed_rows = jnp.concatenate([normed] + [turn_hid(normed, -k) for k in range(1, halves)])
    targets = jnp.concatenate([pick(r, step) for r in ids_rows])
    logits = matmul(normed_rows, head, ((1,), (0,)))
    top = jnp.max(logits, axis=1)
    total = jnp.sum(jnp.exp(logits - top[:, None]), axis=1)
    stats = jnp.stack([top, total]).reshape(2, halves, -1)
    every = [stats] + [jnp.roll(turn_hid(stats, -t), t, axis=1) for t in range(1, halves)]
    tops = jnp.stack([e[0] for e in every]).reshape(halves, -1)
    totals = jnp.stack([e[1] for e in every]).reshape(halves, -1)
    top_all = jnp.max(tops, axis=0)
    lse = top_all + jnp.log(jnp.sum(totals * jnp.exp(tops - top_all), axis=0))
    entry = lax.broadcasted_iota(jnp.int32, logits.shape, 1) + half * block
    onehot = (targets[:, None] == entry).astype(F32)
    loss_weight = 2.0 * entries / frames
    d_logit = ((jnp.exp(logits - lse[:, None]) - onehot) * loss_weight).astype(BF16)

    d_norm_rows = matmul(d_logit, head, ((1,), (1,)))
    away = [d_norm_rows[k * owned : (k + 1) * owned].astype(BF16) for k in range(1, halves)]
    received = [turn_hid(a, k + 1) for k, a in enumerate(away)]
    d_norm = d_norm_rows[:owned]
    for r in received:
        d_norm += r.astype(F32)
    gated = gain * d_norm
    d_x = scale * gated - x_rows * scale**3 * jnp.mean(gated * x_rows, axis=1, keepdims=True)
    d_round = d_x.astype(BF16)
    d_ratio_part = jnp.sum(d_x * proj, axis=1).reshape(steps, part)

    part_out = matmul(normed_rows, after(d_logit, *received), ((0,), (0,))).astype(BF16)
    part_out = lax.all_to_all(part_out.reshape(seqs, depth // seqs, block), "seq", 0, 0)
    part_out = part_out.reshape(groups, steps, hids, head_rows, block).astype(F32).sum(0)
    part_out = part_out.astype(BF16)
    sums = [
        lax.dynamic_index_in_dim(part_out, (j + shift) % hids, 1, False) for shift in range(hids)
    ]
    sums = [along_hid(p, shift) if shift else p for shift, p in enumerate(sums)]
    grad_out = head_gradient(place, sums, halves)

    pieces = [d_round] + [along_hid(d_round, shift) for shift in range(1, hids)]
    ordered = [g.reshape(hids, part, units) for g in group]
    hidden_rows = jnp.concatenate([pick(g, o) for o in order for g in ordered])
    ratio_rows = [
        lax.dynamic_index_in_dim(ratio_group, o, 1, False).reshape(owned, 1) for o in order
    ]
    scaled = jnp.concatenate(
        [(r * p.astype(F32)).astype(BF16) for r, p in zip(ratio_rows, pieces)]
    )
    share = matmul(scaled, hidden_rows, ((0,), (0,))).astype(BF16)
    share = lax.all_to_all(share.reshape(seqs, depth // seqs, units), "seq", 0, 0)
    share = share.reshape(groups, steps, depth // seqs, units).astype(F32).sum(0)
    grad_in = share.transpose(0, 2, 1)

    d_ratio = d_ratio_part[0]
    for m in relations:
        d_ratio += flip_seq(d_ratio_part[m], m)
    d_ratio = [d_ratio] + [along_hid(d_ratio, shift) for shift in range(1, hids)]
    d_ratio = jnp.concatenate(d_ratio[::-1])[:, None]
    back_rows = jnp.zeros((steps, rows, depth), BF16)
    for m in range(steps):
        member = jnp.concatenate([p[m * part : (m + 1) * part] for p in pieces[::-1]])
        member = flip_seq(member, m) if m else member
        back_rows = lax.dynamic_update_index_in_dim(back_rows, member, (step - m) % steps, 0)
    back = matmul(back_rows[0], w_in[0], ((1,), (1,)))
    for s in range(1, steps):
        back += matmul(back_rows[s], w_in[s], ((1,), (1,)))
    ratio_own = jnp.concatenate([r[:part] for r in ratio_rows[::-1]])
    hidden_own = jnp.concatenate([pick(ordered[0], o) for o in order[::-1]]).astype(F32)
    correction = ratio_own**3 * d_ratio / width_in
    grad_hidden = (ratio_own * back - correction * hidden_own).astype(BF16)
    grad_hidden = jnp.concatenate([grad_hidden, grad_hidden])
    grad_hidden = lax.dynamic_slice_in_dim(grad_hidden, (hids - 1 - j) * part, rows, 0)
    return (grad_hidden, grad_in, grad_out)


def solution(mesh):
    placed = (
        P("seq", "hid"),
        P(None, "hid", None),
        P(),
        P(),
        P(("seq", "hid"), None, None),
        P(None, ("seq", "hid")),
    )
    return jax.shard_map(
        shards,
        mesh=mesh,
        in_specs=placed,
        out_specs=(P("seq", "hid"), P(None, "hid", "seq"), P(("seq", "hid"), None, None)),
        check_vma=False,
    )
```

profile of v0, /device:TPU:0, one launch (start us, length us, event | category | flops | bytes accessed | tf_op | source)
XLA Modules:
  0.0 155.8 jit_solution(5130276735478402090)
XLA Ops:
  1.2 1.2 multiply_reduce_fusion
  2.5 1.2 reshape.330
  4.7 6.3 %all-to-all-start = ((bf16[4,72,1024]{2,1,0:T(8,128)(2,1)}), bf16[4,72,1024]{2,1,0:T(8,128)(2,1)S(1)}, u32[]{:S(2)}, u32[]{:S(2)}) async-start(bf16[4,72,1024]{2,1,0:T(8,128)(2,1)} %bitcast.4), calls=%async_computation | async-start | bytes 1179648 | tf_op jit(solution)/shard_map/all_to_all | solution.py:137
  12.0 2.1 %collective-permute-start.8 = (s32[2,128]{1,0:T(2,128)S(1)}, s32[2,128]{1,0:T(2,128)S(1)}, u32[]{:S(2)}, u32[]{:S(2)}) collective-permute-start(s32[2,128]{1,0:T(2,128)S(1)} %pad_add_fusion), channel_id=1, source_target_pairs={{0,1},{1,0},{2,3},{3,2},{4,5},{5,4},{6,7},{7,6},{8,9},{9,8},{10,11... | collective-permute-start | bytes 3080 | tf_op jit(solution)/shard_map/ppermute | solution.py:111
  14.0 3.8 %gather_fusion = bf16[128,1024]{1,0:T(8,128)(2,1)S(1)} fusion(bf16[2048,1024]{1,0:T(8,128)(2,1)} %bitcast.171, s32[1024]{0:T(1024)S(1)} %pad_clamp_fusion), kind=kCustom, calls=%fused_computation | custom fusion | bytes 524800 | tf_op jit(solution)/shard_map/jit(_take)/gather | solution.py:145
  17.8 3.2 %collective-permute-done.8 = s32[2,128]{1,0:T(2,128)S(1)} collective-permute-done((s32[2,128]{1,0:T(2,128)S(1)}, s32[2,128]{1,0:T(2,128)S(1)}, u32[]{:S(2)}, u32[]{:S(2)}) %collective-permute-start.8) | collective-permute-done | bytes 1056 | tf_op jit(solution)/shard_map/ppermute | solution.py:111
  21.2 3.0 %fusion = f32[2,4,64,1024]{3,2,1,0:T(8,128)S(1)} fusion(bf16[2,4,64,1024]{3,2,1,0:T(8,128)(2,1)S(1)} %bitcast.172, bf16[2,1024,1024]{2,1,0:T(8,128)(2,1)} %param.7, s32[]{:T(128)S(6)} %select_n.163), kind=kOutput, calls=%fused_computation.2 | convolution fusion | flops 1073741824 | bytes 5242884 | tf_op jit(solution)/shard_map/dot_general | solution.py:17
  25.1 2.4 %collective-permute-start.3 = (bf16[128,1024]{1,0:T(8,128)(2,1)}, bf16[128,1024]{1,0:T(8,128)(2,1)}, u32[]{:S(2)}, u32[]{:S(2)}) collective-permute-start(bf16[128,1024]{1,0:T(8,128)(2,1)} %bitcast.19), channel_id=1, source_target_pairs={{0,1},{1,2},{2,3},{3,0},{4,5},{5,6},{6,7},{7,4},{8,9},{9,10},{10,1... | collective-permute-start | bytes 786440 | tf_op jit(solution)/shard_map/ppermute | solution.py:108
  27.5 2.1 %collective-permute-start.4 = (bf16[128,1024]{1,0:T(8,128)(2,1)}, bf16[128,1024]{1,0:T(8,128)(2,1)}, u32[]{:S(2)}, u32[]{:S(2)}) collective-permute-start(bf16[128,1024]{1,0:T(8,128)(2,1)} %bitcast.20), channel_id=1, source_target_pairs={{0,2},{1,3},{2,0},{3,1},{4,6},{5,7},{6,4},{7,5},{8,10},{9,11},{10,... | collective-permute-start | bytes 786440 | tf_op jit(solution)/shard_map/ppermute | solution.py:108
  29.6 2.9 %collective-permute-start.5 = (bf16[128,1024]{1,0:T(8,128)(2,1)}, bf16[128,1024]{1,0:T(8,128)(2,1)}, u32[]{:S(2)}, u32[]{:S(2)}) collective-permute-start(bf16[128,1024]{1,0:T(8,128)(2,1)} %bitcast.21), channel_id=1, source_target_pairs={{0,3},{1,0},{2,1},{3,2},{4,7},{5,4},{6,5},{7,6},{8,11},{9,8},{10,9... | collective-permute-start | bytes 786440 | tf_op jit(solution)/shard_map/ppermute | solution.py:108
  34.9 1.6 %broadcast_in_dim.57 = bf16[4,2,128,1024]{3,2,1,0:T(8,128)(2,1)} broadcast(bf16[2,128,1024]{2,1,0:T(8,128)(2,1)S(1)} %bitcast.164), dimensions={1,2,3} | broadcast | bytes 2621440 | tf_op jit(solution)/shard_map/broadcast_in_dim | solution.py:160
  36.5 3.7 %all-to-all-start.1 = ((bf16[8,128,1024]{2,1,0:T(8,128)(2,1)}), bf16[8,128,1024]{2,1,0:T(8,128)(2,1)S(1)}, u32[]{:S(2)}, u32[]{:S(2)}) async-start(bf16[8,128,1024]{2,1,0:T(8,128)(2,1)} %bitcast.155), calls=%async_computation.1 | async-start | bytes 4194304 | tf_op jit(solution)/shard_map/all_to_all | solution.py:162
  42.7 3.3 %collective-permute-done.4 = bf16[128,1024]{1,0:T(8,128)(2,1)} collective-permute-done((bf16[128,1024]{1,0:T(8,128)(2,1)}, bf16[128,1024]{1,0:T(8,128)(2,1)}, u32[]{:S(2)}, u32[]{:S(2)}) %collective-permute-start.4) | collective-permute-done | bytes 262176 | tf_op jit(solution)/shard_map/ppermute | solution.py:108
  46.0 1.6 %multiply_reduce_fusion.3 = (f32[128]{0:T(128)S(1)}, f32[128,1024]{1,0:T(8,128)S(1)}) fusion(pred[]{:T(512)S(6)} %gt.3, bf16[128,1024]{1,0:T(8,128)(2,1)} %collective-permute-done.5, bf16[128,1024]{1,0:T(8,128)(2,1)} %collective-permute-done.4, bf16[128,1024]{1,0:T(8,128)(2,1)} %collective-permute-done.3, ...), kind=kLoop, calls=%fused_computation.52 | loop fusion | flops 1703808 | bytes 2098305 | tf_op jit(solution)/shard_map/reduce_sum | solution.py:173
  47.8 6.1 %collective-permute-start.6 = (bf16[128,1024]{1,0:T(8,128)(2,1)S(1)}, bf16[128,1024]{1,0:T(8,128)(2,1)}, u32[]{:S(2)}, u32[]{:S(2)}) collective-permute-start(bf16[128,1024]{1,0:T(8,128)(2,1)S(1)} %multiply_convert_fusion.5), channel_id=1, source_target_pairs={{0,1},{1,0},{2,3},{3,2},{4,5},{5,4},{6,7},{7,6},{8,9},{9,8},{10,11... | collective-permute-start | bytes 786440 | tf_op jit(solution)/shard_map/ppermute | solution.py:111
  54.7 1.6 %bitcast_dynamic-update-slice_fusion.2 = bf16[512,1024]{1,0:T(8,128)(2,1)} fusion(bf16[512,1024]{1,0:T(8,128)(2,1)} %get-tuple-element.20, bf16[4,64,1024]{2,1,0:T(8,128)(2,1)} %bitcast.168, s32[]{:T(128)S(6)} %select_n.153), kind=kLoop, calls=%fused_computation.61 | loop fusion | bytes 262148
  57.0 3.5 %collective-permute-done.6 = bf16[128,1024]{1,0:T(8,128)(2,1)} collective-permute-done((bf16[128,1024]{1,0:T(8,128)(2,1)S(1)}, bf16[128,1024]{1,0:T(8,128)(2,1)}, u32[]{:S(2)}, u32[]{:S(2)}) %collective-permute-start.6) | collective-permute-done | bytes 262176 | tf_op jit(solution)/shard_map/ppermute | solution.py:111
  60.5 6.3 %all-to-all-done.1 = bf16[8,128,1024]{2,1,0:T(8,128)(2,1)S(1)} async-done(((bf16[8,128,1024]{2,1,0:T(8,128)(2,1)}), bf16[8,128,1024]{2,1,0:T(8,128)(2,1)S(1)}, u32[]{:S(2)}, u32[]{:S(2)}) %all-to-all-start.1) | async-done | bytes 2097184 | tf_op jit(solution)/shard_map/all_to_all | solution.py:162
  66.8 1.8 %fusion.61 = (f32[256]{0:T(256)S(1)}, f32[256,1024]{1,0:T(8,128)S(1)}) fusion(bf16[1024,1024]{1,0:T(8,128)(2,1)S(1)} %bitcast.153, bf16[128,1024]{1,0:T(8,128)(2,1)} %collective-permute-done.6, bf16[128,1024]{1,0:T(8,128)(2,1)S(1)} %multiply_convert_fusion.5), kind=kOutput, calls=%fused_computation.150 | convolution fusion | flops 538181376 | bytes 3671040 | tf_op jit(solution)/shard_map/dot_general | solution.py:17
  69.0 1.6 %bitcast_dynamic-update-slice_fusion.1 = bf16[512,1024]{1,0:T(8,128)(2,1)} fusion(bf16[512,1024]{1,0:T(8,128)(2,1)} %get-tuple-element.18, bf16[4,64,1024]{2,1,0:T(8,128)(2,1)} %bitcast.169, s32[]{:T(128)S(6)} %select_n.151), kind=kLoop, calls=%fused_computation.60 | loop fusion | bytes 262148 | tf_op jit(solution)/shard_map/concatenate | solution.py:216
  70.6 2.0 %collective-permute-done.7 = f32[2,2,128]{2,1,0:T(2,128)S(1)} collective-permute-done((f32[2,2,128]{2,1,0:T(2,128)S(1)}, f32[2,2,128]{2,1,0:T(2,128)S(1)}, u32[]{:S(2)}, u32[]{:S(2)}) %collective-permute-start.7) | collective-permute-done | bytes 2080 | tf_op jit(solution)/shard_map/ppermute | solution.py:111
  77.9 3.3 %collective-permute-done.9 = bf16[128,1024]{1,0:T(8,128)(2,1)S(1)} collective-permute-done((bf16[128,1024]{1,0:T(8,128)(2,1)S(1)}, bf16[128,1024]{1,0:T(8,128)(2,1)S(1)}, u32[]{:S(2)}, u32[]{:S(2)}) %collective-permute-start.9) | collective-permute-done | bytes 262176 | tf_op jit(solution)/shard_map/ppermute | solution.py:111
  81.2 1.2 multiply_reduce_fusion.2
  82.4 2.2 %multiply_convert_fusion.4 = (bf16[128,1024]{1,0:T(8,128)(2,1)}, bf16[128,1024]{1,0:T(8,128)(2,1)}, f32[128,1024]{1,0:T(8,128)}) fusion(f32[128]{0:T(128)S(1)} %mul.174, f32[128]{0:T(128)S(1)} %broadcast_multiply_fusion, f32[128,1024]{1,0:T(8,128)S(1)} %get-tuple-element.29, f32[128]{0:T(128)S(1)} %get-tuple-element.63, ...), kind=kLoop, calls=%fused_computation.47 | loop fusion | flops 1441792 | bytes 2365440 | tf_op jit(solution)/shard_map/convert_element_type | solution.py:221
  84.7 1.5 collective-permute-start.11
  86.7 3.1 %convolution_convert_fusion = bf16[1024,1024]{1,0:T(8,128)(2,1)} fusion(bf16[256,1024]{1,0:T(8,128)(2,1)S(1)} %multiply_convert_fusion, bf16[128,1024]{1,0:T(8,128)(2,1)} %collective-permute-done.6, bf16[128,1024]{1,0:T(8,128)(2,1)S(1)} %copy-done.10), kind=kOutput, calls=%fused_computation.11 | convolution fusion | flops 538968064 | bytes 3145728 | tf_op jit(solution)/shard_map/dot_general | solution.py:17
  89.8 1.6 %fusion.59 = (bf16[64,1024]{1,0:T(8,128)(2,1)}, bf16[64,1024]{1,0:T(8,128)(2,1)S(1)}) fusion(bf16[128,1024]{1,0:T(8,128)(2,1)} %get-tuple-element.16), kind=kLoop, calls=%fused_computation.148 | loop fusion | bytes 524288 | tf_op jit(solution)/shard_map/slice | solution.py:235
  91.4 3.7 %all-to-all-start.3 = ((bf16[8,128,1024]{2,1,0:T(8,128)(2,1)}), bf16[8,128,1024]{2,1,0:T(8,128)(2,1)S(1)}, u32[]{:S(2)}, u32[]{:S(2)}) async-start(bf16[8,128,1024]{2,1,0:T(8,128)(2,1)} %bitcast.158), calls=%async_computation.3 | async-start | bytes 4194304 | tf_op jit(solution)/shard_map/all_to_all | solution.py:205
  95.2 1.4 multiply_reduce_fusion.1
  97.7 7.5 %collective-permute-done.11 = bf16[128,1024]{1,0:T(8,128)(2,1)} collective-permute-done((bf16[128,1024]{1,0:T(8,128)(2,1)}, bf16[128,1024]{1,0:T(8,128)(2,1)}, u32[]{:S(2)}, u32[]{:S(2)}) %collective-permute-start.11) | collective-permute-done | bytes 262176 | tf_op jit(solution)/shard_map/ppermute | solution.py:108
  107.3 1.1 multiply_convert_fusion.2
  108.3 1.1 multiply_convert_fusion.3
  109.4 2.6 %convolution_convert_fusion.1 = bf16[1024,1024]{1,0:T(8,128)(2,1)} fusion(bf16[512,1024]{1,0:T(8,128)(2,1)S(1)} %copy-done.17, bf16[128,1024]{1,0:T(8,128)(2,1)S(1)} %multiply_convert_fusion.1, bf16[128,1024]{1,0:T(8,128)(2,1)S(1)} %multiply_convert_fusion.2, bf16[128,1024]{1,0:T(8,128)(2,1)S(1)} %multiply_convert_fusion.3, bf16[128,1024]{1,0:T(8,128)(2,1)S(1)} %copy-done.12), kind=kOutput, calls=%fused_computation.12 | convolution fusion | flops 1078984704 | bytes 4194304 | tf_op jit(solution)/shard_map/dot_general | solution.py:17
  112.1 9.7 %all-to-all-done.3 = bf16[8,128,1024]{2,1,0:T(8,128)(2,1)S(1)} async-done(((bf16[8,128,1024]{2,1,0:T(8,128)(2,1)}), bf16[8,128,1024]{2,1,0:T(8,128)(2,1)S(1)}, u32[]{:S(2)}, u32[]{:S(2)}) %all-to-all-start.3) | async-done | bytes 2097184 | tf_op jit(solution)/shard_map/all_to_all | solution.py:205
  121.8 1.3 copy-done.1
  123.1 3.6 %all-to-all-start.2 = ((bf16[8,128,1024]{2,1,0:T(8,128)(2,1)}), bf16[8,128,1024]{2,1,0:T(8,128)(2,1)S(1)}, u32[]{:S(2)}, u32[]{:S(2)}) async-start(bf16[8,128,1024]{2,1,0:T(8,128)(2,1)} %bitcast.165), calls=%async_computation.2 | async-start | bytes 4194304 | tf_op jit(solution)/shard_map/all_to_all | solution.py:224
  128.1 3.3 %collective-permute-start.15 = (f32[64]{0:T(128)S(1)}, f32[64]{0:T(128)S(1)}, u32[]{:S(2)}, u32[]{:S(2)}) collective-permute-start(f32[64]{0:T(128)S(1)} %slice_add_fusion.1), channel_id=1, source_target_pairs={{0,3},{1,0},{2,1},{3,2},{4,7},{5,4},{6,5},{7,6},{8,11},{9,8},{10,9... | collective-permute-start | bytes 776 | tf_op jit(solution)/shard_map/ppermute | solution.py:108
  131.4 1.7 %collective-permute-start.17 = (f32[64]{0:T(128)S(1)}, f32[64]{0:T(128)S(1)}, u32[]{:S(2)}, u32[]{:S(2)}) collective-permute-start(f32[64]{0:T(128)S(1)} %slice_add_fusion.1), channel_id=1, source_target_pairs={{0,1},{1,2},{2,3},{3,0},{4,5},{5,6},{6,7},{7,4},{8,9},{9,10},{10,1... | collective-permute-start | bytes 776 | tf_op jit(solution)/shard_map/ppermute | solution.py:108
  133.2 2.7 %collective-permute-done.16 = f32[64]{0:T(128)S(1)} collective-permute-done((f32[64]{0:T(128)S(1)}, f32[64]{0:T(128)S(1)}, u32[]{:S(2)}, u32[]{:S(2)}) %collective-permute-start.16) | collective-permute-done | bytes 288 | tf_op jit(solution)/shard_map/ppermute | solution.py:108
  137.1 1.7 %fusion.2 = f32[256,1024]{1,0:T(8,128)} fusion(bf16[2,1024,1024]{2,1,0:T(8,128)(2,1)S(1)} %copy-done.31, bf16[2,256,1024]{2,1,0:T(8,128)(2,1)S(1)} %bitcast_dynamic-update-slice_fusion), kind=kOutput, calls=%fused_computation.4 | convolution fusion | flops 536870912 | bytes 3670016 | tf_op jit(solution)/shard_map/dot_general | solution.py:17
  138.8 2.1 %reduce_sum.92 = bf16[2,4,32,1024]{3,2,1,0:T(8,128)(2,1)S(1)} reduce(bf16[4,2,4,32,1024]{4,3,2,1,0:T(8,128)(2,1)} %bitcast.157, bf16[]{:T(256)} %constant.191.clone.1), dimensions={0}, to_apply=%region_9.10 | reduce | flops 786432 | bytes 2621442 | tf_op jit(solution)/shard_map/reduce_sum | solution.py:206
  141.0 1.2 collective-permute-start.19
  142.2 2.8 %collective-permute-start.20 = (bf16[2,32,1024]{2,1,0:T(8,128)(2,1)S(1)}, bf16[2,32,1024]{2,1,0:T(8,128)(2,1)S(1)}, u32[]{:S(2)}, u32[]{:S(2)}) collective-permute-start(bf16[2,32,1024]{2,1,0:T(8,128)(2,1)S(1)} %get-tuple-element.33), channel_id=1, source_target_pairs={{0,3},{1,0},{2,1},{3,2},{4,7},{5,4},{6,5},{7,6},{8,11},{9,8},{10,9... | collective-permute-start | bytes 393224 | tf_op jit(solution)/shard_map/ppermute | solution.py:108
  145.1 2.8 %fusion.18 = bf16[256,1024]{1,0:T(8,128)(2,1)S(1)} fusion(f32[256,1024]{1,0:T(8,128)} %fusion.2, bf16[2,1024,1024]{2,1,0:T(8,128)(2,1)} %param.7, bf16[2,256,1024]{2,1,0:T(8,128)(2,1)} %copy-done.8, bf16[64,1024]{1,0:T(8,128)(2,1)S(1)} %copy-done.13, bf16[64,1024]{1,0:T(8,128)(2,1)S(1)} %copy-done.14, bf16[64,1024]{1,0:T(8,128)(2,1)S(1)} %copy-done.15, ...), kind=kOutput, calls=%fused_computation.16 | convolution fusion | flops 540278784 | bytes 4720640 | tf_op jit(solution)/shard_map/dot_general | solution.py:17
  147.9 1.3 fusion.28
  149.3 3.3 %collective-permute-done.19.refs_2_ = bf16[2,32,1024]{2,1,0:T(8,128)(2,1)S(1)} collective-permute-done((bf16[2,32,1024]{2,1,0:T(8,128)(2,1)S(1)}, bf16[2,32,1024]{2,1,0:T(8,128)(2,1)S(1)}, u32[]{:S(2)}, u32[]{:S(2)}) %collective-permute-start.19) | collective-permute-done | bytes 131104 | tf_op jit(solution)/shard_map/ppermute | solution.py:108
  152.7 1.5 shard_map.85
  154.5 1.3 copy.19
  (160 shorter events, 22.6 us)
Async XLA Ops:
  0.6 10.4 %copy-start = (f32[2,1024]{1,0:T(2,128)S(1)}, f32[2,1024]{1,0:T(2,128)}, u32[]{:S(2)}) copy-start(f32[2,1024]{1,0:T(2,128)} %param.9) | copy-start | bytes 24580
  0.6 11.2 %collective-permute-start.2 = (s32[2,64]{1,0:T(2,128)}, s32[2,64]{1,0:T(2,128)S(1)}, u32[]{:S(2)}, u32[]{:S(2)}) collective-permute-start(s32[2,64]{1,0:T(2,128)} %param.11), channel_id=1, source_target_pairs={{0,4},{4,0},{8,12},{12,8},{16,20},{20,16},{24,28},{28,24},{1,5},{5... | collective-permute-start | bytes 1544 | tf_op jit(solution)/shard_map/ppermute | solution.py:118
  1.2 19.9 %collective-permute-start.1 = (bf16[256,1024]{1,0:T(8,128)(2,1)}, bf16[256,1024]{1,0:T(8,128)(2,1)S(1)}, u32[]{:S(2)}, u32[]{:S(2)}) collective-permute-start(bf16[256,1024]{1,0:T(8,128)(2,1)} %param.6), channel_id=1, source_target_pairs={{0,4},{4,0},{8,12},{12,8},{16,20},{20,16},{24,28},{28,24},{1,5},{5... | collective-permute-start | bytes 1572872 | tf_op jit(solution)/shard_map/ppermute | solution.py:118
  2.5 8.7 %copy-start.3 = (bf16[256,1024]{1,0:T(8,128)(2,1)S(1)}, bf16[256,1024]{1,0:T(8,128)(2,1)}, u32[]{:S(2)}) copy-start(bf16[256,1024]{1,0:T(8,128)(2,1)} %param.6) | copy-start | bytes 1572868
  3.7 8.2 %copy-start.25 = (s32[2,64]{1,0:T(2,128)S(1)}, s32[2,64]{1,0:T(2,128)}, u32[]{:S(2)}) copy-start(s32[2,64]{1,0:T(2,128)} %param.11) | copy-start | bytes 1540
  4.7 30.0 %all-to-all-start = ((bf16[4,72,1024]{2,1,0:T(8,128)(2,1)}), bf16[4,72,1024]{2,1,0:T(8,128)(2,1)S(1)}, u32[]{:S(2)}, u32[]{:S(2)}) async-start(bf16[4,72,1024]{2,1,0:T(8,128)(2,1)} %bitcast.4), calls=%async_computation | async-start | bytes 1179648 | tf_op jit(solution)/shard_map/all_to_all | solution.py:137
  12.0 9.1 %collective-permute-start.8 = (s32[2,128]{1,0:T(2,128)S(1)}, s32[2,128]{1,0:T(2,128)S(1)}, u32[]{:S(2)}, u32[]{:S(2)}) collective-permute-start(s32[2,128]{1,0:T(2,128)S(1)} %pad_add_fusion), channel_id=1, source_target_pairs={{0,1},{1,0},{2,3},{3,2},{4,5},{5,4},{6,7},{7,6},{8,9},{9,8},{10,11... | collective-permute-start | bytes 3080 | tf_op jit(solution)/shard_map/ppermute | solution.py:111
  21.1 20.6 %copy-start.6 = (bf16[256,1024]{1,0:T(8,128)(2,1)}, bf16[256,1024]{1,0:T(8,128)(2,1)S(1)}, u32[]{:S(2)}) copy-start(bf16[256,1024]{1,0:T(8,128)(2,1)S(1)} %collective-permute-done.1) | copy-start | bytes 1572868
  25.1 17.6 %collective-permute-start.3 = (bf16[128,1024]{1,0:T(8,128)(2,1)}, bf16[128,1024]{1,0:T(8,128)(2,1)}, u32[]{:S(2)}, u32[]{:S(2)}) collective-permute-start(bf16[128,1024]{1,0:T(8,128)(2,1)} %bitcast.19), channel_id=1, source_target_pairs={{0,1},{1,2},{2,3},{3,0},{4,5},{5,6},{6,7},{7,4},{8,9},{9,10},{10,1... | collective-permute-start | bytes 786440 | tf_op jit(solution)/shard_map/ppermute | solution.py:108
  27.5 18.5 %collective-permute-start.4 = (bf16[128,1024]{1,0:T(8,128)(2,1)}, bf16[128,1024]{1,0:T(8,128)(2,1)}, u32[]{:S(2)}, u32[]{:S(2)}) collective-permute-start(bf16[128,1024]{1,0:T(8,128)(2,1)} %bitcast.20), channel_id=1, source_target_pairs={{0,2},{1,3},{2,0},{3,1},{4,6},{5,7},{6,4},{7,5},{8,10},{9,11},{10,... | collective-permute-start | bytes 786440 | tf_op jit(solution)/shard_map/ppermute | solution.py:108
  29.6 16.4 %collective-permute-start.5 = (bf16[128,1024]{1,0:T(8,128)(2,1)}, bf16[128,1024]{1,0:T(8,128)(2,1)}, u32[]{:S(2)}, u32[]{:S(2)}) collective-permute-start(bf16[128,1024]{1,0:T(8,128)(2,1)} %bitcast.21), channel_id=1, source_target_pairs={{0,3},{1,0},{2,1},{3,2},{4,7},{5,4},{6,5},{7,6},{8,11},{9,8},{10,9... | collective-permute-start | bytes 786440 | tf_op jit(solution)/shard_map/ppermute | solution.py:108
  36.5 30.4 %all-to-all-start.1 = ((bf16[8,128,1024]{2,1,0:T(8,128)(2,1)}), bf16[8,128,1024]{2,1,0:T(8,128)(2,1)S(1)}, u32[]{:S(2)}, u32[]{:S(2)}) async-start(bf16[8,128,1024]{2,1,0:T(8,128)(2,1)} %bitcast.155), calls=%async_computation.1 | async-start | bytes 4194304 | tf_op jit(solution)/shard_map/all_to_all | solution.py:162
  41.1 1.4 collective-permute-start
  47.8 20.8 %copy-start.9 = (bf16[128,1024]{1,0:T(8,128)(2,1)}, bf16[128,1024]{1,0:T(8,128)(2,1)S(1)}, u32[]{:S(2)}) copy-start(bf16[128,1024]{1,0:T(8,128)(2,1)S(1)} %multiply_convert_fusion.5) | copy-start | bytes 786436
  47.8 12.7 %collective-permute-start.6 = (bf16[128,1024]{1,0:T(8,128)(2,1)S(1)}, bf16[128,1024]{1,0:T(8,128)(2,1)}, u32[]{:S(2)}, u32[]{:S(2)}) collective-permute-start(bf16[128,1024]{1,0:T(8,128)(2,1)S(1)} %multiply_convert_fusion.5), channel_id=1, source_target_pairs={{0,1},{1,0},{2,3},{3,2},{4,5},{5,4},{6,7},{7,6},{8,9},{9,8},{10,11... | collective-permute-start | bytes 786440 | tf_op jit(solution)/shard_map/ppermute | solution.py:111
  68.9 3.7 %collective-permute-start.7 = (f32[2,2,128]{2,1,0:T(2,128)S(1)}, f32[2,2,128]{2,1,0:T(2,128)S(1)}, u32[]{:S(2)}, u32[]{:S(2)}) collective-permute-start(f32[2,2,128]{2,1,0:T(2,128)S(1)} %pad_maximum_fusion.5), channel_id=1, source_target_pairs={{0,1},{1,0},{2,3},{3,2},{4,5},{5,4},{6,7},{7,6},{8,9},{9,8},{10,11... | collective-permute-start | bytes 6152 | tf_op jit(solution)/shard_map/ppermute | solution.py:111
  74.7 12.0 %copy-start.10 = (bf16[128,1024]{1,0:T(8,128)(2,1)S(1)}, bf16[128,1024]{1,0:T(8,128)(2,1)}, u32[]{:S(2)}) copy-start(bf16[128,1024]{1,0:T(8,128)(2,1)} %copy-done.9) | copy-start | bytes 786436
  74.8 6.4 %collective-permute-start.9 = (bf16[128,1024]{1,0:T(8,128)(2,1)S(1)}, bf16[128,1024]{1,0:T(8,128)(2,1)S(1)}, u32[]{:S(2)}, u32[]{:S(2)}) collective-permute-start(bf16[128,1024]{1,0:T(8,128)(2,1)S(1)} %slice.199), channel_id=1, source_target_pairs={{0,1},{1,0},{2,3},{3,2},{4,5},{5,4},{6,7},{7,6},{8,9},{9,8},{10,11... | collective-permute-start | bytes 786440 | tf_op jit(solution)/shard_map/ppermute | solution.py:111
  84.7 13.0 %collective-permute-start.10 = (bf16[128,1024]{1,0:T(8,128)(2,1)}, bf16[128,1024]{1,0:T(8,128)(2,1)S(1)}, u32[]{:S(2)}, u32[]{:S(2)}) collective-permute-start(bf16[128,1024]{1,0:T(8,128)(2,1)} %get-tuple-element.16), channel_id=1, source_target_pairs={{0,3},{1,0},{2,1},{3,2},{4,7},{5,4},{6,5},{7,6},{8,11},{9,8},{10,9... | collective-permute-start | bytes 786440 | tf_op jit(solution)/shard_map/ppermute | solution.py:108
  84.7 20.4 %collective-permute-start.11 = (bf16[128,1024]{1,0:T(8,128)(2,1)}, bf16[128,1024]{1,0:T(8,128)(2,1)}, u32[]{:S(2)}, u32[]{:S(2)}) collective-permute-start(bf16[128,1024]{1,0:T(8,128)(2,1)} %get-tuple-element.16), channel_id=1, source_target_pairs={{0,2},{1,3},{2,0},{3,1},{4,6},{5,7},{6,4},{7,5},{8,10},{9,11},{10,... | collective-permute-start | bytes 786440 | tf_op jit(solution)/shard_map/ppermute | solution.py:108
  86.2 20.0 %collective-permute-start.12 = (bf16[128,1024]{1,0:T(8,128)(2,1)}, bf16[128,1024]{1,0:T(8,128)(2,1)}, u32[]{:S(2)}, u32[]{:S(2)}) collective-permute-start(bf16[128,1024]{1,0:T(8,128)(2,1)} %get-tuple-element.16), channel_id=1, source_target_pairs={{0,1},{1,2},{2,3},{3,0},{4,5},{5,6},{6,7},{7,4},{8,9},{9,10},{10,1... | collective-permute-start | bytes 786440 | tf_op jit(solution)/shard_map/ppermute | solution.py:108
  91.4 30.3 %all-to-all-start.3 = ((bf16[8,128,1024]{2,1,0:T(8,128)(2,1)}), bf16[8,128,1024]{2,1,0:T(8,128)(2,1)S(1)}, u32[]{:S(2)}, u32[]{:S(2)}) async-start(bf16[8,128,1024]{2,1,0:T(8,128)(2,1)} %bitcast.158), calls=%async_computation.3 | async-start | bytes 4194304 | tf_op jit(solution)/shard_map/all_to_all | solution.py:205
  95.2 12.0 %copy-start.27 = (f32[128]{0:T(128)S(1)}, f32[128]{0:T(128)}, u32[]{:S(2)}) copy-start(f32[128]{0:T(128)} %mul.183) | copy-start | bytes 1540
  95.2 12.1 %copy-start.26 = (f32[128]{0:T(128)S(1)}, f32[128]{0:T(128)}, u32[]{:S(2)}) copy-start(f32[128]{0:T(128)} %mul.180) | copy-start | bytes 1540
  95.2 13.1 %copy-start.28 = (f32[128]{0:T(128)S(1)}, f32[128]{0:T(128)}, u32[]{:S(2)}) copy-start(f32[128]{0:T(128)} %mul.177) | copy-start | bytes 1540
  95.2 14.2 %copy-start.12 = (bf16[128,1024]{1,0:T(8,128)(2,1)S(1)}, bf16[128,1024]{1,0:T(8,128)(2,1)}, u32[]{:S(2)}) copy-start(bf16[128,1024]{1,0:T(8,128)(2,1)} %get-tuple-element.15) | copy-start | bytes 786436
  95.2 14.2 %copy-start.17 = (bf16[512,1024]{1,0:T(8,128)(2,1)S(1)}, bf16[512,1024]{1,0:T(8,128)(2,1)}, u32[]{:S(2)}) copy-start(bf16[512,1024]{1,0:T(8,128)(2,1)} %bitcast_dynamic-update-slice_fusion.1) | copy-start | bytes 3145732
  96.7 10.6 %copy-start.29 = (f32[128]{0:T(128)}, f32[128]{0:T(128)S(1)}, u32[]{:S(2)}) copy-start(f32[128]{0:T(128)S(1)} %multiply_reduce_fusion.1) | copy-start | bytes 1540
  97.3 29.9 %collective-permute-start.14 = (f32[64]{0:T(128)}, f32[64]{0:T(128)}, u32[]{:S(2)}, u32[]{:S(2)}) collective-permute-start(f32[64]{0:T(128)} %slice.132), channel_id=1, source_target_pairs={{0,4},{4,0},{8,12},{12,8},{16,20},{20,16},{24,28},{28,24},{1,5},{5... | collective-permute-start | bytes 776 | tf_op jit(solution)/shard_map/ppermute | solution.py:118
  121.7 11.3 %copy-start.21 = (f32[64,1]{0,1:T(1,128)S(1)}, f32[64,1]{0,1:T(1,128)}, u32[]{:S(2)}) copy-start(f32[64,1]{0,1:T(1,128)} %get-tuple-element.54) | copy-start | bytes 772
  121.7 11.3 %copy-start.22 = (f32[64,1]{0,1:T(1,128)S(1)}, f32[64,1]{0,1:T(1,128)}, u32[]{:S(2)}) copy-start(f32[64,1]{0,1:T(1,128)} %get-tuple-element.70) | copy-start | bytes 772
  121.8 11.3 %copy-start.23 = (f32[64,1]{0,1:T(1,128)S(1)}, f32[64,1]{0,1:T(1,128)}, u32[]{:S(2)}) copy-start(f32[64,1]{0,1:T(1,128)} %get-tuple-element.58) | copy-start | bytes 772
  121.8 11.3 %copy-start.24 = (f32[64,1]{0,1:T(1,128)S(1)}, f32[64,1]{0,1:T(1,128)}, u32[]{:S(2)}) copy-start(f32[64,1]{0,1:T(1,128)} %get-tuple-element.68) | copy-start | bytes 772
  121.8 15.0 %copy-start.18 = (f32[64]{0:T(128)S(1)}, f32[64]{0:T(128)}, u32[]{:S(2)}) copy-start(f32[64]{0:T(128)} %get-tuple-element.69) | copy-start | bytes 772
  121.8 15.0 %copy-start.19 = (f32[64]{0:T(128)S(1)}, f32[64]{0:T(128)}, u32[]{:S(2)}) copy-start(f32[64]{0:T(128)} %get-tuple-element.59) | copy-start | bytes 772
  121.8 14.9 %copy-start.20 = (f32[64]{0:T(128)S(1)}, f32[64]{0:T(128)}, u32[]{:S(2)}) copy-start(f32[64]{0:T(128)} %get-tuple-element.67) | copy-start | bytes 772
  123.1 31.1 %all-to-all-start.2 = ((bf16[8,128,1024]{2,1,0:T(8,128)(2,1)}), bf16[8,128,1024]{2,1,0:T(8,128)(2,1)S(1)}, u32[]{:S(2)}, u32[]{:S(2)}) async-start(bf16[8,128,1024]{2,1,0:T(8,128)(2,1)} %bitcast.165), calls=%async_computation.2 | async-start | bytes 4194304 | tf_op jit(solution)/shard_map/all_to_all | solution.py:224
  126.7 10.4 %copy-start.31 = (bf16[2,1024,1024]{2,1,0:T(8,128)(2,1)S(1)}, bf16[2,1024,1024]{2,1,0:T(8,128)(2,1)}, u32[]{:S(2)}) copy-start(bf16[2,1024,1024]{2,1,0:T(8,128)(2,1)} %param.7) | copy-start | bytes 12582916
  126.7 10.3 %collective-permute-start.13 = (bf16[256,1024]{1,0:T(8,128)(2,1)S(1)}, bf16[256,1024]{1,0:T(8,128)(2,1)S(1)}, u32[]{:S(2)}, u32[]{:S(2)}) collective-permute-start(bf16[256,1024]{1,0:T(8,128)(2,1)S(1)} %pad_maximum_fusion.2), channel_id=1, source_target_pairs={{0,4},{4,0},{8,12},{12,8},{16,20},{20,16},{24,28},{28,24},{1,5},{5... | collective-permute-start | bytes 1572872 | tf_op jit(solution)/shard_map/ppermute | solution.py:118
  128.1 5.0 %collective-permute-start.15 = (f32[64]{0:T(128)S(1)}, f32[64]{0:T(128)S(1)}, u32[]{:S(2)}, u32[]{:S(2)}) collective-permute-start(f32[64]{0:T(128)S(1)} %slice_add_fusion.1), channel_id=1, source_target_pairs={{0,3},{1,0},{2,1},{3,2},{4,7},{5,4},{6,5},{7,6},{8,11},{9,8},{10,9... | collective-permute-start | bytes 776 | tf_op jit(solution)/shard_map/ppermute | solution.py:108
  131.4 4.4 %collective-permute-start.16 = (f32[64]{0:T(128)S(1)}, f32[64]{0:T(128)S(1)}, u32[]{:S(2)}, u32[]{:S(2)}) collective-permute-start(f32[64]{0:T(128)S(1)} %slice_add_fusion.1), channel_id=1, source_target_pairs={{0,2},{1,3},{2,0},{3,1},{4,6},{5,7},{6,4},{7,5},{8,10},{9,11},{10,... | collective-permute-start | bytes 776 | tf_op jit(solution)/shard_map/ppermute | solution.py:108
  131.4 5.3 %collective-permute-start.17 = (f32[64]{0:T(128)S(1)}, f32[64]{0:T(128)S(1)}, u32[]{:S(2)}, u32[]{:S(2)}) collective-permute-start(f32[64]{0:T(128)S(1)} %slice_add_fusion.1), channel_id=1, source_target_pairs={{0,1},{1,2},{2,3},{3,0},{4,5},{5,6},{6,7},{7,4},{8,9},{9,10},{10,1... | collective-permute-start | bytes 776 | tf_op jit(solution)/shard_map/ppermute | solution.py:108
  138.8 6.3 %copy-start.13 = (bf16[64,1024]{1,0:T(8,128)(2,1)S(1)}, bf16[64,1024]{1,0:T(8,128)(2,1)}, u32[]{:S(2)}) copy-start(bf16[64,1024]{1,0:T(8,128)(2,1)} %get-tuple-element.25) | copy-start | bytes 393220
  138.8 6.3 %copy-start.14 = (bf16[64,1024]{1,0:T(8,128)(2,1)S(1)}, bf16[64,1024]{1,0:T(8,128)(2,1)}, u32[]{:S(2)}) copy-start(bf16[64,1024]{1,0:T(8,128)(2,1)} %get-tuple-element.23) | copy-start | bytes 393220
  138.8 6.3 %copy-start.15 = (bf16[64,1024]{1,0:T(8,128)(2,1)S(1)}, bf16[64,1024]{1,0:T(8,128)(2,1)}, u32[]{:S(2)}) copy-start(bf16[64,1024]{1,0:T(8,128)(2,1)} %get-tuple-element.21) | copy-start | bytes 393220
  141.0 8.3 %collective-permute-start.18 = (bf16[2,32,1024]{2,1,0:T(8,128)(2,1)S(1)}, bf16[2,32,1024]{2,1,0:T(8,128)(2,1)S(1)}, u32[]{:S(2)}, u32[]{:S(2)}) collective-permute-start(bf16[2,32,1024]{2,1,0:T(8,128)(2,1)S(1)} %get-tuple-element.35), channel_id=1, source_target_pairs={{0,1},{1,2},{2,3},{3,0},{4,5},{5,6},{6,7},{7,4},{8,9},{9,10},{10,1... | collective-permute-start | bytes 393224 | tf_op jit(solution)/shard_map/ppermute | solution.py:108
  141.0 11.6 %collective-permute-start.19 = (bf16[2,32,1024]{2,1,0:T(8,128)(2,1)S(1)}, bf16[2,32,1024]{2,1,0:T(8,128)(2,1)S(1)}, u32[]{:S(2)}, u32[]{:S(2)}) collective-permute-start(bf16[2,32,1024]{2,1,0:T(8,128)(2,1)S(1)} %get-tuple-element.34), channel_id=1, source_target_pairs={{0,2},{1,3},{2,0},{3,1},{4,6},{5,7},{6,4},{7,5},{8,10},{9,11},{10,... | collective-permute-start | bytes 393224 | tf_op jit(solution)/shard_map/ppermute | solution.py:108
  142.2 10.4 %collective-permute-start.20 = (bf16[2,32,1024]{2,1,0:T(8,128)(2,1)S(1)}, bf16[2,32,1024]{2,1,0:T(8,128)(2,1)S(1)}, u32[]{:S(2)}, u32[]{:S(2)}) collective-permute-start(bf16[2,32,1024]{2,1,0:T(8,128)(2,1)S(1)} %get-tuple-element.33), channel_id=1, source_target_pairs={{0,3},{1,0},{2,1},{3,2},{4,7},{5,4},{6,5},{7,6},{8,11},{9,8},{10,9... | collective-permute-start | bytes 393224 | tf_op jit(solution)/shard_map/ppermute | solution.py:108
  (9 other events, 29.9 us)
where the time goes:
time: 157 us; the launch traced here: 156 us
  starting transfers between devices  46.2 us (29%)
  waiting for transfers between devices  45.9 us (29%)
  local copies, waits for them, and re-layouts  29.1 us (19%)
  other arithmetic  16.2 us (10%)
  matrix products  15.7 us (10%)
    ppermute x12, starting transfers between devices, along_hid(): lax.ppermute(values, 'hid', [(a, (a + shift) % hids) for a in range(hids)])  18.5 us
    ppermute x12, waiting for transfers between devices, along_hid(): lax.ppermute(values, 'hid', [(a, (a + shift) % hids) for a in range(hids)])  17.7 us
    dot_general x7, matrix products, matmul(): lax.dot_general(a, b, (contract, ((), ())), preferred_element_type=F32)  15.7 us
    ppermute x4, waiting for transfers between devices, turn_hid(): lax.ppermute(values, 'hid', [(a, a - a % halves + (a % halves + shift) %...  12.1 us
    unnamed x74, local copies, waits for them, and re-layouts  10.4 us
    all_to_all x1, waiting for transfers between devices, shards(): lax.all_to_all(part_out.reshape(seqs, depth // seqs, block), 'seq', 0, 0)  9.67 us
    ppermute x4, starting transfers between devices, turn_hid(): lax.ppermute(values, 'hid', [(a, a - a % halves + (a % halves + shift) %...  8.37 us
    all_to_all x1, starting transfers between devices, shards(): head_got = lax.all_to_all(head_send, 'hid', 0, 0)  6.29 us
  transfers between devices with their start and end apart: 25, of which 12 were waited for; matrix products, arithmetic and copies ran while one was open for 32% of the time, Pallas kernels for 1%

commit v1 on v0

--- a/solution.py
+++ b/solution.py
@@ -124,11 +124,14 @@
     place = jnp.stack([step, j]).astype(jnp.int32)
     relations = range(1, steps)
 
+    group = [hidden] + [flip_seq(hidden, -m) for m in relations]
+
     squares_part = jnp.sum(jnp.square(hidden.astype(F32)), axis=1)
     tail = 8 * block
     small = jnp.concatenate(parts_of(squares_part))
     small = jnp.pad(small, (0, tail - small.size)).reshape(1, 1, 8, block)
-    head_send = w_out.reshape(head_rows, steps, halves, block).transpose(2, 1, 0, 3)
+    head_send = after(w_out, *group[1:]).reshape(head_rows, steps, halves, block)
+    head_send = head_send.transpose(2, 1, 0, 3)
     head_send = head_send.reshape(1, halves, steps * head_rows, block)
     small = jnp.broadcast_to(small, (1, halves, 8, block))
     head_send = jnp.concatenate([head_send, small], axis=2)
@@ -144,7 +147,6 @@
     before = jnp.maximum(step - 1, 0)
     looked = jnp.take(pick(embedding, before), pick(ids, before), axis=0)
 
-    group = [hidden] + [after(flip_seq(hidden, -m), looked) for m in relations]
     w_own = pick(w_in, step)
     proj_parts = matmul(jnp.concatenate(group), w_own, ((1,), (0,)))
     proj_parts = proj_parts.reshape(steps, hids, part, depth)
@@ -201,7 +203,7 @@
     d_round = d_x.astype(BF16)
     d_ratio_part = jnp.sum(d_x * proj, axis=1).reshape(steps, part)
 
-    part_out = matmul(normed_rows, after(d_logit, *received), ((0,), (0,))).astype(BF16)
+    part_out = matmul(normed_rows, after(d_logit, *away), ((0,), (0,))).astype(BF16)
     part_out = lax.all_to_all(part_out.reshape(seqs, depth // seqs, block), "seq", 0, 0)
     part_out = part_out.reshape(groups, steps, hids, head_rows, block).astype(F32).sum(0)
     part_out = part_out.astype(BF16)

time: 157 us -> 170 us (1.083)
  waiting for transfers between devices: 45.9 us -> 60.1 us
  starting transfers between devices: 46.2 us -> 37.8 us
  other arithmetic: 16.2 us -> 20.9 us
  local copies, waits for them, and re-layouts: 29.1 us -> 31.3 us
    all_to_all x1, waiting for transfers between devices: 0.01 us -> 15 us  [shards(): head_got = lax.all_to_all(head_send, 'hid', 0, 0)]
    ppermute x12, waiting for transfers between devices: 17.7 us -> 28.4 us  [along_hid(): lax.ppermute(values, 'hid', [(a, (a + shift) % hids) for a in range(hids)])]
    all_to_all x1, waiting for transfers between devices: 9.67 us -> 0.01 us  [shards(): lax.all_to_all(part_out.reshape(seqs, depth // seqs, block), 'seq', 0, 0)]
    ppermute x4, waiting for transfers between devices: 12.1 us -> 6.13 us  [turn_hid(): lax.ppermute(values, 'hid', [(a, a - a % halves + (a % halves + shift) %...]
    slice x4, local copies, waits for them, and re-layouts: 3.63 us -> 0.07 us  [shards(): member = jnp.concatenate([p[m * part:(m + 1) * part] for p in pieces[::-1]])]
    ppermute x4, starting transfers between devices: 8.37 us -> 5.08 us  [turn_hid(): lax.ppermute(values, 'hid', [(a, a - a % halves + (a % halves + shift) %...]
    mul x4, local copies, waits for them, and re-layouts: 1.85 us -> 5.09 us  [shards(): r * p.astype(F32)]
    ppermute x12, starting transfers between devices: 18.5 us -> 15.5 us  [along_hid(): lax.ppermute(values, 'hid', [(a, (a + shift) % hids) for a in range(hids)])]
  transfers between devices with their start and end apart: 25 -> 25, of which waited for: 12 -> 10; matrix products, arithmetic and copies ran while one was open for 32% -> 32% of each run, Pallas kernels for 1% -> 1%
where the time goes in v1:
time: 170 us; the launch traced here: 169 us
  waiting for transfers between devices  60.1 us (35%)
  starting transfers between devices  37.8 us (22%)
  local copies, waits for them, and re-layouts  31.3 us (18%)
  other arithmetic  20.9 us (12%)
  matrix products  15.7 us (9%)
    ppermute x12, waiting for transfers between devices, along_hid(): lax.ppermute(values, 'hid', [(a, (a + shift) % hids) for a in range(hids)])  28.4 us
    dot_general x7, matrix products, matmul(): lax.dot_general(a, b, (contract, ((), ())), preferred_element_type=F32)  15.7 us
    ppermute x12, starting transfers between devices, along_hid(): lax.ppermute(values, 'hid', [(a, (a + shift) % hids) for a in range(hids)])  15.5 us
    all_to_all x1, waiting for transfers between devices, shards(): head_got = lax.all_to_all(head_send, 'hid', 0, 0)  15 us
    unnamed x78, local copies, waits for them, and re-layouts  9.98 us
    all_to_all x1, waiting for transfers between devices, shards(): head = lax.all_to_all(head_send, 'seq', 0, 0).reshape(depth, block)  8.02 us
    ppermute x4, waiting for transfers between devices, turn_hid(): lax.ppermute(values, 'hid', [(a, a - a % halves + (a % halves + shift) %...  6.13 us
    mul x4, local copies, waits for them, and re-layouts, shards(): r * p.astype(F32)  5.09 us
  transfers between devices with their start and end apart: 25, of which 10 were waited for; matrix products, arithmetic and copies ran while one was open for 32% of the time, Pallas kernels for 1%

profile of v1, /device:TPU:0, one launch (start us, length us, event | category | flops | bytes accessed | tf_op | source)
XLA Modules:
  0.0 168.6 jit_solution(4894705494857958038)
XLA Ops:
  1.3 1.2 multiply_reduce_fusion
  3.3 1.6 constant_dynamic-update-slice_fusion.3
  5.6 3.0 %collective-permute-start.8 = (s32[2,128]{1,0:T(2,128)S(1)}, s32[2,128]{1,0:T(2,128)S(1)}, u32[]{:S(2)}, u32[]{:S(2)}) collective-permute-start(s32[2,128]{1,0:T(2,128)S(1)} %pad_add_fusion), channel_id=1, source_target_pairs={{0,1},{1,0},{2,3},{3,2},{4,5},{5,4},{6,7},{7,6},{8,9},{9,8},{10,11... | collective-permute-start | bytes 3080 | tf_op jit(solution)/shard_map/ppermute | solution.py:111
  9.1 3.8 %gather_fusion = bf16[128,1024]{1,0:T(8,128)(2,1)S(1)} fusion(bf16[2048,1024]{1,0:T(8,128)(2,1)} %bitcast.170, s32[1024]{0:T(1024)S(1)} %pad_clamp_fusion), kind=kCustom, calls=%fused_computation | custom fusion | bytes 524800 | tf_op jit(solution)/shard_map/jit(_take)/gather | solution.py:148
  14.7 3.9 %all-to-all-start = ((bf16[4,72,1024]{2,1,0:T(8,128)(2,1)}), bf16[4,72,1024]{2,1,0:T(8,128)(2,1)S(1)}, u32[]{:S(2)}, u32[]{:S(2)}) async-start(bf16[4,72,1024]{2,1,0:T(8,128)(2,1)} %bitcast.4), calls=%async_computation | async-start | bytes 1179648 | tf_op jit(solution)/shard_map/all_to_all | solution.py:140
  18.7 2.9 %fusion = f32[2,4,64,1024]{3,2,1,0:T(8,128)S(1)} fusion(bf16[2,4,64,1024]{3,2,1,0:T(8,128)(2,1)S(1)} %bitcast.171, bf16[2,1024,1024]{2,1,0:T(8,128)(2,1)} %param.7, s32[]{:T(128)S(6)} %select_n.160), kind=kOutput, calls=%fused_computation.2 | convolution fusion | flops 1073741824 | bytes 5242884 | tf_op jit(solution)/shard_map/dot_general | solution.py:17
  22.5 2.0 %collective-permute-start.2 = (bf16[128,1024]{1,0:T(8,128)(2,1)}, bf16[128,1024]{1,0:T(8,128)(2,1)}, u32[]{:S(2)}, u32[]{:S(2)}) collective-permute-start(bf16[128,1024]{1,0:T(8,128)(2,1)} %bitcast.15), channel_id=1, source_target_pairs={{0,1},{1,2},{2,3},{3,0},{4,5},{5,6},{6,7},{7,4},{8,9},{9,10},{10,1... | collective-permute-start | bytes 786440 | tf_op jit(solution)/shard_map/ppermute | solution.py:108
  24.5 2.4 %collective-permute-start.3 = (bf16[128,1024]{1,0:T(8,128)(2,1)}, bf16[128,1024]{1,0:T(8,128)(2,1)}, u32[]{:S(2)}, u32[]{:S(2)}) collective-permute-start(bf16[128,1024]{1,0:T(8,128)(2,1)} %bitcast.16), channel_id=1, source_target_pairs={{0,2},{1,3},{2,0},{3,1},{4,6},{5,7},{6,4},{7,5},{8,10},{9,11},{10,... | collective-permute-start | bytes 786440 | tf_op jit(solution)/shard_map/ppermute | solution.py:108
  26.9 1.5 collective-permute-start.4
  31.8 15.0 %all-to-all-done = bf16[4,72,1024]{2,1,0:T(8,128)(2,1)S(1)} async-done(((bf16[4,72,1024]{2,1,0:T(8,128)(2,1)}), bf16[4,72,1024]{2,1,0:T(8,128)(2,1)S(1)}, u32[]{:S(2)}, u32[]{:S(2)}) %all-to-all-start) | async-done | bytes 589856 | tf_op jit(solution)/shard_map/all_to_all | solution.py:140
  46.8 1.6 broadcast_in_dim.57
  48.5 3.7 %all-to-all-start.1 = ((bf16[8,128,1024]{2,1,0:T(8,128)(2,1)}), bf16[8,128,1024]{2,1,0:T(8,128)(2,1)S(1)}, u32[]{:S(2)}, u32[]{:S(2)}) async-start(bf16[8,128,1024]{2,1,0:T(8,128)(2,1)} %bitcast.155), calls=%async_computation.1 | async-start | bytes 4194304 | tf_op jit(solution)/shard_map/all_to_all | solution.py:164
  53.7 1.3 reshape.319
  55.0 1.3 reduce_sum.85
  60.3 1.5 multiply_reduce_fusion.3
  62.5 1.6 bitcast_dynamic-update-slice_fusion.1
  64.7 6.1 %collective-permute-done.6 = bf16[128,1024]{1,0:T(8,128)(2,1)} collective-permute-done((bf16[128,1024]{1,0:T(8,128)(2,1)S(1)}, bf16[128,1024]{1,0:T(8,128)(2,1)}, u32[]{:S(2)}, u32[]{:S(2)}) %collective-permute-start.6) | collective-permute-done | bytes 262176 | tf_op jit(solution)/shard_map/ppermute | solution.py:111
  70.8 8.0 %all-to-all-done.1 = bf16[8,128,1024]{2,1,0:T(8,128)(2,1)S(1)} async-done(((bf16[8,128,1024]{2,1,0:T(8,128)(2,1)}), bf16[8,128,1024]{2,1,0:T(8,128)(2,1)S(1)}, u32[]{:S(2)}, u32[]{:S(2)}) %all-to-all-start.1) | async-done | bytes 2097184 | tf_op jit(solution)/shard_map/all_to_all | solution.py:164
  78.8 1.8 %fusion.61 = (f32[256]{0:T(256)S(1)}, f32[256,1024]{1,0:T(8,128)S(1)}) fusion(bf16[1024,1024]{1,0:T(8,128)(2,1)S(1)} %bitcast.153, bf16[128,1024]{1,0:T(8,128)(2,1)} %collective-permute-done.6, bf16[128,1024]{1,0:T(8,128)(2,1)S(1)} %multiply_convert_fusion.5), kind=kOutput, calls=%fused_computation.149 | convolution fusion | flops 538181376 | bytes 3671040 | tf_op jit(solution)/shard_map/dot_general | solution.py:17
  83.1 1.3 mul.174
  84.4 1.2 mul.183
  85.6 1.3 mul.180
  86.9 1.3 mul.177
  90.4 1.6 multiply_convert_fusion
  94.4 2.0 %collective-permute-start.9 = (bf16[128,1024]{1,0:T(8,128)(2,1)}, bf16[128,1024]{1,0:T(8,128)(2,1)}, u32[]{:S(2)}, u32[]{:S(2)}) collective-permute-start(bf16[128,1024]{1,0:T(8,128)(2,1)} %slice.199), channel_id=1, source_target_pairs={{0,1},{1,0},{2,3},{3,2},{4,5},{5,4},{6,7},{7,6},{8,9},{9,8},{10,11... | collective-permute-start | bytes 786440 | tf_op jit(solution)/shard_map/ppermute | solution.py:111
  96.4 3.1 %convolution_convert_fusion = bf16[1024,1024]{1,0:T(8,128)(2,1)} fusion(bf16[256,1024]{1,0:T(8,128)(2,1)S(1)} %multiply_convert_fusion, bf16[128,1024]{1,0:T(8,128)(2,1)} %collective-permute-done.6, bf16[128,1024]{1,0:T(8,128)(2,1)S(1)} %multiply_convert_fusion.5), kind=kOutput, calls=%fused_computation.11 | convolution fusion | flops 538968064 | bytes 3145728 | tf_op jit(solution)/shard_map/dot_general | solution.py:17
  99.5 3.7 %all-to-all-start.3 = ((bf16[8,128,1024]{2,1,0:T(8,128)(2,1)}), bf16[8,128,1024]{2,1,0:T(8,128)(2,1)S(1)}, u32[]{:S(2)}, u32[]{:S(2)}) async-start(bf16[8,128,1024]{2,1,0:T(8,128)(2,1)} %bitcast.157), calls=%async_computation.3 | async-start | bytes 4194304 | tf_op jit(solution)/shard_map/all_to_all | solution.py:207
  103.3 1.3 multiply_reduce_fusion.2
  104.6 1.3 multiply_convert_fusion.4
  106.1 1.5 collective-permute-start.11
  108.1 1.4 multiply_reduce_fusion.1
  109.6 5.1 %collective-permute-done.10 = bf16[128,1024]{1,0:T(8,128)(2,1)S(1)} collective-permute-done((bf16[128,1024]{1,0:T(8,128)(2,1)S(1)}, bf16[128,1024]{1,0:T(8,128)(2,1)S(1)}, u32[]{:S(2)}, u32[]{:S(2)}) %collective-permute-start.10) | collective-permute-done | bytes 262176 | tf_op jit(solution)/shard_map/ppermute | solution.py:108
  114.8 16.2 %collective-permute-done.11 = bf16[128,1024]{1,0:T(8,128)(2,1)S(1)} collective-permute-done((bf16[128,1024]{1,0:T(8,128)(2,1)S(1)}, bf16[128,1024]{1,0:T(8,128)(2,1)S(1)}, u32[]{:S(2)}, u32[]{:S(2)}) %collective-permute-start.11) | collective-permute-done | bytes 262176 | tf_op jit(solution)/shard_map/ppermute | solution.py:108
  131.4 2.6 %convolution_convert_fusion.1 = bf16[1024,1024]{1,0:T(8,128)(2,1)} fusion(bf16[512,1024]{1,0:T(8,128)(2,1)S(1)} %copy-done.11, bf16[128,1024]{1,0:T(8,128)(2,1)S(1)} %multiply_convert_fusion.1, bf16[128,1024]{1,0:T(8,128)(2,1)S(1)} %multiply_convert_fusion.2, bf16[128,1024]{1,0:T(8,128)(2,1)S(1)} %multiply_convert_fusion.3, ...), kind=kOutput, calls=%fused_computation.12 | convolution fusion | flops 1078984704 | bytes 4194304 | tf_op jit(solution)/shard_map/dot_general | solution.py:17
  134.2 4.4 %all-to-all-start.2 = ((bf16[8,128,1024]{2,1,0:T(8,128)(2,1)}), bf16[8,128,1024]{2,1,0:T(8,128)(2,1)}, u32[]{:S(2)}, u32[]{:S(2)}) async-start(bf16[8,128,1024]{2,1,0:T(8,128)(2,1)} %bitcast.164), calls=%async_computation.2 | async-start | bytes 4194304 | tf_op jit(solution)/shard_map/all_to_all | solution.py:226
  139.0 1.8 %collective-permute-start.16 = (f32[64]{0:T(128)S(1)}, f32[64]{0:T(128)S(1)}, u32[]{:S(2)}, u32[]{:S(2)}) collective-permute-start(f32[64]{0:T(128)S(1)} %slice_add_fusion.1), channel_id=1, source_target_pairs={{0,2},{1,3},{2,0},{3,1},{4,6},{5,7},{6,4},{7,5},{8,10},{9,11},{10,... | collective-permute-start | bytes 776 | tf_op jit(solution)/shard_map/ppermute | solution.py:108
  140.8 2.0 %collective-permute-start.17 = (f32[64]{0:T(128)S(1)}, f32[64]{0:T(128)S(1)}, u32[]{:S(2)}, u32[]{:S(2)}) collective-permute-start(f32[64]{0:T(128)S(1)} %slice_add_fusion.1), channel_id=1, source_target_pairs={{0,1},{1,2},{2,3},{3,0},{4,5},{5,6},{6,7},{7,4},{8,9},{9,10},{10,1... | collective-permute-start | bytes 776 | tf_op jit(solution)/shard_map/ppermute | solution.py:108
  143.5 2.6 %collective-permute-done.17 = f32[64]{0:T(128)S(1)} collective-permute-done((f32[64]{0:T(128)S(1)}, f32[64]{0:T(128)S(1)}, u32[]{:S(2)}, u32[]{:S(2)}) %collective-permute-start.17) | collective-permute-done | bytes 288 | tf_op jit(solution)/shard_map/ppermute | solution.py:108
  147.1 1.7 %fusion.2 = f32[256,1024]{1,0:T(8,128)} fusion(bf16[2,1024,1024]{2,1,0:T(8,128)(2,1)S(1)} %copy-done.33, bf16[2,256,1024]{2,1,0:T(8,128)(2,1)S(1)} %bitcast_dynamic-update-slice_fusion), kind=kOutput, calls=%fused_computation.4 | convolution fusion | flops 536870912 | bytes 3670016 | tf_op jit(solution)/shard_map/dot_general | solution.py:17
  149.5 1.2 collective-permute-start.19
  150.7 2.5 %collective-permute-start.20 = (bf16[2,32,1024]{2,1,0:T(8,128)(2,1)S(1)}, bf16[2,32,1024]{2,1,0:T(8,128)(2,1)S(1)}, u32[]{:S(2)}, u32[]{:S(2)}) collective-permute-start(bf16[2,32,1024]{2,1,0:T(8,128)(2,1)S(1)} %get-tuple-element.33), channel_id=1, source_target_pairs={{0,3},{1,0},{2,1},{3,2},{4,7},{5,4},{6,5},{7,6},{8,11},{9,8},{10,9... | collective-permute-start | bytes 393224 | tf_op jit(solution)/shard_map/ppermute | solution.py:108
  153.2 2.8 %fusion.18 = bf16[256,1024]{1,0:T(8,128)(2,1)S(1)} fusion(f32[256,1024]{1,0:T(8,128)} %fusion.2, bf16[2,1024,1024]{2,1,0:T(8,128)(2,1)} %param.7, bf16[2,256,1024]{2,1,0:T(8,128)(2,1)} %copy-done.6, bf16[64,1024]{1,0:T(8,128)(2,1)S(1)} %get-tuple-element.25, bf16[64,1024]{1,0:T(8,128)(2,1)S(1)} %copy-done.8, bf16[64,1024]{1,0:T(8,128)(2,1)S(1)} %copy-done.9, ...), kind=kOutput, calls=%fused_computation.16 | convolution fusion | flops 540278784 | bytes 4720640 | tf_op jit(solution)/shard_map/dot_general | solution.py:17
  156.0 1.3 fusion.28
  157.6 3.5 %collective-permute-done.19.refs_2_ = bf16[2,32,1024]{2,1,0:T(8,128)(2,1)S(1)} collective-permute-done((bf16[2,32,1024]{2,1,0:T(8,128)(2,1)S(1)}, bf16[2,32,1024]{2,1,0:T(8,128)(2,1)S(1)}, u32[]{:S(2)}, u32[]{:S(2)}) %collective-permute-start.19) | collective-permute-done | bytes 131104 | tf_op jit(solution)/shard_map/ppermute | solution.py:108
  161.1 1.5 shard_map.85
  162.6 2.6 %all-to-all-done.2 = bf16[8,128,1024]{2,1,0:T(8,128)(2,1)} async-done(((bf16[8,128,1024]{2,1,0:T(8,128)(2,1)}), bf16[8,128,1024]{2,1,0:T(8,128)(2,1)}, u32[]{:S(2)}, u32[]{:S(2)}) %all-to-all-start.2) | async-done | bytes 2097184 | tf_op jit(solution)/shard_map/all_to_all | solution.py:226
  165.2 2.1 %convert_reduce_fusion = f32[2,128,1024]{2,1,0:T(8,128)S(1)} fusion(bf16[4,2,128,1024]{3,2,1,0:T(8,128)(2,1)} %bitcast.70), kind=kLoop, calls=%fused_computation.1 | loop fusion | flops 1835008 | bytes 3145728 | tf_op jit(solution)/shard_map/reduce_sum | solution.py:227
  167.3 1.3 copy.19
  (164 shorter events, 27.0 us)
Async XLA Ops:
  0.6 12.9 %copy-start.7 = (bf16[32,2,2048]{2,1,0:T(2,128)(2,1)S(1)}, bf16[32,2,2048]{2,1,0:T(2,128)(2,1)}, u32[]{:S(2)}) copy-start(bf16[32,2,2048]{2,1,0:T(2,128)(2,1)} %param.10) | copy-start | bytes 786436
  0.7 12.9 %collective-permute-start = (bf16[256,1024]{1,0:T(8,128)(2,1)}, bf16[256,1024]{1,0:T(8,128)(2,1)S(1)}, u32[]{:S(2)}, u32[]{:S(2)}) collective-permute-start(bf16[256,1024]{1,0:T(8,128)(2,1)} %param.6), channel_id=1, source_target_pairs={{0,4},{4,0},{8,12},{12,8},{16,20},{20,16},{24,28},{28,24},{1,5},{5... | collective-permute-start | bytes 1572872 | tf_op jit(solution)/shard_map/ppermute | solution.py:118
  1.2 3.7 %collective-permute-start.5 = (s32[2,64]{1,0:T(2,128)}, s32[2,64]{1,0:T(2,128)S(1)}, u32[]{:S(2)}, u32[]{:S(2)}) collective-permute-start(s32[2,64]{1,0:T(2,128)} %param.11), channel_id=1, source_target_pairs={{0,4},{4,0},{8,12},{12,8},{16,20},{20,16},{24,28},{28,24},{1,5},{5... | collective-permute-start | bytes 1544 | tf_op jit(solution)/shard_map/ppermute | solution.py:118
  5.6 7.3 %collective-permute-start.8 = (s32[2,128]{1,0:T(2,128)S(1)}, s32[2,128]{1,0:T(2,128)S(1)}, u32[]{:S(2)}, u32[]{:S(2)}) collective-permute-start(s32[2,128]{1,0:T(2,128)S(1)} %pad_add_fusion), channel_id=1, source_target_pairs={{0,1},{1,0},{2,3},{3,2},{4,5},{5,4},{6,7},{7,6},{8,9},{9,8},{10,11... | collective-permute-start | bytes 3080 | tf_op jit(solution)/shard_map/ppermute | solution.py:111
  12.9 5.7 %copy-start.2 = (bf16[256,1024]{1,0:T(8,128)(2,1)S(1)}, bf16[256,1024]{1,0:T(8,128)(2,1)}, u32[]{:S(2)}) copy-start(bf16[256,1024]{1,0:T(8,128)(2,1)} %param.6) | copy-start | bytes 1572868
  13.5 17.5 %copy-start.5 = (bf16[256,1024]{1,0:T(8,128)(2,1)}, bf16[256,1024]{1,0:T(8,128)(2,1)S(1)}, u32[]{:S(2)}) copy-start(bf16[256,1024]{1,0:T(8,128)(2,1)S(1)} %collective-permute-done) | copy-start | bytes 1572868
  14.7 32.0 %all-to-all-start = ((bf16[4,72,1024]{2,1,0:T(8,128)(2,1)}), bf16[4,72,1024]{2,1,0:T(8,128)(2,1)S(1)}, u32[]{:S(2)}, u32[]{:S(2)}) async-start(bf16[4,72,1024]{2,1,0:T(8,128)(2,1)} %bitcast.4), calls=%async_computation | async-start | bytes 1179648 | tf_op jit(solution)/shard_map/all_to_all | solution.py:140
  22.5 37.8 %collective-permute-start.2 = (bf16[128,1024]{1,0:T(8,128)(2,1)}, bf16[128,1024]{1,0:T(8,128)(2,1)}, u32[]{:S(2)}, u32[]{:S(2)}) collective-permute-start(bf16[128,1024]{1,0:T(8,128)(2,1)} %bitcast.15), channel_id=1, source_target_pairs={{0,1},{1,2},{2,3},{3,0},{4,5},{5,6},{6,7},{7,4},{8,9},{9,10},{10,1... | collective-permute-start | bytes 786440 | tf_op jit(solution)/shard_map/ppermute | solution.py:108
  24.5 35.8 %collective-permute-start.3 = (bf16[128,1024]{1,0:T(8,128)(2,1)}, bf16[128,1024]{1,0:T(8,128)(2,1)}, u32[]{:S(2)}, u32[]{:S(2)}) collective-permute-start(bf16[128,1024]{1,0:T(8,128)(2,1)} %bitcast.16), channel_id=1, source_target_pairs={{0,2},{1,3},{2,0},{3,1},{4,6},{5,7},{6,4},{7,5},{8,10},{9,11},{10,... | collective-permute-start | bytes 786440 | tf_op jit(solution)/shard_map/ppermute | solution.py:108
  26.9 33.4 %collective-permute-start.4 = (bf16[128,1024]{1,0:T(8,128)(2,1)}, bf16[128,1024]{1,0:T(8,128)(2,1)}, u32[]{:S(2)}, u32[]{:S(2)}) collective-permute-start(bf16[128,1024]{1,0:T(8,128)(2,1)} %bitcast.17), channel_id=1, source_target_pairs={{0,3},{1,0},{2,1},{3,2},{4,7},{5,4},{6,5},{7,6},{8,11},{9,8},{10,9... | collective-permute-start | bytes 786440 | tf_op jit(solution)/shard_map/ppermute | solution.py:108
  48.5 30.4 %all-to-all-start.1 = ((bf16[8,128,1024]{2,1,0:T(8,128)(2,1)}), bf16[8,128,1024]{2,1,0:T(8,128)(2,1)S(1)}, u32[]{:S(2)}, u32[]{:S(2)}) async-start(bf16[8,128,1024]{2,1,0:T(8,128)(2,1)} %bitcast.155), calls=%async_computation.1 | async-start | bytes 4194304 | tf_op jit(solution)/shard_map/all_to_all | solution.py:164
  56.3 2.0 %collective-permute-start.1 = (f32[256]{0:T(256)}, f32[256]{0:T(256)}, u32[]{:S(2)}, u32[]{:S(2)}) collective-permute-start(f32[256]{0:T(256)} %reduce_sum.85), channel_id=1, source_target_pairs={{0,4},{4,0},{8,12},{12,8},{16,20},{20,16},{24,28},{28,24},{1,5},{5... | collective-permute-start | bytes 3080 | tf_op jit(solution)/shard_map/ppermute | solution.py:118
  60.3 3.8 %copy-start.16 = (f32[2,1,64]{2,0,1:T(2,128)S(1)}, f32[2,1,64]{2,0,1:T(2,128)}, u32[]{:S(2)}) copy-start(f32[2,1,64]{2,0,1:T(2,128)} %get-tuple-element.45) | copy-start | bytes 1540
  62.4 8.4 %collective-permute-start.6 = (bf16[128,1024]{1,0:T(8,128)(2,1)S(1)}, bf16[128,1024]{1,0:T(8,128)(2,1)}, u32[]{:S(2)}, u32[]{:S(2)}) collective-permute-start(bf16[128,1024]{1,0:T(8,128)(2,1)S(1)} %multiply_convert_fusion.5), channel_id=1, source_target_pairs={{0,1},{1,0},{2,3},{3,2},{4,5},{5,4},{6,7},{7,6},{8,9},{9,8},{10,11... | collective-permute-start | bytes 786440 | tf_op jit(solution)/shard_map/ppermute | solution.py:111
  82.5 5.7 %collective-permute-start.7 = (f32[2,2,128]{2,1,0:T(2,128)}, f32[2,2,128]{2,1,0:T(2,128)}, u32[]{:S(2)}, u32[]{:S(2)}) collective-permute-start(f32[2,2,128]{2,1,0:T(2,128)} %pad_maximum_fusion.5), channel_id=1, source_target_pairs={{0,1},{1,0},{2,3},{3,2},{4,5},{5,4},{6,7},{7,6},{8,9},{9,8},{10,11... | collective-permute-start | bytes 6152 | tf_op jit(solution)/shard_map/ppermute | solution.py:111
  94.4 8.9 %collective-permute-start.9 = (bf16[128,1024]{1,0:T(8,128)(2,1)}, bf16[128,1024]{1,0:T(8,128)(2,1)}, u32[]{:S(2)}, u32[]{:S(2)}) collective-permute-start(bf16[128,1024]{1,0:T(8,128)(2,1)} %slice.199), channel_id=1, source_target_pairs={{0,1},{1,0},{2,3},{3,2},{4,5},{5,4},{6,7},{7,6},{8,9},{9,8},{10,11... | collective-permute-start | bytes 786440 | tf_op jit(solution)/shard_map/ppermute | solution.py:111
  99.5 5.1 %copy-start.27 = (f32[128]{0:T(128)S(1)}, f32[128]{0:T(128)}, u32[]{:S(2)}) copy-start(f32[128]{0:T(128)} %copy-done.26) | copy-start | bytes 1540
  99.5 5.1 %copy-start.31 = (f32[128]{0:T(128)S(1)}, f32[128]{0:T(128)}, u32[]{:S(2)}) copy-start(f32[128]{0:T(128)} %get-tuple-element.63) | copy-start | bytes 1540
  99.5 5.1 %copy-start.32 = (f32[128]{0:T(128)S(1)}, f32[128]{0:T(128)}, u32[]{:S(2)}) copy-start(f32[128]{0:T(128)} %mul.174) | copy-start | bytes 1540
  99.5 34.6 %all-to-all-start.3 = ((bf16[8,128,1024]{2,1,0:T(8,128)(2,1)}), bf16[8,128,1024]{2,1,0:T(8,128)(2,1)S(1)}, u32[]{:S(2)}, u32[]{:S(2)}) async-start(bf16[8,128,1024]{2,1,0:T(8,128)(2,1)} %bitcast.157), calls=%async_computation.3 | async-start | bytes 4194304 | tf_op jit(solution)/shard_map/all_to_all | solution.py:207
  106.0 25.1 %copy-start.30 = (f32[128]{0:T(128)S(1)}, f32[128]{0:T(128)}, u32[]{:S(2)}) copy-start(f32[128]{0:T(128)} %mul.183) | copy-start | bytes 1540
  106.0 8.8 %collective-permute-start.10 = (bf16[128,1024]{1,0:T(8,128)(2,1)S(1)}, bf16[128,1024]{1,0:T(8,128)(2,1)S(1)}, u32[]{:S(2)}, u32[]{:S(2)}) collective-permute-start(bf16[128,1024]{1,0:T(8,128)(2,1)S(1)} %get-tuple-element.16), channel_id=1, source_target_pairs={{0,3},{1,0},{2,1},{3,2},{4,7},{5,4},{6,5},{7,6},{8,11},{9,8},{10,9... | collective-permute-start | bytes 786440 | tf_op jit(solution)/shard_map/ppermute | solution.py:108
  106.1 24.9 %collective-permute-start.11 = (bf16[128,1024]{1,0:T(8,128)(2,1)S(1)}, bf16[128,1024]{1,0:T(8,128)(2,1)S(1)}, u32[]{:S(2)}, u32[]{:S(2)}) collective-permute-start(bf16[128,1024]{1,0:T(8,128)(2,1)S(1)} %get-tuple-element.16), channel_id=1, source_target_pairs={{0,2},{1,3},{2,0},{3,1},{4,6},{5,7},{6,4},{7,5},{8,10},{9,11},{10,... | collective-permute-start | bytes 786440 | tf_op jit(solution)/shard_map/ppermute | solution.py:108
  107.5 23.5 %collective-permute-start.12 = (bf16[128,1024]{1,0:T(8,128)(2,1)S(1)}, bf16[128,1024]{1,0:T(8,128)(2,1)S(1)}, u32[]{:S(2)}, u32[]{:S(2)}) collective-permute-start(bf16[128,1024]{1,0:T(8,128)(2,1)S(1)} %get-tuple-element.16), channel_id=1, source_target_pairs={{0,1},{1,2},{2,3},{3,0},{4,5},{5,6},{6,7},{7,4},{8,9},{9,10},{10,1... | collective-permute-start | bytes 786440 | tf_op jit(solution)/shard_map/ppermute | solution.py:108
  108.1 23.1 %copy-start.29 = (f32[128]{0:T(128)S(1)}, f32[128]{0:T(128)}, u32[]{:S(2)}) copy-start(f32[128]{0:T(128)} %mul.180) | copy-start | bytes 1540
  108.1 23.2 %copy-start.28 = (f32[128]{0:T(128)S(1)}, f32[128]{0:T(128)}, u32[]{:S(2)}) copy-start(f32[128]{0:T(128)} %mul.177) | copy-start | bytes 1540
  108.1 23.3 %copy-start.11 = (bf16[512,1024]{1,0:T(8,128)(2,1)S(1)}, bf16[512,1024]{1,0:T(8,128)(2,1)}, u32[]{:S(2)}) copy-start(bf16[512,1024]{1,0:T(8,128)(2,1)} %bitcast_dynamic-update-slice_fusion.1) | copy-start | bytes 3145732
  109.6 29.4 %collective-permute-start.14 = (f32[64]{0:T(128)S(1)}, f32[64]{0:T(128)S(1)}, u32[]{:S(2)}, u32[]{:S(2)}) collective-permute-start(f32[64]{0:T(128)S(1)} %slice.132), channel_id=1, source_target_pairs={{0,4},{4,0},{8,12},{12,8},{16,20},{20,16},{24,28},{28,24},{1,5},{5... | collective-permute-start | bytes 776 | tf_op jit(solution)/shard_map/ppermute | solution.py:118
  134.1 8.7 %copy-start.22 = (f32[64,1]{0,1:T(1,128)S(1)}, f32[64,1]{0,1:T(1,128)}, u32[]{:S(2)}) copy-start(f32[64,1]{0,1:T(1,128)} %get-tuple-element.54) | copy-start | bytes 772
  134.1 8.7 %copy-start.23 = (f32[64,1]{0,1:T(1,128)S(1)}, f32[64,1]{0,1:T(1,128)}, u32[]{:S(2)}) copy-start(f32[64,1]{0,1:T(1,128)} %get-tuple-element.70) | copy-start | bytes 772
  134.1 8.7 %copy-start.24 = (f32[64,1]{0,1:T(1,128)S(1)}, f32[64,1]{0,1:T(1,128)}, u32[]{:S(2)}) copy-start(f32[64,1]{0,1:T(1,128)} %get-tuple-element.58) | copy-start | bytes 772
  134.1 8.7 %copy-start.25 = (f32[64,1]{0,1:T(1,128)S(1)}, f32[64,1]{0,1:T(1,128)}, u32[]{:S(2)}) copy-start(f32[64,1]{0,1:T(1,128)} %get-tuple-element.68) | copy-start | bytes 772
  134.1 12.0 %copy-start.18 = (f32[64]{0:T(128)S(1)}, f32[64]{0:T(128)}, u32[]{:S(2)}) copy-start(f32[64]{0:T(128)} %get-tuple-element.55) | copy-start | bytes 772
  134.1 12.0 %copy-start.19 = (f32[64]{0:T(128)S(1)}, f32[64]{0:T(128)}, u32[]{:S(2)}) copy-start(f32[64]{0:T(128)} %get-tuple-element.69) | copy-start | bytes 772
  134.1 12.0 %copy-start.20 = (f32[64]{0:T(128)S(1)}, f32[64]{0:T(128)}, u32[]{:S(2)}) copy-start(f32[64]{0:T(128)} %get-tuple-element.59) | copy-start | bytes 772
  134.1 12.0 %copy-start.21 = (f32[64]{0:T(128)S(1)}, f32[64]{0:T(128)}, u32[]{:S(2)}) copy-start(f32[64]{0:T(128)} %get-tuple-element.67) | copy-start | bytes 772
  134.2 31.0 %all-to-all-start.2 = ((bf16[8,128,1024]{2,1,0:T(8,128)(2,1)}), bf16[8,128,1024]{2,1,0:T(8,128)(2,1)}, u32[]{:S(2)}, u32[]{:S(2)}) async-start(bf16[8,128,1024]{2,1,0:T(8,128)(2,1)} %bitcast.164), calls=%async_computation.2 | async-start | bytes 4194304 | tf_op jit(solution)/shard_map/all_to_all | solution.py:226
  138.5 8.5 %copy-start.33 = (bf16[2,1024,1024]{2,1,0:T(8,128)(2,1)S(1)}, bf16[2,1024,1024]{2,1,0:T(8,128)(2,1)}, u32[]{:S(2)}) copy-start(bf16[2,1024,1024]{2,1,0:T(8,128)(2,1)} %param.7) | copy-start | bytes 12582916
  138.6 8.4 %collective-permute-start.13 = (bf16[256,1024]{1,0:T(8,128)(2,1)S(1)}, bf16[256,1024]{1,0:T(8,128)(2,1)S(1)}, u32[]{:S(2)}, u32[]{:S(2)}) collective-permute-start(bf16[256,1024]{1,0:T(8,128)(2,1)S(1)} %pad_maximum_fusion.2), channel_id=1, source_target_pairs={{0,4},{4,0},{8,12},{12,8},{16,20},{20,16},{24,28},{28,24},{1,5},{5... | collective-permute-start | bytes 1572872 | tf_op jit(solution)/shard_map/ppermute | solution.py:118
  139.0 3.8 %collective-permute-start.15 = (f32[64]{0:T(128)S(1)}, f32[64]{0:T(128)S(1)}, u32[]{:S(2)}, u32[]{:S(2)}) collective-permute-start(f32[64]{0:T(128)S(1)} %slice_add_fusion.1), channel_id=1, source_target_pairs={{0,3},{1,0},{2,1},{3,2},{4,7},{5,4},{6,5},{7,6},{8,11},{9,8},{10,9... | collective-permute-start | bytes 776 | tf_op jit(solution)/shard_map/ppermute | solution.py:108
  139.0 4.5 %collective-permute-start.16 = (f32[64]{0:T(128)S(1)}, f32[64]{0:T(128)S(1)}, u32[]{:S(2)}, u32[]{:S(2)}) collective-permute-start(f32[64]{0:T(128)S(1)} %slice_add_fusion.1), channel_id=1, source_target_pairs={{0,2},{1,3},{2,0},{3,1},{4,6},{5,7},{6,4},{7,5},{8,10},{9,11},{10,... | collective-permute-start | bytes 776 | tf_op jit(solution)/shard_map/ppermute | solution.py:108
  140.8 5.3 %collective-permute-start.17 = (f32[64]{0:T(128)S(1)}, f32[64]{0:T(128)S(1)}, u32[]{:S(2)}, u32[]{:S(2)}) collective-permute-start(f32[64]{0:T(128)S(1)} %slice_add_fusion.1), channel_id=1, source_target_pairs={{0,1},{1,2},{2,3},{3,0},{4,5},{5,6},{6,7},{7,4},{8,9},{9,10},{10,1... | collective-permute-start | bytes 776 | tf_op jit(solution)/shard_map/ppermute | solution.py:108
  148.8 4.4 %copy-start.8 = (bf16[64,1024]{1,0:T(8,128)(2,1)S(1)}, bf16[64,1024]{1,0:T(8,128)(2,1)}, u32[]{:S(2)}) copy-start(bf16[64,1024]{1,0:T(8,128)(2,1)} %get-tuple-element.23) | copy-start | bytes 393220
  148.8 4.4 %copy-start.9 = (bf16[64,1024]{1,0:T(8,128)(2,1)S(1)}, bf16[64,1024]{1,0:T(8,128)(2,1)}, u32[]{:S(2)}) copy-start(bf16[64,1024]{1,0:T(8,128)(2,1)} %get-tuple-element.21) | copy-start | bytes 393220
  148.8 4.4 %copy-start.10 = (bf16[64,1024]{1,0:T(8,128)(2,1)S(1)}, bf16[64,1024]{1,0:T(8,128)(2,1)}, u32[]{:S(2)}) copy-start(bf16[64,1024]{1,0:T(8,128)(2,1)} %get-tuple-element.19) | copy-start | bytes 393220
  149.3 8.3 %collective-permute-start.18 = (bf16[2,32,1024]{2,1,0:T(8,128)(2,1)S(1)}, bf16[2,32,1024]{2,1,0:T(8,128)(2,1)S(1)}, u32[]{:S(2)}, u32[]{:S(2)}) collective-permute-start(bf16[2,32,1024]{2,1,0:T(8,128)(2,1)S(1)} %get-tuple-element.35), channel_id=1, source_target_pairs={{0,1},{1,2},{2,3},{3,0},{4,5},{5,6},{6,7},{7,4},{8,9},{9,10},{10,1... | collective-permute-start | bytes 393224 | tf_op jit(solution)/shard_map/ppermute | solution.py:108
  149.5 11.6 %collective-permute-start.19 = (bf16[2,32,1024]{2,1,0:T(8,128)(2,1)S(1)}, bf16[2,32,1024]{2,1,0:T(8,128)(2,1)S(1)}, u32[]{:S(2)}, u32[]{:S(2)}) collective-permute-start(bf16[2,32,1024]{2,1,0:T(8,128)(2,1)S(1)} %get-tuple-element.34), channel_id=1, source_target_pairs={{0,2},{1,3},{2,0},{3,1},{4,6},{5,7},{6,4},{7,5},{8,10},{9,11},{10,... | collective-permute-start | bytes 393224 | tf_op jit(solution)/shard_map/ppermute | solution.py:108
  150.7 10.4 %collective-permute-start.20 = (bf16[2,32,1024]{2,1,0:T(8,128)(2,1)S(1)}, bf16[2,32,1024]{2,1,0:T(8,128)(2,1)S(1)}, u32[]{:S(2)}, u32[]{:S(2)}) collective-permute-start(bf16[2,32,1024]{2,1,0:T(8,128)(2,1)S(1)} %get-tuple-element.33), channel_id=1, source_target_pairs={{0,3},{1,0},{2,1},{3,2},{4,7},{5,4},{6,5},{7,6},{8,11},{9,8},{10,9... | collective-permute-start | bytes 393224 | tf_op jit(solution)/shard_map/ppermute | solution.py:108
  (11 other events, 23.3 us)

commit v2 on v1

--- a/solution.py
+++ b/solution.py
@@ -21,7 +21,7 @@
     return lax.optimization_barrier((value, *others))[0]
 
 
-VMEM = pltpu.CompilerParams(vmem_limit_bytes=16 * 2**20)
+VMEM = pltpu.CompilerParams(vmem_limit_bytes=32 * 2**20)
 
 
 def whole(shape):
@@ -82,6 +82,83 @@
         [],
         hids * steps * rows * block,
         tuple(pieces),
+    )
+
+
+def input_gradient(place, pieces, turned, ratio, seqs):
+    hids, steps = len(pieces), len(turned)
+    owned, depth = pieces[0].shape
+    units, rows = turned[0].shape
+    part = owned // steps
+    slice_wide = depth // seqs
+    wide = max(min(256, depth), slice_wide)
+    count = wide // slice_wide
+
+    def kernel(place_ref, *refs):
+        chunks, turned, ratio = refs[:hids], refs[hids : hids + steps], refs[hids + steps]
+        out, plain, scaled = refs[hids + steps + 1], refs[hids + steps + 2 : -1], refs[-1]
+        j = place_ref[1]
+        for r in range(hids):
+            to = pl.multiple_of(lax.rem(j - r + hids, hids) * part, part)
+            for m in range(steps):
+                values = chunks[r][m * part : (m + 1) * part, :]
+                plain[m][pl.ds(to, part), :] = values
+                factor = ratio[m, pl.ds(to, part), :]
+                scaled[m, pl.ds(to, part), :] = (values.astype(F32) * factor).astype(BF16)
+        total = jnp.dot(turned[0][...], scaled[0], preferred_element_type=F32)
+        for m in range(1, steps):
+            total = total + jnp.dot(turned[m][...], scaled[m], preferred_element_type=F32)
+        for k in range(count):
+            out[k] = total[:, k * slice_wide : (k + 1) * slice_wide].astype(BF16)
+
+    return call(
+        kernel,
+        place,
+        depth // wide,
+        [pl.BlockSpec((owned, wide), lambda n, place: (0, n))] * hids
+        + [whole((units, rows))] * steps
+        + [whole((steps, rows, 1))],
+        [pl.BlockSpec((count, units, slice_wide), lambda n, place: (n, 0, 0))]
+        + [pl.BlockSpec((rows, wide), lambda n, place: (0, n))] * steps,
+        [jax.ShapeDtypeStruct((seqs, units, slice_wide), BF16)]
+        + [jax.ShapeDtypeStruct((rows, depth), BF16)] * steps,
+        [pltpu.VMEM((steps, rows, wide), BF16)],
+        2 * steps * rows * units * depth,
+        (*pieces, *turned, ratio),
+    )
+
+
+def hidden_gradient(place, d_rows, w_in, hidden, factors):
+    steps, units, depth = w_in.shape
+    rows = hidden.shape[0]
+    wide = min(256, units)
+
+    def kernel(place_ref, *refs):
+        d_rows, w, hidden, factors, out = refs[:steps], refs[-4], refs[-3], refs[-2], refs[-1]
+        total = None
+        for r in range(steps):
+            which = lax.rem(place_ref[0] - r + steps, steps)
+            term = lax.dot_general(
+                d_rows[r][...], w[which], (((1,), (1,)), ((), ())), preferred_element_type=F32
+            )
+            total = term if total is None else total + term
+        out[...] = (factors[0] * total - factors[1] * hidden[...].astype(F32)).astype(BF16)
+
+    return call(
+        kernel,
+        place,
+        units // wide,
+        [whole((rows, depth))] * steps
+        + [
+            pl.BlockSpec((steps, wide, depth), lambda n, place: (0, n, 0)),
+            pl.BlockSpec((rows, wide), lambda n, place: (0, n)),
+            whole((2, rows, 1)),
+        ],
+        pl.BlockSpec((rows, wide), lambda n, place: (0, n)),
+        jax.ShapeDtypeStruct((rows, units), BF16),
+        [],
+        2 * steps * rows * units * depth,
+        (*d_rows, w_in, hidden, factors),
     )
 
 
@@ -142,20 +219,21 @@
     squares = head_got[:, steps * head_rows :].reshape(hids, tail)[:, : EXACT * rows]
     squares = jnp.sum(squares.astype(F32).reshape(hids * EXACT, rows), axis=0)
 
-    ids = jnp.concatenate([codebook_ids] + [flip_seq(codebook_ids, -m) for m in relations], axis=1)
+    w_own = pick(w_in, step)
+    proj_parts = matmul(jnp.concatenate(group), w_own, ((1,), (0,)))
+    proj_parts = proj_parts.reshape(steps, hids, part, depth)
+
+    def owner_block(index):
+        return lax.dynamic_index_in_dim(proj_parts, index, 1, False).reshape(owned, depth)
+
+    send = [owner_block((j + shift) % hids).astype(BF16) for shift in range(1, hids)]
+    received = [along_hid(send[shift - 1], shift) for shift in range(1, hids)]
+
+    ids = after(codebook_ids, *send)
+    ids = jnp.concatenate([ids] + [flip_seq(ids, -m) for m in relations], axis=1)
     ids_rows = [ids] + [turn_hid(ids, -k) for k in range(1, halves)]
     before = jnp.maximum(step - 1, 0)
     looked = jnp.take(pick(embedding, before), pick(ids, before), axis=0)
-
-    w_own = pick(w_in, step)
-    proj_parts = matmul(jnp.concatenate(group), w_own, ((1,), (0,)))
-    proj_parts = proj_parts.reshape(steps, hids, part, depth)
-
-    def owner_block(index):
-        return lax.dynamic_index_in_dim(proj_parts, index, 1, False).reshape(owned, depth)
-
-    send = [owner_block((j + shift) % hids).astype(BF16) for shift in range(1, hids)]
-    received = [along_hid(send[shift - 1], shift) for shift in range(1, hids)]
 
     head_send = after(head_mid, *send).transpose(1, 0, 2, 3)
     head_send = head_send.reshape(steps, hids * head_rows, block)
@@ -165,7 +243,6 @@
 
     squares = jnp.stack([squares] + [flip_seq(squares, -m) for m in relations])
     ratio_group = lax.rsqrt(squares / width_in + 1e-06).reshape(steps, hids, part)
-    order = [(j - shift) % hids for shift in range(hids)]
 
     ratio = lax.dynamic_index_in_dim(ratio_group, j, 1, False).reshape(owned, 1)
     proj = owner_block(j)
@@ -213,39 +290,26 @@
     sums = [along_hid(p, shift) if shift else p for shift, p in enumerate(sums)]
     grad_out = head_gradient(place, sums, halves)
 
+    turned = [after(h, normed).T for h in group]
     pieces = [d_round] + [along_hid(d_round, shift) for shift in range(1, hids)]
-    ordered = [g.reshape(hids, part, units) for g in group]
-    hidden_rows = jnp.concatenate([pick(g, o) for o in order for g in ordered])
-    ratio_rows = [
-        lax.dynamic_index_in_dim(ratio_group, o, 1, False).reshape(owned, 1) for o in order
-    ]
-    scaled = jnp.concatenate(
-        [(r * p.astype(F32)).astype(BF16) for r, p in zip(ratio_rows, pieces)]
-    )
-    share = matmul(scaled, hidden_rows, ((0,), (0,))).astype(BF16)
-    share = lax.all_to_all(share.reshape(seqs, depth // seqs, units), "seq", 0, 0)
-    share = share.reshape(groups, steps, depth // seqs, units).astype(F32).sum(0)
-    grad_in = share.transpose(0, 2, 1)
+    ratio_rows = ratio_group.reshape(steps, rows, 1)
+    share, mine, *others = input_gradient(place, pieces, turned, ratio_rows, seqs)
+    share = lax.all_to_all(share, "seq", 0, 0)
+    grad_in = share.reshape(groups, steps, units, depth // seqs).astype(F32).sum(0)
 
     d_ratio = d_ratio_part[0]
     for m in relations:
         d_ratio += flip_seq(d_ratio_part[m], m)
-    d_ratio = [d_ratio] + [along_hid(d_ratio, shift) for shift in range(1, hids)]
-    d_ratio = jnp.concatenate(d_ratio[::-1])[:, None]
-    back_rows = jnp.zeros((steps, rows, depth), BF16)
-    for m in range(steps):
-        member = jnp.concatenate([p[m * part : (m + 1) * part] for p in pieces[::-1]])
-        member = flip_seq(member, m) if m else member
-        back_rows = lax.dynamic_update_index_in_dim(back_rows, member, (step - m) % steps, 0)
-    back = matmul(back_rows[0], w_in[0], ((1,), (1,)))
-    for s in range(1, steps):
-        back += matmul(back_rows[s], w_in[s], ((1,), (1,)))
-    ratio_own = jnp.concatenate([r[:part] for r in ratio_rows[::-1]])
-    hidden_own = jnp.concatenate([pick(ordered[0], o) for o in order[::-1]]).astype(F32)
-    correction = ratio_own**3 * d_ratio / width_in
-    grad_hidden = (ratio_own * back - correction * hidden_own).astype(BF16)
-    grad_hidden = jnp.concatenate([grad_hidden, grad_hidden])
-    grad_hidden = lax.dynamic_slice_in_dim(grad_hidden, (hids - 1 - j) * part, rows, 0)
+    d_rows = jnp.broadcast_to(d_ratio, (hids, part))
+    for shift in range(1, hids):
+        d_rows = lax.dynamic_update_index_in_dim(
+            d_rows, along_hid(d_ratio, shift), (j - shift) % hids, 0
+        )
+    ratio_own = ratio_group[0].reshape(rows)
+    correction = ratio_own**3 * d_rows.reshape(rows) / width_in
+    factors = jnp.stack([ratio_own, correction])[:, :, None]
+    mine = [mine] + [flip_seq(others[m - 1], m) for m in relations]
+    grad_hidden = hidden_gradient(place, mine, w_in, hidden, factors)
     return (grad_hidden, grad_in, grad_out)
 
 

time: 170 us -> 164 us (0.965)
  starting transfers between devices: 37.8 us -> 58.1 us
  local copies, waits for them, and re-layouts: 31.3 us -> 17.6 us
  other arithmetic: 20.9 us -> 9.47 us
  Pallas kernels: 1.47 us -> 9.25 us
  matrix products: 15.7 us -> 9.77 us
  waiting for transfers between devices: 60.1 us -> 57.3 us
    ppermute x4, starting transfers between devices: 5.08 us -> 14.4 us  [turn_hid(): lax.ppermute(values, 'hid', [(a, a - a % halves + (a % halves + shift) %...]
    all_to_all x1, waiting for transfers between devices: 15 us -> 6.69 us  [shards(): head_got = lax.all_to_all(head_send, 'hid', 0, 0)]
    pallas_call x1 -> x3, Pallas kernels: 1.47 us -> 9.25 us  [call(): pl.pallas_call(kernel, grid_spec=pltpu.PrefetchScalarGridSpec(num_scalar_...]
    ppermute x4, waiting for transfers between devices: 6.13 us -> 13.7 us  [turn_hid(): lax.ppermute(values, 'hid', [(a, a - a % halves + (a % halves + shift) %...]
    ppermute x12, starting transfers between devices: 15.5 us -> 22.8 us  [along_hid(): lax.ppermute(values, 'hid', [(a, (a + shift) % hids) for a in range(hids)])]
    dot_general x7 -> x4, matrix products: 15.7 us -> 9.77 us  [matmul(): lax.dot_general(a, b, (contract, ((), ())), preferred_element_type=F32)]
    mul x4 -> x0, local copies, waits for them, and re-layouts: 5.09 us -> none  [shards(): r * p.astype(F32)]
    all_to_all x1, waiting for transfers between devices: 8.02 us -> 3.26 us  [shards(): head = lax.all_to_all(head_send, 'seq', 0, 0).reshape(depth, block)]
  transfers between devices with their start and end apart: 25 -> 25, of which waited for: 10 -> 15; matrix products, arithmetic and copies ran while one was open for 32% -> 10% of each run, Pallas kernels for 1% -> 6%
where the time goes in v2:
time: 164 us; the launch traced here: 163 us
  starting transfers between devices  58.1 us (35%)
  waiting for transfers between devices  57.3 us (35%)
  local copies, waits for them, and re-layouts  17.6 us (11%)
  matrix products  9.77 us (6%)
  other arithmetic  9.47 us (6%)
  Pallas kernels  9.25 us (6%)
    ppermute x12, waiting for transfers between devices, along_hid(): lax.ppermute(values, 'hid', [(a, (a + shift) % hids) for a in range(hids)])  31.6 us
    ppermute x12, starting transfers between devices, along_hid(): lax.ppermute(values, 'hid', [(a, (a + shift) % hids) for a in range(hids)])  22.8 us
    ppermute x4, starting transfers between devices, turn_hid(): lax.ppermute(values, 'hid', [(a, a - a % halves + (a % halves + shift) %...  14.4 us
    ppermute x4, waiting for transfers between devices, turn_hid(): lax.ppermute(values, 'hid', [(a, a - a % halves + (a % halves + shift) %...  13.7 us
    dot_general x4, matrix products, matmul(): lax.dot_general(a, b, (contract, ((), ())), preferred_element_type=F32)  9.77 us
    pallas_call x3, Pallas kernels, call(): pl.pallas_call(kernel, grid_spec=pltpu.PrefetchScalarGridSpec(num_scalar_...  9.25 us
    unnamed x35, local copies, waits for them, and re-layouts  6.85 us
    all_to_all x1, waiting for transfers between devices, shards(): head_got = lax.all_to_all(head_send, 'hid', 0, 0)  6.69 us
  transfers between devices with their start and end apart: 25, of which 15 were waited for; matrix products, arithmetic and copies ran while one was open for 10% of the time, Pallas kernels for 6%

profile of v2, /device:TPU:0, one launch (start us, length us, event | category | flops | bytes accessed | tf_op | source)
XLA Modules:
  0.0 162.6 jit_solution(1893410976036087952)
XLA Ops:
  0.6 1.2 copy.56
  2.4 1.2 multiply_reduce_fusion
  4.0 1.1 reshape.231
  5.2 0.9 broadcast_in_dim.57
  6.1 6.2 %all-to-all-start = ((bf16[4,72,1024]{2,1,0:T(8,128)(2,1)}), bf16[4,72,1024]{2,1,0:T(8,128)(2,1)S(1)}, u32[]{:S(2)}, u32[]{:S(2)}) async-start(bf16[4,72,1024]{2,1,0:T(8,128)(2,1)} %bitcast.6), calls=%async_computation | async-start | bytes 1179648 | tf_op jit(solution)/shard_map/all_to_all | solution.py:217
  13.0 2.9 %fusion = f32[2,4,64,1024]{3,2,1,0:T(8,128)S(1)} fusion(bf16[2,4,64,1024]{3,2,1,0:T(8,128)(2,1)S(1)} %bitcast.98, bf16[2,1024,1024]{2,1,0:T(8,128)(2,1)} %refs_2_.1, s32[]{:T(128)S(6)} %select_n.119), kind=kOutput, calls=%fused_computation.2 | convolution fusion | flops 1073741824 | bytes 5242884 | tf_op jit(solution)/shard_map/dot_general | solution.py:17
  16.7 3.8 %collective-permute-start.4 = (bf16[128,1024]{1,0:T(8,128)(2,1)}, bf16[128,1024]{1,0:T(8,128)(2,1)S(1)}, u32[]{:S(2)}, u32[]{:S(2)}) collective-permute-start(bf16[128,1024]{1,0:T(8,128)(2,1)} %bitcast.14), channel_id=1, source_target_pairs={{0,3},{1,0},{2,1},{3,2},{4,7},{5,4},{6,5},{7,6},{8,11},{9,8},{10,9... | collective-permute-start | bytes 786440 | tf_op jit(solution)/shard_map/ppermute | solution.py:185
  20.5 1.1 collective-permute-start.2
  21.7 1.1 collective-permute-done.5
  22.8 6.7 %all-to-all-done = bf16[4,72,1024]{2,1,0:T(8,128)(2,1)S(1)} async-done(((bf16[4,72,1024]{2,1,0:T(8,128)(2,1)}), bf16[4,72,1024]{2,1,0:T(8,128)(2,1)S(1)}, u32[]{:S(2)}, u32[]{:S(2)}) %all-to-all-start) | async-done | bytes 589856 | tf_op jit(solution)/shard_map/all_to_all | solution.py:217
  29.6 1.6 broadcast_in_dim.61
  31.2 4.3 %all-to-all-start.1 = ((bf16[8,128,1024]{2,1,0:T(8,128)(2,1)}), bf16[8,128,1024]{2,1,0:T(8,128)(2,1)}, u32[]{:S(2)}, u32[]{:S(2)}) async-start(bf16[8,128,1024]{2,1,0:T(8,128)(2,1)} %bitcast.23), calls=%async_computation.1 | async-start | bytes 4194304 | tf_op jit(solution)/shard_map/all_to_all | solution.py:242
  36.1 3.8 %gather_fusion = bf16[128,1024]{1,0:T(8,128)(2,1)S(1)} fusion(bf16[2048,1024]{1,0:T(8,128)(2,1)} %bitcast.97, s32[1024]{0:T(1024)S(1)} %pad_clamp_fusion), kind=kCustom, calls=%fused_computation | custom fusion | bytes 524800 | tf_op jit(solution)/shard_map/jit(_take)/gather | solution.py:236
  40.2 10.8 %collective-permute-done.3 = bf16[128,1024]{1,0:T(8,128)(2,1)S(1)} collective-permute-done((bf16[128,1024]{1,0:T(8,128)(2,1)S(1)}, bf16[128,1024]{1,0:T(8,128)(2,1)S(1)}, u32[]{:S(2)}, u32[]{:S(2)}) %collective-permute-start.3) | collective-permute-done | bytes 262176 | tf_op jit(solution)/shard_map/ppermute | solution.py:185
  51.6 2.0 %collective-permute-start.8 = (s32[2,128]{1,0:T(2,128)S(1)}, s32[2,128]{1,0:T(2,128)S(1)}, u32[]{:S(2)}, u32[]{:S(2)}) collective-permute-start(s32[2,128]{1,0:T(2,128)S(1)} %pad_add_fusion), channel_id=1, source_target_pairs={{0,1},{1,0},{2,3},{3,2},{4,5},{5,4},{6,7},{7,6},{8,9},{9,8},{10,11... | collective-permute-start | bytes 3080 | tf_op jit(solution)/shard_map/ppermute | solution.py:188
  53.6 5.3 %collective-permute-done.8 = s32[2,128]{1,0:T(2,128)S(1)} collective-permute-done((s32[2,128]{1,0:T(2,128)S(1)}, s32[2,128]{1,0:T(2,128)S(1)}, u32[]{:S(2)}, u32[]{:S(2)}) %collective-permute-start.8) | collective-permute-done | bytes 1056 | tf_op jit(solution)/shard_map/ppermute | solution.py:188
  58.9 3.3 %all-to-all-done.1 = bf16[8,128,1024]{2,1,0:T(8,128)(2,1)} async-done(((bf16[8,128,1024]{2,1,0:T(8,128)(2,1)}), bf16[8,128,1024]{2,1,0:T(8,128)(2,1)}, u32[]{:S(2)}, u32[]{:S(2)}) %all-to-all-start.1) | async-done | bytes 2097184 | tf_op jit(solution)/shard_map/all_to_all | solution.py:242
  62.2 2.4 %fusion.31 = (f32[256]{0:T(256)S(1)}, f32[256,1024]{1,0:T(8,128)S(1)}) fusion(bf16[1024,1024]{1,0:T(8,128)(2,1)} %bitcast.24, bf16[128,1024]{1,0:T(8,128)(2,1)S(1)} %collective-permute-done.6, bf16[128,1024]{1,0:T(8,128)(2,1)S(1)} %multiply_convert_fusion.1), kind=kOutput, calls=%fused_computation.95 | convolution fusion | flops 538181376 | bytes 3671040 | tf_op jit(solution)/shard_map/dot_general | solution.py:17
  65.0 10.2 %collective-permute-start.7 = (f32[2,2,128]{2,1,0:T(2,128)S(1)}, f32[2,2,128]{2,1,0:T(2,128)S(1)}, u32[]{:S(2)}, u32[]{:S(2)}) collective-permute-start(f32[2,2,128]{2,1,0:T(2,128)S(1)} %pad_maximum_fusion.4), channel_id=1, source_target_pairs={{0,1},{1,0},{2,3},{3,2},{4,5},{5,4},{6,7},{7,6},{8,9},{9,8},{10,11... | collective-permute-start | bytes 6152 | tf_op jit(solution)/shard_map/ppermute | solution.py:188
  75.2 1.6 collective-permute-done.7
  77.2 2.4 %fusion.32 = f32[256,1024]{1,0:T(8,128)S(1)} fusion(bf16[256,1024]{1,0:T(8,128)(2,1)S(1)} %multiply_convert_fusion, bf16[1024,1024]{1,0:T(8,128)(2,1)} %bitcast.24), kind=kOutput, calls=%fused_computation.96 | convolution fusion | flops 536870912 | bytes 3670016 | tf_op jit(solution)/shard_map/dot_general | solution.py:17
  80.4 2.1 %convolution_convert_fusion = bf16[1024,1024]{1,0:T(8,128)(2,1)} fusion(bf16[256,1024]{1,0:T(8,128)(2,1)S(1)} %multiply_convert_fusion, bf16[128,1024]{1,0:T(8,128)(2,1)S(1)} %copy-done.13, bf16[128,1024]{1,0:T(8,128)(2,1)S(1)} %copy-done.11), kind=kOutput, calls=%fused_computation.5 | convolution fusion | flops 538968064 | bytes 3145728 | tf_op jit(solution)/shard_map/dot_general | solution.py:17
  82.5 4.5 %all-to-all-start.3 = ((bf16[8,128,1024]{2,1,0:T(8,128)(2,1)}), bf16[8,128,1024]{2,1,0:T(8,128)(2,1)}, u32[]{:S(2)}, u32[]{:S(2)}) async-start(bf16[8,128,1024]{2,1,0:T(8,128)(2,1)} %bitcast.94), calls=%async_computation.3 | async-start | bytes 4194304 | tf_op jit(solution)/shard_map/all_to_all | solution.py:284
  87.0 2.1 %collective-permute-start.9 = (bf16[128,1024]{1,0:T(8,128)(2,1)S(1)}, bf16[128,1024]{1,0:T(8,128)(2,1)S(1)}, u32[]{:S(2)}, u32[]{:S(2)}) collective-permute-start(bf16[128,1024]{1,0:T(8,128)(2,1)S(1)} %copy-done.14), channel_id=1, source_target_pairs={{0,1},{1,0},{2,3},{3,2},{4,5},{5,4},{6,7},{7,6},{8,9},{9,8},{10,11... | collective-permute-start | bytes 786440 | tf_op jit(solution)/shard_map/ppermute | solution.py:188
  89.1 6.8 %collective-permute-done.9 = bf16[128,1024]{1,0:T(8,128)(2,1)S(1)} collective-permute-done((bf16[128,1024]{1,0:T(8,128)(2,1)S(1)}, bf16[128,1024]{1,0:T(8,128)(2,1)S(1)}, u32[]{:S(2)}, u32[]{:S(2)}) %collective-permute-start.9) | collective-permute-done | bytes 262176 | tf_op jit(solution)/shard_map/ppermute | solution.py:188
  96.1 1.5 multiply_reduce_fusion.1
  97.6 1.8 %collective-permute-start.10 = (bf16[128,1024]{1,0:T(8,128)(2,1)S(1)}, bf16[128,1024]{1,0:T(8,128)(2,1)S(1)}, u32[]{:S(2)}, u32[]{:S(2)}) collective-permute-start(bf16[128,1024]{1,0:T(8,128)(2,1)S(1)} %get-tuple-element.24.refs_0_), channel_id=1, source_target_pairs={{0,1},{1,2},{2,3},{3,0},{4,5},{5,6},{6,7},{7,4},{8,9},{9,10},{10,1... | collective-permute-start | bytes 786440 | tf_op jit(solution)/shard_map/ppermute | solution.py:185
  99.4 3.3 %collective-permute-start.11 = (bf16[128,1024]{1,0:T(8,128)(2,1)S(1)}, bf16[128,1024]{1,0:T(8,128)(2,1)S(1)}, u32[]{:S(2)}, u32[]{:S(2)}) collective-permute-start(bf16[128,1024]{1,0:T(8,128)(2,1)S(1)} %get-tuple-element.24.refs_0_), channel_id=1, source_target_pairs={{0,2},{1,3},{2,0},{3,1},{4,6},{5,7},{6,4},{7,5},{8,10},{9,11},{10,... | collective-permute-start | bytes 786440 | tf_op jit(solution)/shard_map/ppermute | solution.py:185
  102.7 1.2 collective-permute-start.12
  104.3 5.1 %collective-permute-done.10.refs_1_ = bf16[128,1024]{1,0:T(8,128)(2,1)S(1)} collective-permute-done((bf16[128,1024]{1,0:T(8,128)(2,1)S(1)}, bf16[128,1024]{1,0:T(8,128)(2,1)S(1)}, u32[]{:S(2)}, u32[]{:S(2)}) %collective-permute-start.10) | collective-permute-done | bytes 262176 | tf_op jit(solution)/shard_map/ppermute | solution.py:185
  109.4 10.2 %collective-permute-done.11.refs_2_ = bf16[128,1024]{1,0:T(8,128)(2,1)S(1)} collective-permute-done((bf16[128,1024]{1,0:T(8,128)(2,1)S(1)}, bf16[128,1024]{1,0:T(8,128)(2,1)S(1)}, u32[]{:S(2)}, u32[]{:S(2)}) %collective-permute-start.11) | collective-permute-done | bytes 262176 | tf_op jit(solution)/shard_map/ppermute | solution.py:185
  121.0 0.9 copy-done.4
  122.0 0.9 copy-done.6
  122.9 4.2 %shard_map.85 = (bf16[8,1024,128]{2,1,0:T(8,128)(2,1)}, bf16[256,1024]{1,0:T(8,128)(2,1)S(1)}, bf16[256,1024]{1,0:T(8,128)(2,1)S(1)}) custom-call(s32[2]{0:T(128)S(1)} %pad_add_fusion.2.place_ref, bf16[128,1024]{1,0:T(8,128)(2,1)S(1)} %get-tuple-element.24.refs_0_, bf16[128,1024]{1,0:T(8,128)(2,1)S(1)} %collective-permute-done.10.refs_1_, ...), custom_call_target="tpu_custom_call" | custom-call | flops 1073741824 | bytes 2099200 | tf_op jit(solution)/shard_map/pallas_call | solution.py:33
  127.1 4.4 %all-to-all-start.2 = ((bf16[8,1024,128]{2,1,0:T(8,128)(2,1)}), bf16[8,1024,128]{2,1,0:T(8,128)(2,1)}, u32[]{:S(2)}, u32[]{:S(2)}) async-start(bf16[8,1024,128]{2,1,0:T(8,128)(2,1)} %get-tuple-element.19), calls=%async_computation.2 | async-start | bytes 4194304 | tf_op jit(solution)/shard_map/all_to_all | solution.py:297
  132.8 5.4 %collective-permute-start.15 = (f32[64]{0:T(128)S(1)}, f32[64]{0:T(128)S(1)}, u32[]{:S(2)}, u32[]{:S(2)}) collective-permute-start(f32[64]{0:T(128)S(1)} %slice_add_fusion.1), channel_id=1, source_target_pairs={{0,1},{1,2},{2,3},{3,0},{4,5},{5,6},{6,7},{7,4},{8,9},{9,10},{10,1... | collective-permute-start | bytes 776 | tf_op jit(solution)/shard_map/ppermute | solution.py:185
  138.2 2.3 %collective-permute-start.16 = (f32[64]{0:T(128)S(1)}, f32[64]{0:T(128)S(1)}, u32[]{:S(2)}, u32[]{:S(2)}) collective-permute-start(f32[64]{0:T(128)S(1)} %slice_add_fusion.1), channel_id=1, source_target_pairs={{0,2},{1,3},{2,0},{3,1},{4,6},{5,7},{6,4},{7,5},{8,10},{9,11},{10,... | collective-permute-start | bytes 776 | tf_op jit(solution)/shard_map/ppermute | solution.py:185
  140.5 0.9 collective-permute-done.15
  141.4 1.2 collective-permute-done.16
  142.6 1.3 collective-permute-done.17
  144.1 2.0 %reduce_sum.92 = bf16[2,4,32,1024]{3,2,1,0:T(8,128)(2,1)S(1)} reduce(bf16[4,2,4,32,1024]{4,3,2,1,0:T(8,128)(2,1)} %bitcast.48, bf16[]{:T(256)} %constant.152.clone.1), dimensions={0}, to_apply=%region_9.10 | reduce | flops 786432 | bytes 2621442 | tf_op jit(solution)/shard_map/reduce_sum | solution.py:285
  146.3 2.4 %collective-permute-start.19 = (bf16[2,32,1024]{2,1,0:T(8,128)(2,1)S(1)}, bf16[2,32,1024]{2,1,0:T(8,128)(2,1)S(1)}, u32[]{:S(2)}, u32[]{:S(2)}) collective-permute-start(bf16[2,32,1024]{2,1,0:T(8,128)(2,1)S(1)} %get-tuple-element.33), channel_id=1, source_target_pairs={{0,2},{1,3},{2,0},{3,1},{4,6},{5,7},{6,4},{7,5},{8,10},{9,11},{10,... | collective-permute-start | bytes 393224 | tf_op jit(solution)/shard_map/ppermute | solution.py:185
  148.7 1.4 collective-permute-start.20
  150.3 2.2 %copy-done.2 = bf16[2,1024,1024]{2,1,0:T(8,128)(2,1)S(1)} copy-done((bf16[2,1024,1024]{2,1,0:T(8,128)(2,1)S(1)}, bf16[2,1024,1024]{2,1,0:T(8,128)(2,1)}, u32[]{:S(2)}) %copy-start.2) | copy-done | bytes 4194328
  152.5 3.6 %shard_map.86 = bf16[256,1024]{1,0:T(8,128)(2,1)} custom-call(s32[2]{0:T(128)S(1)} %pad_add_fusion.2.place_ref, bf16[256,1024]{1,0:T(8,128)(2,1)S(1)} %get-tuple-element.17.refs_0_, bf16[256,1024]{1,0:T(8,128)(2,1)S(1)} %collective-permute-done.13.refs_1_, bf16[2,1024,1024]{2,1,0:T(8,128)(2,1)S(1)} %copy-done.2, bf16[256,1024]{1,0:T(8,128)(2,1)S(1)} %copy-done.1, ...), custom_call_target="tpu_custom_call" | custom-call | flops 1073741824 | bytes 5769216 | tf_op jit(solution)/shard_map/pallas_call | solution.py:33
  156.1 2.1 %collective-permute-done.19.refs_2_ = bf16[2,32,1024]{2,1,0:T(8,128)(2,1)S(1)} collective-permute-done((bf16[2,32,1024]{2,1,0:T(8,128)(2,1)S(1)}, bf16[2,32,1024]{2,1,0:T(8,128)(2,1)S(1)}, u32[]{:S(2)}, u32[]{:S(2)}) %collective-permute-start.19) | collective-permute-done | bytes 131104 | tf_op jit(solution)/shard_map/ppermute | solution.py:185
  158.2 1.5 shard_map.87
  159.7 3.0 %convert_reduce_fusion = f32[2,1024,128]{2,1,0:T(8,128)} fusion(bf16[4,2,1024,128]{3,2,1,0:T(8,128)(2,1)} %bitcast.57), kind=kLoop, calls=%fused_computation.1 | loop fusion | flops 1835008 | bytes 3145728 | tf_op jit(solution)/shard_map/reduce_sum | solution.py:298
  (109 shorter events, 9.3 us)
Async XLA Ops:
  0.6 3.1 %copy-start = (f32[2,1024]{1,0:T(2,128)S(1)}, f32[2,1024]{1,0:T(2,128)}, u32[]{:S(2)}) copy-start(f32[2,1024]{1,0:T(2,128)} %param.9) | copy-start | bytes 24580
  1.9 2.1 %collective-permute-start = (bf16[256,1024]{0,1:T(8,128)(2,1)S(1)}, bf16[256,1024]{0,1:T(8,128)(2,1)S(1)}, u32[]{:S(2)}, u32[]{:S(2)}) collective-permute-start(bf16[256,1024]{0,1:T(8,128)(2,1)S(1)} %copy.56), channel_id=1, source_target_pairs={{0,4},{4,0},{8,12},{12,8},{16,20},{20,16},{24,28},{28,24},{1,5},{5... | collective-permute-start | bytes 1572872 | tf_op jit(solution)/shard_map/ppermute | solution.py:195
  6.1 23.4 %all-to-all-start = ((bf16[4,72,1024]{2,1,0:T(8,128)(2,1)}), bf16[4,72,1024]{2,1,0:T(8,128)(2,1)S(1)}, u32[]{:S(2)}, u32[]{:S(2)}) async-start(bf16[4,72,1024]{2,1,0:T(8,128)(2,1)} %bitcast.6), calls=%async_computation | async-start | bytes 1179648 | tf_op jit(solution)/shard_map/all_to_all | solution.py:217
  13.0 8.7 %copy-start.15 = (s32[2,64]{1,0:T(2,128)S(1)}, s32[2,64]{1,0:T(2,128)}, u32[]{:S(2)}) copy-start(s32[2,64]{1,0:T(2,128)} %param.11) | copy-start | bytes 1540
  16.7 23.5 %collective-permute-start.4 = (bf16[128,1024]{1,0:T(8,128)(2,1)}, bf16[128,1024]{1,0:T(8,128)(2,1)S(1)}, u32[]{:S(2)}, u32[]{:S(2)}) collective-permute-start(bf16[128,1024]{1,0:T(8,128)(2,1)} %bitcast.14), channel_id=1, source_target_pairs={{0,3},{1,0},{2,1},{3,2},{4,7},{5,4},{6,5},{7,6},{8,11},{9,8},{10,9... | collective-permute-start | bytes 786440 | tf_op jit(solution)/shard_map/ppermute | solution.py:185
  20.5 30.5 %collective-permute-start.3 = (bf16[128,1024]{1,0:T(8,128)(2,1)S(1)}, bf16[128,1024]{1,0:T(8,128)(2,1)S(1)}, u32[]{:S(2)}, u32[]{:S(2)}) collective-permute-start(bf16[128,1024]{1,0:T(8,128)(2,1)S(1)} %bitcast.102), channel_id=1, source_target_pairs={{0,2},{1,3},{2,0},{3,1},{4,6},{5,7},{6,4},{7,5},{8,10},{9,11},{10,... | collective-permute-start | bytes 786440 | tf_op jit(solution)/shard_map/ppermute | solution.py:185
  20.5 30.5 %collective-permute-start.2 = (bf16[128,1024]{1,0:T(8,128)(2,1)S(1)}, bf16[128,1024]{1,0:T(8,128)(2,1)S(1)}, u32[]{:S(2)}, u32[]{:S(2)}) collective-permute-start(bf16[128,1024]{1,0:T(8,128)(2,1)S(1)} %bitcast.101), channel_id=1, source_target_pairs={{0,1},{1,2},{2,3},{3,0},{4,5},{5,6},{6,7},{7,4},{8,9},{9,10},{10,1... | collective-permute-start | bytes 786440 | tf_op jit(solution)/shard_map/ppermute | solution.py:185
  21.6 1.1 collective-permute-start.5
  31.2 31.0 %all-to-all-start.1 = ((bf16[8,128,1024]{2,1,0:T(8,128)(2,1)}), bf16[8,128,1024]{2,1,0:T(8,128)(2,1)}, u32[]{:S(2)}, u32[]{:S(2)}) async-start(bf16[8,128,1024]{2,1,0:T(8,128)(2,1)} %bitcast.23), calls=%async_computation.1 | async-start | bytes 4194304 | tf_op jit(solution)/shard_map/all_to_all | solution.py:242
  35.7 4.3 %collective-permute-start.1 = (f32[256]{0:T(256)S(1)}, f32[256]{0:T(256)S(1)}, u32[]{:S(2)}, u32[]{:S(2)}) collective-permute-start(f32[256]{0:T(256)S(1)} %reduce_sum.85), channel_id=1, source_target_pairs={{0,4},{4,0},{8,12},{12,8},{16,20},{20,16},{24,28},{28,24},{1,5},{5... | collective-permute-start | bytes 3080 | tf_op jit(solution)/shard_map/ppermute | solution.py:195
  40.2 24.4 %copy-start.7 = (bf16[128,1024]{1,0:T(8,128)(2,1)}, bf16[128,1024]{1,0:T(8,128)(2,1)S(1)}, u32[]{:S(2)}) copy-start(bf16[128,1024]{1,0:T(8,128)(2,1)S(1)} %collective-permute-done.4) | copy-start | bytes 786436
  51.0 13.6 %copy-start.8 = (bf16[128,1024]{1,0:T(8,128)(2,1)}, bf16[128,1024]{1,0:T(8,128)(2,1)S(1)}, u32[]{:S(2)}) copy-start(bf16[128,1024]{1,0:T(8,128)(2,1)S(1)} %collective-permute-done.3) | copy-start | bytes 786436
  51.0 13.6 %copy-start.9 = (bf16[128,1024]{1,0:T(8,128)(2,1)}, bf16[128,1024]{1,0:T(8,128)(2,1)S(1)}, u32[]{:S(2)}) copy-start(bf16[128,1024]{1,0:T(8,128)(2,1)S(1)} %collective-permute-done.2) | copy-start | bytes 786436
  51.5 13.5 %copy-start.10 = (bf16[128,1024]{1,0:T(8,128)(2,1)}, bf16[128,1024]{1,0:T(8,128)(2,1)S(1)}, u32[]{:S(2)}) copy-start(bf16[128,1024]{1,0:T(8,128)(2,1)S(1)} %multiply_convert_fusion.1) | copy-start | bytes 786436
  51.5 7.5 %collective-permute-start.6 = (bf16[128,1024]{1,0:T(8,128)(2,1)S(1)}, bf16[128,1024]{1,0:T(8,128)(2,1)S(1)}, u32[]{:S(2)}, u32[]{:S(2)}) collective-permute-start(bf16[128,1024]{1,0:T(8,128)(2,1)S(1)} %multiply_convert_fusion.1), channel_id=1, source_target_pairs={{0,1},{1,0},{2,3},{3,2},{4,5},{5,4},{6,7},{7,6},{8,9},{9,8},{10,11... | collective-permute-start | bytes 786440 | tf_op jit(solution)/shard_map/ppermute | solution.py:188
  51.6 7.3 %collective-permute-start.8 = (s32[2,128]{1,0:T(2,128)S(1)}, s32[2,128]{1,0:T(2,128)S(1)}, u32[]{:S(2)}, u32[]{:S(2)}) collective-permute-start(s32[2,128]{1,0:T(2,128)S(1)} %pad_add_fusion), channel_id=1, source_target_pairs={{0,1},{1,0},{2,3},{3,2},{4,5},{5,4},{6,7},{7,6},{8,9},{9,8},{10,11... | collective-permute-start | bytes 3080 | tf_op jit(solution)/shard_map/ppermute | solution.py:188
  58.9 6.0 %copy-start.12 = (bf16[128,1024]{1,0:T(8,128)(2,1)}, bf16[128,1024]{1,0:T(8,128)(2,1)S(1)}, u32[]{:S(2)}) copy-start(bf16[128,1024]{1,0:T(8,128)(2,1)S(1)} %collective-permute-done.6) | copy-start | bytes 786436
  65.0 11.8 %collective-permute-start.7 = (f32[2,2,128]{2,1,0:T(2,128)S(1)}, f32[2,2,128]{2,1,0:T(2,128)S(1)}, u32[]{:S(2)}, u32[]{:S(2)}) collective-permute-start(f32[2,2,128]{2,1,0:T(2,128)S(1)} %pad_maximum_fusion.4), channel_id=1, source_target_pairs={{0,1},{1,0},{2,3},{3,2},{4,5},{5,4},{6,7},{7,6},{8,9},{9,8},{10,11... | collective-permute-start | bytes 6152 | tf_op jit(solution)/shard_map/ppermute | solution.py:188
  77.2 3.2 %copy-start.11 = (bf16[128,1024]{1,0:T(8,128)(2,1)S(1)}, bf16[128,1024]{1,0:T(8,128)(2,1)}, u32[]{:S(2)}) copy-start(bf16[128,1024]{1,0:T(8,128)(2,1)} %copy-done.10) | copy-start | bytes 786436
  77.2 3.2 %copy-start.13 = (bf16[128,1024]{1,0:T(8,128)(2,1)S(1)}, bf16[128,1024]{1,0:T(8,128)(2,1)}, u32[]{:S(2)}) copy-start(bf16[128,1024]{1,0:T(8,128)(2,1)} %copy-done.12) | copy-start | bytes 786436
  82.5 4.5 %copy-start.14 = (bf16[128,1024]{1,0:T(8,128)(2,1)S(1)}, bf16[128,1024]{1,0:T(8,128)(2,1)}, u32[]{:S(2)}) copy-start(bf16[128,1024]{1,0:T(8,128)(2,1)} %slice.86) | copy-start | bytes 786436
  82.5 44.6 %all-to-all-start.3 = ((bf16[8,128,1024]{2,1,0:T(8,128)(2,1)}), bf16[8,128,1024]{2,1,0:T(8,128)(2,1)}, u32[]{:S(2)}, u32[]{:S(2)}) async-start(bf16[8,128,1024]{2,1,0:T(8,128)(2,1)} %bitcast.94), calls=%async_computation.3 | async-start | bytes 4194304 | tf_op jit(solution)/shard_map/all_to_all | solution.py:284
  87.0 17.0 %copy-start.1 = (bf16[256,1024]{1,0:T(8,128)(2,1)S(1)}, bf16[256,1024]{1,0:T(8,128)(2,1)}, u32[]{:S(2)}) copy-start(bf16[256,1024]{1,0:T(8,128)(2,1)} %refs_3_.1) | copy-start | bytes 1572868
  87.0 8.9 %collective-permute-start.9 = (bf16[128,1024]{1,0:T(8,128)(2,1)S(1)}, bf16[128,1024]{1,0:T(8,128)(2,1)S(1)}, u32[]{:S(2)}, u32[]{:S(2)}) collective-permute-start(bf16[128,1024]{1,0:T(8,128)(2,1)S(1)} %copy-done.14), channel_id=1, source_target_pairs={{0,1},{1,0},{2,3},{3,2},{4,5},{5,4},{6,7},{7,6},{8,9},{9,8},{10,11... | collective-permute-start | bytes 786440 | tf_op jit(solution)/shard_map/ppermute | solution.py:188
  97.6 11.8 %collective-permute-start.10 = (bf16[128,1024]{1,0:T(8,128)(2,1)S(1)}, bf16[128,1024]{1,0:T(8,128)(2,1)S(1)}, u32[]{:S(2)}, u32[]{:S(2)}) collective-permute-start(bf16[128,1024]{1,0:T(8,128)(2,1)S(1)} %get-tuple-element.24.refs_0_), channel_id=1, source_target_pairs={{0,1},{1,2},{2,3},{3,0},{4,5},{5,6},{6,7},{7,4},{8,9},{9,10},{10,1... | collective-permute-start | bytes 786440 | tf_op jit(solution)/shard_map/ppermute | solution.py:185
  99.4 20.2 %collective-permute-start.11 = (bf16[128,1024]{1,0:T(8,128)(2,1)S(1)}, bf16[128,1024]{1,0:T(8,128)(2,1)S(1)}, u32[]{:S(2)}, u32[]{:S(2)}) collective-permute-start(bf16[128,1024]{1,0:T(8,128)(2,1)S(1)} %get-tuple-element.24.refs_0_), channel_id=1, source_target_pairs={{0,2},{1,3},{2,0},{3,1},{4,6},{5,7},{6,4},{7,5},{8,10},{9,11},{10,... | collective-permute-start | bytes 786440 | tf_op jit(solution)/shard_map/ppermute | solution.py:185
  102.7 17.6 %collective-permute-start.12 = (bf16[128,1024]{1,0:T(8,128)(2,1)S(1)}, bf16[128,1024]{1,0:T(8,128)(2,1)S(1)}, u32[]{:S(2)}, u32[]{:S(2)}) collective-permute-start(bf16[128,1024]{1,0:T(8,128)(2,1)S(1)} %get-tuple-element.24.refs_0_), channel_id=1, source_target_pairs={{0,3},{1,0},{2,1},{3,2},{4,7},{5,4},{6,5},{7,6},{8,11},{9,8},{10,9... | collective-permute-start | bytes 786440 | tf_op jit(solution)/shard_map/ppermute | solution.py:185
  119.6 0.7 copy-start.3
  120.3 0.7 copy-start.5
  121.0 0.9 copy-start.4
  122.0 0.9 copy-start.6
  127.1 32.6 %all-to-all-start.2 = ((bf16[8,1024,128]{2,1,0:T(8,128)(2,1)}), bf16[8,1024,128]{2,1,0:T(8,128)(2,1)}, u32[]{:S(2)}, u32[]{:S(2)}) async-start(bf16[8,1024,128]{2,1,0:T(8,128)(2,1)} %get-tuple-element.19), calls=%async_computation.2 | async-start | bytes 4194304 | tf_op jit(solution)/shard_map/all_to_all | solution.py:297
  131.6 1.2 collective-permute-start.14
  131.9 18.4 %collective-permute-start.13 = (bf16[256,1024]{1,0:T(8,128)(2,1)S(1)}, bf16[256,1024]{1,0:T(8,128)(2,1)S(1)}, u32[]{:S(2)}, u32[]{:S(2)}) collective-permute-start(bf16[256,1024]{1,0:T(8,128)(2,1)S(1)} %get-tuple-element.18), channel_id=1, source_target_pairs={{0,4},{4,0},{8,12},{12,8},{16,20},{20,16},{24,28},{28,24},{1,5},{5... | collective-permute-start | bytes 1572872 | tf_op jit(solution)/shard_map/ppermute | solution.py:195
  132.8 8.6 %collective-permute-start.15 = (f32[64]{0:T(128)S(1)}, f32[64]{0:T(128)S(1)}, u32[]{:S(2)}, u32[]{:S(2)}) collective-permute-start(f32[64]{0:T(128)S(1)} %slice_add_fusion.1), channel_id=1, source_target_pairs={{0,1},{1,2},{2,3},{3,0},{4,5},{5,6},{6,7},{7,4},{8,9},{9,10},{10,1... | collective-permute-start | bytes 776 | tf_op jit(solution)/shard_map/ppermute | solution.py:185
  138.2 4.4 %collective-permute-start.16 = (f32[64]{0:T(128)S(1)}, f32[64]{0:T(128)S(1)}, u32[]{:S(2)}, u32[]{:S(2)}) collective-permute-start(f32[64]{0:T(128)S(1)} %slice_add_fusion.1), channel_id=1, source_target_pairs={{0,2},{1,3},{2,0},{3,1},{4,6},{5,7},{6,4},{7,5},{8,10},{9,11},{10,... | collective-permute-start | bytes 776 | tf_op jit(solution)/shard_map/ppermute | solution.py:185
  140.4 3.5 %collective-permute-start.17 = (f32[64]{0:T(128)S(1)}, f32[64]{0:T(128)S(1)}, u32[]{:S(2)}, u32[]{:S(2)}) collective-permute-start(f32[64]{0:T(128)S(1)} %slice_add_fusion.1), channel_id=1, source_target_pairs={{0,3},{1,0},{2,1},{3,2},{4,7},{5,4},{6,5},{7,6},{8,11},{9,8},{10,9... | collective-permute-start | bytes 776 | tf_op jit(solution)/shard_map/ppermute | solution.py:185
  146.2 9.9 %collective-permute-start.18 = (bf16[2,32,1024]{2,1,0:T(8,128)(2,1)S(1)}, bf16[2,32,1024]{2,1,0:T(8,128)(2,1)S(1)}, u32[]{:S(2)}, u32[]{:S(2)}) collective-permute-start(bf16[2,32,1024]{2,1,0:T(8,128)(2,1)S(1)} %get-tuple-element.34), channel_id=1, source_target_pairs={{0,1},{1,2},{2,3},{3,0},{4,5},{5,6},{6,7},{7,4},{8,9},{9,10},{10,1... | collective-permute-start | bytes 393224 | tf_op jit(solution)/shard_map/ppermute | solution.py:185
  146.3 11.9 %collective-permute-start.19 = (bf16[2,32,1024]{2,1,0:T(8,128)(2,1)S(1)}, bf16[2,32,1024]{2,1,0:T(8,128)(2,1)S(1)}, u32[]{:S(2)}, u32[]{:S(2)}) collective-permute-start(bf16[2,32,1024]{2,1,0:T(8,128)(2,1)S(1)} %get-tuple-element.33), channel_id=1, source_target_pairs={{0,2},{1,3},{2,0},{3,1},{4,6},{5,7},{6,4},{7,5},{8,10},{9,11},{10,... | collective-permute-start | bytes 393224 | tf_op jit(solution)/shard_map/ppermute | solution.py:185
  148.7 9.5 %collective-permute-start.20 = (bf16[2,32,1024]{2,1,0:T(8,128)(2,1)S(1)}, bf16[2,32,1024]{2,1,0:T(8,128)(2,1)S(1)}, u32[]{:S(2)}, u32[]{:S(2)}) collective-permute-start(bf16[2,32,1024]{2,1,0:T(8,128)(2,1)S(1)} %get-tuple-element.32), channel_id=1, source_target_pairs={{0,3},{1,0},{2,1},{3,2},{4,7},{5,4},{6,5},{7,6},{8,11},{9,8},{10,9... | collective-permute-start | bytes 393224 | tf_op jit(solution)/shard_map/ppermute | solution.py:185
  150.3 2.2 %copy-start.2 = (bf16[2,1024,1024]{2,1,0:T(8,128)(2,1)S(1)}, bf16[2,1024,1024]{2,1,0:T(8,128)(2,1)}, u32[]{:S(2)}) copy-start(bf16[2,1024,1024]{2,1,0:T(8,128)(2,1)} %refs_2_.1) | copy-start | bytes 12582916

commit v3 on v2

--- a/solution.py
+++ b/solution.py
@@ -21,7 +21,7 @@
     return lax.optimization_barrier((value, *others))[0]
 
 
-VMEM = pltpu.CompilerParams(vmem_limit_bytes=32 * 2**20)
+VMEM = pltpu.CompilerParams(vmem_limit_bytes=60 * 2**20)
 
 
 def whole(shape):
@@ -85,17 +85,15 @@
     )
 
 
-def input_gradient(place, pieces, turned, ratio, seqs):
-    hids, steps = len(pieces), len(turned)
+def input_gradient(place, pieces, group, ratio, seqs):
+    hids, steps = len(pieces), len(group)
     owned, depth = pieces[0].shape
-    units, rows = turned[0].shape
+    rows, units = group[0].shape
     part = owned // steps
-    slice_wide = depth // seqs
-    wide = max(min(256, depth), slice_wide)
-    count = wide // slice_wide
+    wide = min(512, depth)
 
     def kernel(place_ref, *refs):
-        chunks, turned, ratio = refs[:hids], refs[hids : hids + steps], refs[hids + steps]
+        chunks, group, ratio = refs[:hids], refs[hids : hids + steps], refs[hids + steps]
         out, plain, scaled = refs[hids + steps + 1], refs[hids + steps + 2 : -1], refs[-1]
         j = place_ref[1]
         for r in range(hids):
@@ -105,26 +103,28 @@
                 plain[m][pl.ds(to, part), :] = values
                 factor = ratio[m, pl.ds(to, part), :]
                 scaled[m, pl.ds(to, part), :] = (values.astype(F32) * factor).astype(BF16)
-        total = jnp.dot(turned[0][...], scaled[0], preferred_element_type=F32)
-        for m in range(1, steps):
-            total = total + jnp.dot(turned[m][...], scaled[m], preferred_element_type=F32)
-        for k in range(count):
-            out[k] = total[:, k * slice_wide : (k + 1) * slice_wide].astype(BF16)
+        total = None
+        for m in range(steps):
+            term = lax.dot_general(
+                scaled[m], group[m][...], (((0,), (0,)), ((), ())), preferred_element_type=F32
+            )
+            total = term if total is None else total + term
+        out[...] = total.astype(BF16)
 
     return call(
         kernel,
         place,
         depth // wide,
         [pl.BlockSpec((owned, wide), lambda n, place: (0, n))] * hids
-        + [whole((units, rows))] * steps
+        + [whole((rows, units))] * steps
         + [whole((steps, rows, 1))],
-        [pl.BlockSpec((count, units, slice_wide), lambda n, place: (n, 0, 0))]
+        [pl.BlockSpec((wide, units), lambda n, place: (n, 0))]
         + [pl.BlockSpec((rows, wide), lambda n, place: (0, n))] * steps,
-        [jax.ShapeDtypeStruct((seqs, units, slice_wide), BF16)]
+        [jax.ShapeDtypeStruct((depth, units), BF16)]
         + [jax.ShapeDtypeStruct((rows, depth), BF16)] * steps,
         [pltpu.VMEM((steps, rows, wide), BF16)],
         2 * steps * rows * units * depth,
-        (*pieces, *turned, ratio),
+        (*pieces, *group, ratio),
     )
 
 
@@ -227,6 +227,7 @@
         return lax.dynamic_index_in_dim(proj_parts, index, 1, False).reshape(owned, depth)
 
     send = [owner_block((j + shift) % hids).astype(BF16) for shift in range(1, hids)]
+    send = [after(p, head_got) for p in send]
     received = [along_hid(send[shift - 1], shift) for shift in range(1, hids)]
 
     ids = after(codebook_ids, *send)
@@ -281,7 +282,8 @@
     d_ratio_part = jnp.sum(d_x * proj, axis=1).reshape(steps, part)
 
     part_out = matmul(normed_rows, after(d_logit, *away), ((0,), (0,))).astype(BF16)
-    part_out = lax.all_to_all(part_out.reshape(seqs, depth // seqs, block), "seq", 0, 0)
+    part_out = after(part_out, *received).reshape(seqs, depth // seqs, block)
+    part_out = lax.all_to_all(part_out, "seq", 0, 0)
     part_out = part_out.reshape(groups, steps, hids, head_rows, block).astype(F32).sum(0)
     part_out = part_out.astype(BF16)
     sums = [
@@ -290,12 +292,12 @@
     sums = [along_hid(p, shift) if shift else p for shift, p in enumerate(sums)]
     grad_out = head_gradient(place, sums, halves)
 
-    turned = [after(h, normed).T for h in group]
     pieces = [d_round] + [along_hid(d_round, shift) for shift in range(1, hids)]
     ratio_rows = ratio_group.reshape(steps, rows, 1)
-    share, mine, *others = input_gradient(place, pieces, turned, ratio_rows, seqs)
-    share = lax.all_to_all(share, "seq", 0, 0)
-    grad_in = share.reshape(groups, steps, units, depth // seqs).astype(F32).sum(0)
+    share, mine, *others = input_gradient(place, pieces, group, ratio_rows, seqs)
+    share = lax.all_to_all(share.reshape(seqs, depth // seqs, units), "seq", 0, 0)
+    share = share.reshape(groups, steps, depth // seqs, units).astype(F32).sum(0)
+    grad_in = share.transpose(0, 2, 1)
 
     d_ratio = d_ratio_part[0]
     for m in relations:

time: 164 us -> 151 us (0.921)
  starting transfers between devices: 58.1 us -> 45.7 us
  waiting for transfers between devices: 57.3 us -> 51.9 us
  Pallas kernels: 9.25 us -> 13.7 us
    ppermute x4, starting transfers between devices: 14.4 us -> 7.17 us  [turn_hid(): lax.ppermute(values, 'hid', [(a, a - a % halves + (a % halves + shift) %...]
    ppermute x4, waiting for transfers between devices: 13.7 us -> 7.73 us  [turn_hid(): lax.ppermute(values, 'hid', [(a, a - a % halves + (a % halves + shift) %...]
    all_to_all x1, waiting for transfers between devices: 6.69 us -> 12.2 us  [shards(): head_got = lax.all_to_all(head_send, 'hid', 0, 0)]
    pallas_call x3, Pallas kernels: 9.25 us -> 13.7 us  [call(): pl.pallas_call(kernel, grid_spec=pltpu.PrefetchScalarGridSpec(num_scalar_...]
    ppermute x12, starting transfers between devices: 22.8 us -> 18.9 us  [along_hid(): lax.ppermute(values, 'hid', [(a, (a + shift) % hids) for a in range(hids)])]
    ppermute x12, waiting for transfers between devices: 31.6 us -> 28.1 us  [along_hid(): lax.ppermute(values, 'hid', [(a, (a + shift) % hids) for a in range(hids)])]
    unnamed x35 -> x33, local copies, waits for them, and re-layouts: 6.85 us -> 5.96 us
  transfers between devices with their start and end apart: 25 -> 25, of which waited for: 15 -> 14; matrix products, arithmetic and copies ran while one was open for 10% -> 16% of each run, Pallas kernels for 6% -> 9%
where the time goes in v3:
time: 151 us; the launch traced here: 150 us
  waiting for transfers between devices  51.9 us (34%)
  starting transfers between devices  45.7 us (30%)
  local copies, waits for them, and re-layouts  18.3 us (12%)
  Pallas kernels  13.7 us (9%)
  other arithmetic  10.6 us (7%)
  matrix products  8.46 us (6%)
    ppermute x12, waiting for transfers between devices, along_hid(): lax.ppermute(values, 'hid', [(a, (a + shift) % hids) for a in range(hids)])  28.1 us
    ppermute x12, starting transfers between devices, along_hid(): lax.ppermute(values, 'hid', [(a, (a + shift) % hids) for a in range(hids)])  18.9 us
    pallas_call x3, Pallas kernels, call(): pl.pallas_call(kernel, grid_spec=pltpu.PrefetchScalarGridSpec(num_scalar_...  13.7 us
    all_to_all x1, waiting for transfers between devices, shards(): head_got = lax.all_to_all(head_send, 'hid', 0, 0)  12.2 us
    dot_general x4, matrix products, matmul(): lax.dot_general(a, b, (contract, ((), ())), preferred_element_type=F32)  8.46 us
    ppermute x4, waiting for transfers between devices, turn_hid(): lax.ppermute(values, 'hid', [(a, a - a % halves + (a % halves + shift) %...  7.73 us
    ppermute x4, starting transfers between devices, turn_hid(): lax.ppermute(values, 'hid', [(a, a - a % halves + (a % halves + shift) %...  7.17 us
    all_to_all x1, starting transfers between devices, shards(): head_got = lax.all_to_all(head_send, 'hid', 0, 0)  6.24 us
  transfers between devices with their start and end apart: 25, of which 14 were waited for; matrix products, arithmetic and copies ran while one was open for 16% of the time, Pallas kernels for 9%

profile of v3, /device:TPU:0, one launch (start us, length us, event | category | flops | bytes accessed | tf_op | source)
XLA Modules:
  0.0 149.6 jit_solution(1839621259887173)
XLA Ops:
  1.2 1.2 multiply_reduce_fusion
  2.9 1.3 reshape.235
  4.3 0.9 broadcast_in_dim.57
  5.2 6.2 %all-to-all-start = ((bf16[4,72,1024]{2,1,0:T(8,128)(2,1)}), bf16[4,72,1024]{2,1,0:T(8,128)(2,1)S(1)}, u32[]{:S(2)}, u32[]{:S(2)}) async-start(bf16[4,72,1024]{2,1,0:T(8,128)(2,1)} %bitcast.6), calls=%async_computation | async-start | bytes 1179648 | tf_op jit(solution)/shard_map/all_to_all | solution.py:217
  11.6 2.9 %fusion = f32[2,4,64,1024]{3,2,1,0:T(8,128)S(1)} fusion(bf16[2,4,64,1024]{3,2,1,0:T(8,128)(2,1)S(1)} %bitcast.102, bf16[2,1024,1024]{2,1,0:T(8,128)(2,1)} %refs_2_.1, s32[]{:T(128)S(6)} %select_n.119), kind=kOutput, calls=%fused_computation.2 | convolution fusion | flops 1073741824 | bytes 5242884 | tf_op jit(solution)/shard_map/dot_general | solution.py:17
  14.5 0.9 dynamic-slice_convert_fusion.2
  15.4 12.2 %all-to-all-done = bf16[4,72,1024]{2,1,0:T(8,128)(2,1)S(1)} async-done(((bf16[4,72,1024]{2,1,0:T(8,128)(2,1)}), bf16[4,72,1024]{2,1,0:T(8,128)(2,1)S(1)}, u32[]{:S(2)}, u32[]{:S(2)}) %all-to-all-start) | async-done | bytes 589856 | tf_op jit(solution)/shard_map/all_to_all | solution.py:217
  27.6 1.5 collective-permute-start.4
  29.8 1.6 %broadcast_in_dim.61 = bf16[4,2,128,1024]{3,2,1,0:T(8,128)(2,1)} broadcast(bf16[2,128,1024]{2,1,0:T(8,128)(2,1)S(1)} %bitcast.98), dimensions={1,2,3} | broadcast | bytes 2621440 | tf_op jit(solution)/shard_map/broadcast_in_dim | solution.py:241
  31.4 3.8 %all-to-all-start.1 = ((bf16[8,128,1024]{2,1,0:T(8,128)(2,1)}), bf16[8,128,1024]{2,1,0:T(8,128)(2,1)S(1)}, u32[]{:S(2)}, u32[]{:S(2)}) async-start(bf16[8,128,1024]{2,1,0:T(8,128)(2,1)} %bitcast.94), calls=%async_computation.1 | async-start | bytes 4194304 | tf_op jit(solution)/shard_map/all_to_all | solution.py:243
  36.1 4.5 %gather_fusion = bf16[128,1024]{1,0:T(8,128)(2,1)} fusion(bf16[2048,1024]{1,0:T(8,128)(2,1)} %bitcast.101, s32[1024]{0:T(1024)S(1)} %pad_clamp_fusion), kind=kCustom, calls=%fused_computation | custom fusion | bytes 524800 | tf_op jit(solution)/shard_map/jit(_take)/gather | solution.py:237
  40.7 9.4 %collective-permute-done.3 = bf16[128,1024]{1,0:T(8,128)(2,1)S(1)} collective-permute-done((bf16[128,1024]{1,0:T(8,128)(2,1)}, bf16[128,1024]{1,0:T(8,128)(2,1)S(1)}, u32[]{:S(2)}, u32[]{:S(2)}) %collective-permute-start.3) | collective-permute-done | bytes 262176 | tf_op jit(solution)/shard_map/ppermute | solution.py:185
  50.8 1.4 multiply_reduce_fusion.3
  52.4 0.9 collective-permute-start.6
  53.3 1.2 collective-permute-start.8
  54.5 4.7 %collective-permute-done.8 = s32[2,128]{1,0:T(2,128)S(1)} collective-permute-done((s32[2,128]{1,0:T(2,128)S(1)}, s32[2,128]{1,0:T(2,128)S(1)}, u32[]{:S(2)}, u32[]{:S(2)}) %collective-permute-start.8) | collective-permute-done | bytes 1056 | tf_op jit(solution)/shard_map/ppermute | solution.py:188
  59.3 2.7 %all-to-all-done.1 = bf16[8,128,1024]{2,1,0:T(8,128)(2,1)S(1)} async-done(((bf16[8,128,1024]{2,1,0:T(8,128)(2,1)}), bf16[8,128,1024]{2,1,0:T(8,128)(2,1)S(1)}, u32[]{:S(2)}, u32[]{:S(2)}) %all-to-all-start.1) | async-done | bytes 2097184 | tf_op jit(solution)/shard_map/all_to_all | solution.py:243
  61.9 1.8 %fusion.31 = (f32[256]{0:T(256)S(1)}, f32[256,1024]{1,0:T(8,128)S(1)}) fusion(bf16[1024,1024]{1,0:T(8,128)(2,1)S(1)} %bitcast.92, bf16[128,1024]{1,0:T(8,128)(2,1)} %collective-permute-done.6, bf16[128,1024]{1,0:T(8,128)(2,1)} %copy-done.4), kind=kOutput, calls=%fused_computation.95 | convolution fusion | flops 538181376 | bytes 3671040 | tf_op jit(solution)/shard_map/dot_general | solution.py:17
  64.1 3.0 %collective-permute-start.7 = (f32[2,2,128]{2,1,0:T(2,128)S(1)}, f32[2,2,128]{2,1,0:T(2,128)S(1)}, u32[]{:S(2)}, u32[]{:S(2)}) collective-permute-start(f32[2,2,128]{2,1,0:T(2,128)S(1)} %pad_maximum_fusion.4), channel_id=1, source_target_pairs={{0,1},{1,0},{2,3},{3,2},{4,5},{5,4},{6,7},{7,6},{8,9},{9,8},{10,11... | collective-permute-start | bytes 6152 | tf_op jit(solution)/shard_map/ppermute | solution.py:188
  67.1 1.6 %collective-permute-done.7 = f32[2,2,128]{2,1,0:T(2,128)S(1)} collective-permute-done((f32[2,2,128]{2,1,0:T(2,128)S(1)}, f32[2,2,128]{2,1,0:T(2,128)S(1)}, u32[]{:S(2)}, u32[]{:S(2)}) %collective-permute-start.7) | collective-permute-done | bytes 2080 | tf_op jit(solution)/shard_map/ppermute | solution.py:188
  69.1 0.7 fusion.32
  69.8 1.0 copy-done.1
  70.8 2.1 %collective-permute-start.9 = (bf16[128,1024]{1,0:T(8,128)(2,1)S(1)}, bf16[128,1024]{1,0:T(8,128)(2,1)}, u32[]{:S(2)}, u32[]{:S(2)}) collective-permute-start(bf16[128,1024]{1,0:T(8,128)(2,1)S(1)} %slice.86), channel_id=1, source_target_pairs={{0,1},{1,0},{2,3},{3,2},{4,5},{5,4},{6,7},{7,6},{8,9},{9,8},{10,11... | collective-permute-start | bytes 786440 | tf_op jit(solution)/shard_map/ppermute | solution.py:188
  72.9 3.0 %convolution_convert_fusion = bf16[1024,1024]{1,0:T(8,128)(2,1)} fusion(bf16[256,1024]{1,0:T(8,128)(2,1)S(1)} %multiply_convert_fusion, bf16[128,1024]{1,0:T(8,128)(2,1)} %collective-permute-done.6, bf16[128,1024]{1,0:T(8,128)(2,1)S(1)} %copy-done.5), kind=kOutput, calls=%fused_computation.5 | convolution fusion | flops 538968064 | bytes 3145728 | tf_op jit(solution)/shard_map/dot_general | solution.py:17
  76.0 1.4 collective-permute-done.9
  77.4 3.6 %all-to-all-start.3 = ((bf16[8,128,1024]{2,1,0:T(8,128)(2,1)}), bf16[8,128,1024]{2,1,0:T(8,128)(2,1)S(1)}, u32[]{:S(2)}, u32[]{:S(2)}) async-start(bf16[8,128,1024]{2,1,0:T(8,128)(2,1)} %bitcast.96), calls=%async_computation.3 | async-start | bytes 4194304 | tf_op jit(solution)/shard_map/all_to_all | solution.py:286
  81.0 1.3 multiply_reduce_fusion.2
  82.3 2.3 %multiply_reduce_fusion.1 = (f32[128]{0:T(128)S(1)}, bf16[128,1024]{1,0:T(8,128)(2,1)}) fusion(bf16[128,1024]{1,0:T(8,128)(2,1)S(1)} %collective-permute-done.4, bf16[128,1024]{1,0:T(8,128)(2,1)} %copy-done.3, bf16[128,1024]{1,0:T(8,128)(2,1)} %collective-permute-done.2, f32[2,1,64,1024]{3,2,1,0:T(8,128)S(1)} %constant_dynamic-slice_fusion.4, ...), kind=kLoop, calls=%fused_computation.17 | loop fusion | flops 2097024 | bytes 2889728 | tf_op jit(solution)/shard_map/reduce_sum | solution.py:282
  84.6 2.0 %collective-permute-start.10 = (bf16[128,1024]{1,0:T(8,128)(2,1)}, bf16[128,1024]{1,0:T(8,128)(2,1)S(1)}, u32[]{:S(2)}, u32[]{:S(2)}) collective-permute-start(bf16[128,1024]{1,0:T(8,128)(2,1)} %get-tuple-element.37.refs_0_), channel_id=1, source_target_pairs={{0,1},{1,2},{2,3},{3,0},{4,5},{5,6},{6,7},{7,4},{8,9},{9,10},{10,1... | collective-permute-start | bytes 786440 | tf_op jit(solution)/shard_map/ppermute | solution.py:185
  86.7 0.9 collective-permute-start.11
  87.6 2.0 %collective-permute-start.12 = (bf16[128,1024]{1,0:T(8,128)(2,1)}, bf16[128,1024]{1,0:T(8,128)(2,1)S(1)}, u32[]{:S(2)}, u32[]{:S(2)}) collective-permute-start(bf16[128,1024]{1,0:T(8,128)(2,1)} %get-tuple-element.37.refs_0_), channel_id=1, source_target_pairs={{0,3},{1,0},{2,1},{3,2},{4,7},{5,4},{6,5},{7,6},{8,11},{9,8},{10,9... | collective-permute-start | bytes 786440 | tf_op jit(solution)/shard_map/ppermute | solution.py:185
  90.2 0.9 copy.43.refs_6_
  91.1 4.8 %collective-permute-done.10.refs_1_ = bf16[128,1024]{1,0:T(8,128)(2,1)S(1)} collective-permute-done((bf16[128,1024]{1,0:T(8,128)(2,1)}, bf16[128,1024]{1,0:T(8,128)(2,1)S(1)}, u32[]{:S(2)}, u32[]{:S(2)}) %collective-permute-start.10) | collective-permute-done | bytes 262176 | tf_op jit(solution)/shard_map/ppermute | solution.py:185
  95.9 10.7 %collective-permute-done.11.refs_2_ = bf16[128,1024]{1,0:T(8,128)(2,1)S(1)} collective-permute-done((bf16[128,1024]{1,0:T(8,128)(2,1)}, bf16[128,1024]{1,0:T(8,128)(2,1)S(1)}, u32[]{:S(2)}, u32[]{:S(2)}) %collective-permute-start.11) | collective-permute-done | bytes 262176 | tf_op jit(solution)/shard_map/ppermute | solution.py:185
  108.1 5.1 %shard_map.85 = (bf16[1024,1024]{1,0:T(8,128)(2,1)}, bf16[256,1024]{1,0:T(8,128)(2,1)}, bf16[256,1024]{1,0:T(8,128)(2,1)}) custom-call(s32[2]{0:T(128)} %pad_add_fusion.2.place_ref, bf16[128,1024]{1,0:T(8,128)(2,1)} %get-tuple-element.37.refs_0_, bf16[128,1024]{1,0:T(8,128)(2,1)} %copy-done.12, bf16[128,1024]{1,0:T(8,128)(2,1)} %copy-done.13, ...), custom_call_target="tpu_custom_call" | custom-call | flops 1073741824 | bytes 2099200 | tf_op jit(solution)/shard_map/pallas_call | solution.py:33
  113.2 4.4 %all-to-all-start.2 = ((bf16[8,128,1024]{2,1,0:T(8,128)(2,1)}), bf16[8,128,1024]{2,1,0:T(8,128)(2,1)}, u32[]{:S(2)}, u32[]{:S(2)}) async-start(bf16[8,128,1024]{2,1,0:T(8,128)(2,1)} %bitcast.99), calls=%async_computation.2 | async-start | bytes 4194304 | tf_op jit(solution)/shard_map/all_to_all | solution.py:298
  118.9 5.4 %collective-permute-start.15 = (f32[64]{0:T(128)S(1)}, f32[64]{0:T(128)S(1)}, u32[]{:S(2)}, u32[]{:S(2)}) collective-permute-start(f32[64]{0:T(128)S(1)} %slice_add_fusion.1), channel_id=1, source_target_pairs={{0,1},{1,2},{2,3},{3,0},{4,5},{5,6},{6,7},{7,4},{8,9},{9,10},{10,1... | collective-permute-start | bytes 776 | tf_op jit(solution)/shard_map/ppermute | solution.py:185
  124.3 1.8 %collective-permute-start.16 = (f32[64]{0:T(128)S(1)}, f32[64]{0:T(128)S(1)}, u32[]{:S(2)}, u32[]{:S(2)}) collective-permute-start(f32[64]{0:T(128)S(1)} %slice_add_fusion.1), channel_id=1, source_target_pairs={{0,2},{1,3},{2,0},{3,1},{4,6},{5,7},{6,4},{7,5},{8,10},{9,11},{10,... | collective-permute-start | bytes 776 | tf_op jit(solution)/shard_map/ppermute | solution.py:185
  127.1 1.7 %collective-permute-done.16 = f32[64]{0:T(128)S(1)} collective-permute-done((f32[64]{0:T(128)S(1)}, f32[64]{0:T(128)S(1)}, u32[]{:S(2)}, u32[]{:S(2)}) %collective-permute-start.16) | collective-permute-done | bytes 288 | tf_op jit(solution)/shard_map/ppermute | solution.py:185
  128.8 0.8 collective-permute-done.17
  130.9 3.0 %collective-permute-start.19 = (bf16[2,32,1024]{2,1,0:T(8,128)(2,1)S(1)}, bf16[2,32,1024]{2,1,0:T(8,128)(2,1)S(1)}, u32[]{:S(2)}, u32[]{:S(2)}) collective-permute-start(bf16[2,32,1024]{2,1,0:T(8,128)(2,1)S(1)} %get-tuple-element.46), channel_id=1, source_target_pairs={{0,2},{1,3},{2,0},{3,1},{4,6},{5,7},{6,4},{7,5},{8,10},{9,11},{10,... | collective-permute-start | bytes 393224 | tf_op jit(solution)/shard_map/ppermute | solution.py:185
  133.9 1.1 collective-permute-start.20
  135.0 0.9 copy.44.refs_4_
  135.9 0.8 copy-done.7
  136.7 5.9 %shard_map.86 = bf16[256,1024]{1,0:T(8,128)(2,1)} custom-call(s32[2]{0:T(128)} %pad_add_fusion.2.place_ref, bf16[256,1024]{1,0:T(8,128)(2,1)} %get-tuple-element.20.refs_0_, bf16[256,1024]{1,0:T(8,128)(2,1)} %copy-done.7, bf16[2,1024,1024]{2,1,0:T(8,128)(2,1)} %refs_2_.1, bf16[256,1024]{1,0:T(8,128)(2,1)} %refs_3_.1, f32[2,256,1]{2,1,0:T(8,128)} %copy.44.refs_4_), custom_call_target="tpu_custom_call" | custom-call | flops 1073741824 | bytes 5769216 | tf_op jit(solution)/shard_map/pallas_call | solution.py:33
  143.5 2.7 %shard_map.87 = f32[32,2,2048]{2,1,0:T(2,128)} custom-call(s32[2]{0:T(128)} %pad_add_fusion.2.place_ref, bf16[2,32,1024]{2,1,0:T(8,128)(2,1)} %get-tuple-element.48.refs_0_, bf16[2,32,1024]{2,1,0:T(8,128)(2,1)} %copy-done.8, bf16[2,32,1024]{2,1,0:T(8,128)(2,1)} %copy-done.9, bf16[2,32,1024]{2,1,0:T(8,128)(2,1)} %copy-done.10), custom_call_target="tpu_custom_call" | custom-call | flops 262144 | bytes 524288 | tf_op jit(solution)/shard_map/pallas_call | solution.py:33
  146.2 2.1 %convert_reduce_fusion = f32[2,128,1024]{2,1,0:T(8,128)S(1)} fusion(bf16[4,2,128,1024]{3,2,1,0:T(8,128)(2,1)} %bitcast.57), kind=kLoop, calls=%fused_computation.1 | loop fusion | flops 1835008 | bytes 3145728 | tf_op jit(solution)/shard_map/reduce_sum | solution.py:299
  148.3 1.3 copy.45
  (105 shorter events, 11.2 us)
Async XLA Ops:
  0.6 10.8 %copy-start = (f32[2,1024]{1,0:T(2,128)S(1)}, f32[2,1024]{1,0:T(2,128)}, u32[]{:S(2)}) copy-start(f32[2,1024]{1,0:T(2,128)} %param.9) | copy-start | bytes 24580
  0.6 2.3 %collective-permute-start = (bf16[256,1024]{1,0:T(8,128)(2,1)}, bf16[256,1024]{1,0:T(8,128)(2,1)S(1)}, u32[]{:S(2)}, u32[]{:S(2)}) collective-permute-start(bf16[256,1024]{1,0:T(8,128)(2,1)} %refs_3_.1), channel_id=1, source_target_pairs={{0,4},{4,0},{8,12},{12,8},{16,20},{20,16},{24,28},{28,24},{1,5},{5... | collective-permute-start | bytes 1572872 | tf_op jit(solution)/shard_map/ppermute | solution.py:195
  2.4 9.1 %copy-start.2 = (bf16[256,1024]{1,0:T(8,128)(2,1)S(1)}, bf16[256,1024]{1,0:T(8,128)(2,1)}, u32[]{:S(2)}) copy-start(bf16[256,1024]{1,0:T(8,128)(2,1)} %refs_3_.1) | copy-start | bytes 1572868
  2.9 8.6 %copy-start.6 = (bf16[256,1024]{1,0:T(8,128)(2,1)}, bf16[256,1024]{1,0:T(8,128)(2,1)S(1)}, u32[]{:S(2)}) copy-start(bf16[256,1024]{1,0:T(8,128)(2,1)S(1)} %collective-permute-done.refs_5_) | copy-start | bytes 1572868
  5.2 22.4 %all-to-all-start = ((bf16[4,72,1024]{2,1,0:T(8,128)(2,1)}), bf16[4,72,1024]{2,1,0:T(8,128)(2,1)S(1)}, u32[]{:S(2)}, u32[]{:S(2)}) async-start(bf16[4,72,1024]{2,1,0:T(8,128)(2,1)} %bitcast.6), calls=%async_computation | async-start | bytes 1179648 | tf_op jit(solution)/shard_map/all_to_all | solution.py:217
  14.4 15.2 %copy-start.11 = (s32[2,64]{1,0:T(2,128)S(1)}, s32[2,64]{1,0:T(2,128)}, u32[]{:S(2)}) copy-start(s32[2,64]{1,0:T(2,128)} %param.11) | copy-start | bytes 1540
  27.6 13.1 %collective-permute-start.4 = (bf16[128,1024]{1,0:T(8,128)(2,1)}, bf16[128,1024]{1,0:T(8,128)(2,1)S(1)}, u32[]{:S(2)}, u32[]{:S(2)}) collective-permute-start(bf16[128,1024]{1,0:T(8,128)(2,1)} %bitcast.14), channel_id=1, source_target_pairs={{0,3},{1,0},{2,1},{3,2},{4,7},{5,4},{6,5},{7,6},{8,11},{9,8},{10,9... | collective-permute-start | bytes 786440 | tf_op jit(solution)/shard_map/ppermute | solution.py:185
  29.1 21.0 %collective-permute-start.3 = (bf16[128,1024]{1,0:T(8,128)(2,1)}, bf16[128,1024]{1,0:T(8,128)(2,1)S(1)}, u32[]{:S(2)}, u32[]{:S(2)}) collective-permute-start(bf16[128,1024]{1,0:T(8,128)(2,1)} %bitcast.13), channel_id=1, source_target_pairs={{0,2},{1,3},{2,0},{3,1},{4,6},{5,7},{6,4},{7,5},{8,10},{9,11},{10,... | collective-permute-start | bytes 786440 | tf_op jit(solution)/shard_map/ppermute | solution.py:185
  29.1 21.7 %collective-permute-start.2 = (bf16[128,1024]{1,0:T(8,128)(2,1)S(1)}, bf16[128,1024]{1,0:T(8,128)(2,1)}, u32[]{:S(2)}, u32[]{:S(2)}) collective-permute-start(bf16[128,1024]{1,0:T(8,128)(2,1)S(1)} %bitcast.105), channel_id=1, source_target_pairs={{0,1},{1,2},{2,3},{3,0},{4,5},{5,6},{6,7},{7,4},{8,9},{9,10},{10,1... | collective-permute-start | bytes 786440 | tf_op jit(solution)/shard_map/ppermute | solution.py:185
  29.7 6.3 %collective-permute-start.5 = (s32[2,64]{1,0:T(2,128)S(1)}, s32[2,64]{1,0:T(2,128)S(1)}, u32[]{:S(2)}, u32[]{:S(2)}) collective-permute-start(s32[2,64]{1,0:T(2,128)S(1)} %copy-done.11), channel_id=1, source_target_pairs={{0,4},{4,0},{8,12},{12,8},{16,20},{20,16},{24,28},{28,24},{1,5},{5... | collective-permute-start | bytes 1544 | tf_op jit(solution)/shard_map/ppermute | solution.py:195
  31.4 30.5 %all-to-all-start.1 = ((bf16[8,128,1024]{2,1,0:T(8,128)(2,1)}), bf16[8,128,1024]{2,1,0:T(8,128)(2,1)S(1)}, u32[]{:S(2)}, u32[]{:S(2)}) async-start(bf16[8,128,1024]{2,1,0:T(8,128)(2,1)} %bitcast.94), calls=%async_computation.1 | async-start | bytes 4194304 | tf_op jit(solution)/shard_map/all_to_all | solution.py:243
  35.3 5.2 %collective-permute-start.1 = (f32[256]{0:T(256)S(1)}, f32[256]{0:T(256)S(1)}, u32[]{:S(2)}, u32[]{:S(2)}) collective-permute-start(f32[256]{0:T(256)S(1)} %reduce_sum.85), channel_id=1, source_target_pairs={{0,4},{4,0},{8,12},{12,8},{16,20},{20,16},{24,28},{28,24},{1,5},{5... | collective-permute-start | bytes 3080 | tf_op jit(solution)/shard_map/ppermute | solution.py:195
  50.1 0.7 copy-start.3
  52.4 6.8 %copy-start.4 = (bf16[128,1024]{1,0:T(8,128)(2,1)}, bf16[128,1024]{1,0:T(8,128)(2,1)S(1)}, u32[]{:S(2)}) copy-start(bf16[128,1024]{1,0:T(8,128)(2,1)S(1)} %multiply_convert_fusion.1) | copy-start | bytes 786436
  52.4 6.8 %collective-permute-start.6 = (bf16[128,1024]{1,0:T(8,128)(2,1)S(1)}, bf16[128,1024]{1,0:T(8,128)(2,1)}, u32[]{:S(2)}, u32[]{:S(2)}) collective-permute-start(bf16[128,1024]{1,0:T(8,128)(2,1)S(1)} %multiply_convert_fusion.1), channel_id=1, source_target_pairs={{0,1},{1,0},{2,3},{3,2},{4,5},{5,4},{6,7},{7,6},{8,9},{9,8},{10,11... | collective-permute-start | bytes 786440 | tf_op jit(solution)/shard_map/ppermute | solution.py:188
  53.3 6.0 %collective-permute-start.8 = (s32[2,128]{1,0:T(2,128)S(1)}, s32[2,128]{1,0:T(2,128)S(1)}, u32[]{:S(2)}, u32[]{:S(2)}) collective-permute-start(s32[2,128]{1,0:T(2,128)S(1)} %pad_add_fusion), channel_id=1, source_target_pairs={{0,1},{1,0},{2,3},{3,2},{4,5},{5,4},{6,7},{7,6},{8,9},{9,8},{10,11... | collective-permute-start | bytes 3080 | tf_op jit(solution)/shard_map/ppermute | solution.py:188
  64.1 4.6 %collective-permute-start.7 = (f32[2,2,128]{2,1,0:T(2,128)S(1)}, f32[2,2,128]{2,1,0:T(2,128)S(1)}, u32[]{:S(2)}, u32[]{:S(2)}) collective-permute-start(f32[2,2,128]{2,1,0:T(2,128)S(1)} %pad_maximum_fusion.4), channel_id=1, source_target_pairs={{0,1},{1,0},{2,3},{3,2},{4,5},{5,4},{6,7},{7,6},{8,9},{9,8},{10,11... | collective-permute-start | bytes 6152 | tf_op jit(solution)/shard_map/ppermute | solution.py:188
  69.1 3.9 %copy-start.5 = (bf16[128,1024]{1,0:T(8,128)(2,1)S(1)}, bf16[128,1024]{1,0:T(8,128)(2,1)}, u32[]{:S(2)}) copy-start(bf16[128,1024]{1,0:T(8,128)(2,1)} %copy-done.4) | copy-start | bytes 786436
  69.8 1.0 copy-start.1
  70.8 6.5 %collective-permute-start.9 = (bf16[128,1024]{1,0:T(8,128)(2,1)S(1)}, bf16[128,1024]{1,0:T(8,128)(2,1)}, u32[]{:S(2)}, u32[]{:S(2)}) collective-permute-start(bf16[128,1024]{1,0:T(8,128)(2,1)S(1)} %slice.86), channel_id=1, source_target_pairs={{0,1},{1,0},{2,3},{3,2},{4,5},{5,4},{6,7},{7,6},{8,9},{9,8},{10,11... | collective-permute-start | bytes 786440 | tf_op jit(solution)/shard_map/ppermute | solution.py:188
  77.4 35.8 %all-to-all-start.3 = ((bf16[8,128,1024]{2,1,0:T(8,128)(2,1)}), bf16[8,128,1024]{2,1,0:T(8,128)(2,1)S(1)}, u32[]{:S(2)}, u32[]{:S(2)}) async-start(bf16[8,128,1024]{2,1,0:T(8,128)(2,1)} %bitcast.96), calls=%async_computation.3 | async-start | bytes 4194304 | tf_op jit(solution)/shard_map/all_to_all | solution.py:286
  84.6 11.3 %collective-permute-start.10 = (bf16[128,1024]{1,0:T(8,128)(2,1)}, bf16[128,1024]{1,0:T(8,128)(2,1)S(1)}, u32[]{:S(2)}, u32[]{:S(2)}) collective-permute-start(bf16[128,1024]{1,0:T(8,128)(2,1)} %get-tuple-element.37.refs_0_), channel_id=1, source_target_pairs={{0,1},{1,2},{2,3},{3,0},{4,5},{5,6},{6,7},{7,4},{8,9},{9,10},{10,1... | collective-permute-start | bytes 786440 | tf_op jit(solution)/shard_map/ppermute | solution.py:185
  86.7 20.0 %collective-permute-start.11 = (bf16[128,1024]{1,0:T(8,128)(2,1)}, bf16[128,1024]{1,0:T(8,128)(2,1)S(1)}, u32[]{:S(2)}, u32[]{:S(2)}) collective-permute-start(bf16[128,1024]{1,0:T(8,128)(2,1)} %get-tuple-element.37.refs_0_), channel_id=1, source_target_pairs={{0,2},{1,3},{2,0},{3,1},{4,6},{5,7},{6,4},{7,5},{8,10},{9,11},{10,... | collective-permute-start | bytes 786440 | tf_op jit(solution)/shard_map/ppermute | solution.py:185
  87.6 19.1 %collective-permute-start.12 = (bf16[128,1024]{1,0:T(8,128)(2,1)}, bf16[128,1024]{1,0:T(8,128)(2,1)S(1)}, u32[]{:S(2)}, u32[]{:S(2)}) collective-permute-start(bf16[128,1024]{1,0:T(8,128)(2,1)} %get-tuple-element.37.refs_0_), channel_id=1, source_target_pairs={{0,3},{1,0},{2,1},{3,2},{4,7},{5,4},{6,5},{7,6},{8,11},{9,8},{10,9... | collective-permute-start | bytes 786440 | tf_op jit(solution)/shard_map/ppermute | solution.py:185
  95.9 10.7 %copy-start.12 = (bf16[128,1024]{1,0:T(8,128)(2,1)}, bf16[128,1024]{1,0:T(8,128)(2,1)S(1)}, u32[]{:S(2)}) copy-start(bf16[128,1024]{1,0:T(8,128)(2,1)S(1)} %collective-permute-done.10.refs_1_) | copy-start | bytes 786436
  106.6 0.7 copy-start.13
  107.3 0.7 copy-start.14
  113.2 33.1 %all-to-all-start.2 = ((bf16[8,128,1024]{2,1,0:T(8,128)(2,1)}), bf16[8,128,1024]{2,1,0:T(8,128)(2,1)}, u32[]{:S(2)}, u32[]{:S(2)}) async-start(bf16[8,128,1024]{2,1,0:T(8,128)(2,1)} %bitcast.99), calls=%async_computation.2 | async-start | bytes 4194304 | tf_op jit(solution)/shard_map/all_to_all | solution.py:298
  117.7 1.2 collective-permute-start.14
  118.0 17.9 %collective-permute-start.13 = (bf16[256,1024]{1,0:T(8,128)(2,1)}, bf16[256,1024]{1,0:T(8,128)(2,1)S(1)}, u32[]{:S(2)}, u32[]{:S(2)}) collective-permute-start(bf16[256,1024]{1,0:T(8,128)(2,1)} %get-tuple-element.21), channel_id=1, source_target_pairs={{0,4},{4,0},{8,12},{12,8},{16,20},{20,16},{24,28},{28,24},{1,5},{5... | collective-permute-start | bytes 1572872 | tf_op jit(solution)/shard_map/ppermute | solution.py:195
  118.9 8.1 %collective-permute-start.15 = (f32[64]{0:T(128)S(1)}, f32[64]{0:T(128)S(1)}, u32[]{:S(2)}, u32[]{:S(2)}) collective-permute-start(f32[64]{0:T(128)S(1)} %slice_add_fusion.1), channel_id=1, source_target_pairs={{0,1},{1,2},{2,3},{3,0},{4,5},{5,6},{6,7},{7,4},{8,9},{9,10},{10,1... | collective-permute-start | bytes 776 | tf_op jit(solution)/shard_map/ppermute | solution.py:185
  124.3 4.4 %collective-permute-start.16 = (f32[64]{0:T(128)S(1)}, f32[64]{0:T(128)S(1)}, u32[]{:S(2)}, u32[]{:S(2)}) collective-permute-start(f32[64]{0:T(128)S(1)} %slice_add_fusion.1), channel_id=1, source_target_pairs={{0,2},{1,3},{2,0},{3,1},{4,6},{5,7},{6,4},{7,5},{8,10},{9,11},{10,... | collective-permute-start | bytes 776 | tf_op jit(solution)/shard_map/ppermute | solution.py:185
  126.1 3.5 %collective-permute-start.17 = (f32[64]{0:T(128)S(1)}, f32[64]{0:T(128)S(1)}, u32[]{:S(2)}, u32[]{:S(2)}) collective-permute-start(f32[64]{0:T(128)S(1)} %slice_add_fusion.1), channel_id=1, source_target_pairs={{0,3},{1,0},{2,1},{3,2},{4,7},{5,4},{6,5},{7,6},{8,11},{9,8},{10,9... | collective-permute-start | bytes 776 | tf_op jit(solution)/shard_map/ppermute | solution.py:185
  130.9 11.7 %collective-permute-start.18 = (bf16[2,32,1024]{2,1,0:T(8,128)(2,1)S(1)}, bf16[2,32,1024]{2,1,0:T(8,128)(2,1)S(1)}, u32[]{:S(2)}, u32[]{:S(2)}) collective-permute-start(bf16[2,32,1024]{2,1,0:T(8,128)(2,1)S(1)} %get-tuple-element.47), channel_id=1, source_target_pairs={{0,1},{1,2},{2,3},{3,0},{4,5},{5,6},{6,7},{7,4},{8,9},{9,10},{10,1... | collective-permute-start | bytes 393224 | tf_op jit(solution)/shard_map/ppermute | solution.py:185
  130.9 11.9 %collective-permute-start.19 = (bf16[2,32,1024]{2,1,0:T(8,128)(2,1)S(1)}, bf16[2,32,1024]{2,1,0:T(8,128)(2,1)S(1)}, u32[]{:S(2)}, u32[]{:S(2)}) collective-permute-start(bf16[2,32,1024]{2,1,0:T(8,128)(2,1)S(1)} %get-tuple-element.46), channel_id=1, source_target_pairs={{0,2},{1,3},{2,0},{3,1},{4,6},{5,7},{6,4},{7,5},{8,10},{9,11},{10,... | collective-permute-start | bytes 393224 | tf_op jit(solution)/shard_map/ppermute | solution.py:185
  133.9 9.0 %collective-permute-start.20 = (bf16[2,32,1024]{2,1,0:T(8,128)(2,1)S(1)}, bf16[2,32,1024]{2,1,0:T(8,128)(2,1)S(1)}, u32[]{:S(2)}, u32[]{:S(2)}) collective-permute-start(bf16[2,32,1024]{2,1,0:T(8,128)(2,1)S(1)} %get-tuple-element.45), channel_id=1, source_target_pairs={{0,3},{1,0},{2,1},{3,2},{4,7},{5,4},{6,5},{7,6},{8,11},{9,8},{10,9... | collective-permute-start | bytes 393224 | tf_op jit(solution)/shard_map/ppermute | solution.py:185
  135.9 0.8 copy-start.7
  142.6 0.7 copy-start.8
  142.8 0.7 copy-start.9
  142.8 0.7 copy-start.10

commit v4 on v3

--- a/solution.py
+++ b/solution.py
@@ -43,18 +43,6 @@
         compiler_params=VMEM,
         cost_estimate=pl.CostEstimate(flops=flops, bytes_accessed=moved, transcendentals=0),
     )(place, *args)
-
-
-EXACT = 3
-
-
-def parts_of(values):
-    out = []
-    for _ in range(EXACT):
-        piece = lax.reduce_precision(values, 8, 7)
-        values = values - piece
-        out.append(piece.astype(BF16))
-    return out
 
 
 def head_gradient(place, pieces, halves):
@@ -203,21 +191,16 @@
 
     group = [hidden] + [flip_seq(hidden, -m) for m in relations]
 
-    squares_part = jnp.sum(jnp.square(hidden.astype(F32)), axis=1)
-    tail = 8 * block
-    small = jnp.concatenate(parts_of(squares_part))
-    small = jnp.pad(small, (0, tail - small.size)).reshape(1, 1, 8, block)
-    head_send = after(w_out, *group[1:]).reshape(head_rows, steps, halves, block)
-    head_send = head_send.transpose(2, 1, 0, 3)
-    head_send = head_send.reshape(1, halves, steps * head_rows, block)
-    small = jnp.broadcast_to(small, (1, halves, 8, block))
-    head_send = jnp.concatenate([head_send, small], axis=2)
-    head_send = jnp.broadcast_to(head_send, (hids // halves,) + head_send.shape[1:])
-    head_send = head_send.reshape(hids, steps * head_rows + 8, block)
-    head_got = lax.all_to_all(head_send, "hid", 0, 0)
-    head_mid = head_got[:, : steps * head_rows].reshape(hids, steps, head_rows, block)
-    squares = head_got[:, steps * head_rows :].reshape(hids, tail)[:, : EXACT * rows]
-    squares = jnp.sum(squares.astype(F32).reshape(hids * EXACT, rows), axis=0)
+    head_send = w_out.reshape(head_rows, steps, halves, block).transpose(2, 1, 0, 3)
+    head_send = jnp.broadcast_to(head_send, (hids // halves,) + head_send.shape)
+    head_send = head_send.reshape(hids, steps, head_rows, block)
+    head_mid = lax.all_to_all(head_send, "hid", 0, 0)
+
+    squares = jnp.sum(jnp.square(hidden.astype(F32)), axis=1)
+    squares = [squares] + [along_hid(squares, shift) for shift in range(1, hids)]
+    squares = sum(squares[1:], squares[0])
+    squares = jnp.stack([squares] + [flip_seq(squares, -m) for m in relations])
+    ratio_group = lax.rsqrt(squares / width_in + 1e-06).reshape(steps, hids, part)
 
     w_own = pick(w_in, step)
     proj_parts = matmul(jnp.concatenate(group), w_own, ((1,), (0,)))
@@ -227,7 +210,7 @@
         return lax.dynamic_index_in_dim(proj_parts, index, 1, False).reshape(owned, depth)
 
     send = [owner_block((j + shift) % hids).astype(BF16) for shift in range(1, hids)]
-    send = [after(p, head_got) for p in send]
+    send = [after(p, head_mid, ratio_group) for p in send]
     received = [along_hid(send[shift - 1], shift) for shift in range(1, hids)]
 
     ids = after(codebook_ids, *send)
@@ -241,9 +224,6 @@
     head_send = jnp.broadcast_to(head_send, (groups,) + head_send.shape)
     head_send = head_send.reshape(seqs, hids * head_rows, block)
     head = lax.all_to_all(head_send, "seq", 0, 0).reshape(depth, block)
-
-    squares = jnp.stack([squares] + [flip_seq(squares, -m) for m in relations])
-    ratio_group = lax.rsqrt(squares / width_in + 1e-06).reshape(steps, hids, part)
 
     ratio = lax.dynamic_index_in_dim(ratio_group, j, 1, False).reshape(owned, 1)
     proj = owner_block(j)
@@ -251,6 +231,7 @@
         proj += r.astype(F32)
     x_rows = ratio * proj + jnp.where(step > 0, looked.astype(F32), 0.0)
     scale = lax.rsqrt(jnp.mean(x_rows * x_rows, axis=1, keepdims=True) + 1e-06)
+    x_proj = jnp.sum(x_rows * proj, axis=1, keepdims=True)
     gain = pick(depth_gain, step)[None, :]
     normed = (x_rows * scale * gain).astype(BF16)
 
@@ -277,9 +258,10 @@
     for r in received:
         d_norm += r.astype(F32)
     gated = gain * d_norm
-    d_x = scale * gated - x_rows * scale**3 * jnp.mean(gated * x_rows, axis=1, keepdims=True)
-    d_round = d_x.astype(BF16)
-    d_ratio_part = jnp.sum(d_x * proj, axis=1).reshape(steps, part)
+    back_scale = scale**3 * jnp.mean(gated * x_rows, axis=1, keepdims=True)
+    gated_proj = jnp.sum(gated * proj, axis=1, keepdims=True)
+    d_round = (scale * gated - x_rows * back_scale).astype(BF16)
+    d_ratio_part = (scale * gated_proj - back_scale * x_proj).reshape(steps, part)
 
     part_out = matmul(normed_rows, after(d_logit, *away), ((0,), (0,))).astype(BF16)
     part_out = after(part_out, *received).reshape(seqs, depth // seqs, block)
@@ -294,11 +276,6 @@
 
     pieces = [d_round] + [along_hid(d_round, shift) for shift in range(1, hids)]
     ratio_rows = ratio_group.reshape(steps, rows, 1)
-    share, mine, *others = input_gradient(place, pieces, group, ratio_rows, seqs)
-    share = lax.all_to_all(share.reshape(seqs, depth // seqs, units), "seq", 0, 0)
-    share = share.reshape(groups, steps, depth // seqs, units).astype(F32).sum(0)
-    grad_in = share.transpose(0, 2, 1)
-
     d_ratio = d_ratio_part[0]
     for m in relations:
         d_ratio += flip_seq(d_ratio_part[m], m)
@@ -307,6 +284,11 @@
         d_rows = lax.dynamic_update_index_in_dim(
             d_rows, along_hid(d_ratio, shift), (j - shift) % hids, 0
         )
+    share, mine, *others = input_gradient(after(place, d_rows), pieces, group, ratio_rows, seqs)
+    share = lax.all_to_all(share.reshape(seqs, depth // seqs, units), "seq", 0, 0)
+    share = share.reshape(groups, steps, depth // seqs, units).astype(F32).sum(0)
+    grad_in = share.transpose(0, 2, 1)
+
     ratio_own = ratio_group[0].reshape(rows)
     correction = ratio_own**3 * d_rows.reshape(rows) / width_in
     factors = jnp.stack([ratio_own, correction])[:, :, None]

time: 151 us -> 161 us (1.066)
  waiting for transfers between devices: 51.9 us -> 66.5 us
  starting transfers between devices: 45.7 us -> 43.4 us
  matrix products: 8.46 us -> 6.57 us
    ppermute x12 -> x15, waiting for transfers between devices: 28.1 us -> 39.4 us  [along_hid(): lax.ppermute(values, 'hid', [(a, (a + shift) % hids) for a in range(hids)])]
    all_to_all x1, waiting for transfers between devices: 0.01 us -> 5.39 us  [shards(): lax.all_to_all(share.reshape(seqs, depth // seqs, units), 'seq', 0, 0)]
    ppermute x4, waiting for transfers between devices: 7.73 us -> 12.7 us  [turn_hid(): lax.ppermute(values, 'hid', [(a, a - a % halves + (a % halves + shift) %...]
    ppermute x4, starting transfers between devices: 7.17 us -> 2.77 us  [turn_hid(): lax.ppermute(values, 'hid', [(a, a - a % halves + (a % halves + shift) %...]
    all_to_all x1, waiting for transfers between devices: 12.2 us -> 7.99 us  [shards(): head_mid = lax.all_to_all(head_send, 'hid', 0, 0)]
    ppermute x12 -> x15, starting transfers between devices: 18.9 us -> 21.8 us  [along_hid(): lax.ppermute(values, 'hid', [(a, (a + shift) % hids) for a in range(hids)])]
    all_to_all x1, waiting for transfers between devices: 2.67 us -> 0.01 us  [shards(): head = lax.all_to_all(head_send, 'seq', 0, 0).reshape(depth, block)]
    reduce_sum x4 -> x2, other arithmetic: 4.87 us -> 2.7 us  [the longest x1 1.47 us: shards(): back_scale = scale ** 3 * jnp.mean(gated * x_rows, axis=1, keepdims=True)]
  transfers between devices with their start and end apart: 25 -> 28, of which waited for: 14 -> 13; matrix products, arithmetic and copies ran while one was open for 16% -> 14% of each run, Pallas kernels for 9% -> 9%
where the time goes in v4:
time: 161 us; the launch traced here: 160 us
  waiting for transfers between devices  66.5 us (41%)
  starting transfers between devices  43.4 us (27%)
  local copies, waits for them, and re-layouts  18.9 us (12%)
  Pallas kernels  13.7 us (9%)
  other arithmetic  9.91 us (6%)
  matrix products  6.57 us (4%)
    ppermute x15, waiting for transfers between devices, along_hid(): lax.ppermute(values, 'hid', [(a, (a + shift) % hids) for a in range(hids)])  39.4 us
    ppermute x15, starting transfers between devices, along_hid(): lax.ppermute(values, 'hid', [(a, (a + shift) % hids) for a in range(hids)])  21.8 us
    pallas_call x3, Pallas kernels, call(): pl.pallas_call(kernel, grid_spec=pltpu.PrefetchScalarGridSpec(num_scalar_...  13.7 us
    ppermute x4, waiting for transfers between devices, turn_hid(): lax.ppermute(values, 'hid', [(a, a - a % halves + (a % halves + shift) %...  12.7 us
    all_to_all x1, waiting for transfers between devices, shards(): head_mid = lax.all_to_all(head_send, 'hid', 0, 0)  7.99 us
    dot_general x4, matrix products, matmul(): lax.dot_general(a, b, (contract, ((), ())), preferred_element_type=F32)  6.57 us
    unnamed x33, local copies, waits for them, and re-layouts  6.54 us
    all_to_all x1, waiting for transfers between devices, shards(): lax.all_to_all(share.reshape(seqs, depth // seqs, units), 'seq', 0, 0)  5.39 us
  transfers between devices with their start and end apart: 28, of which 13 were waited for; matrix products, arithmetic and copies ran while one was open for 14% of the time, Pallas kernels for 9%

profile of v4, /device:TPU:0, one launch (start us, length us, event | category | flops | bytes accessed | tf_op | source)
XLA Modules:
  0.0 160.0 jit_solution(2824128214650955348)
XLA Ops:
  1.2 1.2 multiply_reduce_fusion
  2.4 4.7 %collective-permute-start.2 = (f32[256]{0:T(256)S(1)}, f32[256]{0:T(256)S(1)}, u32[]{:S(2)}, u32[]{:S(2)}) collective-permute-start(f32[256]{0:T(256)S(1)} %multiply_reduce_fusion), channel_id=1, source_target_pairs={{0,3},{1,0},{2,1},{3,2},{4,7},{5,4},{6,5},{7,6},{8,11},{9,8},{10,9... | collective-permute-start | bytes 3080 | tf_op jit(solution)/shard_map/ppermute | solution.py:173
  7.1 1.0 collective-permute-start
  8.1 1.1 reshape.241
  9.3 0.9 broadcast_in_dim.45
  10.2 4.1 %all-to-all-start = ((bf16[4,2,32,1024]{3,2,1,0:T(8,128)(2,1)}), bf16[4,2,32,1024]{3,2,1,0:T(8,128)(2,1)S(1)}, u32[]{:S(2)}, u32[]{:S(2)}) async-start(bf16[4,2,32,1024]{3,2,1,0:T(8,128)(2,1)} %bitcast.9), calls=%async_computation | async-start | bytes 1048576 | tf_op jit(solution)/shard_map/all_to_all | solution.py:197
  14.5 1.0 collective-permute-done.3
  15.7 3.0 %fusion = f32[2,4,64,1024]{3,2,1,0:T(8,128)S(1)} fusion(bf16[2,4,64,1024]{3,2,1,0:T(8,128)(2,1)S(1)} %bitcast.111, bf16[2,1024,1024]{2,1,0:T(8,128)(2,1)} %refs_2_.1, s32[]{:T(128)S(6)} %select_n.119), kind=kOutput, calls=%fused_computation.2 | convolution fusion | flops 1073741824 | bytes 5242884 | tf_op jit(solution)/shard_map/dot_general | solution.py:17
  18.7 1.3 copy-done.3
  20.0 0.8 dynamic-slice_convert_fusion
  20.8 8.0 %all-to-all-done = bf16[4,2,32,1024]{3,2,1,0:T(8,128)(2,1)S(1)} async-done(((bf16[4,2,32,1024]{3,2,1,0:T(8,128)(2,1)}), bf16[4,2,32,1024]{3,2,1,0:T(8,128)(2,1)S(1)}, u32[]{:S(2)}, u32[]{:S(2)}) %all-to-all-start) | async-done | bytes 524320 | tf_op jit(solution)/shard_map/all_to_all | solution.py:197
  28.9 1.6 %broadcast_in_dim.49 = bf16[4,2,128,1024]{3,2,1,0:T(8,128)(2,1)} broadcast(bf16[2,128,1024]{2,1,0:T(8,128)(2,1)S(1)} %bitcast.108), dimensions={1,2,3} | broadcast | bytes 2621440 | tf_op jit(solution)/shard_map/broadcast_in_dim | solution.py:224
  30.5 3.9 %all-to-all-start.1 = ((bf16[8,128,1024]{2,1,0:T(8,128)(2,1)}), bf16[8,128,1024]{2,1,0:T(8,128)(2,1)S(1)}, u32[]{:S(2)}, u32[]{:S(2)}) async-start(bf16[8,128,1024]{2,1,0:T(8,128)(2,1)} %bitcast.104), calls=%async_computation.1 | async-start | bytes 4194304 | tf_op jit(solution)/shard_map/all_to_all | solution.py:226
  34.9 1.1 constant_dynamic-slice_fusion.4
  36.1 3.8 %collective-permute-start.7 = (bf16[128,1024]{1,0:T(8,128)(2,1)S(1)}, bf16[128,1024]{1,0:T(8,128)(2,1)}, u32[]{:S(2)}, u32[]{:S(2)}) collective-permute-start(bf16[128,1024]{1,0:T(8,128)(2,1)S(1)} %bitcast.114), channel_id=1, source_target_pairs={{0,3},{1,0},{2,1},{3,2},{4,7},{5,4},{6,5},{7,6},{8,11},{9,8},{10,9... | collective-permute-start | bytes 786440 | tf_op jit(solution)/shard_map/ppermute | solution.py:173
  40.0 3.8 %gather_fusion = bf16[128,1024]{1,0:T(8,128)(2,1)S(1)} fusion(bf16[2048,1024]{1,0:T(8,128)(2,1)} %bitcast.110, s32[1024]{0:T(1024)S(1)} %pad_clamp_fusion), kind=kCustom, calls=%fused_computation | custom fusion | bytes 524800 | tf_op jit(solution)/shard_map/jit(_take)/gather | solution.py:220
  43.8 3.6 %collective-permute-done.5 = bf16[128,1024]{1,0:T(8,128)(2,1)} collective-permute-done((bf16[128,1024]{1,0:T(8,128)(2,1)}, bf16[128,1024]{1,0:T(8,128)(2,1)}, u32[]{:S(2)}, u32[]{:S(2)}) %collective-permute-start.5) | collective-permute-done | bytes 262176 | tf_op jit(solution)/shard_map/ppermute | solution.py:173
  47.4 3.6 %collective-permute-done.7 = bf16[128,1024]{1,0:T(8,128)(2,1)} collective-permute-done((bf16[128,1024]{1,0:T(8,128)(2,1)S(1)}, bf16[128,1024]{1,0:T(8,128)(2,1)}, u32[]{:S(2)}, u32[]{:S(2)}) %collective-permute-start.7) | collective-permute-done | bytes 262176 | tf_op jit(solution)/shard_map/ppermute | solution.py:173
  51.0 10.4 %collective-permute-done.6 = bf16[128,1024]{1,0:T(8,128)(2,1)} collective-permute-done((bf16[128,1024]{1,0:T(8,128)(2,1)S(1)}, bf16[128,1024]{1,0:T(8,128)(2,1)}, u32[]{:S(2)}, u32[]{:S(2)}) %collective-permute-start.6) | collective-permute-done | bytes 262176 | tf_op jit(solution)/shard_map/ppermute | solution.py:173
  61.4 1.4 multiply_reduce_fusion.4
  63.1 2.0 %collective-permute-start.11 = (s32[2,128]{1,0:T(2,128)S(1)}, s32[2,128]{1,0:T(2,128)S(1)}, u32[]{:S(2)}, u32[]{:S(2)}) collective-permute-start(s32[2,128]{1,0:T(2,128)S(1)} %pad_add_fusion), channel_id=1, source_target_pairs={{0,1},{1,0},{2,3},{3,2},{4,5},{5,4},{6,7},{7,6},{8,9},{9,8},{10,11... | collective-permute-start | bytes 3080 | tf_op jit(solution)/shard_map/ppermute | solution.py:176
  65.2 5.4 %collective-permute-done.11 = s32[2,128]{1,0:T(2,128)S(1)} collective-permute-done((s32[2,128]{1,0:T(2,128)S(1)}, s32[2,128]{1,0:T(2,128)S(1)}, u32[]{:S(2)}, u32[]{:S(2)}) %collective-permute-start.11) | collective-permute-done | bytes 1056 | tf_op jit(solution)/shard_map/ppermute | solution.py:176
  70.6 0.8 fusion.30
  72.1 3.3 %collective-permute-done.10 = f32[2,2,128]{2,1,0:T(2,128)S(1)} collective-permute-done((f32[2,2,128]{2,1,0:T(2,128)S(1)}, f32[2,2,128]{2,1,0:T(2,128)S(1)}, u32[]{:S(2)}, u32[]{:S(2)}) %collective-permute-start.10) | collective-permute-done | bytes 2080 | tf_op jit(solution)/shard_map/ppermute | solution.py:176
  76.6 1.0 copy-done.1
  78.0 2.0 %convolution_convert_fusion = bf16[1024,1024]{1,0:T(8,128)(2,1)} fusion(bf16[256,1024]{1,0:T(8,128)(2,1)S(1)} %multiply_convert_fusion, bf16[128,1024]{1,0:T(8,128)(2,1)S(1)} %copy-done.8, bf16[128,1024]{1,0:T(8,128)(2,1)S(1)} %multiply_convert_fusion.1), kind=kOutput, calls=%fused_computation.5 | convolution fusion | flops 538968064 | bytes 3145728 | tf_op jit(solution)/shard_map/dot_general | solution.py:17
  80.0 4.0 %collective-permute-done.12 = bf16[128,1024]{1,0:T(8,128)(2,1)S(1)} collective-permute-done((bf16[128,1024]{1,0:T(8,128)(2,1)S(1)}, bf16[128,1024]{1,0:T(8,128)(2,1)S(1)}, u32[]{:S(2)}, u32[]{:S(2)}) %collective-permute-start.12) | collective-permute-done | bytes 262176 | tf_op jit(solution)/shard_map/ppermute | solution.py:176
  84.0 4.5 %all-to-all-start.3 = ((bf16[8,128,1024]{2,1,0:T(8,128)(2,1)}), bf16[8,128,1024]{2,1,0:T(8,128)(2,1)S(1)}, u32[]{:S(2)}, u32[]{:S(2)}) async-start(bf16[8,128,1024]{2,1,0:T(8,128)(2,1)} %bitcast.106), calls=%async_computation.3 | async-start | bytes 4194304 | tf_op jit(solution)/shard_map/all_to_all | solution.py:268
  89.2 1.5 multiply_reduce_fusion.2
  91.3 1.3 subtract_convert_fusion.refs_0_
  93.4 1.0 collective-permute-start.18
  94.8 2.2 %collective-permute-start.14 = (f32[64]{0:T(128)S(1)}, f32[64]{0:T(128)S(1)}, u32[]{:S(2)}, u32[]{:S(2)}) collective-permute-start(f32[64]{0:T(128)S(1)} %bitcast_add_fusion.1), channel_id=1, source_target_pairs={{0,1},{1,2},{2,3},{3,0},{4,5},{5,6},{6,7},{7,4},{8,9},{9,10},{10,1... | collective-permute-start | bytes 776 | tf_op jit(solution)/shard_map/ppermute | solution.py:173
  96.9 0.9 copy.36.refs_6_
  97.8 1.9 %collective-permute-start.15 = (f32[64]{0:T(128)S(1)}, f32[64]{0:T(128)S(1)}, u32[]{:S(2)}, u32[]{:S(2)}) collective-permute-start(f32[64]{0:T(128)S(1)} %bitcast_add_fusion.1), channel_id=1, source_target_pairs={{0,2},{1,3},{2,0},{3,1},{4,6},{5,7},{6,4},{7,5},{8,10},{9,11},{10,... | collective-permute-start | bytes 776 | tf_op jit(solution)/shard_map/ppermute | solution.py:173
  99.8 11.6 %collective-permute-done.14 = f32[64]{0:T(128)S(1)} collective-permute-done((f32[64]{0:T(128)S(1)}, f32[64]{0:T(128)S(1)}, u32[]{:S(2)}, u32[]{:S(2)}) %collective-permute-start.14) | collective-permute-done | bytes 288 | tf_op jit(solution)/shard_map/ppermute | solution.py:173
  111.4 6.2 %collective-permute-done.15 = f32[64]{0:T(128)S(1)} collective-permute-done((f32[64]{0:T(128)S(1)}, f32[64]{0:T(128)S(1)}, u32[]{:S(2)}, u32[]{:S(2)}) %collective-permute-start.15) | collective-permute-done | bytes 288 | tf_op jit(solution)/shard_map/ppermute | solution.py:173
  117.6 1.3 collective-permute-done.16
  120.5 5.1 %shard_map.85 = (bf16[1024,1024]{1,0:T(8,128)(2,1)}, bf16[256,1024]{1,0:T(8,128)(2,1)}, bf16[256,1024]{1,0:T(8,128)(2,1)}) custom-call(s32[2]{0:T(128)} %pad_add_fusion.2.place_ref, bf16[128,1024]{1,0:T(8,128)(2,1)} %copy-done.6, bf16[128,1024]{1,0:T(8,128)(2,1)} %copy-done.15, bf16[128,1024]{1,0:T(8,128)(2,1)} %copy-done.14, bf16[128,1024]{1,0:T(8,128)(2,1)} %copy-done.13, ...), custom_call_target="tpu_custom_call" | custom-call | flops 1073741824 | bytes 2099200 | tf_op jit(solution)/shard_map/pallas_call | solution.py:33
  125.6 4.3 %all-to-all-start.2 = ((bf16[8,128,1024]{2,1,0:T(8,128)(2,1)}), bf16[8,128,1024]{2,1,0:T(8,128)(2,1)}, u32[]{:S(2)}, u32[]{:S(2)}) async-start(bf16[8,128,1024]{2,1,0:T(8,128)(2,1)} %bitcast.109), calls=%async_computation.2 | async-start | bytes 4194304 | tf_op jit(solution)/shard_map/all_to_all | solution.py:288
  131.6 3.2 %collective-permute-start.23 = (bf16[2,32,1024]{2,1,0:T(8,128)(2,1)S(1)}, bf16[2,32,1024]{2,1,0:T(8,128)(2,1)S(1)}, u32[]{:S(2)}, u32[]{:S(2)}) collective-permute-start(bf16[2,32,1024]{2,1,0:T(8,128)(2,1)S(1)} %get-tuple-element.46), channel_id=1, source_target_pairs={{0,3},{1,0},{2,1},{3,2},{4,7},{5,4},{6,5},{7,6},{8,11},{9,8},{10,9... | collective-permute-start | bytes 393224 | tf_op jit(solution)/shard_map/ppermute | solution.py:173
  135.6 2.0 %collective-permute-start.21 = (bf16[2,32,1024]{2,1,0:T(8,128)(2,1)S(1)}, bf16[2,32,1024]{2,1,0:T(8,128)(2,1)S(1)}, u32[]{:S(2)}, u32[]{:S(2)}) collective-permute-start(bf16[2,32,1024]{2,1,0:T(8,128)(2,1)S(1)} %get-tuple-element.48), channel_id=1, source_target_pairs={{0,1},{1,2},{2,3},{3,0},{4,5},{5,6},{6,7},{7,4},{8,9},{9,10},{10,1... | collective-permute-start | bytes 393224 | tf_op jit(solution)/shard_map/ppermute | solution.py:173
  137.6 0.9 copy.37.refs_4_
  139.2 5.9 %shard_map.86 = bf16[256,1024]{1,0:T(8,128)(2,1)} custom-call(s32[2]{0:T(128)} %pad_add_fusion.2.place_ref, bf16[256,1024]{1,0:T(8,128)(2,1)} %get-tuple-element.20.refs_0_, bf16[256,1024]{1,0:T(8,128)(2,1)} %copy-done.5, bf16[2,1024,1024]{2,1,0:T(8,128)(2,1)} %refs_2_.1, bf16[256,1024]{1,0:T(8,128)(2,1)} %refs_3_.1, f32[2,256,1]{2,1,0:T(8,128)} %copy.37.refs_4_), custom_call_target="tpu_custom_call" | custom-call | flops 1073741824 | bytes 5769216 | tf_op jit(solution)/shard_map/pallas_call | solution.py:33
  145.2 2.7 %collective-permute-done.22.refs_2_ = bf16[2,32,1024]{2,1,0:T(8,128)(2,1)S(1)} collective-permute-done((bf16[2,32,1024]{2,1,0:T(8,128)(2,1)S(1)}, bf16[2,32,1024]{2,1,0:T(8,128)(2,1)S(1)}, u32[]{:S(2)}, u32[]{:S(2)}) %collective-permute-start.22) | collective-permute-done | bytes 131104 | tf_op jit(solution)/shard_map/ppermute | solution.py:173
  148.5 2.7 %shard_map.87 = f32[32,2,2048]{2,1,0:T(2,128)} custom-call(s32[2]{0:T(128)} %pad_add_fusion.2.place_ref, bf16[2,32,1024]{2,1,0:T(8,128)(2,1)} %get-tuple-element.49.refs_0_, bf16[2,32,1024]{2,1,0:T(8,128)(2,1)} %copy-done.11, bf16[2,32,1024]{2,1,0:T(8,128)(2,1)} %copy-done.10, bf16[2,32,1024]{2,1,0:T(8,128)(2,1)} %copy-done.9), custom_call_target="tpu_custom_call" | custom-call | flops 262144 | bytes 524288 | tf_op jit(solution)/shard_map/pallas_call | solution.py:33
  151.2 5.4 %all-to-all-done.2 = bf16[8,128,1024]{2,1,0:T(8,128)(2,1)} async-done(((bf16[8,128,1024]{2,1,0:T(8,128)(2,1)}), bf16[8,128,1024]{2,1,0:T(8,128)(2,1)}, u32[]{:S(2)}, u32[]{:S(2)}) %all-to-all-start.2) | async-done | bytes 2097184 | tf_op jit(solution)/shard_map/all_to_all | solution.py:288
  156.6 2.1 %convert_reduce_fusion = f32[2,128,1024]{2,1,0:T(8,128)S(1)} fusion(bf16[4,2,128,1024]{3,2,1,0:T(8,128)(2,1)} %bitcast.60), kind=kLoop, calls=%fused_computation.1 | loop fusion | flops 1835008 | bytes 3145728 | tf_op jit(solution)/shard_map/reduce_sum | solution.py:289
  158.7 1.3 copy.38
  (105 shorter events, 12.2 us)
Async XLA Ops:
  0.6 33.7 %copy-start = (f32[2,1024]{1,0:T(2,128)S(1)}, f32[2,1024]{1,0:T(2,128)}, u32[]{:S(2)}) copy-start(f32[2,1024]{1,0:T(2,128)} %param.9) | copy-start | bytes 24580
  0.6 15.0 %copy-start.2 = (bf16[256,1024]{1,0:T(8,128)(2,1)S(1)}, bf16[256,1024]{1,0:T(8,128)(2,1)}, u32[]{:S(2)}) copy-start(bf16[256,1024]{1,0:T(8,128)(2,1)} %refs_3_.1) | copy-start | bytes 1572868
  0.7 15.0 %collective-permute-start.4 = (bf16[256,1024]{1,0:T(8,128)(2,1)}, bf16[256,1024]{1,0:T(8,128)(2,1)S(1)}, u32[]{:S(2)}, u32[]{:S(2)}) collective-permute-start(bf16[256,1024]{1,0:T(8,128)(2,1)} %refs_3_.1), channel_id=1, source_target_pairs={{0,4},{4,0},{8,12},{12,8},{16,20},{20,16},{24,28},{28,24},{1,5},{5... | collective-permute-start | bytes 1572872 | tf_op jit(solution)/shard_map/ppermute | solution.py:183
  2.4 11.9 %collective-permute-start.2 = (f32[256]{0:T(256)S(1)}, f32[256]{0:T(256)S(1)}, u32[]{:S(2)}, u32[]{:S(2)}) collective-permute-start(f32[256]{0:T(256)S(1)} %multiply_reduce_fusion), channel_id=1, source_target_pairs={{0,3},{1,0},{2,1},{3,2},{4,7},{5,4},{6,5},{7,6},{8,11},{9,8},{10,9... | collective-permute-start | bytes 3080 | tf_op jit(solution)/shard_map/ppermute | solution.py:173
  7.1 7.2 %collective-permute-start.1 = (f32[256]{0:T(256)S(1)}, f32[256]{0:T(256)S(1)}, u32[]{:S(2)}, u32[]{:S(2)}) collective-permute-start(f32[256]{0:T(256)S(1)} %multiply_reduce_fusion), channel_id=1, source_target_pairs={{0,2},{1,3},{2,0},{3,1},{4,6},{5,7},{6,4},{7,5},{8,10},{9,11},{10,... | collective-permute-start | bytes 3080 | tf_op jit(solution)/shard_map/ppermute | solution.py:173
  7.1 7.2 %collective-permute-start = (f32[256]{0:T(256)S(1)}, f32[256]{0:T(256)S(1)}, u32[]{:S(2)}, u32[]{:S(2)}) collective-permute-start(f32[256]{0:T(256)S(1)} %multiply_reduce_fusion), channel_id=1, source_target_pairs={{0,1},{1,2},{2,3},{3,0},{4,5},{5,6},{6,7},{7,4},{8,9},{9,10},{10,1... | collective-permute-start | bytes 3080 | tf_op jit(solution)/shard_map/ppermute | solution.py:173
  10.2 18.6 %all-to-all-start = ((bf16[4,2,32,1024]{3,2,1,0:T(8,128)(2,1)}), bf16[4,2,32,1024]{3,2,1,0:T(8,128)(2,1)S(1)}, u32[]{:S(2)}, u32[]{:S(2)}) async-start(bf16[4,2,32,1024]{3,2,1,0:T(8,128)(2,1)} %bitcast.9), calls=%async_computation | async-start | bytes 1048576 | tf_op jit(solution)/shard_map/all_to_all | solution.py:197
  14.3 1.2 collective-permute-start.3
  15.6 3.1 %copy-start.4 = (bf16[256,1024]{1,0:T(8,128)(2,1)}, bf16[256,1024]{1,0:T(8,128)(2,1)S(1)}, u32[]{:S(2)}) copy-start(bf16[256,1024]{1,0:T(8,128)(2,1)S(1)} %collective-permute-done.4.refs_5_) | copy-start | bytes 1572868
  18.7 1.3 copy-start.3
  30.5 4.0 %copy-start.12 = (s32[2,64]{1,0:T(2,128)S(1)}, s32[2,64]{1,0:T(2,128)}, u32[]{:S(2)}) copy-start(s32[2,64]{1,0:T(2,128)} %param.11) | copy-start | bytes 1540
  30.5 40.1 %all-to-all-start.1 = ((bf16[8,128,1024]{2,1,0:T(8,128)(2,1)}), bf16[8,128,1024]{2,1,0:T(8,128)(2,1)S(1)}, u32[]{:S(2)}, u32[]{:S(2)}) async-start(bf16[8,128,1024]{2,1,0:T(8,128)(2,1)} %bitcast.104), calls=%async_computation.1 | async-start | bytes 4194304 | tf_op jit(solution)/shard_map/all_to_all | solution.py:226
  34.4 5.5 %collective-permute-start.8 = (s32[2,64]{1,0:T(2,128)S(1)}, s32[2,64]{1,0:T(2,128)S(1)}, u32[]{:S(2)}, u32[]{:S(2)}) collective-permute-start(s32[2,64]{1,0:T(2,128)S(1)} %copy-done.12), channel_id=1, source_target_pairs={{0,4},{4,0},{8,12},{12,8},{16,20},{20,16},{24,28},{28,24},{1,5},{5... | collective-permute-start | bytes 1544 | tf_op jit(solution)/shard_map/ppermute | solution.py:183
  36.0 11.4 %collective-permute-start.5 = (bf16[128,1024]{1,0:T(8,128)(2,1)}, bf16[128,1024]{1,0:T(8,128)(2,1)}, u32[]{:S(2)}, u32[]{:S(2)}) collective-permute-start(bf16[128,1024]{1,0:T(8,128)(2,1)} %bitcast.7), channel_id=1, source_target_pairs={{0,1},{1,2},{2,3},{3,0},{4,5},{5,6},{6,7},{7,4},{8,9},{9,10},{10,1... | collective-permute-start | bytes 786440 | tf_op jit(solution)/shard_map/ppermute | solution.py:173
  36.1 14.9 %collective-permute-start.7 = (bf16[128,1024]{1,0:T(8,128)(2,1)S(1)}, bf16[128,1024]{1,0:T(8,128)(2,1)}, u32[]{:S(2)}, u32[]{:S(2)}) collective-permute-start(bf16[128,1024]{1,0:T(8,128)(2,1)S(1)} %bitcast.114), channel_id=1, source_target_pairs={{0,3},{1,0},{2,1},{3,2},{4,7},{5,4},{6,5},{7,6},{8,11},{9,8},{10,9... | collective-permute-start | bytes 786440 | tf_op jit(solution)/shard_map/ppermute | solution.py:173
  39.9 21.5 %collective-permute-start.6 = (bf16[128,1024]{1,0:T(8,128)(2,1)S(1)}, bf16[128,1024]{1,0:T(8,128)(2,1)}, u32[]{:S(2)}, u32[]{:S(2)}) collective-permute-start(bf16[128,1024]{1,0:T(8,128)(2,1)S(1)} %bitcast.113), channel_id=1, source_target_pairs={{0,2},{1,3},{2,0},{3,1},{4,6},{5,7},{6,4},{7,5},{8,10},{9,11},{10,... | collective-permute-start | bytes 786440 | tf_op jit(solution)/shard_map/ppermute | solution.py:173
  63.1 7.5 %collective-permute-start.9 = (bf16[128,1024]{1,0:T(8,128)(2,1)S(1)}, bf16[128,1024]{1,0:T(8,128)(2,1)S(1)}, u32[]{:S(2)}, u32[]{:S(2)}) collective-permute-start(bf16[128,1024]{1,0:T(8,128)(2,1)S(1)} %multiply_convert_fusion.1), channel_id=1, source_target_pairs={{0,1},{1,0},{2,3},{3,2},{4,5},{5,4},{6,7},{7,6},{8,9},{9,8},{10,11... | collective-permute-start | bytes 786440 | tf_op jit(solution)/shard_map/ppermute | solution.py:176
  63.1 7.4 %collective-permute-start.11 = (s32[2,128]{1,0:T(2,128)S(1)}, s32[2,128]{1,0:T(2,128)S(1)}, u32[]{:S(2)}, u32[]{:S(2)}) collective-permute-start(s32[2,128]{1,0:T(2,128)S(1)} %pad_add_fusion), channel_id=1, source_target_pairs={{0,1},{1,0},{2,3},{3,2},{4,5},{5,4},{6,7},{7,6},{8,9},{9,8},{10,11... | collective-permute-start | bytes 3080 | tf_op jit(solution)/shard_map/ppermute | solution.py:176
  70.6 1.1 copy-start.7
  71.7 3.7 %collective-permute-start.10 = (f32[2,2,128]{2,1,0:T(2,128)S(1)}, f32[2,2,128]{2,1,0:T(2,128)S(1)}, u32[]{:S(2)}, u32[]{:S(2)}) collective-permute-start(f32[2,2,128]{2,1,0:T(2,128)S(1)} %pad_maximum_fusion.4), channel_id=1, source_target_pairs={{0,1},{1,0},{2,3},{3,2},{4,5},{5,4},{6,7},{7,6},{8,9},{9,8},{10,11... | collective-permute-start | bytes 6152 | tf_op jit(solution)/shard_map/ppermute | solution.py:176
  75.8 2.1 %copy-start.8 = (bf16[128,1024]{1,0:T(8,128)(2,1)S(1)}, bf16[128,1024]{1,0:T(8,128)(2,1)}, u32[]{:S(2)}) copy-start(bf16[128,1024]{1,0:T(8,128)(2,1)} %copy-done.7) | copy-start | bytes 786436
  76.6 1.0 copy-start.1
  77.6 6.4 %collective-permute-start.12 = (bf16[128,1024]{1,0:T(8,128)(2,1)S(1)}, bf16[128,1024]{1,0:T(8,128)(2,1)S(1)}, u32[]{:S(2)}, u32[]{:S(2)}) collective-permute-start(bf16[128,1024]{1,0:T(8,128)(2,1)S(1)} %slice.72), channel_id=1, source_target_pairs={{0,1},{1,0},{2,3},{3,2},{4,5},{5,4},{6,7},{7,6},{8,9},{9,8},{10,11... | collective-permute-start | bytes 786440 | tf_op jit(solution)/shard_map/ppermute | solution.py:176
  84.0 41.6 %all-to-all-start.3 = ((bf16[8,128,1024]{2,1,0:T(8,128)(2,1)}), bf16[8,128,1024]{2,1,0:T(8,128)(2,1)S(1)}, u32[]{:S(2)}, u32[]{:S(2)}) async-start(bf16[8,128,1024]{2,1,0:T(8,128)(2,1)} %bitcast.106), calls=%async_computation.3 | async-start | bytes 4194304 | tf_op jit(solution)/shard_map/all_to_all | solution.py:268
  90.8 3.9 %collective-permute-start.13 = (f32[64]{0:T(128)S(1)}, f32[64]{0:T(128)S(1)}, u32[]{:S(2)}, u32[]{:S(2)}) collective-permute-start(f32[64]{0:T(128)S(1)} %slice_bitcast_fusion), channel_id=1, source_target_pairs={{0,4},{4,0},{8,12},{12,8},{16,20},{20,16},{24,28},{28,24},{1,5},{5... | collective-permute-start | bytes 776 | tf_op jit(solution)/shard_map/ppermute | solution.py:183
  92.7 26.4 %copy-start.6 = (bf16[128,1024]{1,0:T(8,128)(2,1)}, bf16[128,1024]{1,0:T(8,128)(2,1)S(1)}, u32[]{:S(2)}) copy-start(bf16[128,1024]{1,0:T(8,128)(2,1)S(1)} %subtract_convert_fusion.refs_0_) | copy-start | bytes 786436
  92.7 26.3 %collective-permute-start.19 = (bf16[128,1024]{1,0:T(8,128)(2,1)S(1)}, bf16[128,1024]{1,0:T(8,128)(2,1)S(1)}, u32[]{:S(2)}, u32[]{:S(2)}) collective-permute-start(bf16[128,1024]{1,0:T(8,128)(2,1)S(1)} %subtract_convert_fusion.refs_0_), channel_id=1, source_target_pairs={{0,3},{1,0},{2,1},{3,2},{4,7},{5,4},{6,5},{7,6},{8,11},{9,8},{10,9... | collective-permute-start | bytes 786440 | tf_op jit(solution)/shard_map/ppermute | solution.py:173
  93.4 25.6 %collective-permute-start.18 = (bf16[128,1024]{1,0:T(8,128)(2,1)S(1)}, bf16[128,1024]{1,0:T(8,128)(2,1)S(1)}, u32[]{:S(2)}, u32[]{:S(2)}) collective-permute-start(bf16[128,1024]{1,0:T(8,128)(2,1)S(1)} %subtract_convert_fusion.refs_0_), channel_id=1, source_target_pairs={{0,2},{1,3},{2,0},{3,1},{4,6},{5,7},{6,4},{7,5},{8,10},{9,11},{10,... | collective-permute-start | bytes 786440 | tf_op jit(solution)/shard_map/ppermute | solution.py:173
  94.5 24.6 %collective-permute-start.17 = (bf16[128,1024]{1,0:T(8,128)(2,1)S(1)}, bf16[128,1024]{1,0:T(8,128)(2,1)S(1)}, u32[]{:S(2)}, u32[]{:S(2)}) collective-permute-start(bf16[128,1024]{1,0:T(8,128)(2,1)S(1)} %subtract_convert_fusion.refs_0_), channel_id=1, source_target_pairs={{0,1},{1,2},{2,3},{3,0},{4,5},{5,6},{6,7},{7,4},{8,9},{9,10},{10,1... | collective-permute-start | bytes 786440 | tf_op jit(solution)/shard_map/ppermute | solution.py:173
  94.8 16.6 %collective-permute-start.14 = (f32[64]{0:T(128)S(1)}, f32[64]{0:T(128)S(1)}, u32[]{:S(2)}, u32[]{:S(2)}) collective-permute-start(f32[64]{0:T(128)S(1)} %bitcast_add_fusion.1), channel_id=1, source_target_pairs={{0,1},{1,2},{2,3},{3,0},{4,5},{5,6},{6,7},{7,4},{8,9},{9,10},{10,1... | collective-permute-start | bytes 776 | tf_op jit(solution)/shard_map/ppermute | solution.py:173
  97.8 19.8 %collective-permute-start.15 = (f32[64]{0:T(128)S(1)}, f32[64]{0:T(128)S(1)}, u32[]{:S(2)}, u32[]{:S(2)}) collective-permute-start(f32[64]{0:T(128)S(1)} %bitcast_add_fusion.1), channel_id=1, source_target_pairs={{0,2},{1,3},{2,0},{3,1},{4,6},{5,7},{6,4},{7,5},{8,10},{9,11},{10,... | collective-permute-start | bytes 776 | tf_op jit(solution)/shard_map/ppermute | solution.py:173
  111.3 7.7 %collective-permute-start.16 = (f32[64]{0:T(128)S(1)}, f32[64]{0:T(128)S(1)}, u32[]{:S(2)}, u32[]{:S(2)}) collective-permute-start(f32[64]{0:T(128)S(1)} %bitcast_add_fusion.1), channel_id=1, source_target_pairs={{0,3},{1,0},{2,1},{3,2},{4,7},{5,4},{6,5},{7,6},{8,11},{9,8},{10,9... | collective-permute-start | bytes 776 | tf_op jit(solution)/shard_map/ppermute | solution.py:173
  119.0 0.7 copy-start.13
  119.0 0.8 copy-start.14
  119.8 0.7 copy-start.15
  125.6 31.0 %all-to-all-start.2 = ((bf16[8,128,1024]{2,1,0:T(8,128)(2,1)}), bf16[8,128,1024]{2,1,0:T(8,128)(2,1)}, u32[]{:S(2)}, u32[]{:S(2)}) async-start(bf16[8,128,1024]{2,1,0:T(8,128)(2,1)} %bitcast.109), calls=%async_computation.2 | async-start | bytes 4194304 | tf_op jit(solution)/shard_map/all_to_all | solution.py:288
  130.0 8.5 %collective-permute-start.20 = (bf16[256,1024]{1,0:T(8,128)(2,1)}, bf16[256,1024]{1,0:T(8,128)(2,1)S(1)}, u32[]{:S(2)}, u32[]{:S(2)}) collective-permute-start(bf16[256,1024]{1,0:T(8,128)(2,1)} %get-tuple-element.21), channel_id=1, source_target_pairs={{0,4},{4,0},{8,12},{12,8},{16,20},{20,16},{24,28},{28,24},{1,5},{5... | collective-permute-start | bytes 1572872 | tf_op jit(solution)/shard_map/ppermute | solution.py:183
  131.6 13.6 %collective-permute-start.23 = (bf16[2,32,1024]{2,1,0:T(8,128)(2,1)S(1)}, bf16[2,32,1024]{2,1,0:T(8,128)(2,1)S(1)}, u32[]{:S(2)}, u32[]{:S(2)}) collective-permute-start(bf16[2,32,1024]{2,1,0:T(8,128)(2,1)S(1)} %get-tuple-element.46), channel_id=1, source_target_pairs={{0,3},{1,0},{2,1},{3,2},{4,7},{5,4},{6,5},{7,6},{8,11},{9,8},{10,9... | collective-permute-start | bytes 393224 | tf_op jit(solution)/shard_map/ppermute | solution.py:173
  134.8 13.1 %collective-permute-start.22 = (bf16[2,32,1024]{2,1,0:T(8,128)(2,1)S(1)}, bf16[2,32,1024]{2,1,0:T(8,128)(2,1)S(1)}, u32[]{:S(2)}, u32[]{:S(2)}) collective-permute-start(bf16[2,32,1024]{2,1,0:T(8,128)(2,1)S(1)} %get-tuple-element.47), channel_id=1, source_target_pairs={{0,2},{1,3},{2,0},{3,1},{4,6},{5,7},{6,4},{7,5},{8,10},{9,11},{10,... | collective-permute-start | bytes 393224 | tf_op jit(solution)/shard_map/ppermute | solution.py:173
  135.6 12.3 %collective-permute-start.21 = (bf16[2,32,1024]{2,1,0:T(8,128)(2,1)S(1)}, bf16[2,32,1024]{2,1,0:T(8,128)(2,1)S(1)}, u32[]{:S(2)}, u32[]{:S(2)}) collective-permute-start(bf16[2,32,1024]{2,1,0:T(8,128)(2,1)S(1)} %get-tuple-element.48), channel_id=1, source_target_pairs={{0,1},{1,2},{2,3},{3,0},{4,5},{5,6},{6,7},{7,4},{8,9},{9,10},{10,1... | collective-permute-start | bytes 393224 | tf_op jit(solution)/shard_map/ppermute | solution.py:173
  138.5 0.8 copy-start.5
  145.2 2.7 %copy-start.9 = (bf16[2,32,1024]{2,1,0:T(8,128)(2,1)}, bf16[2,32,1024]{2,1,0:T(8,128)(2,1)S(1)}, u32[]{:S(2)}) copy-start(bf16[2,32,1024]{2,1,0:T(8,128)(2,1)S(1)} %collective-permute-done.23.refs_3_) | copy-start | bytes 393220
  147.8 0.7 copy-start.10
  147.8 0.7 copy-start.11

commit v5 on v3

--- a/solution.py
+++ b/solution.py
@@ -131,7 +131,7 @@
 def hidden_gradient(place, d_rows, w_in, hidden, factors):
     steps, units, depth = w_in.shape
     rows = hidden.shape[0]
-    wide = min(256, units)
+    wide = min(512, units)
 
     def kernel(place_ref, *refs):
         d_rows, w, hidden, factors, out = refs[:steps], refs[-4], refs[-3], refs[-2], refs[-1]
@@ -251,6 +251,7 @@
         proj += r.astype(F32)
     x_rows = ratio * proj + jnp.where(step > 0, looked.astype(F32), 0.0)
     scale = lax.rsqrt(jnp.mean(x_rows * x_rows, axis=1, keepdims=True) + 1e-06)
+    x_proj = jnp.sum(x_rows * proj, axis=1, keepdims=True)
     gain = pick(depth_gain, step)[None, :]
     normed = (x_rows * scale * gain).astype(BF16)
 
@@ -270,16 +271,19 @@
     loss_weight = 2.0 * entries / frames
     d_logit = ((jnp.exp(logits - lse[:, None]) - onehot) * loss_weight).astype(BF16)
 
-    d_norm_rows = matmul(d_logit, head, ((1,), (1,)))
-    away = [d_norm_rows[k * owned : (k + 1) * owned].astype(BF16) for k in range(1, halves)]
+    away = [
+        matmul(d_logit[k * owned : (k + 1) * owned], head, ((1,), (1,))).astype(BF16)
+        for k in range(1, halves)
+    ]
     received = [turn_hid(a, k + 1) for k, a in enumerate(away)]
-    d_norm = d_norm_rows[:owned]
+    d_norm = matmul(after(d_logit[:owned], *away), head, ((1,), (1,)))
     for r in received:
         d_norm += r.astype(F32)
     gated = gain * d_norm
-    d_x = scale * gated - x_rows * scale**3 * jnp.mean(gated * x_rows, axis=1, keepdims=True)
-    d_round = d_x.astype(BF16)
-    d_ratio_part = jnp.sum(d_x * proj, axis=1).reshape(steps, part)
+    back_scale = scale**3 * jnp.mean(gated * x_rows, axis=1, keepdims=True)
+    gated_proj = jnp.sum(gated * proj, axis=1, keepdims=True)
+    d_round = (scale * gated - x_rows * back_scale).astype(BF16)
+    d_ratio_part = (scale * gated_proj - back_scale * x_proj).reshape(steps, part)
 
     part_out = matmul(normed_rows, after(d_logit, *away), ((0,), (0,))).astype(BF16)
     part_out = after(part_out, *received).reshape(seqs, depth // seqs, block)

time: 151 us -> 153 us (1.013)
  waiting for transfers between devices: 51.9 us -> 61.3 us
  other arithmetic: 10.6 us -> 8.14 us
  local copies, waits for them, and re-layouts: 18.3 us -> 15.9 us
    ppermute x12, waiting for transfers between devices: 28.1 us -> 36.8 us  [along_hid(): lax.ppermute(values, 'hid', [(a, (a + shift) % hids) for a in range(hids)])]
    reduce_sum x2 -> x0, other arithmetic: 3.63 us -> none  [the longest x1 2.31 us: shards(): d_ratio_part = jnp.sum(d_x * proj, axis=1).reshape(steps, part)]
    ppermute x4, waiting for transfers between devices: 7.73 us -> 10.9 us  [turn_hid(): lax.ppermute(values, 'hid', [(a, a - a % halves + (a % halves + shift) %...]
    all_to_all x1, waiting for transfers between devices: 2.67 us -> 0.01 us  [shards(): head = lax.all_to_all(head_send, 'seq', 0, 0).reshape(depth, block)]
    ppermute x4, starting transfers between devices: 7.17 us -> 4.65 us  [turn_hid(): lax.ppermute(values, 'hid', [(a, a - a % halves + (a % halves + shift) %...]
    reduce_sum x1, other arithmetic: 2.11 us -> 0.39 us  [shards(): share.reshape(groups, steps, depth // seqs, units).astype(F32).sum(0)]
    unnamed x33 -> x35, local copies, waits for them, and re-layouts: 5.96 us -> 4.31 us
    reduce_sum x1, other arithmetic: 0.44 us -> 2.03 us  [shards(): part_out.reshape(groups, steps, hids, head_rows, block).astype(F32).sum(0)]
  transfers between devices with their start and end apart: 25 -> 25, of which waited for: 14 -> 14; matrix products, arithmetic and copies ran while one was open for 16% -> 15% of each run, Pallas kernels for 9% -> 8%
where the time goes in v5:
time: 153 us
  waiting for transfers between devices  61.3 us (40%)
  starting transfers between devices  45 us (29%)
  local copies, waits for them, and re-layouts  15.9 us (10%)
  Pallas kernels  12.7 us (8%)
  matrix products  8.58 us (6%)
  other arithmetic  8.14 us (5%)
    ppermute x12, waiting for transfers between devices, along_hid(): lax.ppermute(values, 'hid', [(a, (a + shift) % hids) for a in range(hids)])  36.8 us
    ppermute x12, starting transfers between devices, along_hid(): lax.ppermute(values, 'hid', [(a, (a + shift) % hids) for a in range(hids)])  20.2 us
    pallas_call x3, Pallas kernels, call(): pl.pallas_call(kernel, grid_spec=pltpu.PrefetchScalarGridSpec(num_scalar_...  12.7 us
    all_to_all x1, waiting for transfers between devices, shards(): head_got = lax.all_to_all(head_send, 'hid', 0, 0)  12.3 us
    ppermute x4, waiting for transfers between devices, turn_hid(): lax.ppermute(values, 'hid', [(a, a - a % halves + (a % halves + shift) %...  10.9 us
    dot_general x5, matrix products, matmul(): lax.dot_general(a, b, (contract, ((), ())), preferred_element_type=F32)  8.58 us
    all_to_all x1, starting transfers between devices, shards(): head_got = lax.all_to_all(head_send, 'hid', 0, 0)  6.24 us
    ppermute x4, starting transfers between devices, turn_hid(): lax.ppermute(values, 'hid', [(a, a - a % halves + (a % halves + shift) %...  4.65 us
  transfers between devices with their start and end apart: 25, of which 14 were waited for; matrix products, arithmetic and copies ran while one was open for 15% of the time, Pallas kernels for 8%

profile of v5, /device:TPU:0, one launch (start us, length us, event | category | flops | bytes accessed | tf_op | source)
XLA Modules:
  0.0 152.6 jit_solution(1203661971175261786)
XLA Ops:
  1.2 1.2 multiply_reduce_fusion
  2.9 1.3 reshape.286
  4.3 0.9 broadcast_in_dim.59
  5.2 6.2 %all-to-all-start = ((bf16[4,72,1024]{2,1,0:T(8,128)(2,1)}), bf16[4,72,1024]{2,1,0:T(8,128)(2,1)S(1)}, u32[]{:S(2)}, u32[]{:S(2)}) async-start(bf16[4,72,1024]{2,1,0:T(8,128)(2,1)} %bitcast.6), calls=%async_computation | async-start | bytes 1179648 | tf_op jit(solution)/shard_map/all_to_all | solution.py:217
  11.6 2.9 %fusion = f32[2,4,64,1024]{3,2,1,0:T(8,128)S(1)} fusion(bf16[2,4,64,1024]{3,2,1,0:T(8,128)(2,1)S(1)} %bitcast.121, bf16[2,1024,1024]{2,1,0:T(8,128)(2,1)} %refs_2_.1, s32[]{:T(128)S(6)} %select_n.119), kind=kOutput, calls=%fused_computation.2 | convolution fusion | flops 1073741824 | bytes 5242884 | tf_op jit(solution)/shard_map/dot_general | solution.py:17
  14.5 0.8 dynamic-slice_convert_fusion
  15.3 12.3 %all-to-all-done = bf16[4,72,1024]{2,1,0:T(8,128)(2,1)S(1)} async-done(((bf16[4,72,1024]{2,1,0:T(8,128)(2,1)}), bf16[4,72,1024]{2,1,0:T(8,128)(2,1)S(1)}, u32[]{:S(2)}, u32[]{:S(2)}) %all-to-all-start) | async-done | bytes 589856 | tf_op jit(solution)/shard_map/all_to_all | solution.py:217
  27.8 1.6 %broadcast_in_dim.63 = bf16[4,2,128,1024]{3,2,1,0:T(8,128)(2,1)} broadcast(bf16[2,128,1024]{2,1,0:T(8,128)(2,1)S(1)} %bitcast.117), dimensions={1,2,3} | broadcast | bytes 2621440 | tf_op jit(solution)/shard_map/broadcast_in_dim | solution.py:241
  29.4 3.8 %all-to-all-start.1 = ((bf16[8,128,1024]{2,1,0:T(8,128)(2,1)}), bf16[8,128,1024]{2,1,0:T(8,128)(2,1)S(1)}, u32[]{:S(2)}, u32[]{:S(2)}) async-start(bf16[8,128,1024]{2,1,0:T(8,128)(2,1)} %bitcast.113), calls=%async_computation.1 | async-start | bytes 4194304 | tf_op jit(solution)/shard_map/all_to_all | solution.py:243
  33.9 1.5 collective-permute-start.4
  36.1 3.8 %gather_fusion = bf16[128,1024]{1,0:T(8,128)(2,1)S(1)} fusion(bf16[2048,1024]{1,0:T(8,128)(2,1)} %bitcast.120, s32[1024]{0:T(1024)S(1)} %pad_clamp_fusion), kind=kCustom, calls=%fused_computation | custom fusion | bytes 524800 | tf_op jit(solution)/shard_map/jit(_take)/gather | solution.py:237
  40.0 4.1 %collective-permute-done.4 = bf16[128,1024]{1,0:T(8,128)(2,1)} collective-permute-done((bf16[128,1024]{1,0:T(8,128)(2,1)}, bf16[128,1024]{1,0:T(8,128)(2,1)}, u32[]{:S(2)}, u32[]{:S(2)}) %collective-permute-start.4) | collective-permute-done | bytes 262176 | tf_op jit(solution)/shard_map/ppermute | solution.py:185
  44.1 13.4 %collective-permute-done.3 = bf16[128,1024]{1,0:T(8,128)(2,1)} collective-permute-done((bf16[128,1024]{1,0:T(8,128)(2,1)S(1)}, bf16[128,1024]{1,0:T(8,128)(2,1)}, u32[]{:S(2)}, u32[]{:S(2)}) %collective-permute-start.3) | collective-permute-done | bytes 262176 | tf_op jit(solution)/shard_map/ppermute | solution.py:185
  57.5 1.4 multiply_reduce_fusion.4
  59.2 1.2 collective-permute-start.6
  60.4 0.9 collective-permute-start.8
  61.3 5.4 %collective-permute-done.8 = s32[2,128]{1,0:T(2,128)S(1)} collective-permute-done((s32[2,128]{1,0:T(2,128)S(1)}, s32[2,128]{1,0:T(2,128)S(1)}, u32[]{:S(2)}, u32[]{:S(2)}) %collective-permute-start.8) | collective-permute-done | bytes 1056 | tf_op jit(solution)/shard_map/ppermute | solution.py:188
  66.7 0.8 fusion.36
  67.9 1.3 collective-permute-start.7
  69.2 2.4 %collective-permute-done.7 = f32[2,2,128]{2,1,0:T(2,128)S(1)} collective-permute-done((f32[2,2,128]{2,1,0:T(2,128)S(1)}, f32[2,2,128]{2,1,0:T(2,128)S(1)}, u32[]{:S(2)}, u32[]{:S(2)}) %collective-permute-start.7) | collective-permute-done | bytes 2080 | tf_op jit(solution)/shard_map/ppermute | solution.py:188
  72.0 0.8 convolution_convert_fusion.1
  72.8 1.3 collective-permute-start.9
  74.1 2.1 %convolution_convert_fusion = bf16[1024,1024]{1,0:T(8,128)(2,1)} fusion(bf16[256,1024]{1,0:T(8,128)(2,1)S(1)} %multiply_convert_fusion, bf16[128,1024]{1,0:T(8,128)(2,1)S(1)} %copy-done.7, bf16[128,1024]{1,0:T(8,128)(2,1)S(1)} %copy-done.3), kind=kOutput, calls=%fused_computation.5 | convolution fusion | flops 538968064 | bytes 3145728 | tf_op jit(solution)/shard_map/dot_general | solution.py:17
  76.2 3.2 %collective-permute-done.9 = bf16[128,1024]{1,0:T(8,128)(2,1)} collective-permute-done((bf16[128,1024]{1,0:T(8,128)(2,1)S(1)}, bf16[128,1024]{1,0:T(8,128)(2,1)}, u32[]{:S(2)}, u32[]{:S(2)}) %collective-permute-start.9) | collective-permute-done | bytes 262176 | tf_op jit(solution)/shard_map/ppermute | solution.py:188
  79.4 4.6 %all-to-all-start.3 = ((bf16[8,128,1024]{2,1,0:T(8,128)(2,1)}), bf16[8,128,1024]{2,1,0:T(8,128)(2,1)}, u32[]{:S(2)}, u32[]{:S(2)}) async-start(bf16[8,128,1024]{2,1,0:T(8,128)(2,1)} %bitcast.115), calls=%async_computation.3 | async-start | bytes 4194304 | tf_op jit(solution)/shard_map/all_to_all | solution.py:290
  84.0 2.0 %multiply_reduce_fusion.2 = (f32[128]{0:T(128)S(1)}, f32[128]{0:T(128)S(1)}, f32[128]{0:T(128)S(1)}, f32[128,1024]{1,0:T(8,128)S(1)}) fusion(f32[128,1024]{1,0:T(8,128)S(1)} %get-tuple-element.44, bf16[128,1024]{1,0:T(8,128)(2,1)} %collective-permute-done.9, f32[1024]{0:T(1024)S(1)} %bitcast.128, bf16[128,1024]{1,0:T(8,128)(2,1)S(1)} %gather_fusion, ...), kind=kOutput, calls=%fused_computation.16 | convolution fusion | flops 270270080 | bytes 3938433 | tf_op jit(solution)/shard_map/dot_general | solution.py:17
  86.0 1.2 subtract_convert_fusion.refs_0_
  87.2 1.1 collective-permute-start.10
  88.4 2.3 %collective-permute-start.11 = (bf16[128,1024]{1,0:T(8,128)(2,1)S(1)}, bf16[128,1024]{1,0:T(8,128)(2,1)S(1)}, u32[]{:S(2)}, u32[]{:S(2)}) collective-permute-start(bf16[128,1024]{1,0:T(8,128)(2,1)S(1)} %subtract_convert_fusion.refs_0_), channel_id=1, source_target_pairs={{0,2},{1,3},{2,0},{3,1},{4,6},{5,7},{6,4},{7,5},{8,10},{9,11},{10,... | collective-permute-start | bytes 786440 | tf_op jit(solution)/shard_map/ppermute | solution.py:185
  90.7 2.6 %collective-permute-start.12 = (bf16[128,1024]{1,0:T(8,128)(2,1)S(1)}, bf16[128,1024]{1,0:T(8,128)(2,1)S(1)}, u32[]{:S(2)}, u32[]{:S(2)}) collective-permute-start(bf16[128,1024]{1,0:T(8,128)(2,1)S(1)} %subtract_convert_fusion.refs_0_), channel_id=1, source_target_pairs={{0,3},{1,0},{2,1},{3,2},{4,7},{5,4},{6,5},{7,6},{8,11},{9,8},{10,9... | collective-permute-start | bytes 786440 | tf_op jit(solution)/shard_map/ppermute | solution.py:185
  93.9 0.9 copy.43.refs_6_
  94.7 3.6 %collective-permute-done.10.refs_1_ = bf16[128,1024]{1,0:T(8,128)(2,1)S(1)} collective-permute-done((bf16[128,1024]{1,0:T(8,128)(2,1)S(1)}, bf16[128,1024]{1,0:T(8,128)(2,1)S(1)}, u32[]{:S(2)}, u32[]{:S(2)}) %collective-permute-start.10) | collective-permute-done | bytes 262176 | tf_op jit(solution)/shard_map/ppermute | solution.py:185
  98.3 10.8 %collective-permute-done.11.refs_2_ = bf16[128,1024]{1,0:T(8,128)(2,1)S(1)} collective-permute-done((bf16[128,1024]{1,0:T(8,128)(2,1)S(1)}, bf16[128,1024]{1,0:T(8,128)(2,1)S(1)}, u32[]{:S(2)}, u32[]{:S(2)}) %collective-permute-start.11) | collective-permute-done | bytes 262176 | tf_op jit(solution)/shard_map/ppermute | solution.py:185
  110.6 5.1 %shard_map.85 = (bf16[1024,1024]{1,0:T(8,128)(2,1)}, bf16[256,1024]{1,0:T(8,128)(2,1)}, bf16[256,1024]{1,0:T(8,128)(2,1)}) custom-call(s32[2]{0:T(128)} %pad_add_fusion.2.place_ref, bf16[128,1024]{1,0:T(8,128)(2,1)} %copy-done.8, bf16[128,1024]{1,0:T(8,128)(2,1)} %copy-done.13, bf16[128,1024]{1,0:T(8,128)(2,1)} %copy-done.14, bf16[128,1024]{1,0:T(8,128)(2,1)} %copy-done.15, ...), custom_call_target="tpu_custom_call" | custom-call | flops 1073741824 | bytes 2099200 | tf_op jit(solution)/shard_map/pallas_call | solution.py:33
  115.7 3.9 %all-to-all-start.2 = ((bf16[8,128,1024]{2,1,0:T(8,128)(2,1)}), bf16[8,128,1024]{2,1,0:T(8,128)(2,1)S(1)}, u32[]{:S(2)}, u32[]{:S(2)}) async-start(bf16[8,128,1024]{2,1,0:T(8,128)(2,1)} %bitcast.118), calls=%async_computation.2 | async-start | bytes 4194304 | tf_op jit(solution)/shard_map/all_to_all | solution.py:302
  120.2 0.8 collective-permute-done.14
  121.0 5.3 %collective-permute-start.15 = (f32[64]{0:T(128)S(1)}, f32[64]{0:T(128)S(1)}, u32[]{:S(2)}, u32[]{:S(2)}) collective-permute-start(f32[64]{0:T(128)S(1)} %bitcast_add_fusion.1), channel_id=1, source_target_pairs={{0,1},{1,2},{2,3},{3,0},{4,5},{5,6},{6,7},{7,4},{8,9},{9,10},{10,1... | collective-permute-start | bytes 776 | tf_op jit(solution)/shard_map/ppermute | solution.py:185
  126.3 2.9 %collective-permute-start.16 = (f32[64]{0:T(128)S(1)}, f32[64]{0:T(128)S(1)}, u32[]{:S(2)}, u32[]{:S(2)}) collective-permute-start(f32[64]{0:T(128)S(1)} %bitcast_add_fusion.1), channel_id=1, source_target_pairs={{0,2},{1,3},{2,0},{3,1},{4,6},{5,7},{6,4},{7,5},{8,10},{9,11},{10,... | collective-permute-start | bytes 776 | tf_op jit(solution)/shard_map/ppermute | solution.py:185
  129.3 0.9 collective-permute-done.15
  130.8 2.0 %collective-permute-done.17 = f32[64]{0:T(128)S(1)} collective-permute-done((f32[64]{0:T(128)S(1)}, f32[64]{0:T(128)S(1)}, u32[]{:S(2)}, u32[]{:S(2)}) %collective-permute-start.17) | collective-permute-done | bytes 288 | tf_op jit(solution)/shard_map/ppermute | solution.py:185
  133.0 2.0 %reduce_sum.108 = bf16[2,4,32,1024]{3,2,1,0:T(8,128)(2,1)S(1)} reduce(bf16[4,2,4,32,1024]{4,3,2,1,0:T(8,128)(2,1)} %bitcast.54, bf16[]{:T(256)} %constant.152.clone.1), dimensions={0}, to_apply=%region_10.11 | reduce | flops 786432 | bytes 2621442 | tf_op jit(solution)/shard_map/reduce_sum | solution.py:291
  135.7 2.4 %collective-permute-start.19 = (bf16[2,32,1024]{2,1,0:T(8,128)(2,1)S(1)}, bf16[2,32,1024]{2,1,0:T(8,128)(2,1)S(1)}, u32[]{:S(2)}, u32[]{:S(2)}) collective-permute-start(bf16[2,32,1024]{2,1,0:T(8,128)(2,1)S(1)} %get-tuple-element.49), channel_id=1, source_target_pairs={{0,2},{1,3},{2,0},{3,1},{4,6},{5,7},{6,4},{7,5},{8,10},{9,11},{10,... | collective-permute-start | bytes 393224 | tf_op jit(solution)/shard_map/ppermute | solution.py:185
  138.1 1.5 collective-permute-start.20
  139.6 0.9 copy.44.refs_4_
  141.2 4.9 %shard_map.86 = bf16[256,1024]{1,0:T(8,128)(2,1)} custom-call(s32[2]{0:T(128)} %pad_add_fusion.2.place_ref, bf16[256,1024]{1,0:T(8,128)(2,1)} %get-tuple-element.22.refs_0_, bf16[256,1024]{1,0:T(8,128)(2,1)} %copy-done.5, bf16[2,1024,1024]{2,1,0:T(8,128)(2,1)} %refs_2_.1, bf16[256,1024]{1,0:T(8,128)(2,1)} %refs_3_.1, f32[2,256,1]{2,1,0:T(8,128)} %copy.44.refs_4_), custom_call_target="tpu_custom_call" | custom-call | flops 1073741824 | bytes 5769216 | tf_op jit(solution)/shard_map/pallas_call | solution.py:33
  146.2 1.4 collective-permute-done.19.refs_2_
  148.3 2.7 %shard_map.87 = f32[32,2,2048]{2,1,0:T(2,128)} custom-call(s32[2]{0:T(128)} %pad_add_fusion.2.place_ref, bf16[2,32,1024]{2,1,0:T(8,128)(2,1)} %get-tuple-element.51.refs_0_, bf16[2,32,1024]{2,1,0:T(8,128)(2,1)} %copy-done.9, bf16[2,32,1024]{2,1,0:T(8,128)(2,1)} %copy-done.10, bf16[2,32,1024]{2,1,0:T(8,128)(2,1)} %copy-done.11), custom_call_target="tpu_custom_call" | custom-call | flops 262144 | bytes 524288 | tf_op jit(solution)/shard_map/pallas_call | solution.py:33
  151.3 1.3 copy.45
  (108 shorter events, 10.0 us)
Async XLA Ops:
  0.6 10.8 %copy-start = (f32[2,1024]{1,0:T(2,128)S(1)}, f32[2,1024]{1,0:T(2,128)}, u32[]{:S(2)}) copy-start(f32[2,1024]{1,0:T(2,128)} %param.9) | copy-start | bytes 24580
  0.6 2.3 %collective-permute-start = (bf16[256,1024]{1,0:T(8,128)(2,1)}, bf16[256,1024]{1,0:T(8,128)(2,1)S(1)}, u32[]{:S(2)}, u32[]{:S(2)}) collective-permute-start(bf16[256,1024]{1,0:T(8,128)(2,1)} %refs_3_.1), channel_id=1, source_target_pairs={{0,4},{4,0},{8,12},{12,8},{16,20},{20,16},{24,28},{28,24},{1,5},{5... | collective-permute-start | bytes 1572872 | tf_op jit(solution)/shard_map/ppermute | solution.py:195
  2.4 9.1 %copy-start.1 = (bf16[256,1024]{1,0:T(8,128)(2,1)S(1)}, bf16[256,1024]{1,0:T(8,128)(2,1)}, u32[]{:S(2)}) copy-start(bf16[256,1024]{1,0:T(8,128)(2,1)} %refs_3_.1) | copy-start | bytes 1572868
  2.9 8.6 %copy-start.4 = (bf16[256,1024]{1,0:T(8,128)(2,1)}, bf16[256,1024]{1,0:T(8,128)(2,1)S(1)}, u32[]{:S(2)}) copy-start(bf16[256,1024]{1,0:T(8,128)(2,1)S(1)} %collective-permute-done.refs_5_) | copy-start | bytes 1572868
  5.2 22.4 %all-to-all-start = ((bf16[4,72,1024]{2,1,0:T(8,128)(2,1)}), bf16[4,72,1024]{2,1,0:T(8,128)(2,1)S(1)}, u32[]{:S(2)}, u32[]{:S(2)}) async-start(bf16[4,72,1024]{2,1,0:T(8,128)(2,1)} %bitcast.6), calls=%async_computation | async-start | bytes 1179648 | tf_op jit(solution)/shard_map/all_to_all | solution.py:217
  14.4 13.2 %copy-start.12 = (s32[2,64]{1,0:T(2,128)S(1)}, s32[2,64]{1,0:T(2,128)}, u32[]{:S(2)}) copy-start(s32[2,64]{1,0:T(2,128)} %param.11) | copy-start | bytes 1540
  27.7 8.3 %collective-permute-start.5 = (s32[2,64]{1,0:T(2,128)S(1)}, s32[2,64]{1,0:T(2,128)S(1)}, u32[]{:S(2)}, u32[]{:S(2)}) collective-permute-start(s32[2,64]{1,0:T(2,128)S(1)} %copy-done.12), channel_id=1, source_target_pairs={{0,4},{4,0},{8,12},{12,8},{16,20},{20,16},{24,28},{28,24},{1,5},{5... | collective-permute-start | bytes 1544 | tf_op jit(solution)/shard_map/ppermute | solution.py:195
  29.4 37.3 %all-to-all-start.1 = ((bf16[8,128,1024]{2,1,0:T(8,128)(2,1)}), bf16[8,128,1024]{2,1,0:T(8,128)(2,1)S(1)}, u32[]{:S(2)}, u32[]{:S(2)}) async-start(bf16[8,128,1024]{2,1,0:T(8,128)(2,1)} %bitcast.113), calls=%async_computation.1 | async-start | bytes 4194304 | tf_op jit(solution)/shard_map/all_to_all | solution.py:243
  33.3 6.6 %collective-permute-start.1 = (f32[256]{0:T(256)S(1)}, f32[256]{0:T(256)S(1)}, u32[]{:S(2)}, u32[]{:S(2)}) collective-permute-start(f32[256]{0:T(256)S(1)} %reduce_sum.98), channel_id=1, source_target_pairs={{0,4},{4,0},{8,12},{12,8},{16,20},{20,16},{24,28},{28,24},{1,5},{5... | collective-permute-start | bytes 3080 | tf_op jit(solution)/shard_map/ppermute | solution.py:195
  33.9 10.2 %collective-permute-start.4 = (bf16[128,1024]{1,0:T(8,128)(2,1)}, bf16[128,1024]{1,0:T(8,128)(2,1)}, u32[]{:S(2)}, u32[]{:S(2)}) collective-permute-start(bf16[128,1024]{1,0:T(8,128)(2,1)} %bitcast.14), channel_id=1, source_target_pairs={{0,3},{1,0},{2,1},{3,2},{4,7},{5,4},{6,5},{7,6},{8,11},{9,8},{10,9... | collective-permute-start | bytes 786440 | tf_op jit(solution)/shard_map/ppermute | solution.py:185
  35.4 22.1 %collective-permute-start.3 = (bf16[128,1024]{1,0:T(8,128)(2,1)S(1)}, bf16[128,1024]{1,0:T(8,128)(2,1)}, u32[]{:S(2)}, u32[]{:S(2)}) collective-permute-start(bf16[128,1024]{1,0:T(8,128)(2,1)S(1)} %bitcast.125), channel_id=1, source_target_pairs={{0,2},{1,3},{2,0},{3,1},{4,6},{5,7},{6,4},{7,5},{8,10},{9,11},{10,... | collective-permute-start | bytes 786440 | tf_op jit(solution)/shard_map/ppermute | solution.py:185
  35.4 22.1 %collective-permute-start.2 = (bf16[128,1024]{1,0:T(8,128)(2,1)S(1)}, bf16[128,1024]{1,0:T(8,128)(2,1)}, u32[]{:S(2)}, u32[]{:S(2)}) collective-permute-start(bf16[128,1024]{1,0:T(8,128)(2,1)S(1)} %bitcast.124), channel_id=1, source_target_pairs={{0,1},{1,2},{2,3},{3,0},{4,5},{5,6},{6,7},{7,4},{8,9},{9,10},{10,1... | collective-permute-start | bytes 786440 | tf_op jit(solution)/shard_map/ppermute | solution.py:185
  59.2 8.7 %copy-start.2 = (bf16[128,1024]{1,0:T(8,128)(2,1)}, bf16[128,1024]{1,0:T(8,128)(2,1)S(1)}, u32[]{:S(2)}) copy-start(bf16[128,1024]{1,0:T(8,128)(2,1)S(1)} %multiply_convert_fusion.1) | copy-start | bytes 786436
  59.2 7.5 %collective-permute-start.6 = (bf16[128,1024]{1,0:T(8,128)(2,1)S(1)}, bf16[128,1024]{1,0:T(8,128)(2,1)S(1)}, u32[]{:S(2)}, u32[]{:S(2)}) collective-permute-start(bf16[128,1024]{1,0:T(8,128)(2,1)S(1)} %multiply_convert_fusion.1), channel_id=1, source_target_pairs={{0,1},{1,0},{2,3},{3,2},{4,5},{5,4},{6,7},{7,6},{8,9},{9,8},{10,11... | collective-permute-start | bytes 786440 | tf_op jit(solution)/shard_map/ppermute | solution.py:188
  60.4 6.3 %collective-permute-start.8 = (s32[2,128]{1,0:T(2,128)S(1)}, s32[2,128]{1,0:T(2,128)S(1)}, u32[]{:S(2)}, u32[]{:S(2)}) collective-permute-start(s32[2,128]{1,0:T(2,128)S(1)} %pad_add_fusion), channel_id=1, source_target_pairs={{0,1},{1,0},{2,3},{3,2},{4,5},{5,4},{6,7},{7,6},{8,9},{9,8},{10,11... | collective-permute-start | bytes 3080 | tf_op jit(solution)/shard_map/ppermute | solution.py:188
  66.7 1.2 copy-start.6
  67.9 3.7 %collective-permute-start.7 = (f32[2,2,128]{2,1,0:T(2,128)S(1)}, f32[2,2,128]{2,1,0:T(2,128)S(1)}, u32[]{:S(2)}, u32[]{:S(2)}) collective-permute-start(f32[2,2,128]{2,1,0:T(2,128)S(1)} %pad_maximum_fusion.4), channel_id=1, source_target_pairs={{0,1},{1,0},{2,3},{3,2},{4,5},{5,4},{6,7},{7,6},{8,9},{9,8},{10,11... | collective-permute-start | bytes 6152 | tf_op jit(solution)/shard_map/ppermute | solution.py:188
  71.6 2.5 %copy-start.3 = (bf16[128,1024]{1,0:T(8,128)(2,1)S(1)}, bf16[128,1024]{1,0:T(8,128)(2,1)}, u32[]{:S(2)}) copy-start(bf16[128,1024]{1,0:T(8,128)(2,1)} %copy-done.2) | copy-start | bytes 786436
  71.6 2.5 %copy-start.7 = (bf16[128,1024]{1,0:T(8,128)(2,1)S(1)}, bf16[128,1024]{1,0:T(8,128)(2,1)}, u32[]{:S(2)}) copy-start(bf16[128,1024]{1,0:T(8,128)(2,1)} %copy-done.6) | copy-start | bytes 786436
  72.8 6.5 %collective-permute-start.9 = (bf16[128,1024]{1,0:T(8,128)(2,1)S(1)}, bf16[128,1024]{1,0:T(8,128)(2,1)}, u32[]{:S(2)}, u32[]{:S(2)}) collective-permute-start(bf16[128,1024]{1,0:T(8,128)(2,1)S(1)} %convolution_convert_fusion.1), channel_id=1, source_target_pairs={{0,1},{1,0},{2,3},{3,2},{4,5},{5,4},{6,7},{7,6},{8,9},{9,8},{10,11... | collective-permute-start | bytes 786440 | tf_op jit(solution)/shard_map/ppermute | solution.py:188
  79.4 36.3 %all-to-all-start.3 = ((bf16[8,128,1024]{2,1,0:T(8,128)(2,1)}), bf16[8,128,1024]{2,1,0:T(8,128)(2,1)}, u32[]{:S(2)}, u32[]{:S(2)}) async-start(bf16[8,128,1024]{2,1,0:T(8,128)(2,1)} %bitcast.115), calls=%async_computation.3 | async-start | bytes 4194304 | tf_op jit(solution)/shard_map/all_to_all | solution.py:290
  87.2 22.0 %copy-start.8 = (bf16[128,1024]{1,0:T(8,128)(2,1)}, bf16[128,1024]{1,0:T(8,128)(2,1)S(1)}, u32[]{:S(2)}) copy-start(bf16[128,1024]{1,0:T(8,128)(2,1)S(1)} %subtract_convert_fusion.refs_0_) | copy-start | bytes 786436
  87.2 11.1 %collective-permute-start.10 = (bf16[128,1024]{1,0:T(8,128)(2,1)S(1)}, bf16[128,1024]{1,0:T(8,128)(2,1)S(1)}, u32[]{:S(2)}, u32[]{:S(2)}) collective-permute-start(bf16[128,1024]{1,0:T(8,128)(2,1)S(1)} %subtract_convert_fusion.refs_0_), channel_id=1, source_target_pairs={{0,1},{1,2},{2,3},{3,0},{4,5},{5,6},{6,7},{7,4},{8,9},{9,10},{10,1... | collective-permute-start | bytes 786440 | tf_op jit(solution)/shard_map/ppermute | solution.py:185
  88.4 20.8 %collective-permute-start.11 = (bf16[128,1024]{1,0:T(8,128)(2,1)S(1)}, bf16[128,1024]{1,0:T(8,128)(2,1)S(1)}, u32[]{:S(2)}, u32[]{:S(2)}) collective-permute-start(bf16[128,1024]{1,0:T(8,128)(2,1)S(1)} %subtract_convert_fusion.refs_0_), channel_id=1, source_target_pairs={{0,2},{1,3},{2,0},{3,1},{4,6},{5,7},{6,4},{7,5},{8,10},{9,11},{10,... | collective-permute-start | bytes 786440 | tf_op jit(solution)/shard_map/ppermute | solution.py:185
  90.7 18.5 %collective-permute-start.12 = (bf16[128,1024]{1,0:T(8,128)(2,1)S(1)}, bf16[128,1024]{1,0:T(8,128)(2,1)S(1)}, u32[]{:S(2)}, u32[]{:S(2)}) collective-permute-start(bf16[128,1024]{1,0:T(8,128)(2,1)S(1)} %subtract_convert_fusion.refs_0_), channel_id=1, source_target_pairs={{0,3},{1,0},{2,1},{3,2},{4,7},{5,4},{6,5},{7,6},{8,11},{9,8},{10,9... | collective-permute-start | bytes 786440 | tf_op jit(solution)/shard_map/ppermute | solution.py:185
  98.3 10.9 %copy-start.13 = (bf16[128,1024]{1,0:T(8,128)(2,1)}, bf16[128,1024]{1,0:T(8,128)(2,1)S(1)}, u32[]{:S(2)}) copy-start(bf16[128,1024]{1,0:T(8,128)(2,1)S(1)} %collective-permute-done.10.refs_1_) | copy-start | bytes 786436
  109.2 0.7 copy-start.14
  109.9 0.7 copy-start.15
  115.7 35.3 %all-to-all-start.2 = ((bf16[8,128,1024]{2,1,0:T(8,128)(2,1)}), bf16[8,128,1024]{2,1,0:T(8,128)(2,1)S(1)}, u32[]{:S(2)}, u32[]{:S(2)}) async-start(bf16[8,128,1024]{2,1,0:T(8,128)(2,1)} %bitcast.118), calls=%async_computation.2 | async-start | bytes 4194304 | tf_op jit(solution)/shard_map/all_to_all | solution.py:302
  119.6 1.4 collective-permute-start.14
  120.1 20.3 %collective-permute-start.13 = (bf16[256,1024]{1,0:T(8,128)(2,1)}, bf16[256,1024]{1,0:T(8,128)(2,1)S(1)}, u32[]{:S(2)}, u32[]{:S(2)}) collective-permute-start(bf16[256,1024]{1,0:T(8,128)(2,1)} %get-tuple-element.23), channel_id=1, source_target_pairs={{0,4},{4,0},{8,12},{12,8},{16,20},{20,16},{24,28},{28,24},{1,5},{5... | collective-permute-start | bytes 1572872 | tf_op jit(solution)/shard_map/ppermute | solution.py:195
  121.0 9.2 %collective-permute-start.15 = (f32[64]{0:T(128)S(1)}, f32[64]{0:T(128)S(1)}, u32[]{:S(2)}, u32[]{:S(2)}) collective-permute-start(f32[64]{0:T(128)S(1)} %bitcast_add_fusion.1), channel_id=1, source_target_pairs={{0,1},{1,2},{2,3},{3,0},{4,5},{5,6},{6,7},{7,4},{8,9},{9,10},{10,1... | collective-permute-start | bytes 776 | tf_op jit(solution)/shard_map/ppermute | solution.py:185
  126.3 4.5 %collective-permute-start.16 = (f32[64]{0:T(128)S(1)}, f32[64]{0:T(128)S(1)}, u32[]{:S(2)}, u32[]{:S(2)}) collective-permute-start(f32[64]{0:T(128)S(1)} %bitcast_add_fusion.1), channel_id=1, source_target_pairs={{0,2},{1,3},{2,0},{3,1},{4,6},{5,7},{6,4},{7,5},{8,10},{9,11},{10,... | collective-permute-start | bytes 776 | tf_op jit(solution)/shard_map/ppermute | solution.py:185
  129.3 3.5 %collective-permute-start.17 = (f32[64]{0:T(128)S(1)}, f32[64]{0:T(128)S(1)}, u32[]{:S(2)}, u32[]{:S(2)}) collective-permute-start(f32[64]{0:T(128)S(1)} %bitcast_add_fusion.1), channel_id=1, source_target_pairs={{0,3},{1,0},{2,1},{3,2},{4,7},{5,4},{6,5},{7,6},{8,11},{9,8},{10,9... | collective-permute-start | bytes 776 | tf_op jit(solution)/shard_map/ppermute | solution.py:185
  135.7 10.4 %collective-permute-start.18 = (bf16[2,32,1024]{2,1,0:T(8,128)(2,1)S(1)}, bf16[2,32,1024]{2,1,0:T(8,128)(2,1)S(1)}, u32[]{:S(2)}, u32[]{:S(2)}) collective-permute-start(bf16[2,32,1024]{2,1,0:T(8,128)(2,1)S(1)} %get-tuple-element.50), channel_id=1, source_target_pairs={{0,1},{1,2},{2,3},{3,0},{4,5},{5,6},{6,7},{7,4},{8,9},{9,10},{10,1... | collective-permute-start | bytes 393224 | tf_op jit(solution)/shard_map/ppermute | solution.py:185
  135.7 11.8 %collective-permute-start.19 = (bf16[2,32,1024]{2,1,0:T(8,128)(2,1)S(1)}, bf16[2,32,1024]{2,1,0:T(8,128)(2,1)S(1)}, u32[]{:S(2)}, u32[]{:S(2)}) collective-permute-start(bf16[2,32,1024]{2,1,0:T(8,128)(2,1)S(1)} %get-tuple-element.49), channel_id=1, source_target_pairs={{0,2},{1,3},{2,0},{3,1},{4,6},{5,7},{6,4},{7,5},{8,10},{9,11},{10,... | collective-permute-start | bytes 393224 | tf_op jit(solution)/shard_map/ppermute | solution.py:185
  138.1 9.5 %collective-permute-start.20 = (bf16[2,32,1024]{2,1,0:T(8,128)(2,1)S(1)}, bf16[2,32,1024]{2,1,0:T(8,128)(2,1)S(1)}, u32[]{:S(2)}, u32[]{:S(2)}) collective-permute-start(bf16[2,32,1024]{2,1,0:T(8,128)(2,1)S(1)} %get-tuple-element.48), channel_id=1, source_target_pairs={{0,3},{1,0},{2,1},{3,2},{4,7},{5,4},{6,5},{7,6},{8,11},{9,8},{10,9... | collective-permute-start | bytes 393224 | tf_op jit(solution)/shard_map/ppermute | solution.py:185
  140.5 0.8 copy-start.5
  146.1 1.4 copy-start.9
  147.5 0.7 copy-start.10
  147.6 0.7 copy-start.11

commit v6 on v5

--- a/solution.py
+++ b/solution.py
@@ -206,18 +206,20 @@
     squares_part = jnp.sum(jnp.square(hidden.astype(F32)), axis=1)
     tail = 8 * block
     small = jnp.concatenate(parts_of(squares_part))
-    small = jnp.pad(small, (0, tail - small.size)).reshape(1, 1, 8, block)
-    head_send = after(w_out, *group[1:]).reshape(head_rows, steps, halves, block)
-    head_send = head_send.transpose(2, 1, 0, 3)
-    head_send = head_send.reshape(1, halves, steps * head_rows, block)
-    small = jnp.broadcast_to(small, (1, halves, 8, block))
-    head_send = jnp.concatenate([head_send, small], axis=2)
-    head_send = jnp.broadcast_to(head_send, (hids // halves,) + head_send.shape[1:])
-    head_send = head_send.reshape(hids, steps * head_rows + 8, block)
-    head_got = lax.all_to_all(head_send, "hid", 0, 0)
-    head_mid = head_got[:, : steps * head_rows].reshape(hids, steps, head_rows, block)
-    squares = head_got[:, steps * head_rows :].reshape(hids, tail)[:, : EXACT * rows]
-    squares = jnp.sum(squares.astype(F32).reshape(hids * EXACT, rows), axis=0)
+    small = jnp.pad(small, (0, tail - small.size)).reshape(8, block)
+    head_parts = w_out.reshape(head_rows, steps, halves, block)
+    head_send = []
+    for k in range(halves):
+        piece = lax.dynamic_index_in_dim(head_parts, (half + k) % halves, 2, False)
+        piece = piece.transpose(1, 0, 2).reshape(steps * head_rows, block)
+        head_send.append(jnp.concatenate([piece, small]))
+    head_got = [head_send[0]]
+    head_got += [along_hid(head_send[shift % halves], shift) for shift in range(1, hids)]
+    squares = sum(g[steps * head_rows :].astype(F32) for g in head_got).reshape(tail)
+    squares = jnp.sum(squares[: EXACT * rows].reshape(EXACT, rows), axis=0)
+    head_mid = jnp.stack([g[: steps * head_rows] for g in head_got[::-1]] * 2)
+    head_mid = lax.dynamic_slice_in_dim(head_mid, hids - 1 - j, hids, 0)
+    head_mid = head_mid.reshape(hids, steps, head_rows, block)
 
     w_own = pick(w_in, step)
     proj_parts = matmul(jnp.concatenate(group), w_own, ((1,), (0,)))
@@ -227,7 +229,7 @@
         return lax.dynamic_index_in_dim(proj_parts, index, 1, False).reshape(owned, depth)
 
     send = [owner_block((j + shift) % hids).astype(BF16) for shift in range(1, hids)]
-    send = [after(p, head_got) for p in send]
+    send = [after(p, *head_got[1:]) for p in send]
     received = [along_hid(send[shift - 1], shift) for shift in range(1, hids)]
 
     ids = after(codebook_ids, *send)

time: 153 us -> 153 us (level)
  local copies, waits for them, and re-layouts: 15.9 us -> 18.8 us
  starting transfers between devices: 45 us -> 43.4 us
  matrix products: 8.58 us -> 6.99 us
    all_to_all x1 -> x0, waiting for transfers between devices: 12.3 us -> none  [shards(): head_got = lax.all_to_all(head_send, 'hid', 0, 0)]
    ppermute x12 -> x15, waiting for transfers between devices: 36.8 us -> 47.2 us  [along_hid(): lax.ppermute(values, 'hid', [(a, (a + shift) % hids) for a in range(hids)])]
    ppermute x12 -> x15, starting transfers between devices: 20.2 us -> 27.6 us  [along_hid(): lax.ppermute(values, 'hid', [(a, (a + shift) % hids) for a in range(hids)])]
    all_to_all x1 -> x0, starting transfers between devices: 6.24 us -> none  [shards(): head_got = lax.all_to_all(head_send, 'hid', 0, 0)]
    ppermute x4, waiting for transfers between devices: 10.9 us -> 13.3 us  [turn_hid(): lax.ppermute(values, 'hid', [(a, a - a % halves + (a % halves + shift) %...]
    unnamed x35 -> x46, local copies, waits for them, and re-layouts: 4.31 us -> 6.61 us
    ppermute x4, starting transfers between devices: 4.65 us -> 2.77 us  [turn_hid(): lax.ppermute(values, 'hid', [(a, a - a % halves + (a % halves + shift) %...]
    dot_general x5, matrix products: 8.58 us -> 6.99 us  [matmul(): lax.dot_general(a, b, (contract, ((), ())), preferred_element_type=F32)]
  transfers between devices with their start and end apart: 25 -> 27, of which waited for: 14 -> 15; matrix products, arithmetic and copies ran while one was open for 15% -> 14% of each run, Pallas kernels for 8% -> 8%
where the time goes in v6:
time: 153 us
  waiting for transfers between devices  61.4 us (40%)
  starting transfers between devices  43.4 us (28%)
  local copies, waits for them, and re-layouts  18.8 us (12%)
  Pallas kernels  12.7 us (8%)
  other arithmetic  8.31 us (5%)
  matrix products  6.99 us (5%)
    ppermute x15, waiting for transfers between devices, along_hid(): lax.ppermute(values, 'hid', [(a, (a + shift) % hids) for a in range(hids)])  47.2 us
    ppermute x15, starting transfers between devices, along_hid(): lax.ppermute(values, 'hid', [(a, (a + shift) % hids) for a in range(hids)])  27.6 us
    ppermute x4, waiting for transfers between devices, turn_hid(): lax.ppermute(values, 'hid', [(a, a - a % halves + (a % halves + shift) %...  13.3 us
    pallas_call x3, Pallas kernels, call(): pl.pallas_call(kernel, grid_spec=pltpu.PrefetchScalarGridSpec(num_scalar_...  12.7 us
    dot_general x5, matrix products, matmul(): lax.dot_general(a, b, (contract, ((), ())), preferred_element_type=F32)  6.99 us
    unnamed x46, local copies, waits for them, and re-layouts  6.61 us
    all_to_all x1, starting transfers between devices, shards(): part_out = lax.all_to_all(part_out, 'seq', 0, 0)  4.34 us
    all_to_all x1, starting transfers between devices, shards(): lax.all_to_all(share.reshape(seqs, depth // seqs, units), 'seq', 0, 0)  4.01 us
  transfers between devices with their start and end apart: 27, of which 15 were waited for; matrix products, arithmetic and copies ran while one was open for 14% of the time, Pallas kernels for 8%

profile of v6, /device:TPU:0, one launch (start us, length us, event | category | flops | bytes accessed | tf_op | source)
XLA Modules:
  0.0 152.7 jit_solution(13965673018573917603)
XLA Ops:
  0.7 1.3 multiply_reduce_fusion
  2.0 1.1 reshape.276
  3.9 3.1 %collective-permute-start = (bf16[72,1024]{1,0:T(8,128)(2,1)S(1)}, bf16[72,1024]{1,0:T(8,128)(2,1)S(1)}, u32[]{:S(2)}, u32[]{:S(2)}) collective-permute-start(bf16[72,1024]{1,0:T(8,128)(2,1)S(1)} %get-tuple-element.53), channel_id=1, source_target_pairs={{0,1},{1,2},{2,3},{3,0},{4,5},{5,6},{6,7},{7,4},{8,9},{9,10},{10,1... | collective-permute-start | bytes 442376 | tf_op jit(solution)/shard_map/ppermute | solution.py:185
  7.0 2.6 %collective-permute-start.1 = (bf16[72,1024]{1,0:T(8,128)(2,1)S(1)}, bf16[72,1024]{1,0:T(8,128)(2,1)S(1)}, u32[]{:S(2)}, u32[]{:S(2)}) collective-permute-start(bf16[72,1024]{1,0:T(8,128)(2,1)S(1)} %get-tuple-element.52), channel_id=1, source_target_pairs={{0,2},{1,3},{2,0},{3,1},{4,6},{5,7},{6,4},{7,5},{8,10},{9,11},{10,... | collective-permute-start | bytes 442376 | tf_op jit(solution)/shard_map/ppermute | solution.py:185
  9.6 1.3 collective-permute-start.2
  10.9 2.9 %collective-permute-done = bf16[72,1024]{1,0:T(8,128)(2,1)S(1)} collective-permute-done((bf16[72,1024]{1,0:T(8,128)(2,1)S(1)}, bf16[72,1024]{1,0:T(8,128)(2,1)S(1)}, u32[]{:S(2)}, u32[]{:S(2)}) %collective-permute-start) | collective-permute-done | bytes 147488 | tf_op jit(solution)/shard_map/ppermute | solution.py:185
  13.8 5.5 %collective-permute-done.1 = bf16[72,1024]{1,0:T(8,128)(2,1)S(1)} collective-permute-done((bf16[72,1024]{1,0:T(8,128)(2,1)S(1)}, bf16[72,1024]{1,0:T(8,128)(2,1)S(1)}, u32[]{:S(2)}, u32[]{:S(2)}) %collective-permute-start.1) | collective-permute-done | bytes 147488 | tf_op jit(solution)/shard_map/ppermute | solution.py:185
  19.7 2.1 %copy-done.2 = bf16[2,1024,1024]{2,1,0:T(8,128)(2,1)S(1)} copy-done((bf16[2,1024,1024]{2,1,0:T(8,128)(2,1)S(1)}, bf16[2,1024,1024]{2,1,0:T(8,128)(2,1)}, u32[]{:S(2)}) %copy-start.2) | copy-done | bytes 4194328
  21.9 1.3 fusion
  23.2 0.9 dynamic-slice_convert_fusion
  24.1 1.6 %broadcast_in_dim.45 = bf16[4,2,128,1024]{3,2,1,0:T(8,128)(2,1)} broadcast(bf16[2,128,1024]{2,1,0:T(8,128)(2,1)S(1)} %bitcast.141), dimensions={1,2,3} | broadcast | bytes 2621440 | tf_op jit(solution)/shard_map/broadcast_in_dim | solution.py:243
  25.7 4.0 %all-to-all-start = ((bf16[8,128,1024]{2,1,0:T(8,128)(2,1)}), bf16[8,128,1024]{2,1,0:T(8,128)(2,1)S(1)}, u32[]{:S(2)}, u32[]{:S(2)}) async-start(bf16[8,128,1024]{2,1,0:T(8,128)(2,1)} %bitcast.137), calls=%async_computation | async-start | bytes 4194304 | tf_op jit(solution)/shard_map/all_to_all | solution.py:245
  30.0 4.7 %collective-permute-start.7 = (bf16[128,1024]{1,0:T(8,128)(2,1)}, bf16[128,1024]{1,0:T(8,128)(2,1)}, u32[]{:S(2)}, u32[]{:S(2)}) collective-permute-start(bf16[128,1024]{1,0:T(8,128)(2,1)} %bitcast.13), channel_id=1, source_target_pairs={{0,3},{1,0},{2,1},{3,2},{4,7},{5,4},{6,5},{7,6},{8,11},{9,8},{10,9... | collective-permute-start | bytes 786440 | tf_op jit(solution)/shard_map/ppermute | solution.py:185
  35.3 1.1 constant_dynamic-slice_fusion.6
  36.5 3.8 %gather_fusion = bf16[128,1024]{1,0:T(8,128)(2,1)S(1)} fusion(bf16[2048,1024]{1,0:T(8,128)(2,1)} %bitcast.147, s32[1024]{0:T(1024)S(1)} %pad_clamp_fusion), kind=kCustom, calls=%fused_computation | custom fusion | bytes 524800 | tf_op jit(solution)/shard_map/jit(_take)/gather | solution.py:239
  40.3 1.4 collective-permute-done.7
  41.7 17.2 %collective-permute-done.6 = bf16[128,1024]{1,0:T(8,128)(2,1)} collective-permute-done((bf16[128,1024]{1,0:T(8,128)(2,1)S(1)}, bf16[128,1024]{1,0:T(8,128)(2,1)}, u32[]{:S(2)}, u32[]{:S(2)}) %collective-permute-start.6) | collective-permute-done | bytes 262176 | tf_op jit(solution)/shard_map/ppermute | solution.py:185
  58.9 1.4 multiply_reduce_fusion.4
  60.7 2.0 %collective-permute-start.11 = (s32[2,128]{1,0:T(2,128)S(1)}, s32[2,128]{1,0:T(2,128)S(1)}, u32[]{:S(2)}, u32[]{:S(2)}) collective-permute-start(s32[2,128]{1,0:T(2,128)S(1)} %pad_add_fusion), channel_id=1, source_target_pairs={{0,1},{1,0},{2,3},{3,2},{4,5},{5,4},{6,7},{7,6},{8,9},{9,8},{10,11... | collective-permute-start | bytes 3080 | tf_op jit(solution)/shard_map/ppermute | solution.py:188
  62.7 5.9 %collective-permute-done.11 = s32[2,128]{1,0:T(2,128)S(1)} collective-permute-done((s32[2,128]{1,0:T(2,128)S(1)}, s32[2,128]{1,0:T(2,128)S(1)}, u32[]{:S(2)}, u32[]{:S(2)}) %collective-permute-start.11) | collective-permute-done | bytes 1056 | tf_op jit(solution)/shard_map/ppermute | solution.py:188
  68.7 0.8 fusion.42
  70.2 3.3 %collective-permute-done.10 = f32[2,2,128]{2,1,0:T(2,128)S(1)} collective-permute-done((f32[2,2,128]{2,1,0:T(2,128)S(1)}, f32[2,2,128]{2,1,0:T(2,128)S(1)}, u32[]{:S(2)}, u32[]{:S(2)}) %collective-permute-start.10) | collective-permute-done | bytes 2080 | tf_op jit(solution)/shard_map/ppermute | solution.py:188
  74.0 0.8 convolution_convert_fusion.1
  75.2 2.1 %convolution_convert_fusion = bf16[1024,1024]{1,0:T(8,128)(2,1)} fusion(bf16[256,1024]{1,0:T(8,128)(2,1)S(1)} %multiply_convert_fusion, bf16[128,1024]{1,0:T(8,128)(2,1)S(1)} %copy-done.9, bf16[128,1024]{1,0:T(8,128)(2,1)S(1)} %copy-done.4), kind=kOutput, calls=%fused_computation.5 | convolution fusion | flops 538968064 | bytes 3145728 | tf_op jit(solution)/shard_map/dot_general | solution.py:17
  77.3 4.1 %collective-permute-done.12 = bf16[128,1024]{1,0:T(8,128)(2,1)} collective-permute-done((bf16[128,1024]{1,0:T(8,128)(2,1)S(1)}, bf16[128,1024]{1,0:T(8,128)(2,1)}, u32[]{:S(2)}, u32[]{:S(2)}) %collective-permute-start.12) | collective-permute-done | bytes 262176 | tf_op jit(solution)/shard_map/ppermute | solution.py:188
  81.4 4.3 %all-to-all-start.2 = ((bf16[8,128,1024]{2,1,0:T(8,128)(2,1)}), bf16[8,128,1024]{2,1,0:T(8,128)(2,1)}, u32[]{:S(2)}, u32[]{:S(2)}) async-start(bf16[8,128,1024]{2,1,0:T(8,128)(2,1)} %bitcast.139), calls=%async_computation.2 | async-start | bytes 4194304 | tf_op jit(solution)/shard_map/all_to_all | solution.py:292
  85.7 2.0 %multiply_reduce_fusion.2 = (f32[128]{0:T(128)S(1)}, f32[128]{0:T(128)S(1)}, f32[128]{0:T(128)S(1)}, f32[128,1024]{1,0:T(8,128)S(1)}) fusion(f32[128,1024]{1,0:T(8,128)S(1)} %get-tuple-element.42, bf16[128,1024]{1,0:T(8,128)(2,1)} %collective-permute-done.12, f32[1024]{0:T(1024)S(1)} %bitcast.153, bf16[128,1024]{1,0:T(8,128)(2,1)S(1)} %gather_fusion, ...), kind=kOutput, calls=%fused_computation.16 | convolution fusion | flops 270270080 | bytes 3938433 | tf_op jit(solution)/shard_map/dot_general | solution.py:17
  87.7 1.2 subtract_convert_fusion.refs_0_
  89.3 1.5 collective-permute-start.14
  90.8 2.6 %collective-permute-start.15 = (bf16[128,1024]{1,0:T(8,128)(2,1)S(1)}, bf16[128,1024]{1,0:T(8,128)(2,1)S(1)}, u32[]{:S(2)}, u32[]{:S(2)}) collective-permute-start(bf16[128,1024]{1,0:T(8,128)(2,1)S(1)} %subtract_convert_fusion.refs_0_), channel_id=1, source_target_pairs={{0,3},{1,0},{2,1},{3,2},{4,7},{5,4},{6,5},{7,6},{8,11},{9,8},{10,9... | collective-permute-start | bytes 786440 | tf_op jit(solution)/shard_map/ppermute | solution.py:185
  94.2 0.9 copy.39.refs_6_
  95.0 5.1 %collective-permute-done.13.refs_1_ = bf16[128,1024]{1,0:T(8,128)(2,1)S(1)} collective-permute-done((bf16[128,1024]{1,0:T(8,128)(2,1)S(1)}, bf16[128,1024]{1,0:T(8,128)(2,1)S(1)}, u32[]{:S(2)}, u32[]{:S(2)}) %collective-permute-start.13) | collective-permute-done | bytes 262176 | tf_op jit(solution)/shard_map/ppermute | solution.py:185
  100.1 10.5 %collective-permute-done.14.refs_2_ = bf16[128,1024]{1,0:T(8,128)(2,1)S(1)} collective-permute-done((bf16[128,1024]{1,0:T(8,128)(2,1)S(1)}, bf16[128,1024]{1,0:T(8,128)(2,1)S(1)}, u32[]{:S(2)}, u32[]{:S(2)}) %collective-permute-start.14) | collective-permute-done | bytes 262176 | tf_op jit(solution)/shard_map/ppermute | solution.py:185
  112.1 5.1 %shard_map.85 = (bf16[1024,1024]{1,0:T(8,128)(2,1)}, bf16[256,1024]{1,0:T(8,128)(2,1)}, bf16[256,1024]{1,0:T(8,128)(2,1)}) custom-call(s32[2]{0:T(128)} %pad_add_fusion.2.place_ref, bf16[128,1024]{1,0:T(8,128)(2,1)} %copy-done.10, bf16[128,1024]{1,0:T(8,128)(2,1)} %copy-done.15, bf16[128,1024]{1,0:T(8,128)(2,1)} %copy-done.16, bf16[128,1024]{1,0:T(8,128)(2,1)} %copy-done.17, ...), custom_call_target="tpu_custom_call" | custom-call | flops 1073741824 | bytes 2099200 | tf_op jit(solution)/shard_map/pallas_call | solution.py:33
  117.1 4.0 %all-to-all-start.1 = ((bf16[8,128,1024]{2,1,0:T(8,128)(2,1)}), bf16[8,128,1024]{2,1,0:T(8,128)(2,1)S(1)}, u32[]{:S(2)}, u32[]{:S(2)}) async-start(bf16[8,128,1024]{2,1,0:T(8,128)(2,1)} %bitcast.142), calls=%async_computation.1 | async-start | bytes 4194304 | tf_op jit(solution)/shard_map/all_to_all | solution.py:304
  121.8 0.8 collective-permute-done.17
  122.6 4.6 %collective-permute-start.18 = (f32[64]{0:T(128)S(1)}, f32[64]{0:T(128)S(1)}, u32[]{:S(2)}, u32[]{:S(2)}) collective-permute-start(f32[64]{0:T(128)S(1)} %bitcast_add_fusion.1), channel_id=1, source_target_pairs={{0,1},{1,2},{2,3},{3,0},{4,5},{5,6},{6,7},{7,4},{8,9},{9,10},{10,1... | collective-permute-start | bytes 776 | tf_op jit(solution)/shard_map/ppermute | solution.py:185
  127.2 2.1 %collective-permute-start.19 = (f32[64]{0:T(128)S(1)}, f32[64]{0:T(128)S(1)}, u32[]{:S(2)}, u32[]{:S(2)}) collective-permute-start(f32[64]{0:T(128)S(1)} %bitcast_add_fusion.1), channel_id=1, source_target_pairs={{0,2},{1,3},{2,0},{3,1},{4,6},{5,7},{6,4},{7,5},{8,10},{9,11},{10,... | collective-permute-start | bytes 776 | tf_op jit(solution)/shard_map/ppermute | solution.py:185
  130.3 1.4 collective-permute-done.19
  131.7 1.2 collective-permute-done.20
  133.0 2.0 %reduce_sum.108 = bf16[2,4,32,1024]{3,2,1,0:T(8,128)(2,1)S(1)} reduce(bf16[4,2,4,32,1024]{4,3,2,1,0:T(8,128)(2,1)} %bitcast.57, bf16[]{:T(256)} %constant.168.clone.1), dimensions={0}, to_apply=%region_10.11 | reduce | flops 786432 | bytes 2621442 | tf_op jit(solution)/shard_map/reduce_sum | solution.py:293
  135.7 2.6 %collective-permute-start.22 = (bf16[2,32,1024]{2,1,0:T(8,128)(2,1)S(1)}, bf16[2,32,1024]{2,1,0:T(8,128)(2,1)S(1)}, u32[]{:S(2)}, u32[]{:S(2)}) collective-permute-start(bf16[2,32,1024]{2,1,0:T(8,128)(2,1)S(1)} %get-tuple-element.47), channel_id=1, source_target_pairs={{0,2},{1,3},{2,0},{3,1},{4,6},{5,7},{6,4},{7,5},{8,10},{9,11},{10,... | collective-permute-start | bytes 393224 | tf_op jit(solution)/shard_map/ppermute | solution.py:185
  138.4 1.2 collective-permute-start.23
  139.6 0.9 copy.40.refs_4_
  141.2 4.9 %shard_map.86 = bf16[256,1024]{1,0:T(8,128)(2,1)} custom-call(s32[2]{0:T(128)} %pad_add_fusion.2.place_ref, bf16[256,1024]{1,0:T(8,128)(2,1)} %get-tuple-element.20.refs_0_, bf16[256,1024]{1,0:T(8,128)(2,1)} %copy-done.7, bf16[2,1024,1024]{2,1,0:T(8,128)(2,1)} %refs_2_.1, bf16[256,1024]{1,0:T(8,128)(2,1)} %refs_3_.1, f32[2,256,1]{2,1,0:T(8,128)} %copy.40.refs_4_), custom_call_target="tpu_custom_call" | custom-call | flops 1073741824 | bytes 5769216 | tf_op jit(solution)/shard_map/pallas_call | solution.py:33
  146.2 1.4 collective-permute-done.22.refs_2_
  148.3 2.7 %shard_map.87 = f32[32,2,2048]{2,1,0:T(2,128)} custom-call(s32[2]{0:T(128)} %pad_add_fusion.2.place_ref, bf16[2,32,1024]{2,1,0:T(8,128)(2,1)} %get-tuple-element.49.refs_0_, bf16[2,32,1024]{2,1,0:T(8,128)(2,1)} %copy-done.11, bf16[2,32,1024]{2,1,0:T(8,128)(2,1)} %copy-done.12, bf16[2,32,1024]{2,1,0:T(8,128)(2,1)} %copy-done.13), custom_call_target="tpu_custom_call" | custom-call | flops 262144 | bytes 524288 | tf_op jit(solution)/shard_map/pallas_call | solution.py:33
  151.3 1.3 copy.41
  (122 shorter events, 10.9 us)
Async XLA Ops:
  0.6 29.1 %copy-start = (f32[2,1024]{1,0:T(2,128)S(1)}, f32[2,1024]{1,0:T(2,128)}, u32[]{:S(2)}) copy-start(f32[2,1024]{1,0:T(2,128)} %param.9) | copy-start | bytes 24580
  0.6 10.3 %copy-start.1 = (bf16[256,1024]{1,0:T(8,128)(2,1)S(1)}, bf16[256,1024]{1,0:T(8,128)(2,1)}, u32[]{:S(2)}) copy-start(bf16[256,1024]{1,0:T(8,128)(2,1)} %refs_3_.1) | copy-start | bytes 1572868
  3.9 9.9 %collective-permute-start = (bf16[72,1024]{1,0:T(8,128)(2,1)S(1)}, bf16[72,1024]{1,0:T(8,128)(2,1)S(1)}, u32[]{:S(2)}, u32[]{:S(2)}) collective-permute-start(bf16[72,1024]{1,0:T(8,128)(2,1)S(1)} %get-tuple-element.53), channel_id=1, source_target_pairs={{0,1},{1,2},{2,3},{3,0},{4,5},{5,6},{6,7},{7,4},{8,9},{9,10},{10,1... | collective-permute-start | bytes 442376 | tf_op jit(solution)/shard_map/ppermute | solution.py:185
  7.0 12.3 %collective-permute-start.1 = (bf16[72,1024]{1,0:T(8,128)(2,1)S(1)}, bf16[72,1024]{1,0:T(8,128)(2,1)S(1)}, u32[]{:S(2)}, u32[]{:S(2)}) collective-permute-start(bf16[72,1024]{1,0:T(8,128)(2,1)S(1)} %get-tuple-element.52), channel_id=1, source_target_pairs={{0,2},{1,3},{2,0},{3,1},{4,6},{5,7},{6,4},{7,5},{8,10},{9,11},{10,... | collective-permute-start | bytes 442376 | tf_op jit(solution)/shard_map/ppermute | solution.py:185
  9.6 9.7 %collective-permute-start.2 = (bf16[72,1024]{1,0:T(8,128)(2,1)S(1)}, bf16[72,1024]{1,0:T(8,128)(2,1)S(1)}, u32[]{:S(2)}, u32[]{:S(2)}) collective-permute-start(bf16[72,1024]{1,0:T(8,128)(2,1)S(1)} %get-tuple-element.53), channel_id=1, source_target_pairs={{0,3},{1,0},{2,1},{3,2},{4,7},{5,4},{6,5},{7,6},{8,11},{9,8},{10,9... | collective-permute-start | bytes 442376 | tf_op jit(solution)/shard_map/ppermute | solution.py:185
  10.9 8.7 %collective-permute-start.4 = (bf16[256,1024]{1,0:T(8,128)(2,1)S(1)}, bf16[256,1024]{1,0:T(8,128)(2,1)S(1)}, u32[]{:S(2)}, u32[]{:S(2)}) collective-permute-start(bf16[256,1024]{1,0:T(8,128)(2,1)S(1)} %copy-done.1), channel_id=1, source_target_pairs={{0,4},{4,0},{8,12},{12,8},{16,20},{20,16},{24,28},{28,24},{1,5},{5... | collective-permute-start | bytes 1572872 | tf_op jit(solution)/shard_map/ppermute | solution.py:195
  19.3 10.5 %collective-permute-start.3 = (f32[256]{0:T(256)S(1)}, f32[256]{0:T(256)S(1)}, u32[]{:S(2)}, u32[]{:S(2)}) collective-permute-start(f32[256]{0:T(256)S(1)} %slice_reduce_fusion), channel_id=1, source_target_pairs={{0,4},{4,0},{8,12},{12,8},{16,20},{20,16},{24,28},{28,24},{1,5},{5... | collective-permute-start | bytes 3080 | tf_op jit(solution)/shard_map/ppermute | solution.py:195
  19.5 2.4 %copy-start.2 = (bf16[2,1024,1024]{2,1,0:T(8,128)(2,1)S(1)}, bf16[2,1024,1024]{2,1,0:T(8,128)(2,1)}, u32[]{:S(2)}) copy-start(bf16[2,1024,1024]{2,1,0:T(8,128)(2,1)} %refs_2_.1) | copy-start | bytes 12582916
  19.6 3.5 %copy-start.6 = (bf16[256,1024]{1,0:T(8,128)(2,1)}, bf16[256,1024]{1,0:T(8,128)(2,1)S(1)}, u32[]{:S(2)}) copy-start(bf16[256,1024]{1,0:T(8,128)(2,1)S(1)} %collective-permute-done.4.refs_5_) | copy-start | bytes 1572868
  23.1 2.6 %copy-start.5 = (f32[2,4,64,1024]{3,2,1,0:T(8,128)}, f32[2,4,64,1024]{3,2,1,0:T(8,128)S(1)}, u32[]{:S(2)}) copy-start(f32[2,4,64,1024]{3,2,1,0:T(8,128)S(1)} %fusion) | copy-start | bytes 6291460
  25.7 9.6 %copy-start.14 = (s32[2,64]{1,0:T(2,128)S(1)}, s32[2,64]{1,0:T(2,128)}, u32[]{:S(2)}) copy-start(s32[2,64]{1,0:T(2,128)} %param.11) | copy-start | bytes 1540
  25.7 43.0 %all-to-all-start = ((bf16[8,128,1024]{2,1,0:T(8,128)(2,1)}), bf16[8,128,1024]{2,1,0:T(8,128)(2,1)S(1)}, u32[]{:S(2)}, u32[]{:S(2)}) async-start(bf16[8,128,1024]{2,1,0:T(8,128)(2,1)} %bitcast.137), calls=%async_computation | async-start | bytes 4194304 | tf_op jit(solution)/shard_map/all_to_all | solution.py:245
  30.0 11.7 %collective-permute-start.7 = (bf16[128,1024]{1,0:T(8,128)(2,1)}, bf16[128,1024]{1,0:T(8,128)(2,1)}, u32[]{:S(2)}, u32[]{:S(2)}) collective-permute-start(bf16[128,1024]{1,0:T(8,128)(2,1)} %bitcast.13), channel_id=1, source_target_pairs={{0,3},{1,0},{2,1},{3,2},{4,7},{5,4},{6,5},{7,6},{8,11},{9,8},{10,9... | collective-permute-start | bytes 786440 | tf_op jit(solution)/shard_map/ppermute | solution.py:185
  34.7 24.2 %collective-permute-start.6 = (bf16[128,1024]{1,0:T(8,128)(2,1)S(1)}, bf16[128,1024]{1,0:T(8,128)(2,1)}, u32[]{:S(2)}, u32[]{:S(2)}) collective-permute-start(bf16[128,1024]{1,0:T(8,128)(2,1)S(1)} %bitcast.151), channel_id=1, source_target_pairs={{0,2},{1,3},{2,0},{3,1},{4,6},{5,7},{6,4},{7,5},{8,10},{9,11},{10,... | collective-permute-start | bytes 786440 | tf_op jit(solution)/shard_map/ppermute | solution.py:185
  35.1 23.9 %collective-permute-start.5 = (bf16[128,1024]{1,0:T(8,128)(2,1)S(1)}, bf16[128,1024]{1,0:T(8,128)(2,1)}, u32[]{:S(2)}, u32[]{:S(2)}) collective-permute-start(bf16[128,1024]{1,0:T(8,128)(2,1)S(1)} %bitcast.150), channel_id=1, source_target_pairs={{0,1},{1,2},{2,3},{3,0},{4,5},{5,6},{6,7},{7,4},{8,9},{9,10},{10,1... | collective-permute-start | bytes 786440 | tf_op jit(solution)/shard_map/ppermute | solution.py:185
  35.3 1.1 collective-permute-start.8
  60.6 9.2 %copy-start.3 = (bf16[128,1024]{1,0:T(8,128)(2,1)}, bf16[128,1024]{1,0:T(8,128)(2,1)S(1)}, u32[]{:S(2)}) copy-start(bf16[128,1024]{1,0:T(8,128)(2,1)S(1)} %multiply_convert_fusion.1) | copy-start | bytes 786436
  60.6 8.1 %collective-permute-start.9 = (bf16[128,1024]{1,0:T(8,128)(2,1)S(1)}, bf16[128,1024]{1,0:T(8,128)(2,1)S(1)}, u32[]{:S(2)}, u32[]{:S(2)}) collective-permute-start(bf16[128,1024]{1,0:T(8,128)(2,1)S(1)} %multiply_convert_fusion.1), channel_id=1, source_target_pairs={{0,1},{1,0},{2,3},{3,2},{4,5},{5,4},{6,7},{7,6},{8,9},{9,8},{10,11... | collective-permute-start | bytes 786440 | tf_op jit(solution)/shard_map/ppermute | solution.py:188
  60.7 8.0 %collective-permute-start.11 = (s32[2,128]{1,0:T(2,128)S(1)}, s32[2,128]{1,0:T(2,128)S(1)}, u32[]{:S(2)}, u32[]{:S(2)}) collective-permute-start(s32[2,128]{1,0:T(2,128)S(1)} %pad_add_fusion), channel_id=1, source_target_pairs={{0,1},{1,0},{2,3},{3,2},{4,5},{5,4},{6,7},{7,6},{8,9},{9,8},{10,11... | collective-permute-start | bytes 3080 | tf_op jit(solution)/shard_map/ppermute | solution.py:188
  68.7 1.2 copy-start.8
  69.9 3.7 %collective-permute-start.10 = (f32[2,2,128]{2,1,0:T(2,128)S(1)}, f32[2,2,128]{2,1,0:T(2,128)S(1)}, u32[]{:S(2)}, u32[]{:S(2)}) collective-permute-start(f32[2,2,128]{2,1,0:T(2,128)S(1)} %pad_maximum_fusion.6), channel_id=1, source_target_pairs={{0,1},{1,0},{2,3},{3,2},{4,5},{5,4},{6,7},{7,6},{8,9},{9,8},{10,11... | collective-permute-start | bytes 6152 | tf_op jit(solution)/shard_map/ppermute | solution.py:188
  73.6 1.6 %copy-start.4 = (bf16[128,1024]{1,0:T(8,128)(2,1)S(1)}, bf16[128,1024]{1,0:T(8,128)(2,1)}, u32[]{:S(2)}) copy-start(bf16[128,1024]{1,0:T(8,128)(2,1)} %copy-done.3) | copy-start | bytes 786436
  73.6 1.6 %copy-start.9 = (bf16[128,1024]{1,0:T(8,128)(2,1)S(1)}, bf16[128,1024]{1,0:T(8,128)(2,1)}, u32[]{:S(2)}) copy-start(bf16[128,1024]{1,0:T(8,128)(2,1)} %copy-done.8) | copy-start | bytes 786436
  74.8 6.5 %collective-permute-start.12 = (bf16[128,1024]{1,0:T(8,128)(2,1)S(1)}, bf16[128,1024]{1,0:T(8,128)(2,1)}, u32[]{:S(2)}, u32[]{:S(2)}) collective-permute-start(bf16[128,1024]{1,0:T(8,128)(2,1)S(1)} %convolution_convert_fusion.1), channel_id=1, source_target_pairs={{0,1},{1,0},{2,3},{3,2},{4,5},{5,4},{6,7},{7,6},{8,9},{9,8},{10,11... | collective-permute-start | bytes 786440 | tf_op jit(solution)/shard_map/ppermute | solution.py:188
  81.4 35.8 %all-to-all-start.2 = ((bf16[8,128,1024]{2,1,0:T(8,128)(2,1)}), bf16[8,128,1024]{2,1,0:T(8,128)(2,1)}, u32[]{:S(2)}, u32[]{:S(2)}) async-start(bf16[8,128,1024]{2,1,0:T(8,128)(2,1)} %bitcast.139), calls=%async_computation.2 | async-start | bytes 4194304 | tf_op jit(solution)/shard_map/all_to_all | solution.py:292
  89.0 21.7 %copy-start.10 = (bf16[128,1024]{1,0:T(8,128)(2,1)}, bf16[128,1024]{1,0:T(8,128)(2,1)S(1)}, u32[]{:S(2)}) copy-start(bf16[128,1024]{1,0:T(8,128)(2,1)S(1)} %subtract_convert_fusion.refs_0_) | copy-start | bytes 786436
  89.0 11.1 %collective-permute-start.13 = (bf16[128,1024]{1,0:T(8,128)(2,1)S(1)}, bf16[128,1024]{1,0:T(8,128)(2,1)S(1)}, u32[]{:S(2)}, u32[]{:S(2)}) collective-permute-start(bf16[128,1024]{1,0:T(8,128)(2,1)S(1)} %subtract_convert_fusion.refs_0_), channel_id=1, source_target_pairs={{0,1},{1,2},{2,3},{3,0},{4,5},{5,6},{6,7},{7,4},{8,9},{9,10},{10,1... | collective-permute-start | bytes 786440 | tf_op jit(solution)/shard_map/ppermute | solution.py:185
  89.3 21.3 %collective-permute-start.14 = (bf16[128,1024]{1,0:T(8,128)(2,1)S(1)}, bf16[128,1024]{1,0:T(8,128)(2,1)S(1)}, u32[]{:S(2)}, u32[]{:S(2)}) collective-permute-start(bf16[128,1024]{1,0:T(8,128)(2,1)S(1)} %subtract_convert_fusion.refs_0_), channel_id=1, source_target_pairs={{0,2},{1,3},{2,0},{3,1},{4,6},{5,7},{6,4},{7,5},{8,10},{9,11},{10,... | collective-permute-start | bytes 786440 | tf_op jit(solution)/shard_map/ppermute | solution.py:185
  90.8 19.8 %collective-permute-start.15 = (bf16[128,1024]{1,0:T(8,128)(2,1)S(1)}, bf16[128,1024]{1,0:T(8,128)(2,1)S(1)}, u32[]{:S(2)}, u32[]{:S(2)}) collective-permute-start(bf16[128,1024]{1,0:T(8,128)(2,1)S(1)} %subtract_convert_fusion.refs_0_), channel_id=1, source_target_pairs={{0,3},{1,0},{2,1},{3,2},{4,7},{5,4},{6,5},{7,6},{8,11},{9,8},{10,9... | collective-permute-start | bytes 786440 | tf_op jit(solution)/shard_map/ppermute | solution.py:185
  100.1 10.6 %copy-start.15 = (bf16[128,1024]{1,0:T(8,128)(2,1)}, bf16[128,1024]{1,0:T(8,128)(2,1)S(1)}, u32[]{:S(2)}) copy-start(bf16[128,1024]{1,0:T(8,128)(2,1)S(1)} %collective-permute-done.13.refs_1_) | copy-start | bytes 786436
  110.7 0.7 copy-start.16
  111.4 0.7 copy-start.17
  117.1 33.8 %all-to-all-start.1 = ((bf16[8,128,1024]{2,1,0:T(8,128)(2,1)}), bf16[8,128,1024]{2,1,0:T(8,128)(2,1)S(1)}, u32[]{:S(2)}, u32[]{:S(2)}) async-start(bf16[8,128,1024]{2,1,0:T(8,128)(2,1)} %bitcast.142), calls=%async_computation.1 | async-start | bytes 4194304 | tf_op jit(solution)/shard_map/all_to_all | solution.py:304
  121.2 1.4 collective-permute-start.17
  121.7 18.7 %collective-permute-start.16 = (bf16[256,1024]{1,0:T(8,128)(2,1)}, bf16[256,1024]{1,0:T(8,128)(2,1)S(1)}, u32[]{:S(2)}, u32[]{:S(2)}) collective-permute-start(bf16[256,1024]{1,0:T(8,128)(2,1)} %get-tuple-element.21), channel_id=1, source_target_pairs={{0,4},{4,0},{8,12},{12,8},{16,20},{20,16},{24,28},{28,24},{1,5},{5... | collective-permute-start | bytes 1572872 | tf_op jit(solution)/shard_map/ppermute | solution.py:195
  122.6 7.6 %collective-permute-start.18 = (f32[64]{0:T(128)S(1)}, f32[64]{0:T(128)S(1)}, u32[]{:S(2)}, u32[]{:S(2)}) collective-permute-start(f32[64]{0:T(128)S(1)} %bitcast_add_fusion.1), channel_id=1, source_target_pairs={{0,1},{1,2},{2,3},{3,0},{4,5},{5,6},{6,7},{7,4},{8,9},{9,10},{10,1... | collective-permute-start | bytes 776 | tf_op jit(solution)/shard_map/ppermute | solution.py:185
  127.2 4.4 %collective-permute-start.19 = (f32[64]{0:T(128)S(1)}, f32[64]{0:T(128)S(1)}, u32[]{:S(2)}, u32[]{:S(2)}) collective-permute-start(f32[64]{0:T(128)S(1)} %bitcast_add_fusion.1), channel_id=1, source_target_pairs={{0,2},{1,3},{2,0},{3,1},{4,6},{5,7},{6,4},{7,5},{8,10},{9,11},{10,... | collective-permute-start | bytes 776 | tf_op jit(solution)/shard_map/ppermute | solution.py:185
  129.3 3.5 %collective-permute-start.20 = (f32[64]{0:T(128)S(1)}, f32[64]{0:T(128)S(1)}, u32[]{:S(2)}, u32[]{:S(2)}) collective-permute-start(f32[64]{0:T(128)S(1)} %bitcast_add_fusion.1), channel_id=1, source_target_pairs={{0,3},{1,0},{2,1},{3,2},{4,7},{5,4},{6,5},{7,6},{8,11},{9,8},{10,9... | collective-permute-start | bytes 776 | tf_op jit(solution)/shard_map/ppermute | solution.py:185
  135.7 10.4 %collective-permute-start.21 = (bf16[2,32,1024]{2,1,0:T(8,128)(2,1)S(1)}, bf16[2,32,1024]{2,1,0:T(8,128)(2,1)S(1)}, u32[]{:S(2)}, u32[]{:S(2)}) collective-permute-start(bf16[2,32,1024]{2,1,0:T(8,128)(2,1)S(1)} %get-tuple-element.48), channel_id=1, source_target_pairs={{0,1},{1,2},{2,3},{3,0},{4,5},{5,6},{6,7},{7,4},{8,9},{9,10},{10,1... | collective-permute-start | bytes 393224 | tf_op jit(solution)/shard_map/ppermute | solution.py:185
  135.7 11.8 %collective-permute-start.22 = (bf16[2,32,1024]{2,1,0:T(8,128)(2,1)S(1)}, bf16[2,32,1024]{2,1,0:T(8,128)(2,1)S(1)}, u32[]{:S(2)}, u32[]{:S(2)}) collective-permute-start(bf16[2,32,1024]{2,1,0:T(8,128)(2,1)S(1)} %get-tuple-element.47), channel_id=1, source_target_pairs={{0,2},{1,3},{2,0},{3,1},{4,6},{5,7},{6,4},{7,5},{8,10},{9,11},{10,... | collective-permute-start | bytes 393224 | tf_op jit(solution)/shard_map/ppermute | solution.py:185
  138.4 9.2 %collective-permute-start.23 = (bf16[2,32,1024]{2,1,0:T(8,128)(2,1)S(1)}, bf16[2,32,1024]{2,1,0:T(8,128)(2,1)S(1)}, u32[]{:S(2)}, u32[]{:S(2)}) collective-permute-start(bf16[2,32,1024]{2,1,0:T(8,128)(2,1)S(1)} %get-tuple-element.46), channel_id=1, source_target_pairs={{0,3},{1,0},{2,1},{3,2},{4,7},{5,4},{6,5},{7,6},{8,11},{9,8},{10,9... | collective-permute-start | bytes 393224 | tf_op jit(solution)/shard_map/ppermute | solution.py:185
  140.5 0.8 copy-start.7
  146.2 1.4 copy-start.11
  147.6 0.6 copy-start.12
  147.6 0.7 copy-start.13

commit v7 on v6

--- a/solution.py
+++ b/solution.py
@@ -229,7 +229,6 @@
         return lax.dynamic_index_in_dim(proj_parts, index, 1, False).reshape(owned, depth)
 
     send = [owner_block((j + shift) % hids).astype(BF16) for shift in range(1, hids)]
-    send = [after(p, *head_got[1:]) for p in send]
     received = [along_hid(send[shift - 1], shift) for shift in range(1, hids)]
 
     ids = after(codebook_ids, *send)

time: 153 us -> 154 us (level)
  waiting for transfers between devices: 61.4 us -> 63.2 us
    ppermute x15, waiting for transfers between devices: 47.2 us -> 48.8 us  [along_hid(): lax.ppermute(values, 'hid', [(a, (a + shift) % hids) for a in range(hids)])]
  transfers between devices with their start and end apart: 27 -> 27, of which waited for: 15 -> 14; matrix products, arithmetic and copies ran while one was open for 14% -> 14% of each run, Pallas kernels for 8% -> 8%
where the time goes in v7:
time: 154 us; the launch traced here: 153 us
  waiting for transfers between devices  63.2 us (41%)
  starting transfers between devices  41.9 us (27%)
  local copies, waits for them, and re-layouts  18.8 us (12%)
  Pallas kernels  12.7 us (8%)
  other arithmetic  8.31 us (5%)
  matrix products  6.99 us (5%)
    ppermute x15, waiting for transfers between devices, along_hid(): lax.ppermute(values, 'hid', [(a, (a + shift) % hids) for a in range(hids)])  48.8 us
    ppermute x15, starting transfers between devices, along_hid(): lax.ppermute(values, 'hid', [(a, (a + shift) % hids) for a in range(hids)])  26.2 us
    ppermute x4, waiting for transfers between devices, turn_hid(): lax.ppermute(values, 'hid', [(a, a - a % halves + (a % halves + shift) %...  13.5 us
    pallas_call x3, Pallas kernels, call(): pl.pallas_call(kernel, grid_spec=pltpu.PrefetchScalarGridSpec(num_scalar_...  12.7 us
    dot_general x5, matrix products, matmul(): lax.dot_general(a, b, (contract, ((), ())), preferred_element_type=F32)  6.99 us
    unnamed x46, local copies, waits for them, and re-layouts  6.61 us
    all_to_all x1, starting transfers between devices, shards(): part_out = lax.all_to_all(part_out, 'seq', 0, 0)  4.34 us
    all_to_all x1, starting transfers between devices, shards(): lax.all_to_all(share.reshape(seqs, depth // seqs, units), 'seq', 0, 0)  4 us
  transfers between devices with their start and end apart: 27, of which 14 were waited for; matrix products, arithmetic and copies ran while one was open for 14% of the time, Pallas kernels for 8%

profile of v7, /device:TPU:0, one launch (start us, length us, event | category | flops | bytes accessed | tf_op | source)
XLA Modules:
  0.0 153.0 jit_solution(3154551441826237818)
XLA Ops:
  0.7 1.3 multiply_reduce_fusion
  2.0 1.1 reshape.276
  3.9 5.1 %collective-permute-start.2 = (bf16[72,1024]{1,0:T(8,128)(2,1)S(1)}, bf16[72,1024]{1,0:T(8,128)(2,1)S(1)}, u32[]{:S(2)}, u32[]{:S(2)}) collective-permute-start(bf16[72,1024]{1,0:T(8,128)(2,1)S(1)} %get-tuple-element.47), channel_id=1, source_target_pairs={{0,3},{1,0},{2,1},{3,2},{4,7},{5,4},{6,5},{7,6},{8,11},{9,8},{10,9... | collective-permute-start | bytes 442376 | tf_op jit(solution)/shard_map/ppermute | solution.py:185
  9.0 1.0 collective-permute-start
  10.0 3.3 %collective-permute-done.2 = bf16[72,1024]{1,0:T(8,128)(2,1)S(1)} collective-permute-done((bf16[72,1024]{1,0:T(8,128)(2,1)S(1)}, bf16[72,1024]{1,0:T(8,128)(2,1)S(1)}, u32[]{:S(2)}, u32[]{:S(2)}) %collective-permute-start.2) | collective-permute-done | bytes 147488 | tf_op jit(solution)/shard_map/ppermute | solution.py:185
  13.3 8.2 %collective-permute-done.1 = bf16[72,1024]{1,0:T(8,128)(2,1)S(1)} collective-permute-done((bf16[72,1024]{1,0:T(8,128)(2,1)S(1)}, bf16[72,1024]{1,0:T(8,128)(2,1)S(1)}, u32[]{:S(2)}, u32[]{:S(2)}) %collective-permute-start.1) | collective-permute-done | bytes 147488 | tf_op jit(solution)/shard_map/ppermute | solution.py:185
  21.9 2.1 %copy-done.2 = bf16[2,1024,1024]{2,1,0:T(8,128)(2,1)S(1)} copy-done((bf16[2,1024,1024]{2,1,0:T(8,128)(2,1)S(1)}, bf16[2,1024,1024]{2,1,0:T(8,128)(2,1)}, u32[]{:S(2)}) %copy-start.2) | copy-done | bytes 4194328
  24.1 1.3 fusion
  25.4 0.9 dynamic-slice_convert_fusion
  26.4 1.6 %broadcast_in_dim.45 = bf16[4,2,128,1024]{3,2,1,0:T(8,128)(2,1)} broadcast(bf16[2,128,1024]{2,1,0:T(8,128)(2,1)S(1)} %bitcast.141), dimensions={1,2,3} | broadcast | bytes 2621440 | tf_op jit(solution)/shard_map/broadcast_in_dim | solution.py:242
  28.0 4.0 %all-to-all-start = ((bf16[8,128,1024]{2,1,0:T(8,128)(2,1)}), bf16[8,128,1024]{2,1,0:T(8,128)(2,1)S(1)}, u32[]{:S(2)}, u32[]{:S(2)}) async-start(bf16[8,128,1024]{2,1,0:T(8,128)(2,1)} %bitcast.137), calls=%async_computation | async-start | bytes 4194304 | tf_op jit(solution)/shard_map/all_to_all | solution.py:244
  32.2 1.4 collective-permute-start.7
  33.6 1.4 collective-permute-start.6
  35.1 2.0 %collective-permute-start.5 = (bf16[128,1024]{1,0:T(8,128)(2,1)S(1)}, bf16[128,1024]{1,0:T(8,128)(2,1)}, u32[]{:S(2)}, u32[]{:S(2)}) collective-permute-start(bf16[128,1024]{1,0:T(8,128)(2,1)S(1)} %bitcast.150), channel_id=1, source_target_pairs={{0,1},{1,2},{2,3},{3,0},{4,5},{5,6},{6,7},{7,4},{8,9},{9,10},{10,1... | collective-permute-start | bytes 786440 | tf_op jit(solution)/shard_map/ppermute | solution.py:185
  37.0 1.1 constant_dynamic-slice_fusion.6
  38.3 3.8 %gather_fusion = bf16[128,1024]{1,0:T(8,128)(2,1)S(1)} fusion(bf16[2048,1024]{1,0:T(8,128)(2,1)} %bitcast.147, s32[1024]{0:T(1024)S(1)} %pad_clamp_fusion), kind=kCustom, calls=%fused_computation | custom fusion | bytes 524800 | tf_op jit(solution)/shard_map/jit(_take)/gather | solution.py:238
  42.1 17.1 %collective-permute-done.6 = bf16[128,1024]{1,0:T(8,128)(2,1)} collective-permute-done((bf16[128,1024]{1,0:T(8,128)(2,1)S(1)}, bf16[128,1024]{1,0:T(8,128)(2,1)}, u32[]{:S(2)}, u32[]{:S(2)}) %collective-permute-start.6) | collective-permute-done | bytes 262176 | tf_op jit(solution)/shard_map/ppermute | solution.py:185
  59.1 1.4 multiply_reduce_fusion.4
  60.9 2.0 %collective-permute-start.11 = (s32[2,128]{1,0:T(2,128)S(1)}, s32[2,128]{1,0:T(2,128)S(1)}, u32[]{:S(2)}, u32[]{:S(2)}) collective-permute-start(s32[2,128]{1,0:T(2,128)S(1)} %pad_add_fusion), channel_id=1, source_target_pairs={{0,1},{1,0},{2,3},{3,2},{4,5},{5,4},{6,7},{7,6},{8,9},{9,8},{10,11... | collective-permute-start | bytes 3080 | tf_op jit(solution)/shard_map/ppermute | solution.py:188
  63.0 6.2 %collective-permute-done.11 = s32[2,128]{1,0:T(2,128)S(1)} collective-permute-done((s32[2,128]{1,0:T(2,128)S(1)}, s32[2,128]{1,0:T(2,128)S(1)}, u32[]{:S(2)}, u32[]{:S(2)}) %collective-permute-start.11) | collective-permute-done | bytes 1056 | tf_op jit(solution)/shard_map/ppermute | solution.py:188
  69.1 0.8 fusion.42
  70.6 3.3 %collective-permute-done.10 = f32[2,2,128]{2,1,0:T(2,128)S(1)} collective-permute-done((f32[2,2,128]{2,1,0:T(2,128)S(1)}, f32[2,2,128]{2,1,0:T(2,128)S(1)}, u32[]{:S(2)}, u32[]{:S(2)}) %collective-permute-start.10) | collective-permute-done | bytes 2080 | tf_op jit(solution)/shard_map/ppermute | solution.py:188
  74.4 0.8 convolution_convert_fusion.1
  75.6 2.1 %convolution_convert_fusion = bf16[1024,1024]{1,0:T(8,128)(2,1)} fusion(bf16[256,1024]{1,0:T(8,128)(2,1)S(1)} %multiply_convert_fusion, bf16[128,1024]{1,0:T(8,128)(2,1)S(1)} %copy-done.9, bf16[128,1024]{1,0:T(8,128)(2,1)S(1)} %copy-done.4), kind=kOutput, calls=%fused_computation.5 | convolution fusion | flops 538968064 | bytes 3145728 | tf_op jit(solution)/shard_map/dot_general | solution.py:17
  77.7 4.1 %collective-permute-done.12 = bf16[128,1024]{1,0:T(8,128)(2,1)} collective-permute-done((bf16[128,1024]{1,0:T(8,128)(2,1)S(1)}, bf16[128,1024]{1,0:T(8,128)(2,1)}, u32[]{:S(2)}, u32[]{:S(2)}) %collective-permute-start.12) | collective-permute-done | bytes 262176 | tf_op jit(solution)/shard_map/ppermute | solution.py:188
  81.8 4.3 %all-to-all-start.2 = ((bf16[8,128,1024]{2,1,0:T(8,128)(2,1)}), bf16[8,128,1024]{2,1,0:T(8,128)(2,1)}, u32[]{:S(2)}, u32[]{:S(2)}) async-start(bf16[8,128,1024]{2,1,0:T(8,128)(2,1)} %bitcast.139), calls=%async_computation.2 | async-start | bytes 4194304 | tf_op jit(solution)/shard_map/all_to_all | solution.py:291
  86.1 2.0 %multiply_reduce_fusion.2 = (f32[128]{0:T(128)S(1)}, f32[128]{0:T(128)S(1)}, f32[128]{0:T(128)S(1)}, f32[128,1024]{1,0:T(8,128)S(1)}) fusion(f32[128,1024]{1,0:T(8,128)S(1)} %get-tuple-element.36, bf16[128,1024]{1,0:T(8,128)(2,1)} %collective-permute-done.12, f32[1024]{0:T(1024)S(1)} %bitcast.153, bf16[128,1024]{1,0:T(8,128)(2,1)S(1)} %gather_fusion, ...), kind=kOutput, calls=%fused_computation.16 | convolution fusion | flops 270270080 | bytes 3938433 | tf_op jit(solution)/shard_map/dot_general | solution.py:17
  88.2 1.2 subtract_convert_fusion.refs_0_
  89.8 1.6 %collective-permute-start.14 = (bf16[128,1024]{1,0:T(8,128)(2,1)S(1)}, bf16[128,1024]{1,0:T(8,128)(2,1)S(1)}, u32[]{:S(2)}, u32[]{:S(2)}) collective-permute-start(bf16[128,1024]{1,0:T(8,128)(2,1)S(1)} %subtract_convert_fusion.refs_0_), channel_id=1, source_target_pairs={{0,2},{1,3},{2,0},{3,1},{4,6},{5,7},{6,4},{7,5},{8,10},{9,11},{10,... | collective-permute-start | bytes 786440 | tf_op jit(solution)/shard_map/ppermute | solution.py:185
  91.3 2.5 %collective-permute-start.15 = (bf16[128,1024]{1,0:T(8,128)(2,1)S(1)}, bf16[128,1024]{1,0:T(8,128)(2,1)S(1)}, u32[]{:S(2)}, u32[]{:S(2)}) collective-permute-start(bf16[128,1024]{1,0:T(8,128)(2,1)S(1)} %subtract_convert_fusion.refs_0_), channel_id=1, source_target_pairs={{0,3},{1,0},{2,1},{3,2},{4,7},{5,4},{6,5},{7,6},{8,11},{9,8},{10,9... | collective-permute-start | bytes 786440 | tf_op jit(solution)/shard_map/ppermute | solution.py:185
  94.5 0.9 copy.39.refs_6_
  95.4 5.2 %collective-permute-done.13.refs_1_ = bf16[128,1024]{1,0:T(8,128)(2,1)S(1)} collective-permute-done((bf16[128,1024]{1,0:T(8,128)(2,1)S(1)}, bf16[128,1024]{1,0:T(8,128)(2,1)S(1)}, u32[]{:S(2)}, u32[]{:S(2)}) %collective-permute-start.13) | collective-permute-done | bytes 262176 | tf_op jit(solution)/shard_map/ppermute | solution.py:185
  100.5 10.6 %collective-permute-done.14.refs_2_ = bf16[128,1024]{1,0:T(8,128)(2,1)S(1)} collective-permute-done((bf16[128,1024]{1,0:T(8,128)(2,1)S(1)}, bf16[128,1024]{1,0:T(8,128)(2,1)S(1)}, u32[]{:S(2)}, u32[]{:S(2)}) %collective-permute-start.14) | collective-permute-done | bytes 262176 | tf_op jit(solution)/shard_map/ppermute | solution.py:185
  112.5 5.1 %shard_map.85 = (bf16[1024,1024]{1,0:T(8,128)(2,1)}, bf16[256,1024]{1,0:T(8,128)(2,1)}, bf16[256,1024]{1,0:T(8,128)(2,1)}) custom-call(s32[2]{0:T(128)} %pad_add_fusion.2.place_ref, bf16[128,1024]{1,0:T(8,128)(2,1)} %copy-done.10, bf16[128,1024]{1,0:T(8,128)(2,1)} %copy-done.15, bf16[128,1024]{1,0:T(8,128)(2,1)} %copy-done.16, bf16[128,1024]{1,0:T(8,128)(2,1)} %copy-done.17, ...), custom_call_target="tpu_custom_call" | custom-call | flops 1073741824 | bytes 2099200 | tf_op jit(solution)/shard_map/pallas_call | solution.py:33
  117.6 4.0 %all-to-all-start.1 = ((bf16[8,128,1024]{2,1,0:T(8,128)(2,1)}), bf16[8,128,1024]{2,1,0:T(8,128)(2,1)S(1)}, u32[]{:S(2)}, u32[]{:S(2)}) async-start(bf16[8,128,1024]{2,1,0:T(8,128)(2,1)} %bitcast.142), calls=%async_computation.1 | async-start | bytes 4194304 | tf_op jit(solution)/shard_map/all_to_all | solution.py:303
  122.3 0.8 collective-permute-done.17
  123.1 4.6 %collective-permute-start.18 = (f32[64]{0:T(128)S(1)}, f32[64]{0:T(128)S(1)}, u32[]{:S(2)}, u32[]{:S(2)}) collective-permute-start(f32[64]{0:T(128)S(1)} %bitcast_add_fusion.1), channel_id=1, source_target_pairs={{0,1},{1,2},{2,3},{3,0},{4,5},{5,6},{6,7},{7,4},{8,9},{9,10},{10,1... | collective-permute-start | bytes 776 | tf_op jit(solution)/shard_map/ppermute | solution.py:185
  127.6 2.0 %collective-permute-start.19 = (f32[64]{0:T(128)S(1)}, f32[64]{0:T(128)S(1)}, u32[]{:S(2)}, u32[]{:S(2)}) collective-permute-start(f32[64]{0:T(128)S(1)} %bitcast_add_fusion.1), channel_id=1, source_target_pairs={{0,2},{1,3},{2,0},{3,1},{4,6},{5,7},{6,4},{7,5},{8,10},{9,11},{10,... | collective-permute-start | bytes 776 | tf_op jit(solution)/shard_map/ppermute | solution.py:185
  130.6 1.4 collective-permute-done.19
  132.1 1.1 collective-permute-done.20
  133.3 2.0 %reduce_sum.108 = bf16[2,4,32,1024]{3,2,1,0:T(8,128)(2,1)S(1)} reduce(bf16[4,2,4,32,1024]{4,3,2,1,0:T(8,128)(2,1)} %bitcast.57, bf16[]{:T(256)} %constant.168.clone.1), dimensions={0}, to_apply=%region_10.11 | reduce | flops 786432 | bytes 2621442 | tf_op jit(solution)/shard_map/reduce_sum | solution.py:292
  136.1 2.7 %collective-permute-start.22 = (bf16[2,32,1024]{2,1,0:T(8,128)(2,1)S(1)}, bf16[2,32,1024]{2,1,0:T(8,128)(2,1)S(1)}, u32[]{:S(2)}, u32[]{:S(2)}) collective-permute-start(bf16[2,32,1024]{2,1,0:T(8,128)(2,1)S(1)} %get-tuple-element.41), channel_id=1, source_target_pairs={{0,2},{1,3},{2,0},{3,1},{4,6},{5,7},{6,4},{7,5},{8,10},{9,11},{10,... | collective-permute-start | bytes 393224 | tf_op jit(solution)/shard_map/ppermute | solution.py:185
  138.8 1.1 collective-permute-start.23
  139.9 0.9 copy.40.refs_4_
  141.6 4.9 %shard_map.86 = bf16[256,1024]{1,0:T(8,128)(2,1)} custom-call(s32[2]{0:T(128)} %pad_add_fusion.2.place_ref, bf16[256,1024]{1,0:T(8,128)(2,1)} %get-tuple-element.14.refs_0_, bf16[256,1024]{1,0:T(8,128)(2,1)} %copy-done.7, bf16[2,1024,1024]{2,1,0:T(8,128)(2,1)} %refs_2_.1, bf16[256,1024]{1,0:T(8,128)(2,1)} %refs_3_.1, f32[2,256,1]{2,1,0:T(8,128)} %copy.40.refs_4_), custom_call_target="tpu_custom_call" | custom-call | flops 1073741824 | bytes 5769216 | tf_op jit(solution)/shard_map/pallas_call | solution.py:33
  146.5 1.4 collective-permute-done.22.refs_2_
  148.6 2.7 %shard_map.87 = f32[32,2,2048]{2,1,0:T(2,128)} custom-call(s32[2]{0:T(128)} %pad_add_fusion.2.place_ref, bf16[2,32,1024]{2,1,0:T(8,128)(2,1)} %get-tuple-element.43.refs_0_, bf16[2,32,1024]{2,1,0:T(8,128)(2,1)} %copy-done.11, bf16[2,32,1024]{2,1,0:T(8,128)(2,1)} %copy-done.12, bf16[2,32,1024]{2,1,0:T(8,128)(2,1)} %copy-done.13), custom_call_target="tpu_custom_call" | custom-call | flops 262144 | bytes 524288 | tf_op jit(solution)/shard_map/pallas_call | solution.py:33
  151.7 1.3 copy.41
  (122 shorter events, 10.3 us)
Async XLA Ops:
  0.6 31.3 %copy-start = (f32[2,1024]{1,0:T(2,128)S(1)}, f32[2,1024]{1,0:T(2,128)}, u32[]{:S(2)}) copy-start(f32[2,1024]{1,0:T(2,128)} %param.9) | copy-start | bytes 24580
  0.6 9.4 %copy-start.1 = (bf16[256,1024]{1,0:T(8,128)(2,1)S(1)}, bf16[256,1024]{1,0:T(8,128)(2,1)}, u32[]{:S(2)}) copy-start(bf16[256,1024]{1,0:T(8,128)(2,1)} %refs_3_.1) | copy-start | bytes 1572868
  3.9 9.4 %collective-permute-start.2 = (bf16[72,1024]{1,0:T(8,128)(2,1)S(1)}, bf16[72,1024]{1,0:T(8,128)(2,1)S(1)}, u32[]{:S(2)}, u32[]{:S(2)}) collective-permute-start(bf16[72,1024]{1,0:T(8,128)(2,1)S(1)} %get-tuple-element.47), channel_id=1, source_target_pairs={{0,3},{1,0},{2,1},{3,2},{4,7},{5,4},{6,5},{7,6},{8,11},{9,8},{10,9... | collective-permute-start | bytes 442376 | tf_op jit(solution)/shard_map/ppermute | solution.py:185
  9.0 12.5 %collective-permute-start.1 = (bf16[72,1024]{1,0:T(8,128)(2,1)S(1)}, bf16[72,1024]{1,0:T(8,128)(2,1)S(1)}, u32[]{:S(2)}, u32[]{:S(2)}) collective-permute-start(bf16[72,1024]{1,0:T(8,128)(2,1)S(1)} %get-tuple-element.46), channel_id=1, source_target_pairs={{0,2},{1,3},{2,0},{3,1},{4,6},{5,7},{6,4},{7,5},{8,10},{9,11},{10,... | collective-permute-start | bytes 442376 | tf_op jit(solution)/shard_map/ppermute | solution.py:185
  9.0 12.5 %collective-permute-start = (bf16[72,1024]{1,0:T(8,128)(2,1)S(1)}, bf16[72,1024]{1,0:T(8,128)(2,1)S(1)}, u32[]{:S(2)}, u32[]{:S(2)}) collective-permute-start(bf16[72,1024]{1,0:T(8,128)(2,1)S(1)} %get-tuple-element.47), channel_id=1, source_target_pairs={{0,1},{1,2},{2,3},{3,0},{4,5},{5,6},{6,7},{7,4},{8,9},{9,10},{10,1... | collective-permute-start | bytes 442376 | tf_op jit(solution)/shard_map/ppermute | solution.py:185
  10.0 11.8 %collective-permute-start.4 = (bf16[256,1024]{1,0:T(8,128)(2,1)S(1)}, bf16[256,1024]{1,0:T(8,128)(2,1)S(1)}, u32[]{:S(2)}, u32[]{:S(2)}) collective-permute-start(bf16[256,1024]{1,0:T(8,128)(2,1)S(1)} %copy-done.1), channel_id=1, source_target_pairs={{0,4},{4,0},{8,12},{12,8},{16,20},{20,16},{24,28},{28,24},{1,5},{5... | collective-permute-start | bytes 1572872 | tf_op jit(solution)/shard_map/ppermute | solution.py:195
  21.6 10.5 %collective-permute-start.3 = (f32[256]{0:T(256)S(1)}, f32[256]{0:T(256)S(1)}, u32[]{:S(2)}, u32[]{:S(2)}) collective-permute-start(f32[256]{0:T(256)S(1)} %slice_reduce_fusion), channel_id=1, source_target_pairs={{0,4},{4,0},{8,12},{12,8},{16,20},{20,16},{24,28},{28,24},{1,5},{5... | collective-permute-start | bytes 3080 | tf_op jit(solution)/shard_map/ppermute | solution.py:195
  21.7 2.4 %copy-start.2 = (bf16[2,1024,1024]{2,1,0:T(8,128)(2,1)S(1)}, bf16[2,1024,1024]{2,1,0:T(8,128)(2,1)}, u32[]{:S(2)}) copy-start(bf16[2,1024,1024]{2,1,0:T(8,128)(2,1)} %refs_2_.1) | copy-start | bytes 12582916
  21.9 3.5 %copy-start.6 = (bf16[256,1024]{1,0:T(8,128)(2,1)}, bf16[256,1024]{1,0:T(8,128)(2,1)S(1)}, u32[]{:S(2)}) copy-start(bf16[256,1024]{1,0:T(8,128)(2,1)S(1)} %collective-permute-done.4.refs_5_) | copy-start | bytes 1572868
  25.4 2.6 %copy-start.5 = (f32[2,4,64,1024]{3,2,1,0:T(8,128)}, f32[2,4,64,1024]{3,2,1,0:T(8,128)S(1)}, u32[]{:S(2)}) copy-start(f32[2,4,64,1024]{3,2,1,0:T(8,128)S(1)} %fusion) | copy-start | bytes 6291460
  28.0 9.1 %copy-start.14 = (s32[2,64]{1,0:T(2,128)S(1)}, s32[2,64]{1,0:T(2,128)}, u32[]{:S(2)}) copy-start(s32[2,64]{1,0:T(2,128)} %param.11) | copy-start | bytes 1540
  28.0 41.2 %all-to-all-start = ((bf16[8,128,1024]{2,1,0:T(8,128)(2,1)}), bf16[8,128,1024]{2,1,0:T(8,128)(2,1)S(1)}, u32[]{:S(2)}, u32[]{:S(2)}) async-start(bf16[8,128,1024]{2,1,0:T(8,128)(2,1)} %bitcast.137), calls=%async_computation | async-start | bytes 4194304 | tf_op jit(solution)/shard_map/all_to_all | solution.py:244
  32.2 9.9 %collective-permute-start.7 = (bf16[128,1024]{1,0:T(8,128)(2,1)}, bf16[128,1024]{1,0:T(8,128)(2,1)}, u32[]{:S(2)}, u32[]{:S(2)}) collective-permute-start(bf16[128,1024]{1,0:T(8,128)(2,1)} %bitcast.13), channel_id=1, source_target_pairs={{0,3},{1,0},{2,1},{3,2},{4,7},{5,4},{6,5},{7,6},{8,11},{9,8},{10,9... | collective-permute-start | bytes 786440 | tf_op jit(solution)/shard_map/ppermute | solution.py:185
  33.6 25.5 %collective-permute-start.6 = (bf16[128,1024]{1,0:T(8,128)(2,1)S(1)}, bf16[128,1024]{1,0:T(8,128)(2,1)}, u32[]{:S(2)}, u32[]{:S(2)}) collective-permute-start(bf16[128,1024]{1,0:T(8,128)(2,1)S(1)} %bitcast.151), channel_id=1, source_target_pairs={{0,2},{1,3},{2,0},{3,1},{4,6},{5,7},{6,4},{7,5},{8,10},{9,11},{10,... | collective-permute-start | bytes 786440 | tf_op jit(solution)/shard_map/ppermute | solution.py:185
  35.1 24.1 %collective-permute-start.5 = (bf16[128,1024]{1,0:T(8,128)(2,1)S(1)}, bf16[128,1024]{1,0:T(8,128)(2,1)}, u32[]{:S(2)}, u32[]{:S(2)}) collective-permute-start(bf16[128,1024]{1,0:T(8,128)(2,1)S(1)} %bitcast.150), channel_id=1, source_target_pairs={{0,1},{1,2},{2,3},{3,0},{4,5},{5,6},{6,7},{7,4},{8,9},{9,10},{10,1... | collective-permute-start | bytes 786440 | tf_op jit(solution)/shard_map/ppermute | solution.py:185
  37.0 1.1 collective-permute-start.8
  60.8 9.4 %copy-start.3 = (bf16[128,1024]{1,0:T(8,128)(2,1)}, bf16[128,1024]{1,0:T(8,128)(2,1)S(1)}, u32[]{:S(2)}) copy-start(bf16[128,1024]{1,0:T(8,128)(2,1)S(1)} %multiply_convert_fusion.1) | copy-start | bytes 786436
  60.8 8.3 %collective-permute-start.9 = (bf16[128,1024]{1,0:T(8,128)(2,1)S(1)}, bf16[128,1024]{1,0:T(8,128)(2,1)S(1)}, u32[]{:S(2)}, u32[]{:S(2)}) collective-permute-start(bf16[128,1024]{1,0:T(8,128)(2,1)S(1)} %multiply_convert_fusion.1), channel_id=1, source_target_pairs={{0,1},{1,0},{2,3},{3,2},{4,5},{5,4},{6,7},{7,6},{8,9},{9,8},{10,11... | collective-permute-start | bytes 786440 | tf_op jit(solution)/shard_map/ppermute | solution.py:188
  60.9 8.2 %collective-permute-start.11 = (s32[2,128]{1,0:T(2,128)S(1)}, s32[2,128]{1,0:T(2,128)S(1)}, u32[]{:S(2)}, u32[]{:S(2)}) collective-permute-start(s32[2,128]{1,0:T(2,128)S(1)} %pad_add_fusion), channel_id=1, source_target_pairs={{0,1},{1,0},{2,3},{3,2},{4,5},{5,4},{6,7},{7,6},{8,9},{9,8},{10,11... | collective-permute-start | bytes 3080 | tf_op jit(solution)/shard_map/ppermute | solution.py:188
  69.1 1.2 copy-start.8
  70.3 3.7 %collective-permute-start.10 = (f32[2,2,128]{2,1,0:T(2,128)S(1)}, f32[2,2,128]{2,1,0:T(2,128)S(1)}, u32[]{:S(2)}, u32[]{:S(2)}) collective-permute-start(f32[2,2,128]{2,1,0:T(2,128)S(1)} %pad_maximum_fusion.6), channel_id=1, source_target_pairs={{0,1},{1,0},{2,3},{3,2},{4,5},{5,4},{6,7},{7,6},{8,9},{9,8},{10,11... | collective-permute-start | bytes 6152 | tf_op jit(solution)/shard_map/ppermute | solution.py:188
  74.0 1.6 %copy-start.4 = (bf16[128,1024]{1,0:T(8,128)(2,1)S(1)}, bf16[128,1024]{1,0:T(8,128)(2,1)}, u32[]{:S(2)}) copy-start(bf16[128,1024]{1,0:T(8,128)(2,1)} %copy-done.3) | copy-start | bytes 786436
  74.0 1.6 %copy-start.9 = (bf16[128,1024]{1,0:T(8,128)(2,1)S(1)}, bf16[128,1024]{1,0:T(8,128)(2,1)}, u32[]{:S(2)}) copy-start(bf16[128,1024]{1,0:T(8,128)(2,1)} %copy-done.8) | copy-start | bytes 786436
  75.2 6.5 %collective-permute-start.12 = (bf16[128,1024]{1,0:T(8,128)(2,1)S(1)}, bf16[128,1024]{1,0:T(8,128)(2,1)}, u32[]{:S(2)}, u32[]{:S(2)}) collective-permute-start(bf16[128,1024]{1,0:T(8,128)(2,1)S(1)} %convolution_convert_fusion.1), channel_id=1, source_target_pairs={{0,1},{1,0},{2,3},{3,2},{4,5},{5,4},{6,7},{7,6},{8,9},{9,8},{10,11... | collective-permute-start | bytes 786440 | tf_op jit(solution)/shard_map/ppermute | solution.py:188
  81.8 35.8 %all-to-all-start.2 = ((bf16[8,128,1024]{2,1,0:T(8,128)(2,1)}), bf16[8,128,1024]{2,1,0:T(8,128)(2,1)}, u32[]{:S(2)}, u32[]{:S(2)}) async-start(bf16[8,128,1024]{2,1,0:T(8,128)(2,1)} %bitcast.139), calls=%async_computation.2 | async-start | bytes 4194304 | tf_op jit(solution)/shard_map/all_to_all | solution.py:291
  89.4 21.7 %copy-start.10 = (bf16[128,1024]{1,0:T(8,128)(2,1)}, bf16[128,1024]{1,0:T(8,128)(2,1)S(1)}, u32[]{:S(2)}) copy-start(bf16[128,1024]{1,0:T(8,128)(2,1)S(1)} %subtract_convert_fusion.refs_0_) | copy-start | bytes 786436
  89.4 11.1 %collective-permute-start.13 = (bf16[128,1024]{1,0:T(8,128)(2,1)S(1)}, bf16[128,1024]{1,0:T(8,128)(2,1)S(1)}, u32[]{:S(2)}, u32[]{:S(2)}) collective-permute-start(bf16[128,1024]{1,0:T(8,128)(2,1)S(1)} %subtract_convert_fusion.refs_0_), channel_id=1, source_target_pairs={{0,1},{1,2},{2,3},{3,0},{4,5},{5,6},{6,7},{7,4},{8,9},{9,10},{10,1... | collective-permute-start | bytes 786440 | tf_op jit(solution)/shard_map/ppermute | solution.py:185
  89.8 21.3 %collective-permute-start.14 = (bf16[128,1024]{1,0:T(8,128)(2,1)S(1)}, bf16[128,1024]{1,0:T(8,128)(2,1)S(1)}, u32[]{:S(2)}, u32[]{:S(2)}) collective-permute-start(bf16[128,1024]{1,0:T(8,128)(2,1)S(1)} %subtract_convert_fusion.refs_0_), channel_id=1, source_target_pairs={{0,2},{1,3},{2,0},{3,1},{4,6},{5,7},{6,4},{7,5},{8,10},{9,11},{10,... | collective-permute-start | bytes 786440 | tf_op jit(solution)/shard_map/ppermute | solution.py:185
  91.3 19.8 %collective-permute-start.15 = (bf16[128,1024]{1,0:T(8,128)(2,1)S(1)}, bf16[128,1024]{1,0:T(8,128)(2,1)S(1)}, u32[]{:S(2)}, u32[]{:S(2)}) collective-permute-start(bf16[128,1024]{1,0:T(8,128)(2,1)S(1)} %subtract_convert_fusion.refs_0_), channel_id=1, source_target_pairs={{0,3},{1,0},{2,1},{3,2},{4,7},{5,4},{6,5},{7,6},{8,11},{9,8},{10,9... | collective-permute-start | bytes 786440 | tf_op jit(solution)/shard_map/ppermute | solution.py:185
  100.5 10.6 %copy-start.15 = (bf16[128,1024]{1,0:T(8,128)(2,1)}, bf16[128,1024]{1,0:T(8,128)(2,1)S(1)}, u32[]{:S(2)}) copy-start(bf16[128,1024]{1,0:T(8,128)(2,1)S(1)} %collective-permute-done.13.refs_1_) | copy-start | bytes 786436
  111.1 0.7 copy-start.16
  111.8 0.7 copy-start.17
  117.6 33.7 %all-to-all-start.1 = ((bf16[8,128,1024]{2,1,0:T(8,128)(2,1)}), bf16[8,128,1024]{2,1,0:T(8,128)(2,1)S(1)}, u32[]{:S(2)}, u32[]{:S(2)}) async-start(bf16[8,128,1024]{2,1,0:T(8,128)(2,1)} %bitcast.142), calls=%async_computation.1 | async-start | bytes 4194304 | tf_op jit(solution)/shard_map/all_to_all | solution.py:303
  121.7 1.4 collective-permute-start.17
  122.2 18.6 %collective-permute-start.16 = (bf16[256,1024]{1,0:T(8,128)(2,1)}, bf16[256,1024]{1,0:T(8,128)(2,1)S(1)}, u32[]{:S(2)}, u32[]{:S(2)}) collective-permute-start(bf16[256,1024]{1,0:T(8,128)(2,1)} %get-tuple-element.15), channel_id=1, source_target_pairs={{0,4},{4,0},{8,12},{12,8},{16,20},{20,16},{24,28},{28,24},{1,5},{5... | collective-permute-start | bytes 1572872 | tf_op jit(solution)/shard_map/ppermute | solution.py:195
  123.1 7.5 %collective-permute-start.18 = (f32[64]{0:T(128)S(1)}, f32[64]{0:T(128)S(1)}, u32[]{:S(2)}, u32[]{:S(2)}) collective-permute-start(f32[64]{0:T(128)S(1)} %bitcast_add_fusion.1), channel_id=1, source_target_pairs={{0,1},{1,2},{2,3},{3,0},{4,5},{5,6},{6,7},{7,4},{8,9},{9,10},{10,1... | collective-permute-start | bytes 776 | tf_op jit(solution)/shard_map/ppermute | solution.py:185
  127.6 4.4 %collective-permute-start.19 = (f32[64]{0:T(128)S(1)}, f32[64]{0:T(128)S(1)}, u32[]{:S(2)}, u32[]{:S(2)}) collective-permute-start(f32[64]{0:T(128)S(1)} %bitcast_add_fusion.1), channel_id=1, source_target_pairs={{0,2},{1,3},{2,0},{3,1},{4,6},{5,7},{6,4},{7,5},{8,10},{9,11},{10,... | collective-permute-start | bytes 776 | tf_op jit(solution)/shard_map/ppermute | solution.py:185
  129.6 3.5 %collective-permute-start.20 = (f32[64]{0:T(128)S(1)}, f32[64]{0:T(128)S(1)}, u32[]{:S(2)}, u32[]{:S(2)}) collective-permute-start(f32[64]{0:T(128)S(1)} %bitcast_add_fusion.1), channel_id=1, source_target_pairs={{0,3},{1,0},{2,1},{3,2},{4,7},{5,4},{6,5},{7,6},{8,11},{9,8},{10,9... | collective-permute-start | bytes 776 | tf_op jit(solution)/shard_map/ppermute | solution.py:185
  136.1 10.4 %collective-permute-start.21 = (bf16[2,32,1024]{2,1,0:T(8,128)(2,1)S(1)}, bf16[2,32,1024]{2,1,0:T(8,128)(2,1)S(1)}, u32[]{:S(2)}, u32[]{:S(2)}) collective-permute-start(bf16[2,32,1024]{2,1,0:T(8,128)(2,1)S(1)} %get-tuple-element.42), channel_id=1, source_target_pairs={{0,1},{1,2},{2,3},{3,0},{4,5},{5,6},{6,7},{7,4},{8,9},{9,10},{10,1... | collective-permute-start | bytes 393224 | tf_op jit(solution)/shard_map/ppermute | solution.py:185
  136.1 11.8 %collective-permute-start.22 = (bf16[2,32,1024]{2,1,0:T(8,128)(2,1)S(1)}, bf16[2,32,1024]{2,1,0:T(8,128)(2,1)S(1)}, u32[]{:S(2)}, u32[]{:S(2)}) collective-permute-start(bf16[2,32,1024]{2,1,0:T(8,128)(2,1)S(1)} %get-tuple-element.41), channel_id=1, source_target_pairs={{0,2},{1,3},{2,0},{3,1},{4,6},{5,7},{6,4},{7,5},{8,10},{9,11},{10,... | collective-permute-start | bytes 393224 | tf_op jit(solution)/shard_map/ppermute | solution.py:185
  138.8 9.1 %collective-permute-start.23 = (bf16[2,32,1024]{2,1,0:T(8,128)(2,1)S(1)}, bf16[2,32,1024]{2,1,0:T(8,128)(2,1)S(1)}, u32[]{:S(2)}, u32[]{:S(2)}) collective-permute-start(bf16[2,32,1024]{2,1,0:T(8,128)(2,1)S(1)} %get-tuple-element.40), channel_id=1, source_target_pairs={{0,3},{1,0},{2,1},{3,2},{4,7},{5,4},{6,5},{7,6},{8,11},{9,8},{10,9... | collective-permute-start | bytes 393224 | tf_op jit(solution)/shard_map/ppermute | solution.py:185
  140.8 0.8 copy-start.7
  146.5 1.4 copy-start.11
  147.9 0.6 copy-start.12
  147.9 0.7 copy-start.13

commit v8 on v7

--- a/solution.py
+++ b/solution.py
@@ -215,29 +215,30 @@
         head_send.append(jnp.concatenate([piece, small]))
     head_got = [head_send[0]]
     head_got += [along_hid(head_send[shift % halves], shift) for shift in range(1, hids)]
+    w_own = pick(w_in, step)
+    proj_parts = matmul(jnp.concatenate(group), w_own, ((1,), (0,)))
+    proj_parts = proj_parts.reshape(steps, hids, part, depth)
+
+    def owner_block(index):
+        return lax.dynamic_index_in_dim(proj_parts, index, 1, False).reshape(owned, depth)
+
+    send = [owner_block((j + shift) % hids).astype(BF16) for shift in range(1, hids)]
+    received = [along_hid(send[shift - 1], shift) for shift in range(1, hids)]
+
+    head_got = [head_got[0]] + [after(g, received[0]) for g in head_got[1:]]
     squares = sum(g[steps * head_rows :].astype(F32) for g in head_got).reshape(tail)
     squares = jnp.sum(squares[: EXACT * rows].reshape(EXACT, rows), axis=0)
     head_mid = jnp.stack([g[: steps * head_rows] for g in head_got[::-1]] * 2)
     head_mid = lax.dynamic_slice_in_dim(head_mid, hids - 1 - j, hids, 0)
     head_mid = head_mid.reshape(hids, steps, head_rows, block)
 
-    w_own = pick(w_in, step)
-    proj_parts = matmul(jnp.concatenate(group), w_own, ((1,), (0,)))
-    proj_parts = proj_parts.reshape(steps, hids, part, depth)
-
-    def owner_block(index):
-        return lax.dynamic_index_in_dim(proj_parts, index, 1, False).reshape(owned, depth)
-
-    send = [owner_block((j + shift) % hids).astype(BF16) for shift in range(1, hids)]
-    received = [along_hid(send[shift - 1], shift) for shift in range(1, hids)]
-
     ids = after(codebook_ids, *send)
     ids = jnp.concatenate([ids] + [flip_seq(ids, -m) for m in relations], axis=1)
     ids_rows = [ids] + [turn_hid(ids, -k) for k in range(1, halves)]
     before = jnp.maximum(step - 1, 0)
     looked = jnp.take(pick(embedding, before), pick(ids, before), axis=0)
 
-    head_send = after(head_mid, *send).transpose(1, 0, 2, 3)
+    head_send = head_mid.transpose(1, 0, 2, 3)
     head_send = head_send.reshape(steps, hids * head_rows, block)
     head_send = jnp.broadcast_to(head_send, (groups,) + head_send.shape)
     head_send = head_send.reshape(seqs, hids * head_rows, block)

time: 154 us -> 163 us (1.058)
  starting transfers between devices: 41.9 us -> 68.4 us
  waiting for transfers between devices: 63.2 us -> 39.7 us
  local copies, waits for them, and re-layouts: 18.8 us -> 22.4 us
    ppermute x15, waiting for transfers between devices: 48.8 us -> 26.3 us  [along_hid(): lax.ppermute(values, 'hid', [(a, (a + shift) % hids) for a in range(hids)])]
    ppermute x4, starting transfers between devices: 2.78 us -> 24.2 us  [turn_hid(): lax.ppermute(values, 'hid', [(a, a - a % halves + (a % halves + shift) %...]
    unnamed x46, local copies, waits for them, and re-layouts: 6.61 us -> 11.3 us
    ppermute x15, starting transfers between devices: 26.2 us -> 30.4 us  [along_hid(): lax.ppermute(values, 'hid', [(a, (a + shift) % hids) for a in range(hids)])]
    ppermute x4, waiting for transfers between devices: 13.5 us -> 10.4 us  [turn_hid(): lax.ppermute(values, 'hid', [(a, a - a % halves + (a % halves + shift) %...]
  transfers between devices with their start and end apart: 27 -> 27, of which waited for: 14 -> 14; matrix products, arithmetic and copies ran while one was open for 14% -> 20% of each run, Pallas kernels for 8% -> 8%
where the time goes in v8:
time: 163 us
  starting transfers between devices  68.4 us (42%)
  waiting for transfers between devices  39.7 us (24%)
  local copies, waits for them, and re-layouts  22.4 us (14%)
  Pallas kernels  12.7 us (8%)
  other arithmetic  9.71 us (6%)
  matrix products  8.6 us (5%)
    ppermute x15, starting transfers between devices, along_hid(): lax.ppermute(values, 'hid', [(a, (a + shift) % hids) for a in range(hids)])  30.4 us
    ppermute x15, waiting for transfers between devices, along_hid(): lax.ppermute(values, 'hid', [(a, (a + shift) % hids) for a in range(hids)])  26.3 us
    ppermute x4, starting transfers between devices, turn_hid(): lax.ppermute(values, 'hid', [(a, a - a % halves + (a % halves + shift) %...  24.2 us
    pallas_call x3, Pallas kernels, call(): pl.pallas_call(kernel, grid_spec=pltpu.PrefetchScalarGridSpec(num_scalar_...  12.7 us
    unnamed x46, local copies, waits for them, and re-layouts  11.3 us
    ppermute x4, waiting for transfers between devices, turn_hid(): lax.ppermute(values, 'hid', [(a, a - a % halves + (a % halves + shift) %...  10.4 us
    dot_general x5, matrix products, matmul(): lax.dot_general(a, b, (contract, ((), ())), preferred_element_type=F32)  8.6 us
    all_to_all x1, starting transfers between devices, shards(): part_out = lax.all_to_all(part_out, 'seq', 0, 0)  4.34 us
  transfers between devices with their start and end apart: 27, of which 14 were waited for; matrix products, arithmetic and copies ran while one was open for 20% of the time, Pallas kernels for 8%

profile of v8, /device:TPU:0, one launch (start us, length us, event | category | flops | bytes accessed | tf_op | source)
XLA Modules:
  0.0 162.6 jit_solution(5571660957101459824)
XLA Ops:
  1.2 1.2 multiply_reduce_fusion
  2.5 1.1 reshape.276
  5.1 4.7 %collective-permute-start.4 = (bf16[72,1024]{1,0:T(8,128)(2,1)}, bf16[72,1024]{1,0:T(8,128)(2,1)}, u32[]{:S(2)}, u32[]{:S(2)}) collective-permute-start(bf16[72,1024]{1,0:T(8,128)(2,1)} %get-tuple-element.51), channel_id=1, source_target_pairs={{0,3},{1,0},{2,1},{3,2},{4,7},{5,4},{6,5},{7,6},{8,11},{9,8},{10,9... | collective-permute-start | bytes 442376 | tf_op jit(solution)/shard_map/ppermute | solution.py:185
  9.8 1.0 collective-permute-start.3
  11.6 2.9 %fusion = f32[2,4,64,1024]{3,2,1,0:T(8,128)S(1)} fusion(bf16[2,4,64,1024]{3,2,1,0:T(8,128)(2,1)S(1)} %bitcast.140, bf16[2,1024,1024]{2,1,0:T(8,128)(2,1)} %refs_2_.1, s32[]{:T(128)S(6)} %select_n.139), kind=kOutput, calls=%fused_computation.2 | convolution fusion | flops 1073741824 | bytes 5242884 | tf_op jit(solution)/shard_map/dot_general | solution.py:17
  14.4 0.9 dynamic-slice_convert_fusion
  15.4 3.4 %collective-permute-start.2 = (bf16[128,1024]{1,0:T(8,128)(2,1)S(1)}, bf16[128,1024]{1,0:T(8,128)(2,1)S(1)}, u32[]{:S(2)}, u32[]{:S(2)}) collective-permute-start(bf16[128,1024]{1,0:T(8,128)(2,1)S(1)} %bitcast.142), channel_id=1, source_target_pairs={{0,1},{1,2},{2,3},{3,0},{4,5},{5,6},{6,7},{7,4},{8,9},{9,10},{10,1... | collective-permute-start | bytes 786440 | tf_op jit(solution)/shard_map/ppermute | solution.py:185
  18.9 1.1 collective-permute-done.8
  20.5 1.0 collective-permute-start.6
  21.5 5.9 %collective-permute-done.2 = bf16[128,1024]{1,0:T(8,128)(2,1)S(1)} collective-permute-done((bf16[128,1024]{1,0:T(8,128)(2,1)S(1)}, bf16[128,1024]{1,0:T(8,128)(2,1)S(1)}, u32[]{:S(2)}, u32[]{:S(2)}) %collective-permute-start.2) | collective-permute-done | bytes 262176 | tf_op jit(solution)/shard_map/ppermute | solution.py:185
  27.4 2.3 %collective-permute-done.3 = bf16[72,1024]{1,0:T(8,128)(2,1)} collective-permute-done((bf16[72,1024]{1,0:T(8,128)(2,1)}, bf16[72,1024]{1,0:T(8,128)(2,1)}, u32[]{:S(2)}, u32[]{:S(2)}) %collective-permute-start.3) | collective-permute-done | bytes 147488 | tf_op jit(solution)/shard_map/ppermute | solution.py:185
  30.6 0.9 bitcast_dynamic-update-slice_fusion.2
  32.4 0.9 bitcast_dynamic-update-slice_fusion.5
  33.3 0.9 bitcast_dynamic-update-slice_fusion.3
  34.3 0.9 bitcast_dynamic-update-slice_fusion.1
  35.3 1.6 broadcast_in_dim.45
  36.9 3.7 %all-to-all-start = ((bf16[8,128,1024]{2,1,0:T(8,128)(2,1)}), bf16[8,128,1024]{2,1,0:T(8,128)(2,1)S(1)}, u32[]{:S(2)}, u32[]{:S(2)}) async-start(bf16[8,128,1024]{2,1,0:T(8,128)(2,1)} %bitcast.129), calls=%async_computation | async-start | bytes 4194304 | tf_op jit(solution)/shard_map/all_to_all | solution.py:245
  42.0 3.8 %gather_fusion = bf16[128,1024]{1,0:T(8,128)(2,1)S(1)} fusion(bf16[2048,1024]{1,0:T(8,128)(2,1)} %bitcast.139, s32[1024]{0:T(1024)S(1)} %pad_clamp_fusion), kind=kCustom, calls=%fused_computation | custom fusion | bytes 524800 | tf_op jit(solution)/shard_map/jit(_take)/gather | solution.py:239
  46.8 1.4 multiply_reduce_fusion.4
  48.5 11.0 %collective-permute-start.9 = (bf16[128,1024]{1,0:T(8,128)(2,1)S(1)}, bf16[128,1024]{1,0:T(8,128)(2,1)S(1)}, u32[]{:S(2)}, u32[]{:S(2)}) collective-permute-start(bf16[128,1024]{1,0:T(8,128)(2,1)S(1)} %multiply_convert_fusion.1), channel_id=1, source_target_pairs={{0,1},{1,0},{2,3},{3,2},{4,5},{5,4},{6,7},{7,6},{8,9},{9,8},{10,11... | collective-permute-start | bytes 786440 | tf_op jit(solution)/shard_map/ppermute | solution.py:188
  59.6 6.5 %collective-permute-done.11 = s32[2,128]{1,0:T(2,128)S(1)} collective-permute-done((s32[2,128]{1,0:T(2,128)S(1)}, s32[2,128]{1,0:T(2,128)S(1)}, u32[]{:S(2)}, u32[]{:S(2)}) %collective-permute-start.11) | collective-permute-done | bytes 1056 | tf_op jit(solution)/shard_map/ppermute | solution.py:188
  66.1 1.2 all-to-all-done
  68.4 11.0 %collective-permute-start.10 = (f32[2,2,128]{2,1,0:T(2,128)S(1)}, f32[2,2,128]{2,1,0:T(2,128)S(1)}, u32[]{:S(2)}, u32[]{:S(2)}) collective-permute-start(f32[2,2,128]{2,1,0:T(2,128)S(1)} %pad_maximum_fusion.6), channel_id=1, source_target_pairs={{0,1},{1,0},{2,3},{3,2},{4,5},{5,4},{6,7},{7,6},{8,9},{9,8},{10,11... | collective-permute-start | bytes 6152 | tf_op jit(solution)/shard_map/ppermute | solution.py:188
  79.5 1.6 collective-permute-done.10
  82.3 2.1 %collective-permute-start.12 = (bf16[128,1024]{1,0:T(8,128)(2,1)S(1)}, bf16[128,1024]{1,0:T(8,128)(2,1)}, u32[]{:S(2)}, u32[]{:S(2)}) collective-permute-start(bf16[128,1024]{1,0:T(8,128)(2,1)S(1)} %convolution_convert_fusion.1), channel_id=1, source_target_pairs={{0,1},{1,0},{2,3},{3,2},{4,5},{5,4},{6,7},{7,6},{8,9},{9,8},{10,11... | collective-permute-start | bytes 786440 | tf_op jit(solution)/shard_map/ppermute | solution.py:188
  84.4 2.1 %convolution_convert_fusion = bf16[1024,1024]{1,0:T(8,128)(2,1)} fusion(bf16[256,1024]{1,0:T(8,128)(2,1)S(1)} %multiply_convert_fusion, bf16[128,1024]{1,0:T(8,128)(2,1)S(1)} %copy-done.9, bf16[128,1024]{1,0:T(8,128)(2,1)S(1)} %copy-done.3), kind=kOutput, calls=%fused_computation.5 | convolution fusion | flops 538968064 | bytes 3145728 | tf_op jit(solution)/shard_map/dot_general | solution.py:17
  86.5 2.3 %collective-permute-done.12 = bf16[128,1024]{1,0:T(8,128)(2,1)} collective-permute-done((bf16[128,1024]{1,0:T(8,128)(2,1)S(1)}, bf16[128,1024]{1,0:T(8,128)(2,1)}, u32[]{:S(2)}, u32[]{:S(2)}) %collective-permute-start.12) | collective-permute-done | bytes 262176 | tf_op jit(solution)/shard_map/ppermute | solution.py:188
  88.9 4.3 %all-to-all-start.2 = ((bf16[8,128,1024]{2,1,0:T(8,128)(2,1)}), bf16[8,128,1024]{2,1,0:T(8,128)(2,1)}, u32[]{:S(2)}, u32[]{:S(2)}) async-start(bf16[8,128,1024]{2,1,0:T(8,128)(2,1)} %bitcast.131), calls=%async_computation.2 | async-start | bytes 4194304 | tf_op jit(solution)/shard_map/all_to_all | solution.py:292
  93.2 2.0 %multiply_reduce_fusion.2 = (f32[128]{0:T(128)S(1)}, f32[128]{0:T(128)S(1)}, f32[128]{0:T(128)S(1)}, f32[128,1024]{1,0:T(8,128)S(1)}) fusion(f32[128,1024]{1,0:T(8,128)S(1)} %get-tuple-element.40, bf16[128,1024]{1,0:T(8,128)(2,1)} %collective-permute-done.12, f32[1024]{0:T(1024)S(1)} %bitcast.144, bf16[128,1024]{1,0:T(8,128)(2,1)S(1)} %gather_fusion, ...), kind=kOutput, calls=%fused_computation.16 | convolution fusion | flops 270270080 | bytes 3938433 | tf_op jit(solution)/shard_map/dot_general | solution.py:17
  95.2 1.2 subtract_convert_fusion.refs_0_
  96.5 2.1 %collective-permute-start.13 = (bf16[128,1024]{1,0:T(8,128)(2,1)S(1)}, bf16[128,1024]{1,0:T(8,128)(2,1)S(1)}, u32[]{:S(2)}, u32[]{:S(2)}) collective-permute-start(bf16[128,1024]{1,0:T(8,128)(2,1)S(1)} %subtract_convert_fusion.refs_0_), channel_id=1, source_target_pairs={{0,1},{1,2},{2,3},{3,0},{4,5},{5,6},{6,7},{7,4},{8,9},{9,10},{10,1... | collective-permute-start | bytes 786440 | tf_op jit(solution)/shard_map/ppermute | solution.py:185
  98.6 2.0 %collective-permute-start.14 = (bf16[128,1024]{1,0:T(8,128)(2,1)S(1)}, bf16[128,1024]{1,0:T(8,128)(2,1)S(1)}, u32[]{:S(2)}, u32[]{:S(2)}) collective-permute-start(bf16[128,1024]{1,0:T(8,128)(2,1)S(1)} %subtract_convert_fusion.refs_0_), channel_id=1, source_target_pairs={{0,2},{1,3},{2,0},{3,1},{4,6},{5,7},{6,4},{7,5},{8,10},{9,11},{10,... | collective-permute-start | bytes 786440 | tf_op jit(solution)/shard_map/ppermute | solution.py:185
  100.6 2.8 %collective-permute-start.15 = (bf16[128,1024]{1,0:T(8,128)(2,1)S(1)}, bf16[128,1024]{1,0:T(8,128)(2,1)S(1)}, u32[]{:S(2)}, u32[]{:S(2)}) collective-permute-start(bf16[128,1024]{1,0:T(8,128)(2,1)S(1)} %subtract_convert_fusion.refs_0_), channel_id=1, source_target_pairs={{0,3},{1,0},{2,1},{3,2},{4,7},{5,4},{6,5},{7,6},{8,11},{9,8},{10,9... | collective-permute-start | bytes 786440 | tf_op jit(solution)/shard_map/ppermute | solution.py:185
  105.0 2.6 %collective-permute-done.13.refs_1_ = bf16[128,1024]{1,0:T(8,128)(2,1)S(1)} collective-permute-done((bf16[128,1024]{1,0:T(8,128)(2,1)S(1)}, bf16[128,1024]{1,0:T(8,128)(2,1)S(1)}, u32[]{:S(2)}, u32[]{:S(2)}) %collective-permute-start.13) | collective-permute-done | bytes 262176 | tf_op jit(solution)/shard_map/ppermute | solution.py:185
  107.6 10.7 %collective-permute-done.14.refs_2_ = bf16[128,1024]{1,0:T(8,128)(2,1)S(1)} collective-permute-done((bf16[128,1024]{1,0:T(8,128)(2,1)S(1)}, bf16[128,1024]{1,0:T(8,128)(2,1)S(1)}, u32[]{:S(2)}, u32[]{:S(2)}) %collective-permute-start.14) | collective-permute-done | bytes 262176 | tf_op jit(solution)/shard_map/ppermute | solution.py:185
  119.7 5.1 %shard_map.85 = (bf16[1024,1024]{1,0:T(8,128)(2,1)}, bf16[256,1024]{1,0:T(8,128)(2,1)}, bf16[256,1024]{1,0:T(8,128)(2,1)}) custom-call(s32[2]{0:T(128)} %pad_add_fusion.2.place_ref, bf16[128,1024]{1,0:T(8,128)(2,1)} %copy-done.10, bf16[128,1024]{1,0:T(8,128)(2,1)} %copy-done.15, bf16[128,1024]{1,0:T(8,128)(2,1)} %copy-done.16, bf16[128,1024]{1,0:T(8,128)(2,1)} %copy-done.17, ...), custom_call_target="tpu_custom_call" | custom-call | flops 1073741824 | bytes 2099200 | tf_op jit(solution)/shard_map/pallas_call | solution.py:33
  124.8 3.9 %all-to-all-start.1 = ((bf16[8,128,1024]{2,1,0:T(8,128)(2,1)}), bf16[8,128,1024]{2,1,0:T(8,128)(2,1)S(1)}, u32[]{:S(2)}, u32[]{:S(2)}) async-start(bf16[8,128,1024]{2,1,0:T(8,128)(2,1)} %bitcast.134), calls=%async_computation.1 | async-start | bytes 4194304 | tf_op jit(solution)/shard_map/all_to_all | solution.py:304
  130.2 5.7 %collective-permute-start.18 = (f32[64]{0:T(128)S(1)}, f32[64]{0:T(128)S(1)}, u32[]{:S(2)}, u32[]{:S(2)}) collective-permute-start(f32[64]{0:T(128)S(1)} %bitcast_add_fusion.1), channel_id=1, source_target_pairs={{0,1},{1,2},{2,3},{3,0},{4,5},{5,6},{6,7},{7,4},{8,9},{9,10},{10,1... | collective-permute-start | bytes 776 | tf_op jit(solution)/shard_map/ppermute | solution.py:185
  135.9 3.4 %collective-permute-start.19 = (f32[64]{0:T(128)S(1)}, f32[64]{0:T(128)S(1)}, u32[]{:S(2)}, u32[]{:S(2)}) collective-permute-start(f32[64]{0:T(128)S(1)} %bitcast_add_fusion.1), channel_id=1, source_target_pairs={{0,2},{1,3},{2,0},{3,1},{4,6},{5,7},{6,4},{7,5},{8,10},{9,11},{10,... | collective-permute-start | bytes 776 | tf_op jit(solution)/shard_map/ppermute | solution.py:185
  139.3 0.9 collective-permute-done.18
  140.8 2.0 %collective-permute-done.20 = f32[64]{0:T(128)S(1)} collective-permute-done((f32[64]{0:T(128)S(1)}, f32[64]{0:T(128)S(1)}, u32[]{:S(2)}, u32[]{:S(2)}) %collective-permute-start.20) | collective-permute-done | bytes 288 | tf_op jit(solution)/shard_map/ppermute | solution.py:185
  142.9 2.0 %reduce_sum.108 = bf16[2,4,32,1024]{3,2,1,0:T(8,128)(2,1)S(1)} reduce(bf16[4,2,4,32,1024]{4,3,2,1,0:T(8,128)(2,1)} %bitcast.57, bf16[]{:T(256)} %constant.168.clone.1), dimensions={0}, to_apply=%region_10.11 | reduce | flops 786432 | bytes 2621442 | tf_op jit(solution)/shard_map/reduce_sum | solution.py:293
  145.7 2.4 %collective-permute-start.22 = (bf16[2,32,1024]{2,1,0:T(8,128)(2,1)S(1)}, bf16[2,32,1024]{2,1,0:T(8,128)(2,1)S(1)}, u32[]{:S(2)}, u32[]{:S(2)}) collective-permute-start(bf16[2,32,1024]{2,1,0:T(8,128)(2,1)S(1)} %get-tuple-element.45), channel_id=1, source_target_pairs={{0,2},{1,3},{2,0},{3,1},{4,6},{5,7},{6,4},{7,5},{8,10},{9,11},{10,... | collective-permute-start | bytes 393224 | tf_op jit(solution)/shard_map/ppermute | solution.py:185
  148.0 1.5 collective-permute-start.23
  151.2 4.9 %shard_map.86 = bf16[256,1024]{1,0:T(8,128)(2,1)} custom-call(s32[2]{0:T(128)} %pad_add_fusion.2.place_ref, bf16[256,1024]{1,0:T(8,128)(2,1)} %get-tuple-element.18.refs_0_, bf16[256,1024]{1,0:T(8,128)(2,1)} %copy-done.5, bf16[2,1024,1024]{2,1,0:T(8,128)(2,1)} %refs_2_.1, bf16[256,1024]{1,0:T(8,128)(2,1)} %refs_3_.1, f32[2,256,1]{2,1,0:T(8,128)} %copy.40.refs_4_), custom_call_target="tpu_custom_call" | custom-call | flops 1073741824 | bytes 5769216 | tf_op jit(solution)/shard_map/pallas_call | solution.py:33
  156.1 1.4 collective-permute-done.22.refs_2_
  158.2 2.7 %shard_map.87 = f32[32,2,2048]{2,1,0:T(2,128)} custom-call(s32[2]{0:T(128)} %pad_add_fusion.2.place_ref, bf16[2,32,1024]{2,1,0:T(8,128)(2,1)} %get-tuple-element.47.refs_0_, bf16[2,32,1024]{2,1,0:T(8,128)(2,1)} %copy-done.11, bf16[2,32,1024]{2,1,0:T(8,128)(2,1)} %copy-done.12, bf16[2,32,1024]{2,1,0:T(8,128)(2,1)} %copy-done.13), custom_call_target="tpu_custom_call" | custom-call | flops 262144 | bytes 524288 | tf_op jit(solution)/shard_map/pallas_call | solution.py:33
  161.3 1.3 copy.41
  (122 shorter events, 19.1 us)
Async XLA Ops:
  0.6 18.1 %copy-start = (f32[2,1024]{1,0:T(2,128)S(1)}, f32[2,1024]{1,0:T(2,128)}, u32[]{:S(2)}) copy-start(f32[2,1024]{1,0:T(2,128)} %param.9) | copy-start | bytes 24580
  0.6 10.1 %copy-start.1 = (bf16[256,1024]{1,0:T(8,128)(2,1)S(1)}, bf16[256,1024]{1,0:T(8,128)(2,1)}, u32[]{:S(2)}) copy-start(bf16[256,1024]{1,0:T(8,128)(2,1)} %refs_3_.1) | copy-start | bytes 1572868
  0.7 10.1 %collective-permute-start.1 = (bf16[256,1024]{1,0:T(8,128)(2,1)}, bf16[256,1024]{1,0:T(8,128)(2,1)S(1)}, u32[]{:S(2)}, u32[]{:S(2)}) collective-permute-start(bf16[256,1024]{1,0:T(8,128)(2,1)} %refs_3_.1), channel_id=1, source_target_pairs={{0,4},{4,0},{8,12},{12,8},{16,20},{20,16},{24,28},{28,24},{1,5},{5... | collective-permute-start | bytes 1572872 | tf_op jit(solution)/shard_map/ppermute | solution.py:195
  5.1 15.4 %collective-permute-start.4 = (bf16[72,1024]{1,0:T(8,128)(2,1)}, bf16[72,1024]{1,0:T(8,128)(2,1)}, u32[]{:S(2)}, u32[]{:S(2)}) collective-permute-start(bf16[72,1024]{1,0:T(8,128)(2,1)} %get-tuple-element.51), channel_id=1, source_target_pairs={{0,3},{1,0},{2,1},{3,2},{4,7},{5,4},{6,5},{7,6},{8,11},{9,8},{10,9... | collective-permute-start | bytes 442376 | tf_op jit(solution)/shard_map/ppermute | solution.py:185
  9.8 19.9 %collective-permute-start = (bf16[72,1024]{1,0:T(8,128)(2,1)}, bf16[72,1024]{1,0:T(8,128)(2,1)}, u32[]{:S(2)}, u32[]{:S(2)}) collective-permute-start(bf16[72,1024]{1,0:T(8,128)(2,1)} %get-tuple-element.51), channel_id=1, source_target_pairs={{0,1},{1,2},{2,3},{3,0},{4,5},{5,6},{6,7},{7,4},{8,9},{9,10},{10,1... | collective-permute-start | bytes 442376 | tf_op jit(solution)/shard_map/ppermute | solution.py:185
  9.8 19.9 %collective-permute-start.3 = (bf16[72,1024]{1,0:T(8,128)(2,1)}, bf16[72,1024]{1,0:T(8,128)(2,1)}, u32[]{:S(2)}, u32[]{:S(2)}) collective-permute-start(bf16[72,1024]{1,0:T(8,128)(2,1)} %get-tuple-element.50), channel_id=1, source_target_pairs={{0,2},{1,3},{2,0},{3,1},{4,6},{5,7},{6,4},{7,5},{8,10},{9,11},{10,... | collective-permute-start | bytes 442376 | tf_op jit(solution)/shard_map/ppermute | solution.py:185
  10.8 0.8 copy-start.4
  11.6 7.2 %copy-start.14 = (s32[2,64]{1,0:T(2,128)S(1)}, s32[2,64]{1,0:T(2,128)}, u32[]{:S(2)}) copy-start(s32[2,64]{1,0:T(2,128)} %param.11) | copy-start | bytes 1540
  15.4 12.0 %collective-permute-start.2 = (bf16[128,1024]{1,0:T(8,128)(2,1)S(1)}, bf16[128,1024]{1,0:T(8,128)(2,1)S(1)}, u32[]{:S(2)}, u32[]{:S(2)}) collective-permute-start(bf16[128,1024]{1,0:T(8,128)(2,1)S(1)} %bitcast.142), channel_id=1, source_target_pairs={{0,1},{1,2},{2,3},{3,0},{4,5},{5,6},{6,7},{7,4},{8,9},{9,10},{10,1... | collective-permute-start | bytes 786440 | tf_op jit(solution)/shard_map/ppermute | solution.py:185
  18.8 1.2 collective-permute-start.8
  20.0 26.1 %collective-permute-start.7 = (bf16[128,1024]{1,0:T(8,128)(2,1)}, bf16[128,1024]{1,0:T(8,128)(2,1)S(1)}, u32[]{:S(2)}, u32[]{:S(2)}) collective-permute-start(bf16[128,1024]{1,0:T(8,128)(2,1)} %bitcast.13), channel_id=1, source_target_pairs={{0,3},{1,0},{2,1},{3,2},{4,7},{5,4},{6,5},{7,6},{8,11},{9,8},{10,9... | collective-permute-start | bytes 786440 | tf_op jit(solution)/shard_map/ppermute | solution.py:185
  20.5 26.3 %collective-permute-start.6 = (bf16[128,1024]{1,0:T(8,128)(2,1)}, bf16[128,1024]{1,0:T(8,128)(2,1)}, u32[]{:S(2)}, u32[]{:S(2)}) collective-permute-start(bf16[128,1024]{1,0:T(8,128)(2,1)} %bitcast.12), channel_id=1, source_target_pairs={{0,2},{1,3},{2,0},{3,1},{4,6},{5,7},{6,4},{7,5},{8,10},{9,11},{10,... | collective-permute-start | bytes 786440 | tf_op jit(solution)/shard_map/ppermute | solution.py:185
  27.4 7.9 %copy-start.6 = (bf16[128,1024]{1,0:T(8,128)(2,1)}, bf16[128,1024]{1,0:T(8,128)(2,1)S(1)}, u32[]{:S(2)}) copy-start(bf16[128,1024]{1,0:T(8,128)(2,1)S(1)} %collective-permute-done.2) | copy-start | bytes 786436
  36.9 30.4 %all-to-all-start = ((bf16[8,128,1024]{2,1,0:T(8,128)(2,1)}), bf16[8,128,1024]{2,1,0:T(8,128)(2,1)S(1)}, u32[]{:S(2)}, u32[]{:S(2)}) async-start(bf16[8,128,1024]{2,1,0:T(8,128)(2,1)} %bitcast.129), calls=%async_computation | async-start | bytes 4194304 | tf_op jit(solution)/shard_map/all_to_all | solution.py:245
  41.5 4.4 %collective-permute-start.5 = (f32[256]{0:T(256)S(1)}, f32[256]{0:T(256)S(1)}, u32[]{:S(2)}, u32[]{:S(2)}) collective-permute-start(f32[256]{0:T(256)S(1)} %slice_reduce_fusion), channel_id=1, source_target_pairs={{0,4},{4,0},{8,12},{12,8},{16,20},{20,16},{24,28},{28,24},{1,5},{5... | collective-permute-start | bytes 3080 | tf_op jit(solution)/shard_map/ppermute | solution.py:195
  46.1 0.7 copy-start.7
  48.5 19.9 %copy-start.2 = (bf16[128,1024]{1,0:T(8,128)(2,1)}, bf16[128,1024]{1,0:T(8,128)(2,1)S(1)}, u32[]{:S(2)}) copy-start(bf16[128,1024]{1,0:T(8,128)(2,1)S(1)} %multiply_convert_fusion.1) | copy-start | bytes 786436
  48.5 17.6 %collective-permute-start.9 = (bf16[128,1024]{1,0:T(8,128)(2,1)S(1)}, bf16[128,1024]{1,0:T(8,128)(2,1)S(1)}, u32[]{:S(2)}, u32[]{:S(2)}) collective-permute-start(bf16[128,1024]{1,0:T(8,128)(2,1)S(1)} %multiply_convert_fusion.1), channel_id=1, source_target_pairs={{0,1},{1,0},{2,3},{3,2},{4,5},{5,4},{6,7},{7,6},{8,9},{9,8},{10,11... | collective-permute-start | bytes 786440 | tf_op jit(solution)/shard_map/ppermute | solution.py:188
  59.5 6.5 %collective-permute-start.11 = (s32[2,128]{1,0:T(2,128)S(1)}, s32[2,128]{1,0:T(2,128)S(1)}, u32[]{:S(2)}, u32[]{:S(2)}) collective-permute-start(s32[2,128]{1,0:T(2,128)S(1)} %pad_add_fusion), channel_id=1, source_target_pairs={{0,1},{1,0},{2,3},{3,2},{4,5},{5,4},{6,7},{7,6},{8,9},{9,8},{10,11... | collective-permute-start | bytes 3080 | tf_op jit(solution)/shard_map/ppermute | solution.py:188
  66.1 2.3 %copy-start.8 = (bf16[128,1024]{1,0:T(8,128)(2,1)}, bf16[128,1024]{1,0:T(8,128)(2,1)S(1)}, u32[]{:S(2)}) copy-start(bf16[128,1024]{1,0:T(8,128)(2,1)S(1)} %collective-permute-done.9) | copy-start | bytes 786436
  68.4 12.6 %collective-permute-start.10 = (f32[2,2,128]{2,1,0:T(2,128)S(1)}, f32[2,2,128]{2,1,0:T(2,128)S(1)}, u32[]{:S(2)}, u32[]{:S(2)}) collective-permute-start(f32[2,2,128]{2,1,0:T(2,128)S(1)} %pad_maximum_fusion.6), channel_id=1, source_target_pairs={{0,1},{1,0},{2,3},{3,2},{4,5},{5,4},{6,7},{7,6},{8,9},{9,8},{10,11... | collective-permute-start | bytes 6152 | tf_op jit(solution)/shard_map/ppermute | solution.py:188
  81.1 3.3 %copy-start.3 = (bf16[128,1024]{1,0:T(8,128)(2,1)S(1)}, bf16[128,1024]{1,0:T(8,128)(2,1)}, u32[]{:S(2)}) copy-start(bf16[128,1024]{1,0:T(8,128)(2,1)} %copy-done.2) | copy-start | bytes 786436
  81.1 3.3 %copy-start.9 = (bf16[128,1024]{1,0:T(8,128)(2,1)S(1)}, bf16[128,1024]{1,0:T(8,128)(2,1)}, u32[]{:S(2)}) copy-start(bf16[128,1024]{1,0:T(8,128)(2,1)} %copy-done.8) | copy-start | bytes 786436
  82.3 6.6 %collective-permute-start.12 = (bf16[128,1024]{1,0:T(8,128)(2,1)S(1)}, bf16[128,1024]{1,0:T(8,128)(2,1)}, u32[]{:S(2)}, u32[]{:S(2)}) collective-permute-start(bf16[128,1024]{1,0:T(8,128)(2,1)S(1)} %convolution_convert_fusion.1), channel_id=1, source_target_pairs={{0,1},{1,0},{2,3},{3,2},{4,5},{5,4},{6,7},{7,6},{8,9},{9,8},{10,11... | collective-permute-start | bytes 786440 | tf_op jit(solution)/shard_map/ppermute | solution.py:188
  88.9 35.9 %all-to-all-start.2 = ((bf16[8,128,1024]{2,1,0:T(8,128)(2,1)}), bf16[8,128,1024]{2,1,0:T(8,128)(2,1)}, u32[]{:S(2)}, u32[]{:S(2)}) async-start(bf16[8,128,1024]{2,1,0:T(8,128)(2,1)} %bitcast.131), calls=%async_computation.2 | async-start | bytes 4194304 | tf_op jit(solution)/shard_map/all_to_all | solution.py:292
  96.5 21.8 %copy-start.10 = (bf16[128,1024]{1,0:T(8,128)(2,1)}, bf16[128,1024]{1,0:T(8,128)(2,1)S(1)}, u32[]{:S(2)}) copy-start(bf16[128,1024]{1,0:T(8,128)(2,1)S(1)} %subtract_convert_fusion.refs_0_) | copy-start | bytes 786436
  96.5 11.1 %collective-permute-start.13 = (bf16[128,1024]{1,0:T(8,128)(2,1)S(1)}, bf16[128,1024]{1,0:T(8,128)(2,1)S(1)}, u32[]{:S(2)}, u32[]{:S(2)}) collective-permute-start(bf16[128,1024]{1,0:T(8,128)(2,1)S(1)} %subtract_convert_fusion.refs_0_), channel_id=1, source_target_pairs={{0,1},{1,2},{2,3},{3,0},{4,5},{5,6},{6,7},{7,4},{8,9},{9,10},{10,1... | collective-permute-start | bytes 786440 | tf_op jit(solution)/shard_map/ppermute | solution.py:185
  98.6 19.7 %collective-permute-start.14 = (bf16[128,1024]{1,0:T(8,128)(2,1)S(1)}, bf16[128,1024]{1,0:T(8,128)(2,1)S(1)}, u32[]{:S(2)}, u32[]{:S(2)}) collective-permute-start(bf16[128,1024]{1,0:T(8,128)(2,1)S(1)} %subtract_convert_fusion.refs_0_), channel_id=1, source_target_pairs={{0,2},{1,3},{2,0},{3,1},{4,6},{5,7},{6,4},{7,5},{8,10},{9,11},{10,... | collective-permute-start | bytes 786440 | tf_op jit(solution)/shard_map/ppermute | solution.py:185
  100.6 17.7 %collective-permute-start.15 = (bf16[128,1024]{1,0:T(8,128)(2,1)S(1)}, bf16[128,1024]{1,0:T(8,128)(2,1)S(1)}, u32[]{:S(2)}, u32[]{:S(2)}) collective-permute-start(bf16[128,1024]{1,0:T(8,128)(2,1)S(1)} %subtract_convert_fusion.refs_0_), channel_id=1, source_target_pairs={{0,3},{1,0},{2,1},{3,2},{4,7},{5,4},{6,5},{7,6},{8,11},{9,8},{10,9... | collective-permute-start | bytes 786440 | tf_op jit(solution)/shard_map/ppermute | solution.py:185
  107.6 10.7 %copy-start.15 = (bf16[128,1024]{1,0:T(8,128)(2,1)}, bf16[128,1024]{1,0:T(8,128)(2,1)S(1)}, u32[]{:S(2)}) copy-start(bf16[128,1024]{1,0:T(8,128)(2,1)S(1)} %collective-permute-done.13.refs_1_) | copy-start | bytes 786436
  118.3 0.7 copy-start.16
  119.0 0.7 copy-start.17
  124.8 36.1 %all-to-all-start.1 = ((bf16[8,128,1024]{2,1,0:T(8,128)(2,1)}), bf16[8,128,1024]{2,1,0:T(8,128)(2,1)S(1)}, u32[]{:S(2)}, u32[]{:S(2)}) async-start(bf16[8,128,1024]{2,1,0:T(8,128)(2,1)} %bitcast.134), calls=%async_computation.1 | async-start | bytes 4194304 | tf_op jit(solution)/shard_map/all_to_all | solution.py:304
  128.7 1.4 collective-permute-start.17
  129.3 21.1 %collective-permute-start.16 = (bf16[256,1024]{1,0:T(8,128)(2,1)}, bf16[256,1024]{1,0:T(8,128)(2,1)S(1)}, u32[]{:S(2)}, u32[]{:S(2)}) collective-permute-start(bf16[256,1024]{1,0:T(8,128)(2,1)} %get-tuple-element.19), channel_id=1, source_target_pairs={{0,4},{4,0},{8,12},{12,8},{16,20},{20,16},{24,28},{28,24},{1,5},{5... | collective-permute-start | bytes 1572872 | tf_op jit(solution)/shard_map/ppermute | solution.py:195
  130.2 10.1 %collective-permute-start.18 = (f32[64]{0:T(128)S(1)}, f32[64]{0:T(128)S(1)}, u32[]{:S(2)}, u32[]{:S(2)}) collective-permute-start(f32[64]{0:T(128)S(1)} %bitcast_add_fusion.1), channel_id=1, source_target_pairs={{0,1},{1,2},{2,3},{3,0},{4,5},{5,6},{6,7},{7,4},{8,9},{9,10},{10,1... | collective-permute-start | bytes 776 | tf_op jit(solution)/shard_map/ppermute | solution.py:185
  135.9 4.9 %collective-permute-start.19 = (f32[64]{0:T(128)S(1)}, f32[64]{0:T(128)S(1)}, u32[]{:S(2)}, u32[]{:S(2)}) collective-permute-start(f32[64]{0:T(128)S(1)} %bitcast_add_fusion.1), channel_id=1, source_target_pairs={{0,2},{1,3},{2,0},{3,1},{4,6},{5,7},{6,4},{7,5},{8,10},{9,11},{10,... | collective-permute-start | bytes 776 | tf_op jit(solution)/shard_map/ppermute | solution.py:185
  139.3 3.5 %collective-permute-start.20 = (f32[64]{0:T(128)S(1)}, f32[64]{0:T(128)S(1)}, u32[]{:S(2)}, u32[]{:S(2)}) collective-permute-start(f32[64]{0:T(128)S(1)} %bitcast_add_fusion.1), channel_id=1, source_target_pairs={{0,3},{1,0},{2,1},{3,2},{4,7},{5,4},{6,5},{7,6},{8,11},{9,8},{10,9... | collective-permute-start | bytes 776 | tf_op jit(solution)/shard_map/ppermute | solution.py:185
  145.7 10.4 %collective-permute-start.21 = (bf16[2,32,1024]{2,1,0:T(8,128)(2,1)S(1)}, bf16[2,32,1024]{2,1,0:T(8,128)(2,1)S(1)}, u32[]{:S(2)}, u32[]{:S(2)}) collective-permute-start(bf16[2,32,1024]{2,1,0:T(8,128)(2,1)S(1)} %get-tuple-element.46), channel_id=1, source_target_pairs={{0,1},{1,2},{2,3},{3,0},{4,5},{5,6},{6,7},{7,4},{8,9},{9,10},{10,1... | collective-permute-start | bytes 393224 | tf_op jit(solution)/shard_map/ppermute | solution.py:185
  145.7 11.8 %collective-permute-start.22 = (bf16[2,32,1024]{2,1,0:T(8,128)(2,1)S(1)}, bf16[2,32,1024]{2,1,0:T(8,128)(2,1)S(1)}, u32[]{:S(2)}, u32[]{:S(2)}) collective-permute-start(bf16[2,32,1024]{2,1,0:T(8,128)(2,1)S(1)} %get-tuple-element.45), channel_id=1, source_target_pairs={{0,2},{1,3},{2,0},{3,1},{4,6},{5,7},{6,4},{7,5},{8,10},{9,11},{10,... | collective-permute-start | bytes 393224 | tf_op jit(solution)/shard_map/ppermute | solution.py:185
  148.0 9.5 %collective-permute-start.23 = (bf16[2,32,1024]{2,1,0:T(8,128)(2,1)S(1)}, bf16[2,32,1024]{2,1,0:T(8,128)(2,1)S(1)}, u32[]{:S(2)}, u32[]{:S(2)}) collective-permute-start(bf16[2,32,1024]{2,1,0:T(8,128)(2,1)S(1)} %get-tuple-element.44), channel_id=1, source_target_pairs={{0,3},{1,0},{2,1},{3,2},{4,7},{5,4},{6,5},{7,6},{8,11},{9,8},{10,9... | collective-permute-start | bytes 393224 | tf_op jit(solution)/shard_map/ppermute | solution.py:185
  150.4 0.8 copy-start.5
  156.1 1.4 copy-start.11
  157.5 0.6 copy-start.12
  157.5 0.7 copy-start.13

commit v9 on v8

--- a/solution.py
+++ b/solution.py
@@ -223,9 +223,10 @@
         return lax.dynamic_index_in_dim(proj_parts, index, 1, False).reshape(owned, depth)
 
     send = [owner_block((j + shift) % hids).astype(BF16) for shift in range(1, hids)]
-    received = [along_hid(send[shift - 1], shift) for shift in range(1, hids)]
-
-    head_got = [head_got[0]] + [after(g, received[0]) for g in head_got[1:]]
+    ready = [after(p, *head_got[1:]) for p in send]
+    received = [along_hid(ready[shift - 1], shift) for shift in range(1, hids)]
+
+    head_got = [head_got[0]] + [after(g, *send) for g in head_got[1:]]
     squares = sum(g[steps * head_rows :].astype(F32) for g in head_got).reshape(tail)
     squares = jnp.sum(squares[: EXACT * rows].reshape(EXACT, rows), axis=0)
     head_mid = jnp.stack([g[: steps * head_rows] for g in head_got[::-1]] * 2)

time: 163 us -> 150 us (0.920)
  starting transfers between devices: 68.4 us -> 45.3 us
  waiting for transfers between devices: 39.7 us -> 55.1 us
  local copies, waits for them, and re-layouts: 22.4 us -> 17.8 us
    ppermute x4, starting transfers between devices: 24.2 us -> 4.35 us  [turn_hid(): lax.ppermute(values, 'hid', [(a, a - a % halves + (a % halves + shift) %...]
    ppermute x15, waiting for transfers between devices: 26.3 us -> 42.6 us  [along_hid(): lax.ppermute(values, 'hid', [(a, (a + shift) % hids) for a in range(hids)])]
    unnamed x46 -> x44, local copies, waits for them, and re-layouts: 11.3 us -> 5.76 us
    ppermute x15, starting transfers between devices: 30.4 us -> 27.2 us  [along_hid(): lax.ppermute(values, 'hid', [(a, (a + shift) % hids) for a in range(hids)])]
  transfers between devices with their start and end apart: 27 -> 27, of which waited for: 14 -> 13; matrix products, arithmetic and copies ran while one was open for 20% -> 17% of each run, Pallas kernels for 8% -> 9%
where the time goes in v9:
time: 150 us; the launch traced here: 149 us
  waiting for transfers between devices  55.1 us (37%)
  starting transfers between devices  45.3 us (30%)
  local copies, waits for them, and re-layouts  17.8 us (12%)
  Pallas kernels  12.7 us (8%)
  matrix products  8.71 us (6%)
  other arithmetic  8.24 us (5%)
    ppermute x15, waiting for transfers between devices, along_hid(): lax.ppermute(values, 'hid', [(a, (a + shift) % hids) for a in range(hids)])  42.6 us
    ppermute x15, starting transfers between devices, along_hid(): lax.ppermute(values, 'hid', [(a, (a + shift) % hids) for a in range(hids)])  27.2 us
    pallas_call x3, Pallas kernels, call(): pl.pallas_call(kernel, grid_spec=pltpu.PrefetchScalarGridSpec(num_scalar_...  12.7 us
    ppermute x4, waiting for transfers between devices, turn_hid(): lax.ppermute(values, 'hid', [(a, a - a % halves + (a % halves + shift) %...  11.7 us
    dot_general x5, matrix products, matmul(): lax.dot_general(a, b, (contract, ((), ())), preferred_element_type=F32)  8.71 us
    unnamed x44, local copies, waits for them, and re-layouts  5.76 us
    ppermute x4, starting transfers between devices, turn_hid(): lax.ppermute(values, 'hid', [(a, a - a % halves + (a % halves + shift) %...  4.35 us
    all_to_all x1, starting transfers between devices, shards(): part_out = lax.all_to_all(part_out, 'seq', 0, 0)  4.35 us
  transfers between devices with their start and end apart: 27, of which 13 were waited for; matrix products, arithmetic and copies ran while one was open for 17% of the time, Pallas kernels for 9%

profile of v9, /device:TPU:0, one launch (start us, length us, event | category | flops | bytes accessed | tf_op | source)
XLA Modules:
  0.0 149.0 jit_solution(3190998963886801193)
XLA Ops:
  1.2 1.2 multiply_reduce_fusion
  2.5 1.1 reshape.276
  4.4 4.7 %collective-permute-start.3 = (bf16[72,1024]{1,0:T(8,128)(2,1)S(1)}, bf16[72,1024]{1,0:T(8,128)(2,1)S(1)}, u32[]{:S(2)}, u32[]{:S(2)}) collective-permute-start(bf16[72,1024]{1,0:T(8,128)(2,1)S(1)} %get-tuple-element.57), channel_id=1, source_target_pairs={{0,3},{1,0},{2,1},{3,2},{4,7},{5,4},{6,5},{7,6},{8,11},{9,8},{10,9... | collective-permute-start | bytes 442376 | tf_op jit(solution)/shard_map/ppermute | solution.py:185
  9.1 1.0 collective-permute-start.2
  10.2 3.0 %fusion = f32[2,4,64,1024]{3,2,1,0:T(8,128)S(1)} fusion(bf16[2,4,64,1024]{3,2,1,0:T(8,128)(2,1)S(1)} %bitcast.140, bf16[2,1024,1024]{2,1,0:T(8,128)(2,1)} %refs_2_.1, s32[]{:T(128)S(6)} %select_n.139), kind=kOutput, calls=%fused_computation.2 | convolution fusion | flops 1073741824 | bytes 5242884 | tf_op jit(solution)/shard_map/dot_general | solution.py:17
  13.2 1.3 copy-done.4
  14.5 0.8 dynamic-slice_convert_fusion
  15.3 6.9 %collective-permute-done.2 = bf16[72,1024]{1,0:T(8,128)(2,1)S(1)} collective-permute-done((bf16[72,1024]{1,0:T(8,128)(2,1)S(1)}, bf16[72,1024]{1,0:T(8,128)(2,1)S(1)}, u32[]{:S(2)}, u32[]{:S(2)}) %collective-permute-start.2) | collective-permute-done | bytes 147488 | tf_op jit(solution)/shard_map/ppermute | solution.py:185
  22.5 1.6 %broadcast_in_dim.45 = bf16[4,2,128,1024]{3,2,1,0:T(8,128)(2,1)} broadcast(bf16[2,128,1024]{2,1,0:T(8,128)(2,1)S(1)} %bitcast.133), dimensions={1,2,3} | broadcast | bytes 2621440 | tf_op jit(solution)/shard_map/broadcast_in_dim | solution.py:244
  24.1 3.9 %all-to-all-start = ((bf16[8,128,1024]{2,1,0:T(8,128)(2,1)}), bf16[8,128,1024]{2,1,0:T(8,128)(2,1)S(1)}, u32[]{:S(2)}, u32[]{:S(2)}) async-start(bf16[8,128,1024]{2,1,0:T(8,128)(2,1)} %bitcast.129), calls=%async_computation | async-start | bytes 4194304 | tf_op jit(solution)/shard_map/all_to_all | solution.py:246
  28.7 2.6 %collective-permute-start.7 = (bf16[128,1024]{1,0:T(8,128)(2,1)}, bf16[128,1024]{1,0:T(8,128)(2,1)}, u32[]{:S(2)}, u32[]{:S(2)}) collective-permute-start(bf16[128,1024]{1,0:T(8,128)(2,1)} %bitcast.10), channel_id=1, source_target_pairs={{0,3},{1,0},{2,1},{3,2},{4,7},{5,4},{6,5},{7,6},{8,11},{9,8},{10,9... | collective-permute-start | bytes 786440 | tf_op jit(solution)/shard_map/ppermute | solution.py:185
  32.0 1.1 constant_dynamic-slice_fusion.6
  33.2 3.8 %gather_fusion = bf16[128,1024]{1,0:T(8,128)(2,1)S(1)} fusion(bf16[2048,1024]{1,0:T(8,128)(2,1)} %bitcast.139, s32[1024]{0:T(1024)S(1)} %pad_clamp_fusion), kind=kCustom, calls=%fused_computation | custom fusion | bytes 524800 | tf_op jit(solution)/shard_map/jit(_take)/gather | solution.py:240
  37.1 2.2 %collective-permute-done.7 = bf16[128,1024]{1,0:T(8,128)(2,1)} collective-permute-done((bf16[128,1024]{1,0:T(8,128)(2,1)}, bf16[128,1024]{1,0:T(8,128)(2,1)}, u32[]{:S(2)}, u32[]{:S(2)}) %collective-permute-start.7) | collective-permute-done | bytes 262176 | tf_op jit(solution)/shard_map/ppermute | solution.py:185
  39.3 14.5 %collective-permute-done.6 = bf16[128,1024]{1,0:T(8,128)(2,1)} collective-permute-done((bf16[128,1024]{1,0:T(8,128)(2,1)S(1)}, bf16[128,1024]{1,0:T(8,128)(2,1)}, u32[]{:S(2)}, u32[]{:S(2)}) %collective-permute-start.6) | collective-permute-done | bytes 262176 | tf_op jit(solution)/shard_map/ppermute | solution.py:185
  53.8 1.4 multiply_reduce_fusion.4
  55.5 1.2 collective-permute-start.9
  56.7 0.9 collective-permute-start.11
  57.6 5.9 %collective-permute-done.11 = s32[2,128]{1,0:T(2,128)S(1)} collective-permute-done((s32[2,128]{1,0:T(2,128)S(1)}, s32[2,128]{1,0:T(2,128)S(1)}, u32[]{:S(2)}, u32[]{:S(2)}) %collective-permute-start.11) | collective-permute-done | bytes 1056 | tf_op jit(solution)/shard_map/ppermute | solution.py:188
  64.7 1.1 collective-permute-start.10
  65.8 2.5 %collective-permute-done.10 = f32[2,2,128]{2,1,0:T(2,128)S(1)} collective-permute-done((f32[2,2,128]{2,1,0:T(2,128)S(1)}, f32[2,2,128]{2,1,0:T(2,128)S(1)}, u32[]{:S(2)}, u32[]{:S(2)}) %collective-permute-start.10) | collective-permute-done | bytes 2080 | tf_op jit(solution)/shard_map/ppermute | solution.py:188
  68.8 0.8 convolution_convert_fusion.1
  69.6 1.1 collective-permute-start.12
  70.7 2.1 %convolution_convert_fusion = bf16[1024,1024]{1,0:T(8,128)(2,1)} fusion(bf16[256,1024]{1,0:T(8,128)(2,1)S(1)} %multiply_convert_fusion, bf16[128,1024]{1,0:T(8,128)(2,1)S(1)} %copy-done.8, bf16[128,1024]{1,0:T(8,128)(2,1)S(1)} %copy-done.3), kind=kOutput, calls=%fused_computation.5 | convolution fusion | flops 538968064 | bytes 3145728 | tf_op jit(solution)/shard_map/dot_general | solution.py:17
  72.8 3.3 %collective-permute-done.12 = bf16[128,1024]{1,0:T(8,128)(2,1)} collective-permute-done((bf16[128,1024]{1,0:T(8,128)(2,1)S(1)}, bf16[128,1024]{1,0:T(8,128)(2,1)}, u32[]{:S(2)}, u32[]{:S(2)}) %collective-permute-start.12) | collective-permute-done | bytes 262176 | tf_op jit(solution)/shard_map/ppermute | solution.py:188
  76.1 4.4 %all-to-all-start.2 = ((bf16[8,128,1024]{2,1,0:T(8,128)(2,1)}), bf16[8,128,1024]{2,1,0:T(8,128)(2,1)}, u32[]{:S(2)}, u32[]{:S(2)}) async-start(bf16[8,128,1024]{2,1,0:T(8,128)(2,1)} %bitcast.131), calls=%async_computation.2 | async-start | bytes 4194304 | tf_op jit(solution)/shard_map/all_to_all | solution.py:293
  80.5 2.0 %multiply_reduce_fusion.2 = (f32[128]{0:T(128)S(1)}, f32[128]{0:T(128)S(1)}, f32[128]{0:T(128)S(1)}, f32[128,1024]{1,0:T(8,128)S(1)}) fusion(f32[128,1024]{1,0:T(8,128)S(1)} %get-tuple-element.46, bf16[128,1024]{1,0:T(8,128)(2,1)} %collective-permute-done.12, f32[1024]{0:T(1024)S(1)} %bitcast.145, bf16[128,1024]{1,0:T(8,128)(2,1)S(1)} %gather_fusion, ...), kind=kOutput, calls=%fused_computation.16 | convolution fusion | flops 270270080 | bytes 3938433 | tf_op jit(solution)/shard_map/dot_general | solution.py:17
  82.5 1.2 subtract_convert_fusion.refs_0_
  83.8 1.1 collective-permute-start.13
  84.9 2.3 %collective-permute-start.14 = (bf16[128,1024]{1,0:T(8,128)(2,1)S(1)}, bf16[128,1024]{1,0:T(8,128)(2,1)S(1)}, u32[]{:S(2)}, u32[]{:S(2)}) collective-permute-start(bf16[128,1024]{1,0:T(8,128)(2,1)S(1)} %subtract_convert_fusion.refs_0_), channel_id=1, source_target_pairs={{0,2},{1,3},{2,0},{3,1},{4,6},{5,7},{6,4},{7,5},{8,10},{9,11},{10,... | collective-permute-start | bytes 786440 | tf_op jit(solution)/shard_map/ppermute | solution.py:185
  87.2 2.6 %collective-permute-start.15 = (bf16[128,1024]{1,0:T(8,128)(2,1)S(1)}, bf16[128,1024]{1,0:T(8,128)(2,1)S(1)}, u32[]{:S(2)}, u32[]{:S(2)}) collective-permute-start(bf16[128,1024]{1,0:T(8,128)(2,1)S(1)} %subtract_convert_fusion.refs_0_), channel_id=1, source_target_pairs={{0,3},{1,0},{2,1},{3,2},{4,7},{5,4},{6,5},{7,6},{8,11},{9,8},{10,9... | collective-permute-start | bytes 786440 | tf_op jit(solution)/shard_map/ppermute | solution.py:185
  90.5 0.9 copy.39.refs_6_
  91.4 3.5 %collective-permute-done.13.refs_1_ = bf16[128,1024]{1,0:T(8,128)(2,1)S(1)} collective-permute-done((bf16[128,1024]{1,0:T(8,128)(2,1)S(1)}, bf16[128,1024]{1,0:T(8,128)(2,1)S(1)}, u32[]{:S(2)}, u32[]{:S(2)}) %collective-permute-start.13) | collective-permute-done | bytes 262176 | tf_op jit(solution)/shard_map/ppermute | solution.py:185
  94.9 10.7 %collective-permute-done.14.refs_2_ = bf16[128,1024]{1,0:T(8,128)(2,1)S(1)} collective-permute-done((bf16[128,1024]{1,0:T(8,128)(2,1)S(1)}, bf16[128,1024]{1,0:T(8,128)(2,1)S(1)}, u32[]{:S(2)}, u32[]{:S(2)}) %collective-permute-start.14) | collective-permute-done | bytes 262176 | tf_op jit(solution)/shard_map/ppermute | solution.py:185
  107.0 5.1 %shard_map.85 = (bf16[1024,1024]{1,0:T(8,128)(2,1)}, bf16[256,1024]{1,0:T(8,128)(2,1)}, bf16[256,1024]{1,0:T(8,128)(2,1)}) custom-call(s32[2]{0:T(128)} %pad_add_fusion.2.place_ref, bf16[128,1024]{1,0:T(8,128)(2,1)} %copy-done.9, bf16[128,1024]{1,0:T(8,128)(2,1)} %copy-done.14, bf16[128,1024]{1,0:T(8,128)(2,1)} %copy-done.15, bf16[128,1024]{1,0:T(8,128)(2,1)} %copy-done.16, ...), custom_call_target="tpu_custom_call" | custom-call | flops 1073741824 | bytes 2099200 | tf_op jit(solution)/shard_map/pallas_call | solution.py:33
  112.1 3.9 %all-to-all-start.1 = ((bf16[8,128,1024]{2,1,0:T(8,128)(2,1)}), bf16[8,128,1024]{2,1,0:T(8,128)(2,1)S(1)}, u32[]{:S(2)}, u32[]{:S(2)}) async-start(bf16[8,128,1024]{2,1,0:T(8,128)(2,1)} %bitcast.134), calls=%async_computation.1 | async-start | bytes 4194304 | tf_op jit(solution)/shard_map/all_to_all | solution.py:305
  117.4 5.3 %collective-permute-start.18 = (f32[64]{0:T(128)S(1)}, f32[64]{0:T(128)S(1)}, u32[]{:S(2)}, u32[]{:S(2)}) collective-permute-start(f32[64]{0:T(128)S(1)} %bitcast_add_fusion.1), channel_id=1, source_target_pairs={{0,1},{1,2},{2,3},{3,0},{4,5},{5,6},{6,7},{7,4},{8,9},{9,10},{10,1... | collective-permute-start | bytes 776 | tf_op jit(solution)/shard_map/ppermute | solution.py:185
  122.7 2.9 %collective-permute-start.19 = (f32[64]{0:T(128)S(1)}, f32[64]{0:T(128)S(1)}, u32[]{:S(2)}, u32[]{:S(2)}) collective-permute-start(f32[64]{0:T(128)S(1)} %bitcast_add_fusion.1), channel_id=1, source_target_pairs={{0,2},{1,3},{2,0},{3,1},{4,6},{5,7},{6,4},{7,5},{8,10},{9,11},{10,... | collective-permute-start | bytes 776 | tf_op jit(solution)/shard_map/ppermute | solution.py:185
  125.7 0.9 collective-permute-done.18
  127.2 2.0 %collective-permute-done.20 = f32[64]{0:T(128)S(1)} collective-permute-done((f32[64]{0:T(128)S(1)}, f32[64]{0:T(128)S(1)}, u32[]{:S(2)}, u32[]{:S(2)}) %collective-permute-start.20) | collective-permute-done | bytes 288 | tf_op jit(solution)/shard_map/ppermute | solution.py:185
  129.4 2.0 %reduce_sum.108 = bf16[2,4,32,1024]{3,2,1,0:T(8,128)(2,1)S(1)} reduce(bf16[4,2,4,32,1024]{4,3,2,1,0:T(8,128)(2,1)} %bitcast.57, bf16[]{:T(256)} %constant.168.clone.1), dimensions={0}, to_apply=%region_10.11 | reduce | flops 786432 | bytes 2621442 | tf_op jit(solution)/shard_map/reduce_sum | solution.py:294
  132.1 2.4 %collective-permute-start.22 = (bf16[2,32,1024]{2,1,0:T(8,128)(2,1)S(1)}, bf16[2,32,1024]{2,1,0:T(8,128)(2,1)S(1)}, u32[]{:S(2)}, u32[]{:S(2)}) collective-permute-start(bf16[2,32,1024]{2,1,0:T(8,128)(2,1)S(1)} %get-tuple-element.51), channel_id=1, source_target_pairs={{0,2},{1,3},{2,0},{3,1},{4,6},{5,7},{6,4},{7,5},{8,10},{9,11},{10,... | collective-permute-start | bytes 393224 | tf_op jit(solution)/shard_map/ppermute | solution.py:185
  134.5 1.5 %collective-permute-start.23 = (bf16[2,32,1024]{2,1,0:T(8,128)(2,1)S(1)}, bf16[2,32,1024]{2,1,0:T(8,128)(2,1)S(1)}, u32[]{:S(2)}, u32[]{:S(2)}) collective-permute-start(bf16[2,32,1024]{2,1,0:T(8,128)(2,1)S(1)} %get-tuple-element.50), channel_id=1, source_target_pairs={{0,3},{1,0},{2,1},{3,2},{4,7},{5,4},{6,5},{7,6},{8,11},{9,8},{10,9... | collective-permute-start | bytes 393224 | tf_op jit(solution)/shard_map/ppermute | solution.py:185
  136.0 0.9 copy.40.refs_4_
  137.6 4.9 %shard_map.86 = bf16[256,1024]{1,0:T(8,128)(2,1)} custom-call(s32[2]{0:T(128)} %pad_add_fusion.2.place_ref, bf16[256,1024]{1,0:T(8,128)(2,1)} %get-tuple-element.24.refs_0_, bf16[256,1024]{1,0:T(8,128)(2,1)} %copy-done.6, bf16[2,1024,1024]{2,1,0:T(8,128)(2,1)} %refs_2_.1, bf16[256,1024]{1,0:T(8,128)(2,1)} %refs_3_.1, f32[2,256,1]{2,1,0:T(8,128)} %copy.40.refs_4_), custom_call_target="tpu_custom_call" | custom-call | flops 1073741824 | bytes 5769216 | tf_op jit(solution)/shard_map/pallas_call | solution.py:33
  142.5 1.4 collective-permute-done.22.refs_2_
  144.7 2.7 %shard_map.87 = f32[32,2,2048]{2,1,0:T(2,128)} custom-call(s32[2]{0:T(128)} %pad_add_fusion.2.place_ref, bf16[2,32,1024]{2,1,0:T(8,128)(2,1)} %get-tuple-element.53.refs_0_, bf16[2,32,1024]{2,1,0:T(8,128)(2,1)} %copy-done.10, bf16[2,32,1024]{2,1,0:T(8,128)(2,1)} %copy-done.11, bf16[2,32,1024]{2,1,0:T(8,128)(2,1)} %copy-done.12), custom_call_target="tpu_custom_call" | custom-call | flops 262144 | bytes 524288 | tf_op jit(solution)/shard_map/pallas_call | solution.py:33
  147.7 1.3 copy.41
  (120 shorter events, 12.0 us)
Async XLA Ops:
  0.6 9.5 %copy-start = (f32[2,1024]{1,0:T(2,128)S(1)}, f32[2,1024]{1,0:T(2,128)}, u32[]{:S(2)}) copy-start(f32[2,1024]{1,0:T(2,128)} %param.9) | copy-start | bytes 24580
  0.6 9.5 %copy-start.1 = (bf16[256,1024]{1,0:T(8,128)(2,1)S(1)}, bf16[256,1024]{1,0:T(8,128)(2,1)}, u32[]{:S(2)}) copy-start(bf16[256,1024]{1,0:T(8,128)(2,1)} %refs_3_.1) | copy-start | bytes 1572868
  0.7 9.5 %collective-permute-start.1 = (bf16[256,1024]{1,0:T(8,128)(2,1)}, bf16[256,1024]{1,0:T(8,128)(2,1)S(1)}, u32[]{:S(2)}, u32[]{:S(2)}) collective-permute-start(bf16[256,1024]{1,0:T(8,128)(2,1)} %refs_3_.1), channel_id=1, source_target_pairs={{0,4},{4,0},{8,12},{12,8},{16,20},{20,16},{24,28},{28,24},{1,5},{5... | collective-permute-start | bytes 1572872 | tf_op jit(solution)/shard_map/ppermute | solution.py:195
  4.4 11.0 %collective-permute-start.3 = (bf16[72,1024]{1,0:T(8,128)(2,1)S(1)}, bf16[72,1024]{1,0:T(8,128)(2,1)S(1)}, u32[]{:S(2)}, u32[]{:S(2)}) collective-permute-start(bf16[72,1024]{1,0:T(8,128)(2,1)S(1)} %get-tuple-element.57), channel_id=1, source_target_pairs={{0,3},{1,0},{2,1},{3,2},{4,7},{5,4},{6,5},{7,6},{8,11},{9,8},{10,9... | collective-permute-start | bytes 442376 | tf_op jit(solution)/shard_map/ppermute | solution.py:185
  9.1 13.1 %collective-permute-start = (bf16[72,1024]{1,0:T(8,128)(2,1)S(1)}, bf16[72,1024]{1,0:T(8,128)(2,1)S(1)}, u32[]{:S(2)}, u32[]{:S(2)}) collective-permute-start(bf16[72,1024]{1,0:T(8,128)(2,1)S(1)} %get-tuple-element.57), channel_id=1, source_target_pairs={{0,1},{1,2},{2,3},{3,0},{4,5},{5,6},{6,7},{7,4},{8,9},{9,10},{10,1... | collective-permute-start | bytes 442376 | tf_op jit(solution)/shard_map/ppermute | solution.py:185
  9.1 13.1 %collective-permute-start.2 = (bf16[72,1024]{1,0:T(8,128)(2,1)S(1)}, bf16[72,1024]{1,0:T(8,128)(2,1)S(1)}, u32[]{:S(2)}, u32[]{:S(2)}) collective-permute-start(bf16[72,1024]{1,0:T(8,128)(2,1)S(1)} %get-tuple-element.56), channel_id=1, source_target_pairs={{0,2},{1,3},{2,0},{3,1},{4,6},{5,7},{6,4},{7,5},{8,10},{9,11},{10,... | collective-permute-start | bytes 442376 | tf_op jit(solution)/shard_map/ppermute | solution.py:185
  10.1 3.1 %copy-start.5 = (bf16[256,1024]{1,0:T(8,128)(2,1)}, bf16[256,1024]{1,0:T(8,128)(2,1)S(1)}, u32[]{:S(2)}) copy-start(bf16[256,1024]{1,0:T(8,128)(2,1)S(1)} %collective-permute-done.1.refs_5_) | copy-start | bytes 1572868
  13.2 1.3 copy-start.4
  24.1 4.5 %copy-start.13 = (s32[2,64]{1,0:T(2,128)S(1)}, s32[2,64]{1,0:T(2,128)}, u32[]{:S(2)}) copy-start(s32[2,64]{1,0:T(2,128)} %param.11) | copy-start | bytes 1540
  24.1 39.4 %all-to-all-start = ((bf16[8,128,1024]{2,1,0:T(8,128)(2,1)}), bf16[8,128,1024]{2,1,0:T(8,128)(2,1)S(1)}, u32[]{:S(2)}, u32[]{:S(2)}) async-start(bf16[8,128,1024]{2,1,0:T(8,128)(2,1)} %bitcast.129), calls=%async_computation | async-start | bytes 4194304 | tf_op jit(solution)/shard_map/all_to_all | solution.py:246
  28.0 8.9 %collective-permute-start.4 = (f32[256]{0:T(256)S(1)}, f32[256]{0:T(256)S(1)}, u32[]{:S(2)}, u32[]{:S(2)}) collective-permute-start(f32[256]{0:T(256)S(1)} %slice_reduce_fusion), channel_id=1, source_target_pairs={{0,4},{4,0},{8,12},{12,8},{16,20},{20,16},{24,28},{28,24},{1,5},{5... | collective-permute-start | bytes 3080 | tf_op jit(solution)/shard_map/ppermute | solution.py:195
  28.6 4.4 %collective-permute-start.8 = (s32[2,64]{1,0:T(2,128)S(1)}, s32[2,64]{1,0:T(2,128)S(1)}, u32[]{:S(2)}, u32[]{:S(2)}) collective-permute-start(s32[2,64]{1,0:T(2,128)S(1)} %copy-done.13), channel_id=1, source_target_pairs={{0,4},{4,0},{8,12},{12,8},{16,20},{20,16},{24,28},{28,24},{1,5},{5... | collective-permute-start | bytes 1544 | tf_op jit(solution)/shard_map/ppermute | solution.py:195
  28.7 10.6 %collective-permute-start.7 = (bf16[128,1024]{1,0:T(8,128)(2,1)}, bf16[128,1024]{1,0:T(8,128)(2,1)}, u32[]{:S(2)}, u32[]{:S(2)}) collective-permute-start(bf16[128,1024]{1,0:T(8,128)(2,1)} %bitcast.10), channel_id=1, source_target_pairs={{0,3},{1,0},{2,1},{3,2},{4,7},{5,4},{6,5},{7,6},{8,11},{9,8},{10,9... | collective-permute-start | bytes 786440 | tf_op jit(solution)/shard_map/ppermute | solution.py:185
  31.3 22.5 %collective-permute-start.6 = (bf16[128,1024]{1,0:T(8,128)(2,1)S(1)}, bf16[128,1024]{1,0:T(8,128)(2,1)}, u32[]{:S(2)}, u32[]{:S(2)}) collective-permute-start(bf16[128,1024]{1,0:T(8,128)(2,1)S(1)} %bitcast.143), channel_id=1, source_target_pairs={{0,2},{1,3},{2,0},{3,1},{4,6},{5,7},{6,4},{7,5},{8,10},{9,11},{10,... | collective-permute-start | bytes 786440 | tf_op jit(solution)/shard_map/ppermute | solution.py:185
  31.3 22.5 %collective-permute-start.5 = (bf16[128,1024]{1,0:T(8,128)(2,1)S(1)}, bf16[128,1024]{1,0:T(8,128)(2,1)}, u32[]{:S(2)}, u32[]{:S(2)}) collective-permute-start(bf16[128,1024]{1,0:T(8,128)(2,1)S(1)} %bitcast.142), channel_id=1, source_target_pairs={{0,1},{1,2},{2,3},{3,0},{4,5},{5,6},{6,7},{7,4},{8,9},{9,10},{10,1... | collective-permute-start | bytes 786440 | tf_op jit(solution)/shard_map/ppermute | solution.py:185
  55.5 9.2 %copy-start.2 = (bf16[128,1024]{1,0:T(8,128)(2,1)}, bf16[128,1024]{1,0:T(8,128)(2,1)S(1)}, u32[]{:S(2)}) copy-start(bf16[128,1024]{1,0:T(8,128)(2,1)S(1)} %multiply_convert_fusion.1) | copy-start | bytes 786436
  55.5 8.0 %collective-permute-start.9 = (bf16[128,1024]{1,0:T(8,128)(2,1)S(1)}, bf16[128,1024]{1,0:T(8,128)(2,1)S(1)}, u32[]{:S(2)}, u32[]{:S(2)}) collective-permute-start(bf16[128,1024]{1,0:T(8,128)(2,1)S(1)} %multiply_convert_fusion.1), channel_id=1, source_target_pairs={{0,1},{1,0},{2,3},{3,2},{4,5},{5,4},{6,7},{7,6},{8,9},{9,8},{10,11... | collective-permute-start | bytes 786440 | tf_op jit(solution)/shard_map/ppermute | solution.py:188
  56.7 6.8 %collective-permute-start.11 = (s32[2,128]{1,0:T(2,128)S(1)}, s32[2,128]{1,0:T(2,128)S(1)}, u32[]{:S(2)}, u32[]{:S(2)}) collective-permute-start(s32[2,128]{1,0:T(2,128)S(1)} %pad_add_fusion), channel_id=1, source_target_pairs={{0,1},{1,0},{2,3},{3,2},{4,5},{5,4},{6,7},{7,6},{8,9},{9,8},{10,11... | collective-permute-start | bytes 3080 | tf_op jit(solution)/shard_map/ppermute | solution.py:188
  63.5 1.2 copy-start.7
  64.7 3.7 %collective-permute-start.10 = (f32[2,2,128]{2,1,0:T(2,128)S(1)}, f32[2,2,128]{2,1,0:T(2,128)S(1)}, u32[]{:S(2)}, u32[]{:S(2)}) collective-permute-start(f32[2,2,128]{2,1,0:T(2,128)S(1)} %pad_maximum_fusion.6), channel_id=1, source_target_pairs={{0,1},{1,0},{2,3},{3,2},{4,5},{5,4},{6,7},{7,6},{8,9},{9,8},{10,11... | collective-permute-start | bytes 6152 | tf_op jit(solution)/shard_map/ppermute | solution.py:188
  68.4 2.3 %copy-start.3 = (bf16[128,1024]{1,0:T(8,128)(2,1)S(1)}, bf16[128,1024]{1,0:T(8,128)(2,1)}, u32[]{:S(2)}) copy-start(bf16[128,1024]{1,0:T(8,128)(2,1)} %copy-done.2) | copy-start | bytes 786436
  68.4 2.3 %copy-start.8 = (bf16[128,1024]{1,0:T(8,128)(2,1)S(1)}, bf16[128,1024]{1,0:T(8,128)(2,1)}, u32[]{:S(2)}) copy-start(bf16[128,1024]{1,0:T(8,128)(2,1)} %copy-done.7) | copy-start | bytes 786436
  69.6 6.5 %collective-permute-start.12 = (bf16[128,1024]{1,0:T(8,128)(2,1)S(1)}, bf16[128,1024]{1,0:T(8,128)(2,1)}, u32[]{:S(2)}, u32[]{:S(2)}) collective-permute-start(bf16[128,1024]{1,0:T(8,128)(2,1)S(1)} %convolution_convert_fusion.1), channel_id=1, source_target_pairs={{0,1},{1,0},{2,3},{3,2},{4,5},{5,4},{6,7},{7,6},{8,9},{9,8},{10,11... | collective-permute-start | bytes 786440 | tf_op jit(solution)/shard_map/ppermute | solution.py:188
  76.1 35.9 %all-to-all-start.2 = ((bf16[8,128,1024]{2,1,0:T(8,128)(2,1)}), bf16[8,128,1024]{2,1,0:T(8,128)(2,1)}, u32[]{:S(2)}, u32[]{:S(2)}) async-start(bf16[8,128,1024]{2,1,0:T(8,128)(2,1)} %bitcast.131), calls=%async_computation.2 | async-start | bytes 4194304 | tf_op jit(solution)/shard_map/all_to_all | solution.py:293
  83.8 21.8 %copy-start.9 = (bf16[128,1024]{1,0:T(8,128)(2,1)}, bf16[128,1024]{1,0:T(8,128)(2,1)S(1)}, u32[]{:S(2)}) copy-start(bf16[128,1024]{1,0:T(8,128)(2,1)S(1)} %subtract_convert_fusion.refs_0_) | copy-start | bytes 786436
  83.8 11.1 %collective-permute-start.13 = (bf16[128,1024]{1,0:T(8,128)(2,1)S(1)}, bf16[128,1024]{1,0:T(8,128)(2,1)S(1)}, u32[]{:S(2)}, u32[]{:S(2)}) collective-permute-start(bf16[128,1024]{1,0:T(8,128)(2,1)S(1)} %subtract_convert_fusion.refs_0_), channel_id=1, source_target_pairs={{0,1},{1,2},{2,3},{3,0},{4,5},{5,6},{6,7},{7,4},{8,9},{9,10},{10,1... | collective-permute-start | bytes 786440 | tf_op jit(solution)/shard_map/ppermute | solution.py:185
  84.9 20.7 %collective-permute-start.14 = (bf16[128,1024]{1,0:T(8,128)(2,1)S(1)}, bf16[128,1024]{1,0:T(8,128)(2,1)S(1)}, u32[]{:S(2)}, u32[]{:S(2)}) collective-permute-start(bf16[128,1024]{1,0:T(8,128)(2,1)S(1)} %subtract_convert_fusion.refs_0_), channel_id=1, source_target_pairs={{0,2},{1,3},{2,0},{3,1},{4,6},{5,7},{6,4},{7,5},{8,10},{9,11},{10,... | collective-permute-start | bytes 786440 | tf_op jit(solution)/shard_map/ppermute | solution.py:185
  87.2 18.4 %collective-permute-start.15 = (bf16[128,1024]{1,0:T(8,128)(2,1)S(1)}, bf16[128,1024]{1,0:T(8,128)(2,1)S(1)}, u32[]{:S(2)}, u32[]{:S(2)}) collective-permute-start(bf16[128,1024]{1,0:T(8,128)(2,1)S(1)} %subtract_convert_fusion.refs_0_), channel_id=1, source_target_pairs={{0,3},{1,0},{2,1},{3,2},{4,7},{5,4},{6,5},{7,6},{8,11},{9,8},{10,9... | collective-permute-start | bytes 786440 | tf_op jit(solution)/shard_map/ppermute | solution.py:185
  94.9 10.7 %copy-start.14 = (bf16[128,1024]{1,0:T(8,128)(2,1)}, bf16[128,1024]{1,0:T(8,128)(2,1)S(1)}, u32[]{:S(2)}) copy-start(bf16[128,1024]{1,0:T(8,128)(2,1)S(1)} %collective-permute-done.13.refs_1_) | copy-start | bytes 786436
  105.6 0.7 copy-start.15
  106.3 0.7 copy-start.16
  112.1 35.3 %all-to-all-start.1 = ((bf16[8,128,1024]{2,1,0:T(8,128)(2,1)}), bf16[8,128,1024]{2,1,0:T(8,128)(2,1)S(1)}, u32[]{:S(2)}, u32[]{:S(2)}) async-start(bf16[8,128,1024]{2,1,0:T(8,128)(2,1)} %bitcast.134), calls=%async_computation.1 | async-start | bytes 4194304 | tf_op jit(solution)/shard_map/all_to_all | solution.py:305
  116.0 1.4 collective-permute-start.17
  116.6 20.3 %collective-permute-start.16 = (bf16[256,1024]{1,0:T(8,128)(2,1)}, bf16[256,1024]{1,0:T(8,128)(2,1)S(1)}, u32[]{:S(2)}, u32[]{:S(2)}) collective-permute-start(bf16[256,1024]{1,0:T(8,128)(2,1)} %get-tuple-element.25), channel_id=1, source_target_pairs={{0,4},{4,0},{8,12},{12,8},{16,20},{20,16},{24,28},{28,24},{1,5},{5... | collective-permute-start | bytes 1572872 | tf_op jit(solution)/shard_map/ppermute | solution.py:195
  117.4 9.2 %collective-permute-start.18 = (f32[64]{0:T(128)S(1)}, f32[64]{0:T(128)S(1)}, u32[]{:S(2)}, u32[]{:S(2)}) collective-permute-start(f32[64]{0:T(128)S(1)} %bitcast_add_fusion.1), channel_id=1, source_target_pairs={{0,1},{1,2},{2,3},{3,0},{4,5},{5,6},{6,7},{7,4},{8,9},{9,10},{10,1... | collective-permute-start | bytes 776 | tf_op jit(solution)/shard_map/ppermute | solution.py:185
  122.7 4.5 %collective-permute-start.19 = (f32[64]{0:T(128)S(1)}, f32[64]{0:T(128)S(1)}, u32[]{:S(2)}, u32[]{:S(2)}) collective-permute-start(f32[64]{0:T(128)S(1)} %bitcast_add_fusion.1), channel_id=1, source_target_pairs={{0,2},{1,3},{2,0},{3,1},{4,6},{5,7},{6,4},{7,5},{8,10},{9,11},{10,... | collective-permute-start | bytes 776 | tf_op jit(solution)/shard_map/ppermute | solution.py:185
  125.7 3.5 %collective-permute-start.20 = (f32[64]{0:T(128)S(1)}, f32[64]{0:T(128)S(1)}, u32[]{:S(2)}, u32[]{:S(2)}) collective-permute-start(f32[64]{0:T(128)S(1)} %bitcast_add_fusion.1), channel_id=1, source_target_pairs={{0,3},{1,0},{2,1},{3,2},{4,7},{5,4},{6,5},{7,6},{8,11},{9,8},{10,9... | collective-permute-start | bytes 776 | tf_op jit(solution)/shard_map/ppermute | solution.py:185
  132.1 10.4 %collective-permute-start.21 = (bf16[2,32,1024]{2,1,0:T(8,128)(2,1)S(1)}, bf16[2,32,1024]{2,1,0:T(8,128)(2,1)S(1)}, u32[]{:S(2)}, u32[]{:S(2)}) collective-permute-start(bf16[2,32,1024]{2,1,0:T(8,128)(2,1)S(1)} %get-tuple-element.52), channel_id=1, source_target_pairs={{0,1},{1,2},{2,3},{3,0},{4,5},{5,6},{6,7},{7,4},{8,9},{9,10},{10,1... | collective-permute-start | bytes 393224 | tf_op jit(solution)/shard_map/ppermute | solution.py:185
  132.1 11.8 %collective-permute-start.22 = (bf16[2,32,1024]{2,1,0:T(8,128)(2,1)S(1)}, bf16[2,32,1024]{2,1,0:T(8,128)(2,1)S(1)}, u32[]{:S(2)}, u32[]{:S(2)}) collective-permute-start(bf16[2,32,1024]{2,1,0:T(8,128)(2,1)S(1)} %get-tuple-element.51), channel_id=1, source_target_pairs={{0,2},{1,3},{2,0},{3,1},{4,6},{5,7},{6,4},{7,5},{8,10},{9,11},{10,... | collective-permute-start | bytes 393224 | tf_op jit(solution)/shard_map/ppermute | solution.py:185
  134.5 9.5 %collective-permute-start.23 = (bf16[2,32,1024]{2,1,0:T(8,128)(2,1)S(1)}, bf16[2,32,1024]{2,1,0:T(8,128)(2,1)S(1)}, u32[]{:S(2)}, u32[]{:S(2)}) collective-permute-start(bf16[2,32,1024]{2,1,0:T(8,128)(2,1)S(1)} %get-tuple-element.50), channel_id=1, source_target_pairs={{0,3},{1,0},{2,1},{3,2},{4,7},{5,4},{6,5},{7,6},{8,11},{9,8},{10,9... | collective-permute-start | bytes 393224 | tf_op jit(solution)/shard_map/ppermute | solution.py:185
  136.8 0.8 copy-start.6
  142.5 1.4 copy-start.10
  143.9 0.7 copy-start.11
  144.0 0.7 copy-start.12

commit v10 on v9

--- a/solution.py
+++ b/solution.py
@@ -289,7 +289,7 @@
     d_ratio_part = (scale * gated_proj - back_scale * x_proj).reshape(steps, part)
 
     part_out = matmul(normed_rows, after(d_logit, *away), ((0,), (0,))).astype(BF16)
-    part_out = after(part_out, *received).reshape(seqs, depth // seqs, block)
+    part_out = part_out.reshape(seqs, depth // seqs, block)
     part_out = lax.all_to_all(part_out, "seq", 0, 0)
     part_out = part_out.reshape(groups, steps, hids, head_rows, block).astype(F32).sum(0)
     part_out = part_out.astype(BF16)
@@ -301,11 +301,7 @@
 
     pieces = [d_round] + [along_hid(d_round, shift) for shift in range(1, hids)]
     ratio_rows = ratio_group.reshape(steps, rows, 1)
-    share, mine, *others = input_gradient(place, pieces, group, ratio_rows, seqs)
-    share = lax.all_to_all(share.reshape(seqs, depth // seqs, units), "seq", 0, 0)
-    share = share.reshape(groups, steps, depth // seqs, units).astype(F32).sum(0)
-    grad_in = share.transpose(0, 2, 1)
-
+    d_ratio_part = after(d_ratio_part, pieces[1])
     d_ratio = d_ratio_part[0]
     for m in relations:
         d_ratio += flip_seq(d_ratio_part[m], m)
@@ -314,6 +310,11 @@
         d_rows = lax.dynamic_update_index_in_dim(
             d_rows, along_hid(d_ratio, shift), (j - shift) % hids, 0
         )
+    share, mine, *others = input_gradient(after(place, d_rows), pieces, group, ratio_rows, seqs)
+    share = lax.all_to_all(share.reshape(seqs, depth // seqs, units), "seq", 0, 0)
+    share = share.reshape(groups, steps, depth // seqs, units).astype(F32).sum(0)
+    grad_in = share.transpose(0, 2, 1)
+
     ratio_own = ratio_group[0].reshape(rows)
     correction = ratio_own**3 * d_rows.reshape(rows) / width_in
     factors = jnp.stack([ratio_own, correction])[:, :, None]

time: 150 us -> 151 us (level)
  waiting for transfers between devices: 55.1 us -> 61.7 us
  starting transfers between devices: 45.3 us -> 39.1 us
    all_to_all x1, waiting for transfers between devices: 0.01 us -> 6.94 us  [shards(): lax.all_to_all(share.reshape(seqs, depth // seqs, units), 'seq', 0, 0)]
    ppermute x15, starting transfers between devices: 27.2 us -> 21.1 us  [along_hid(): lax.ppermute(values, 'hid', [(a, (a + shift) % hids) for a in range(hids)])]
    ppermute x15, waiting for transfers between devices: 42.6 us -> 46.3 us  [along_hid(): lax.ppermute(values, 'hid', [(a, (a + shift) % hids) for a in range(hids)])]
    ppermute x4, waiting for transfers between devices: 11.7 us -> 8.41 us  [turn_hid(): lax.ppermute(values, 'hid', [(a, a - a % halves + (a % halves + shift) %...]
  transfers between devices with their start and end apart: 27 -> 27, of which waited for: 13 -> 10; matrix products, arithmetic and copies ran while one was open for 17% -> 17% of each run, Pallas kernels for 9% -> 8%
where the time goes in v10:
time: 151 us; the launch traced here: 150 us
  waiting for transfers between devices  61.7 us (41%)
  starting transfers between devices  39.1 us (26%)
  local copies, waits for them, and re-layouts  18 us (12%)
  Pallas kernels  12.7 us (8%)
  matrix products  9.41 us (6%)
  other arithmetic  8.24 us (5%)
    ppermute x15, waiting for transfers between devices, along_hid(): lax.ppermute(values, 'hid', [(a, (a + shift) % hids) for a in range(hids)])  46.3 us
    ppermute x15, starting transfers between devices, along_hid(): lax.ppermute(values, 'hid', [(a, (a + shift) % hids) for a in range(hids)])  21.1 us
    pallas_call x3, Pallas kernels, call(): pl.pallas_call(kernel, grid_spec=pltpu.PrefetchScalarGridSpec(num_scalar_...  12.7 us
    dot_general x5, matrix products, matmul(): lax.dot_general(a, b, (contract, ((), ())), preferred_element_type=F32)  9.41 us
    ppermute x4, waiting for transfers between devices, turn_hid(): lax.ppermute(values, 'hid', [(a, a - a % halves + (a % halves + shift) %...  8.41 us
    all_to_all x1, waiting for transfers between devices, shards(): lax.all_to_all(share.reshape(seqs, depth // seqs, units), 'seq', 0, 0)  6.94 us
    unnamed x44, local copies, waits for them, and re-layouts  5.73 us
    all_to_all x1, starting transfers between devices, shards(): part_out = lax.all_to_all(part_out, 'seq', 0, 0)  4.34 us
  transfers between devices with their start and end apart: 27, of which 10 were waited for; matrix products, arithmetic and copies ran while one was open for 17% of the time, Pallas kernels for 8%

profile of v10, /device:TPU:0, one launch (start us, length us, event | category | flops | bytes accessed | tf_op | source)
XLA Modules:
  0.0 150.3 jit_solution(17816257410113483908)
XLA Ops:
  1.2 1.2 multiply_reduce_fusion
  2.5 1.1 reshape.241
  4.4 4.7 %collective-permute-start.3 = (bf16[72,1024]{1,0:T(8,128)(2,1)S(1)}, bf16[72,1024]{1,0:T(8,128)(2,1)S(1)}, u32[]{:S(2)}, u32[]{:S(2)}) collective-permute-start(bf16[72,1024]{1,0:T(8,128)(2,1)S(1)} %get-tuple-element.59), channel_id=1, source_target_pairs={{0,3},{1,0},{2,1},{3,2},{4,7},{5,4},{6,5},{7,6},{8,11},{9,8},{10,9... | collective-permute-start | bytes 442376 | tf_op jit(solution)/shard_map/ppermute | solution.py:185
  9.1 1.0 collective-permute-start.2
  10.2 3.0 %fusion = f32[2,4,64,1024]{3,2,1,0:T(8,128)S(1)} fusion(bf16[2,4,64,1024]{3,2,1,0:T(8,128)(2,1)S(1)} %bitcast.123, bf16[2,1024,1024]{2,1,0:T(8,128)(2,1)} %refs_2_.1, s32[]{:T(128)S(6)} %select_n.139), kind=kOutput, calls=%fused_computation.2 | convolution fusion | flops 1073741824 | bytes 5242884 | tf_op jit(solution)/shard_map/dot_general | solution.py:17
  13.2 1.3 copy-done.4
  14.5 0.8 dynamic-slice_convert_fusion
  15.3 6.9 %collective-permute-done.2 = bf16[72,1024]{1,0:T(8,128)(2,1)S(1)} collective-permute-done((bf16[72,1024]{1,0:T(8,128)(2,1)S(1)}, bf16[72,1024]{1,0:T(8,128)(2,1)S(1)}, u32[]{:S(2)}, u32[]{:S(2)}) %collective-permute-start.2) | collective-permute-done | bytes 147488 | tf_op jit(solution)/shard_map/ppermute | solution.py:185
  22.5 1.6 %broadcast_in_dim.45 = bf16[4,2,128,1024]{3,2,1,0:T(8,128)(2,1)} broadcast(bf16[2,128,1024]{2,1,0:T(8,128)(2,1)S(1)} %bitcast.116), dimensions={1,2,3} | broadcast | bytes 2621440 | tf_op jit(solution)/shard_map/broadcast_in_dim | solution.py:244
  24.1 3.9 %all-to-all-start = ((bf16[8,128,1024]{2,1,0:T(8,128)(2,1)}), bf16[8,128,1024]{2,1,0:T(8,128)(2,1)S(1)}, u32[]{:S(2)}, u32[]{:S(2)}) async-start(bf16[8,128,1024]{2,1,0:T(8,128)(2,1)} %bitcast.112), calls=%async_computation | async-start | bytes 4194304 | tf_op jit(solution)/shard_map/all_to_all | solution.py:246
  28.7 2.6 %collective-permute-start.7 = (bf16[128,1024]{1,0:T(8,128)(2,1)}, bf16[128,1024]{1,0:T(8,128)(2,1)}, u32[]{:S(2)}, u32[]{:S(2)}) collective-permute-start(bf16[128,1024]{1,0:T(8,128)(2,1)} %bitcast.10), channel_id=1, source_target_pairs={{0,3},{1,0},{2,1},{3,2},{4,7},{5,4},{6,5},{7,6},{8,11},{9,8},{10,9... | collective-permute-start | bytes 786440 | tf_op jit(solution)/shard_map/ppermute | solution.py:185
  32.0 1.1 constant_dynamic-slice_fusion.6
  33.2 3.8 %gather_fusion = bf16[128,1024]{1,0:T(8,128)(2,1)S(1)} fusion(bf16[2048,1024]{1,0:T(8,128)(2,1)} %bitcast.122, s32[1024]{0:T(1024)S(1)} %pad_clamp_fusion), kind=kCustom, calls=%fused_computation | custom fusion | bytes 524800 | tf_op jit(solution)/shard_map/jit(_take)/gather | solution.py:240
  37.1 2.2 %collective-permute-done.7 = bf16[128,1024]{1,0:T(8,128)(2,1)} collective-permute-done((bf16[128,1024]{1,0:T(8,128)(2,1)}, bf16[128,1024]{1,0:T(8,128)(2,1)}, u32[]{:S(2)}, u32[]{:S(2)}) %collective-permute-start.7) | collective-permute-done | bytes 262176 | tf_op jit(solution)/shard_map/ppermute | solution.py:185
  39.3 14.5 %collective-permute-done.6 = bf16[128,1024]{1,0:T(8,128)(2,1)} collective-permute-done((bf16[128,1024]{1,0:T(8,128)(2,1)S(1)}, bf16[128,1024]{1,0:T(8,128)(2,1)}, u32[]{:S(2)}, u32[]{:S(2)}) %collective-permute-start.6) | collective-permute-done | bytes 262176 | tf_op jit(solution)/shard_map/ppermute | solution.py:185
  53.8 1.4 multiply_reduce_fusion.4
  55.5 1.2 collective-permute-start.9
  56.7 0.9 collective-permute-start.11
  57.6 5.9 %collective-permute-done.11 = s32[2,128]{1,0:T(2,128)S(1)} collective-permute-done((s32[2,128]{1,0:T(2,128)S(1)}, s32[2,128]{1,0:T(2,128)S(1)}, u32[]{:S(2)}, u32[]{:S(2)}) %collective-permute-start.11) | collective-permute-done | bytes 1056 | tf_op jit(solution)/shard_map/ppermute | solution.py:188
  63.5 0.8 fusion.36
  64.7 1.1 collective-permute-start.10
  65.8 2.5 %collective-permute-done.10 = f32[2,2,128]{2,1,0:T(2,128)S(1)} collective-permute-done((f32[2,2,128]{2,1,0:T(2,128)S(1)}, f32[2,2,128]{2,1,0:T(2,128)S(1)}, u32[]{:S(2)}, u32[]{:S(2)}) %collective-permute-start.10) | collective-permute-done | bytes 2080 | tf_op jit(solution)/shard_map/ppermute | solution.py:188
  68.8 1.5 %convolution_convert_fusion.1 = bf16[128,1024]{1,0:T(8,128)(2,1)} fusion(bf16[1024,1024]{1,0:T(8,128)(2,1)S(1)} %bitcast.110, bf16[256,1024]{1,0:T(8,128)(2,1)S(1)} %multiply_convert_fusion), kind=kOutput, calls=%fused_computation.6 | convolution fusion | flops 268566528 | bytes 2621440 | tf_op jit(solution)/shard_map/dot_general | solution.py:17
  70.3 1.1 collective-permute-start.12
  71.4 2.1 %convolution_convert_fusion = bf16[1024,1024]{1,0:T(8,128)(2,1)} fusion(bf16[256,1024]{1,0:T(8,128)(2,1)S(1)} %multiply_convert_fusion, bf16[128,1024]{1,0:T(8,128)(2,1)S(1)} %copy-done.9, bf16[128,1024]{1,0:T(8,128)(2,1)S(1)} %copy-done.3), kind=kOutput, calls=%fused_computation.5 | convolution fusion | flops 538968064 | bytes 3145728 | tf_op jit(solution)/shard_map/dot_general | solution.py:17
  73.5 4.3 %all-to-all-start.2 = ((bf16[8,128,1024]{2,1,0:T(8,128)(2,1)}), bf16[8,128,1024]{2,1,0:T(8,128)(2,1)}, u32[]{:S(2)}, u32[]{:S(2)}) async-start(bf16[8,128,1024]{2,1,0:T(8,128)(2,1)} %bitcast.113), calls=%async_computation.2 | async-start | bytes 4194304 | tf_op jit(solution)/shard_map/all_to_all | solution.py:293
  77.9 2.0 %multiply_reduce_fusion.3 = (f32[128]{0:T(128)S(1)}, f32[128]{0:T(128)S(1)}, f32[128]{0:T(128)S(1)}, f32[128,1024]{1,0:T(8,128)S(1)}) fusion(f32[128,1024]{1,0:T(8,128)S(1)} %get-tuple-element.48, bf16[128,1024]{1,0:T(8,128)(2,1)} %collective-permute-done.12, f32[1024]{0:T(1024)S(1)} %bitcast.128, bf16[128,1024]{1,0:T(8,128)(2,1)S(1)} %gather_fusion, ...), kind=kOutput, calls=%fused_computation.18 | convolution fusion | flops 270270080 | bytes 3938433 | tf_op jit(solution)/shard_map/dot_general | solution.py:17
  79.9 1.2 subtract_convert_fusion.refs_0_
  81.1 1.0 collective-permute-start.13
  83.1 8.4 %collective-permute-done.13.refs_1_ = bf16[128,1024]{1,0:T(8,128)(2,1)S(1)} collective-permute-done((bf16[128,1024]{1,0:T(8,128)(2,1)S(1)}, bf16[128,1024]{1,0:T(8,128)(2,1)S(1)}, u32[]{:S(2)}, u32[]{:S(2)}) %collective-permute-start.13) | collective-permute-done | bytes 262176 | tf_op jit(solution)/shard_map/ppermute | solution.py:185
  92.1 1.2 collective-permute-start.19
  94.2 0.9 copy.39.refs_6_
  95.1 2.4 %collective-permute-start.16 = (f32[64]{0:T(128)S(1)}, f32[64]{0:T(128)S(1)}, u32[]{:S(2)}, u32[]{:S(2)}) collective-permute-start(f32[64]{0:T(128)S(1)} %bitcast_add_fusion.1), channel_id=1, source_target_pairs={{0,2},{1,3},{2,0},{3,1},{4,6},{5,7},{6,4},{7,5},{8,10},{9,11},{10,... | collective-permute-start | bytes 776 | tf_op jit(solution)/shard_map/ppermute | solution.py:185
  97.5 1.7 %collective-permute-start.17 = (f32[64]{0:T(128)S(1)}, f32[64]{0:T(128)S(1)}, u32[]{:S(2)}, u32[]{:S(2)}) collective-permute-start(f32[64]{0:T(128)S(1)} %bitcast_add_fusion.1), channel_id=1, source_target_pairs={{0,3},{1,0},{2,1},{3,2},{4,7},{5,4},{6,5},{7,6},{8,11},{9,8},{10,9... | collective-permute-start | bytes 776 | tf_op jit(solution)/shard_map/ppermute | solution.py:185
  99.2 6.7 %collective-permute-done.15 = f32[64]{0:T(128)S(1)} collective-permute-done((f32[64]{0:T(128)S(1)}, f32[64]{0:T(128)S(1)}, u32[]{:S(2)}, u32[]{:S(2)}) %collective-permute-start.15) | collective-permute-done | bytes 288 | tf_op jit(solution)/shard_map/ppermute | solution.py:185
  105.9 5.6 %collective-permute-done.16 = f32[64]{0:T(128)S(1)} collective-permute-done((f32[64]{0:T(128)S(1)}, f32[64]{0:T(128)S(1)}, u32[]{:S(2)}, u32[]{:S(2)}) %collective-permute-start.16) | collective-permute-done | bytes 288 | tf_op jit(solution)/shard_map/ppermute | solution.py:185
  113.0 5.1 %shard_map.85 = (bf16[1024,1024]{1,0:T(8,128)(2,1)}, bf16[256,1024]{1,0:T(8,128)(2,1)}, bf16[256,1024]{1,0:T(8,128)(2,1)}) custom-call(s32[2]{0:T(128)} %pad_add_fusion.2.place_ref, bf16[128,1024]{1,0:T(8,128)(2,1)} %copy-done.7, bf16[128,1024]{1,0:T(8,128)(2,1)} %copy-done.14, bf16[128,1024]{1,0:T(8,128)(2,1)} %copy-done.15, bf16[128,1024]{1,0:T(8,128)(2,1)} %copy-done.16, ...), custom_call_target="tpu_custom_call" | custom-call | flops 1073741824 | bytes 2099200 | tf_op jit(solution)/shard_map/pallas_call | solution.py:33
  118.1 3.9 %all-to-all-start.1 = ((bf16[8,128,1024]{2,1,0:T(8,128)(2,1)}), bf16[8,128,1024]{2,1,0:T(8,128)(2,1)S(1)}, u32[]{:S(2)}, u32[]{:S(2)}) async-start(bf16[8,128,1024]{2,1,0:T(8,128)(2,1)} %bitcast.117), calls=%async_computation.1 | async-start | bytes 4194304 | tf_op jit(solution)/shard_map/all_to_all | solution.py:314
  122.6 2.0 %reduce_sum.108 = bf16[2,4,32,1024]{3,2,1,0:T(8,128)(2,1)S(1)} reduce(bf16[4,2,4,32,1024]{4,3,2,1,0:T(8,128)(2,1)} %bitcast.53, bf16[]{:T(256)} %constant.168.clone.1), dimensions={0}, to_apply=%region_10.11 | reduce | flops 786432 | bytes 2621442 | tf_op jit(solution)/shard_map/reduce_sum | solution.py:294
  125.9 2.4 %collective-permute-start.22 = (bf16[2,32,1024]{2,1,0:T(8,128)(2,1)S(1)}, bf16[2,32,1024]{2,1,0:T(8,128)(2,1)S(1)}, u32[]{:S(2)}, u32[]{:S(2)}) collective-permute-start(bf16[2,32,1024]{2,1,0:T(8,128)(2,1)S(1)} %get-tuple-element.53), channel_id=1, source_target_pairs={{0,2},{1,3},{2,0},{3,1},{4,6},{5,7},{6,4},{7,5},{8,10},{9,11},{10,... | collective-permute-start | bytes 393224 | tf_op jit(solution)/shard_map/ppermute | solution.py:185
  128.3 1.4 collective-permute-start.23
  129.7 0.9 copy.40.refs_4_
  130.6 0.8 copy-done.6
  131.4 4.9 %shard_map.86 = bf16[256,1024]{1,0:T(8,128)(2,1)} custom-call(s32[2]{0:T(128)} %pad_add_fusion.2.place_ref, bf16[256,1024]{1,0:T(8,128)(2,1)} %get-tuple-element.27.refs_0_, bf16[256,1024]{1,0:T(8,128)(2,1)} %copy-done.6, bf16[2,1024,1024]{2,1,0:T(8,128)(2,1)} %refs_2_.1, bf16[256,1024]{1,0:T(8,128)(2,1)} %refs_3_.1, f32[2,256,1]{2,1,0:T(8,128)} %copy.40.refs_4_), custom_call_target="tpu_custom_call" | custom-call | flops 1073741824 | bytes 5769216 | tf_op jit(solution)/shard_map/pallas_call | solution.py:33
  136.3 2.0 %collective-permute-done.22.refs_2_ = bf16[2,32,1024]{2,1,0:T(8,128)(2,1)S(1)} collective-permute-done((bf16[2,32,1024]{2,1,0:T(8,128)(2,1)S(1)}, bf16[2,32,1024]{2,1,0:T(8,128)(2,1)S(1)}, u32[]{:S(2)}, u32[]{:S(2)}) %collective-permute-start.22) | collective-permute-done | bytes 131104 | tf_op jit(solution)/shard_map/ppermute | solution.py:185
  139.0 2.7 %shard_map.87 = f32[32,2,2048]{2,1,0:T(2,128)} custom-call(s32[2]{0:T(128)} %pad_add_fusion.2.place_ref, bf16[2,32,1024]{2,1,0:T(8,128)(2,1)} %get-tuple-element.55.refs_0_, bf16[2,32,1024]{2,1,0:T(8,128)(2,1)} %copy-done.10, bf16[2,32,1024]{2,1,0:T(8,128)(2,1)} %copy-done.11, bf16[2,32,1024]{2,1,0:T(8,128)(2,1)} %copy-done.12), custom_call_target="tpu_custom_call" | custom-call | flops 262144 | bytes 524288 | tf_op jit(solution)/shard_map/pallas_call | solution.py:33
  141.7 6.9 %all-to-all-done.1 = bf16[8,128,1024]{2,1,0:T(8,128)(2,1)S(1)} async-done(((bf16[8,128,1024]{2,1,0:T(8,128)(2,1)}), bf16[8,128,1024]{2,1,0:T(8,128)(2,1)S(1)}, u32[]{:S(2)}, u32[]{:S(2)}) %all-to-all-start.1) | async-done | bytes 2097184 | tf_op jit(solution)/shard_map/all_to_all | solution.py:314
  149.0 1.3 copy.41
  (124 shorter events, 11.2 us)
Async XLA Ops:
  0.6 9.5 %copy-start = (f32[2,1024]{1,0:T(2,128)S(1)}, f32[2,1024]{1,0:T(2,128)}, u32[]{:S(2)}) copy-start(f32[2,1024]{1,0:T(2,128)} %param.9) | copy-start | bytes 24580
  0.6 9.5 %copy-start.1 = (bf16[256,1024]{1,0:T(8,128)(2,1)S(1)}, bf16[256,1024]{1,0:T(8,128)(2,1)}, u32[]{:S(2)}) copy-start(bf16[256,1024]{1,0:T(8,128)(2,1)} %refs_3_.1) | copy-start | bytes 1572868
  0.7 9.5 %collective-permute-start.1 = (bf16[256,1024]{1,0:T(8,128)(2,1)}, bf16[256,1024]{1,0:T(8,128)(2,1)S(1)}, u32[]{:S(2)}, u32[]{:S(2)}) collective-permute-start(bf16[256,1024]{1,0:T(8,128)(2,1)} %refs_3_.1), channel_id=1, source_target_pairs={{0,4},{4,0},{8,12},{12,8},{16,20},{20,16},{24,28},{28,24},{1,5},{5... | collective-permute-start | bytes 1572872 | tf_op jit(solution)/shard_map/ppermute | solution.py:195
  4.4 11.0 %collective-permute-start.3 = (bf16[72,1024]{1,0:T(8,128)(2,1)S(1)}, bf16[72,1024]{1,0:T(8,128)(2,1)S(1)}, u32[]{:S(2)}, u32[]{:S(2)}) collective-permute-start(bf16[72,1024]{1,0:T(8,128)(2,1)S(1)} %get-tuple-element.59), channel_id=1, source_target_pairs={{0,3},{1,0},{2,1},{3,2},{4,7},{5,4},{6,5},{7,6},{8,11},{9,8},{10,9... | collective-permute-start | bytes 442376 | tf_op jit(solution)/shard_map/ppermute | solution.py:185
  9.1 13.1 %collective-permute-start = (bf16[72,1024]{1,0:T(8,128)(2,1)S(1)}, bf16[72,1024]{1,0:T(8,128)(2,1)S(1)}, u32[]{:S(2)}, u32[]{:S(2)}) collective-permute-start(bf16[72,1024]{1,0:T(8,128)(2,1)S(1)} %get-tuple-element.59), channel_id=1, source_target_pairs={{0,1},{1,2},{2,3},{3,0},{4,5},{5,6},{6,7},{7,4},{8,9},{9,10},{10,1... | collective-permute-start | bytes 442376 | tf_op jit(solution)/shard_map/ppermute | solution.py:185
  9.1 13.1 %collective-permute-start.2 = (bf16[72,1024]{1,0:T(8,128)(2,1)S(1)}, bf16[72,1024]{1,0:T(8,128)(2,1)S(1)}, u32[]{:S(2)}, u32[]{:S(2)}) collective-permute-start(bf16[72,1024]{1,0:T(8,128)(2,1)S(1)} %get-tuple-element.58), channel_id=1, source_target_pairs={{0,2},{1,3},{2,0},{3,1},{4,6},{5,7},{6,4},{7,5},{8,10},{9,11},{10,... | collective-permute-start | bytes 442376 | tf_op jit(solution)/shard_map/ppermute | solution.py:185
  10.1 3.1 %copy-start.5 = (bf16[256,1024]{1,0:T(8,128)(2,1)}, bf16[256,1024]{1,0:T(8,128)(2,1)S(1)}, u32[]{:S(2)}) copy-start(bf16[256,1024]{1,0:T(8,128)(2,1)S(1)} %collective-permute-done.1.refs_5_) | copy-start | bytes 1572868
  13.2 1.3 copy-start.4
  24.1 4.5 %copy-start.13 = (s32[2,64]{1,0:T(2,128)S(1)}, s32[2,64]{1,0:T(2,128)}, u32[]{:S(2)}) copy-start(s32[2,64]{1,0:T(2,128)} %param.11) | copy-start | bytes 1540
  24.1 39.4 %all-to-all-start = ((bf16[8,128,1024]{2,1,0:T(8,128)(2,1)}), bf16[8,128,1024]{2,1,0:T(8,128)(2,1)S(1)}, u32[]{:S(2)}, u32[]{:S(2)}) async-start(bf16[8,128,1024]{2,1,0:T(8,128)(2,1)} %bitcast.112), calls=%async_computation | async-start | bytes 4194304 | tf_op jit(solution)/shard_map/all_to_all | solution.py:246
  28.0 8.9 %collective-permute-start.4 = (f32[256]{0:T(256)S(1)}, f32[256]{0:T(256)S(1)}, u32[]{:S(2)}, u32[]{:S(2)}) collective-permute-start(f32[256]{0:T(256)S(1)} %slice_reduce_fusion), channel_id=1, source_target_pairs={{0,4},{4,0},{8,12},{12,8},{16,20},{20,16},{24,28},{28,24},{1,5},{5... | collective-permute-start | bytes 3080 | tf_op jit(solution)/shard_map/ppermute | solution.py:195
  28.6 4.4 %collective-permute-start.8 = (s32[2,64]{1,0:T(2,128)S(1)}, s32[2,64]{1,0:T(2,128)S(1)}, u32[]{:S(2)}, u32[]{:S(2)}) collective-permute-start(s32[2,64]{1,0:T(2,128)S(1)} %copy-done.13), channel_id=1, source_target_pairs={{0,4},{4,0},{8,12},{12,8},{16,20},{20,16},{24,28},{28,24},{1,5},{5... | collective-permute-start | bytes 1544 | tf_op jit(solution)/shard_map/ppermute | solution.py:195
  28.7 10.6 %collective-permute-start.7 = (bf16[128,1024]{1,0:T(8,128)(2,1)}, bf16[128,1024]{1,0:T(8,128)(2,1)}, u32[]{:S(2)}, u32[]{:S(2)}) collective-permute-start(bf16[128,1024]{1,0:T(8,128)(2,1)} %bitcast.10), channel_id=1, source_target_pairs={{0,3},{1,0},{2,1},{3,2},{4,7},{5,4},{6,5},{7,6},{8,11},{9,8},{10,9... | collective-permute-start | bytes 786440 | tf_op jit(solution)/shard_map/ppermute | solution.py:185
  31.3 22.5 %collective-permute-start.6 = (bf16[128,1024]{1,0:T(8,128)(2,1)S(1)}, bf16[128,1024]{1,0:T(8,128)(2,1)}, u32[]{:S(2)}, u32[]{:S(2)}) collective-permute-start(bf16[128,1024]{1,0:T(8,128)(2,1)S(1)} %bitcast.126), channel_id=1, source_target_pairs={{0,2},{1,3},{2,0},{3,1},{4,6},{5,7},{6,4},{7,5},{8,10},{9,11},{10,... | collective-permute-start | bytes 786440 | tf_op jit(solution)/shard_map/ppermute | solution.py:185
  31.3 22.5 %collective-permute-start.5 = (bf16[128,1024]{1,0:T(8,128)(2,1)S(1)}, bf16[128,1024]{1,0:T(8,128)(2,1)}, u32[]{:S(2)}, u32[]{:S(2)}) collective-permute-start(bf16[128,1024]{1,0:T(8,128)(2,1)S(1)} %bitcast.125), channel_id=1, source_target_pairs={{0,1},{1,2},{2,3},{3,0},{4,5},{5,6},{6,7},{7,4},{8,9},{9,10},{10,1... | collective-permute-start | bytes 786440 | tf_op jit(solution)/shard_map/ppermute | solution.py:185
  55.5 9.2 %copy-start.2 = (bf16[128,1024]{1,0:T(8,128)(2,1)}, bf16[128,1024]{1,0:T(8,128)(2,1)S(1)}, u32[]{:S(2)}) copy-start(bf16[128,1024]{1,0:T(8,128)(2,1)S(1)} %multiply_convert_fusion.1) | copy-start | bytes 786436
  55.5 8.0 %collective-permute-start.9 = (bf16[128,1024]{1,0:T(8,128)(2,1)S(1)}, bf16[128,1024]{1,0:T(8,128)(2,1)S(1)}, u32[]{:S(2)}, u32[]{:S(2)}) collective-permute-start(bf16[128,1024]{1,0:T(8,128)(2,1)S(1)} %multiply_convert_fusion.1), channel_id=1, source_target_pairs={{0,1},{1,0},{2,3},{3,2},{4,5},{5,4},{6,7},{7,6},{8,9},{9,8},{10,11... | collective-permute-start | bytes 786440 | tf_op jit(solution)/shard_map/ppermute | solution.py:188
  56.7 6.8 %collective-permute-start.11 = (s32[2,128]{1,0:T(2,128)S(1)}, s32[2,128]{1,0:T(2,128)S(1)}, u32[]{:S(2)}, u32[]{:S(2)}) collective-permute-start(s32[2,128]{1,0:T(2,128)S(1)} %pad_add_fusion), channel_id=1, source_target_pairs={{0,1},{1,0},{2,3},{3,2},{4,5},{5,4},{6,7},{7,6},{8,9},{9,8},{10,11... | collective-permute-start | bytes 3080 | tf_op jit(solution)/shard_map/ppermute | solution.py:188
  63.5 1.2 copy-start.8
  64.7 3.7 %collective-permute-start.10 = (f32[2,2,128]{2,1,0:T(2,128)S(1)}, f32[2,2,128]{2,1,0:T(2,128)S(1)}, u32[]{:S(2)}, u32[]{:S(2)}) collective-permute-start(f32[2,2,128]{2,1,0:T(2,128)S(1)} %pad_maximum_fusion.6), channel_id=1, source_target_pairs={{0,1},{1,0},{2,3},{3,2},{4,5},{5,4},{6,7},{7,6},{8,9},{9,8},{10,11... | collective-permute-start | bytes 6152 | tf_op jit(solution)/shard_map/ppermute | solution.py:188
  68.4 3.0 %copy-start.3 = (bf16[128,1024]{1,0:T(8,128)(2,1)S(1)}, bf16[128,1024]{1,0:T(8,128)(2,1)}, u32[]{:S(2)}) copy-start(bf16[128,1024]{1,0:T(8,128)(2,1)} %copy-done.2) | copy-start | bytes 786436
  68.4 3.0 %copy-start.9 = (bf16[128,1024]{1,0:T(8,128)(2,1)S(1)}, bf16[128,1024]{1,0:T(8,128)(2,1)}, u32[]{:S(2)}) copy-start(bf16[128,1024]{1,0:T(8,128)(2,1)} %copy-done.8) | copy-start | bytes 786436
  70.3 7.6 %collective-permute-start.12 = (bf16[128,1024]{1,0:T(8,128)(2,1)}, bf16[128,1024]{1,0:T(8,128)(2,1)}, u32[]{:S(2)}, u32[]{:S(2)}) collective-permute-start(bf16[128,1024]{1,0:T(8,128)(2,1)} %convolution_convert_fusion.1), channel_id=1, source_target_pairs={{0,1},{1,0},{2,3},{3,2},{4,5},{5,4},{6,7},{7,6},{8,9},{9,8},{10,11... | collective-permute-start | bytes 786440 | tf_op jit(solution)/shard_map/ppermute | solution.py:188
  73.5 44.6 %all-to-all-start.2 = ((bf16[8,128,1024]{2,1,0:T(8,128)(2,1)}), bf16[8,128,1024]{2,1,0:T(8,128)(2,1)}, u32[]{:S(2)}, u32[]{:S(2)}) async-start(bf16[8,128,1024]{2,1,0:T(8,128)(2,1)} %bitcast.113), calls=%async_computation.2 | async-start | bytes 4194304 | tf_op jit(solution)/shard_map/all_to_all | solution.py:293
  81.1 30.5 %copy-start.7 = (bf16[128,1024]{1,0:T(8,128)(2,1)}, bf16[128,1024]{1,0:T(8,128)(2,1)S(1)}, u32[]{:S(2)}) copy-start(bf16[128,1024]{1,0:T(8,128)(2,1)S(1)} %subtract_convert_fusion.refs_0_) | copy-start | bytes 786436
  81.1 10.4 %collective-permute-start.13 = (bf16[128,1024]{1,0:T(8,128)(2,1)S(1)}, bf16[128,1024]{1,0:T(8,128)(2,1)S(1)}, u32[]{:S(2)}, u32[]{:S(2)}) collective-permute-start(bf16[128,1024]{1,0:T(8,128)(2,1)S(1)} %subtract_convert_fusion.refs_0_), channel_id=1, source_target_pairs={{0,1},{1,2},{2,3},{3,0},{4,5},{5,6},{6,7},{7,4},{8,9},{9,10},{10,1... | collective-permute-start | bytes 786440 | tf_op jit(solution)/shard_map/ppermute | solution.py:185
  91.5 20.1 %copy-start.14 = (bf16[128,1024]{1,0:T(8,128)(2,1)}, bf16[128,1024]{1,0:T(8,128)(2,1)S(1)}, u32[]{:S(2)}) copy-start(bf16[128,1024]{1,0:T(8,128)(2,1)S(1)} %collective-permute-done.13.refs_1_) | copy-start | bytes 786436
  91.5 1.8 %collective-permute-start.14 = (f32[64]{0:T(128)S(1)}, f32[64]{0:T(128)S(1)}, u32[]{:S(2)}, u32[]{:S(2)}) collective-permute-start(f32[64]{0:T(128)S(1)} %slice_bitcast_fusion), channel_id=1, source_target_pairs={{0,4},{4,0},{8,12},{12,8},{16,20},{20,16},{24,28},{28,24},{1,5},{5... | collective-permute-start | bytes 776 | tf_op jit(solution)/shard_map/ppermute | solution.py:195
  91.6 20.0 %collective-permute-start.18 = (bf16[128,1024]{1,0:T(8,128)(2,1)S(1)}, bf16[128,1024]{1,0:T(8,128)(2,1)S(1)}, u32[]{:S(2)}, u32[]{:S(2)}) collective-permute-start(bf16[128,1024]{1,0:T(8,128)(2,1)S(1)} %subtract_convert_fusion.refs_0_), channel_id=1, source_target_pairs={{0,2},{1,3},{2,0},{3,1},{4,6},{5,7},{6,4},{7,5},{8,10},{9,11},{10,... | collective-permute-start | bytes 786440 | tf_op jit(solution)/shard_map/ppermute | solution.py:185
  92.1 19.4 %collective-permute-start.19 = (bf16[128,1024]{1,0:T(8,128)(2,1)S(1)}, bf16[128,1024]{1,0:T(8,128)(2,1)S(1)}, u32[]{:S(2)}, u32[]{:S(2)}) collective-permute-start(bf16[128,1024]{1,0:T(8,128)(2,1)S(1)} %subtract_convert_fusion.refs_0_), channel_id=1, source_target_pairs={{0,3},{1,0},{2,1},{3,2},{4,7},{5,4},{6,5},{7,6},{8,11},{9,8},{10,9... | collective-permute-start | bytes 786440 | tf_op jit(solution)/shard_map/ppermute | solution.py:185
  93.4 12.5 %collective-permute-start.15 = (f32[64]{0:T(128)S(1)}, f32[64]{0:T(128)S(1)}, u32[]{:S(2)}, u32[]{:S(2)}) collective-permute-start(f32[64]{0:T(128)S(1)} %bitcast_add_fusion.1), channel_id=1, source_target_pairs={{0,1},{1,2},{2,3},{3,0},{4,5},{5,6},{6,7},{7,4},{8,9},{9,10},{10,1... | collective-permute-start | bytes 776 | tf_op jit(solution)/shard_map/ppermute | solution.py:185
  95.1 16.4 %collective-permute-start.16 = (f32[64]{0:T(128)S(1)}, f32[64]{0:T(128)S(1)}, u32[]{:S(2)}, u32[]{:S(2)}) collective-permute-start(f32[64]{0:T(128)S(1)} %bitcast_add_fusion.1), channel_id=1, source_target_pairs={{0,2},{1,3},{2,0},{3,1},{4,6},{5,7},{6,4},{7,5},{8,10},{9,11},{10,... | collective-permute-start | bytes 776 | tf_op jit(solution)/shard_map/ppermute | solution.py:185
  97.5 14.1 %collective-permute-start.17 = (f32[64]{0:T(128)S(1)}, f32[64]{0:T(128)S(1)}, u32[]{:S(2)}, u32[]{:S(2)}) collective-permute-start(f32[64]{0:T(128)S(1)} %bitcast_add_fusion.1), channel_id=1, source_target_pairs={{0,3},{1,0},{2,1},{3,2},{4,7},{5,4},{6,5},{7,6},{8,11},{9,8},{10,9... | collective-permute-start | bytes 776 | tf_op jit(solution)/shard_map/ppermute | solution.py:185
  111.6 0.7 copy-start.15
  112.3 0.7 copy-start.16
  118.1 30.5 %all-to-all-start.1 = ((bf16[8,128,1024]{2,1,0:T(8,128)(2,1)}), bf16[8,128,1024]{2,1,0:T(8,128)(2,1)S(1)}, u32[]{:S(2)}, u32[]{:S(2)}) async-start(bf16[8,128,1024]{2,1,0:T(8,128)(2,1)} %bitcast.117), calls=%async_computation.1 | async-start | bytes 4194304 | tf_op jit(solution)/shard_map/all_to_all | solution.py:314
  122.0 8.6 %collective-permute-start.20 = (bf16[256,1024]{1,0:T(8,128)(2,1)}, bf16[256,1024]{1,0:T(8,128)(2,1)S(1)}, u32[]{:S(2)}, u32[]{:S(2)}) collective-permute-start(bf16[256,1024]{1,0:T(8,128)(2,1)} %get-tuple-element.28), channel_id=1, source_target_pairs={{0,4},{4,0},{8,12},{12,8},{16,20},{20,16},{24,28},{28,24},{1,5},{5... | collective-permute-start | bytes 1572872 | tf_op jit(solution)/shard_map/ppermute | solution.py:195
  125.3 11.0 %collective-permute-start.21 = (bf16[2,32,1024]{2,1,0:T(8,128)(2,1)S(1)}, bf16[2,32,1024]{2,1,0:T(8,128)(2,1)S(1)}, u32[]{:S(2)}, u32[]{:S(2)}) collective-permute-start(bf16[2,32,1024]{2,1,0:T(8,128)(2,1)S(1)} %get-tuple-element.54), channel_id=1, source_target_pairs={{0,1},{1,2},{2,3},{3,0},{4,5},{5,6},{6,7},{7,4},{8,9},{9,10},{10,1... | collective-permute-start | bytes 393224 | tf_op jit(solution)/shard_map/ppermute | solution.py:185
  125.9 12.4 %collective-permute-start.22 = (bf16[2,32,1024]{2,1,0:T(8,128)(2,1)S(1)}, bf16[2,32,1024]{2,1,0:T(8,128)(2,1)S(1)}, u32[]{:S(2)}, u32[]{:S(2)}) collective-permute-start(bf16[2,32,1024]{2,1,0:T(8,128)(2,1)S(1)} %get-tuple-element.53), channel_id=1, source_target_pairs={{0,2},{1,3},{2,0},{3,1},{4,6},{5,7},{6,4},{7,5},{8,10},{9,11},{10,... | collective-permute-start | bytes 393224 | tf_op jit(solution)/shard_map/ppermute | solution.py:185
  128.3 10.0 %collective-permute-start.23 = (bf16[2,32,1024]{2,1,0:T(8,128)(2,1)S(1)}, bf16[2,32,1024]{2,1,0:T(8,128)(2,1)S(1)}, u32[]{:S(2)}, u32[]{:S(2)}) collective-permute-start(bf16[2,32,1024]{2,1,0:T(8,128)(2,1)S(1)} %get-tuple-element.52), channel_id=1, source_target_pairs={{0,3},{1,0},{2,1},{3,2},{4,7},{5,4},{6,5},{7,6},{8,11},{9,8},{10,9... | collective-permute-start | bytes 393224 | tf_op jit(solution)/shard_map/ppermute | solution.py:185
  130.6 0.8 copy-start.6
  136.3 2.0 %copy-start.10 = (bf16[2,32,1024]{2,1,0:T(8,128)(2,1)}, bf16[2,32,1024]{2,1,0:T(8,128)(2,1)S(1)}, u32[]{:S(2)}) copy-start(bf16[2,32,1024]{2,1,0:T(8,128)(2,1)S(1)} %collective-permute-done.21.refs_1_) | copy-start | bytes 393220
  138.3 0.6 copy-start.11
  138.3 0.7 copy-start.12

commit v11 on v10

--- a/solution.py
+++ b/solution.py
@@ -301,7 +301,7 @@
 
     pieces = [d_round] + [along_hid(d_round, shift) for shift in range(1, hids)]
     ratio_rows = ratio_group.reshape(steps, rows, 1)
-    d_ratio_part = after(d_ratio_part, pieces[1])
+    d_ratio_part = after(d_ratio_part, d_round)
     d_ratio = d_ratio_part[0]
     for m in relations:
         d_ratio += flip_seq(d_ratio_part[m], m)

time: 151 us -> 150 us (level)
  waiting for transfers between devices: 61.7 us -> 58.7 us
    ppermute x15, waiting for transfers between devices: 46.3 us -> 43.8 us  [along_hid(): lax.ppermute(values, 'hid', [(a, (a + shift) % hids) for a in range(hids)])]
  transfers between devices with their start and end apart: 27 -> 27, of which waited for: 10 -> 9; matrix products, arithmetic and copies ran while one was open for 17% -> 17% of each run, Pallas kernels for 8% -> 9%
where the time goes in v11:
time: 150 us; the launch traced here: 149 us
  waiting for transfers between devices  58.7 us (39%)
  starting transfers between devices  40.4 us (27%)
  local copies, waits for them, and re-layouts  18.1 us (12%)
  Pallas kernels  12.7 us (8%)
  matrix products  9.41 us (6%)
  other arithmetic  8.25 us (6%)
    ppermute x15, waiting for transfers between devices, along_hid(): lax.ppermute(values, 'hid', [(a, (a + shift) % hids) for a in range(hids)])  43.8 us
    ppermute x15, starting transfers between devices, along_hid(): lax.ppermute(values, 'hid', [(a, (a + shift) % hids) for a in range(hids)])  21.9 us
    pallas_call x3, Pallas kernels, call(): pl.pallas_call(kernel, grid_spec=pltpu.PrefetchScalarGridSpec(num_scalar_...  12.7 us
    dot_general x5, matrix products, matmul(): lax.dot_general(a, b, (contract, ((), ())), preferred_element_type=F32)  9.41 us
    ppermute x4, waiting for transfers between devices, turn_hid(): lax.ppermute(values, 'hid', [(a, a - a % halves + (a % halves + shift) %...  8.41 us
    all_to_all x1, waiting for transfers between devices, shards(): lax.all_to_all(share.reshape(seqs, depth // seqs, units), 'seq', 0, 0)  6.53 us
    unnamed x44, local copies, waits for them, and re-layouts  5.8 us
    all_to_all x1, starting transfers between devices, shards(): part_out = lax.all_to_all(part_out, 'seq', 0, 0)  4.34 us
  transfers between devices with their start and end apart: 27, of which 9 were waited for; matrix products, arithmetic and copies ran while one was open for 17% of the time, Pallas kernels for 9%

profile of v11, /device:TPU:0, one launch (start us, length us, event | category | flops | bytes accessed | tf_op | source)
XLA Modules:
  0.0 148.8 jit_solution(11361731018865723555)
XLA Ops:
  1.2 1.2 multiply_reduce_fusion
  2.5 1.1 reshape.241
  4.4 4.7 %collective-permute-start.3 = (bf16[72,1024]{1,0:T(8,128)(2,1)S(1)}, bf16[72,1024]{1,0:T(8,128)(2,1)S(1)}, u32[]{:S(2)}, u32[]{:S(2)}) collective-permute-start(bf16[72,1024]{1,0:T(8,128)(2,1)S(1)} %get-tuple-element.59), channel_id=1, source_target_pairs={{0,3},{1,0},{2,1},{3,2},{4,7},{5,4},{6,5},{7,6},{8,11},{9,8},{10,9... | collective-permute-start | bytes 442376 | tf_op jit(solution)/shard_map/ppermute | solution.py:185
  9.1 1.0 collective-permute-start.2
  10.2 3.0 %fusion = f32[2,4,64,1024]{3,2,1,0:T(8,128)S(1)} fusion(bf16[2,4,64,1024]{3,2,1,0:T(8,128)(2,1)S(1)} %bitcast.123, bf16[2,1024,1024]{2,1,0:T(8,128)(2,1)} %refs_2_.1, s32[]{:T(128)S(6)} %select_n.139), kind=kOutput, calls=%fused_computation.2 | convolution fusion | flops 1073741824 | bytes 5242884 | tf_op jit(solution)/shard_map/dot_general | solution.py:17
  13.2 1.3 copy-done.4
  14.5 0.8 dynamic-slice_convert_fusion
  15.3 6.9 %collective-permute-done.2 = bf16[72,1024]{1,0:T(8,128)(2,1)S(1)} collective-permute-done((bf16[72,1024]{1,0:T(8,128)(2,1)S(1)}, bf16[72,1024]{1,0:T(8,128)(2,1)S(1)}, u32[]{:S(2)}, u32[]{:S(2)}) %collective-permute-start.2) | collective-permute-done | bytes 147488 | tf_op jit(solution)/shard_map/ppermute | solution.py:185
  22.5 1.6 %broadcast_in_dim.45 = bf16[4,2,128,1024]{3,2,1,0:T(8,128)(2,1)} broadcast(bf16[2,128,1024]{2,1,0:T(8,128)(2,1)S(1)} %bitcast.116), dimensions={1,2,3} | broadcast | bytes 2621440 | tf_op jit(solution)/shard_map/broadcast_in_dim | solution.py:244
  24.1 3.9 %all-to-all-start = ((bf16[8,128,1024]{2,1,0:T(8,128)(2,1)}), bf16[8,128,1024]{2,1,0:T(8,128)(2,1)S(1)}, u32[]{:S(2)}, u32[]{:S(2)}) async-start(bf16[8,128,1024]{2,1,0:T(8,128)(2,1)} %bitcast.112), calls=%async_computation | async-start | bytes 4194304 | tf_op jit(solution)/shard_map/all_to_all | solution.py:246
  28.7 2.6 %collective-permute-start.7 = (bf16[128,1024]{1,0:T(8,128)(2,1)}, bf16[128,1024]{1,0:T(8,128)(2,1)}, u32[]{:S(2)}, u32[]{:S(2)}) collective-permute-start(bf16[128,1024]{1,0:T(8,128)(2,1)} %bitcast.10), channel_id=1, source_target_pairs={{0,3},{1,0},{2,1},{3,2},{4,7},{5,4},{6,5},{7,6},{8,11},{9,8},{10,9... | collective-permute-start | bytes 786440 | tf_op jit(solution)/shard_map/ppermute | solution.py:185
  32.0 1.1 constant_dynamic-slice_fusion.6
  33.2 3.8 %gather_fusion = bf16[128,1024]{1,0:T(8,128)(2,1)S(1)} fusion(bf16[2048,1024]{1,0:T(8,128)(2,1)} %bitcast.122, s32[1024]{0:T(1024)S(1)} %pad_clamp_fusion), kind=kCustom, calls=%fused_computation | custom fusion | bytes 524800 | tf_op jit(solution)/shard_map/jit(_take)/gather | solution.py:240
  37.1 2.2 %collective-permute-done.7 = bf16[128,1024]{1,0:T(8,128)(2,1)} collective-permute-done((bf16[128,1024]{1,0:T(8,128)(2,1)}, bf16[128,1024]{1,0:T(8,128)(2,1)}, u32[]{:S(2)}, u32[]{:S(2)}) %collective-permute-start.7) | collective-permute-done | bytes 262176 | tf_op jit(solution)/shard_map/ppermute | solution.py:185
  39.3 14.5 %collective-permute-done.6 = bf16[128,1024]{1,0:T(8,128)(2,1)} collective-permute-done((bf16[128,1024]{1,0:T(8,128)(2,1)S(1)}, bf16[128,1024]{1,0:T(8,128)(2,1)}, u32[]{:S(2)}, u32[]{:S(2)}) %collective-permute-start.6) | collective-permute-done | bytes 262176 | tf_op jit(solution)/shard_map/ppermute | solution.py:185
  53.8 1.4 multiply_reduce_fusion.4
  55.5 1.2 collective-permute-start.9
  56.7 0.9 collective-permute-start.11
  57.6 5.9 %collective-permute-done.11 = s32[2,128]{1,0:T(2,128)S(1)} collective-permute-done((s32[2,128]{1,0:T(2,128)S(1)}, s32[2,128]{1,0:T(2,128)S(1)}, u32[]{:S(2)}, u32[]{:S(2)}) %collective-permute-start.11) | collective-permute-done | bytes 1056 | tf_op jit(solution)/shard_map/ppermute | solution.py:188
  63.5 0.8 fusion.36
  64.7 1.1 collective-permute-start.10
  65.8 2.5 %collective-permute-done.10 = f32[2,2,128]{2,1,0:T(2,128)S(1)} collective-permute-done((f32[2,2,128]{2,1,0:T(2,128)S(1)}, f32[2,2,128]{2,1,0:T(2,128)S(1)}, u32[]{:S(2)}, u32[]{:S(2)}) %collective-permute-start.10) | collective-permute-done | bytes 2080 | tf_op jit(solution)/shard_map/ppermute | solution.py:188
  68.8 1.5 %convolution_convert_fusion.1 = bf16[128,1024]{1,0:T(8,128)(2,1)} fusion(bf16[1024,1024]{1,0:T(8,128)(2,1)S(1)} %bitcast.110, bf16[256,1024]{1,0:T(8,128)(2,1)S(1)} %multiply_convert_fusion), kind=kOutput, calls=%fused_computation.6 | convolution fusion | flops 268566528 | bytes 2621440 | tf_op jit(solution)/shard_map/dot_general | solution.py:17
  70.3 1.1 collective-permute-start.12
  71.4 2.1 %convolution_convert_fusion = bf16[1024,1024]{1,0:T(8,128)(2,1)} fusion(bf16[256,1024]{1,0:T(8,128)(2,1)S(1)} %multiply_convert_fusion, bf16[128,1024]{1,0:T(8,128)(2,1)S(1)} %copy-done.9, bf16[128,1024]{1,0:T(8,128)(2,1)S(1)} %copy-done.3), kind=kOutput, calls=%fused_computation.5 | convolution fusion | flops 538968064 | bytes 3145728 | tf_op jit(solution)/shard_map/dot_general | solution.py:17
  73.5 4.3 %all-to-all-start.2 = ((bf16[8,128,1024]{2,1,0:T(8,128)(2,1)}), bf16[8,128,1024]{2,1,0:T(8,128)(2,1)}, u32[]{:S(2)}, u32[]{:S(2)}) async-start(bf16[8,128,1024]{2,1,0:T(8,128)(2,1)} %bitcast.113), calls=%async_computation.2 | async-start | bytes 4194304 | tf_op jit(solution)/shard_map/all_to_all | solution.py:293
  78.6 2.0 %multiply_reduce_fusion.3 = (f32[128]{0:T(128)S(1)}, f32[128]{0:T(128)S(1)}, f32[128]{0:T(128)S(1)}, f32[128,1024]{1,0:T(8,128)S(1)}) fusion(f32[128,1024]{1,0:T(8,128)S(1)} %get-tuple-element.48, bf16[128,1024]{1,0:T(8,128)(2,1)} %collective-permute-done.12, f32[1024]{0:T(1024)S(1)} %bitcast.128, bf16[128,1024]{1,0:T(8,128)(2,1)S(1)} %gather_fusion, ...), kind=kOutput, calls=%fused_computation.18 | convolution fusion | flops 270270080 | bytes 3938433 | tf_op jit(solution)/shard_map/dot_general | solution.py:17
  80.9 1.2 subtract_convert_fusion.refs_0_
  82.5 1.0 collective-permute-start.17
  83.5 3.1 %collective-permute-start.18 = (bf16[128,1024]{1,0:T(8,128)(2,1)S(1)}, bf16[128,1024]{1,0:T(8,128)(2,1)S(1)}, u32[]{:S(2)}, u32[]{:S(2)}) collective-permute-start(bf16[128,1024]{1,0:T(8,128)(2,1)S(1)} %subtract_convert_fusion.refs_0_), channel_id=1, source_target_pairs={{0,2},{1,3},{2,0},{3,1},{4,6},{5,7},{6,4},{7,5},{8,10},{9,11},{10,... | collective-permute-start | bytes 786440 | tf_op jit(solution)/shard_map/ppermute | solution.py:185
  86.6 1.2 collective-permute-start.19
  87.8 0.8 collective-permute-start.14
  88.6 0.9 copy.39.refs_6_
  89.5 14.6 %collective-permute-done.14 = f32[64]{0:T(128)S(1)} collective-permute-done((f32[64]{0:T(128)S(1)}, f32[64]{0:T(128)S(1)}, u32[]{:S(2)}, u32[]{:S(2)}) %collective-permute-start.14) | collective-permute-done | bytes 288 | tf_op jit(solution)/shard_map/ppermute | solution.py:185
  104.1 5.5 %collective-permute-done.15 = f32[64]{0:T(128)S(1)} collective-permute-done((f32[64]{0:T(128)S(1)}, f32[64]{0:T(128)S(1)}, u32[]{:S(2)}, u32[]{:S(2)}) %collective-permute-start.15) | collective-permute-done | bytes 288 | tf_op jit(solution)/shard_map/ppermute | solution.py:185
  111.3 5.1 %shard_map.85 = (bf16[1024,1024]{1,0:T(8,128)(2,1)}, bf16[256,1024]{1,0:T(8,128)(2,1)}, bf16[256,1024]{1,0:T(8,128)(2,1)}) custom-call(s32[2]{0:T(128)} %pad_add_fusion.2.place_ref, bf16[128,1024]{1,0:T(8,128)(2,1)} %copy-done.7, bf16[128,1024]{1,0:T(8,128)(2,1)} %copy-done.14, bf16[128,1024]{1,0:T(8,128)(2,1)} %copy-done.15, bf16[128,1024]{1,0:T(8,128)(2,1)} %copy-done.16, ...), custom_call_target="tpu_custom_call" | custom-call | flops 1073741824 | bytes 2099200 | tf_op jit(solution)/shard_map/pallas_call | solution.py:33
  116.4 4.1 %all-to-all-start.1 = ((bf16[8,128,1024]{2,1,0:T(8,128)(2,1)}), bf16[8,128,1024]{2,1,0:T(8,128)(2,1)S(1)}, u32[]{:S(2)}, u32[]{:S(2)}) async-start(bf16[8,128,1024]{2,1,0:T(8,128)(2,1)} %bitcast.117), calls=%async_computation.1 | async-start | bytes 4194304 | tf_op jit(solution)/shard_map/all_to_all | solution.py:314
  121.1 2.0 %reduce_sum.108 = bf16[2,4,32,1024]{3,2,1,0:T(8,128)(2,1)S(1)} reduce(bf16[4,2,4,32,1024]{4,3,2,1,0:T(8,128)(2,1)} %bitcast.53, bf16[]{:T(256)} %constant.168.clone.1), dimensions={0}, to_apply=%region_10.11 | reduce | flops 786432 | bytes 2621442 | tf_op jit(solution)/shard_map/reduce_sum | solution.py:294
  123.1 0.7 dynamic-slice_bitcast_fusion
  123.8 2.4 %collective-permute-start.21 = (bf16[2,32,1024]{2,1,0:T(8,128)(2,1)S(1)}, bf16[2,32,1024]{2,1,0:T(8,128)(2,1)S(1)}, u32[]{:S(2)}, u32[]{:S(2)}) collective-permute-start(bf16[2,32,1024]{2,1,0:T(8,128)(2,1)S(1)} %get-tuple-element.54), channel_id=1, source_target_pairs={{0,1},{1,2},{2,3},{3,0},{4,5},{5,6},{6,7},{7,4},{8,9},{9,10},{10,1... | collective-permute-start | bytes 393224 | tf_op jit(solution)/shard_map/ppermute | solution.py:185
  126.2 1.5 collective-permute-start.22
  127.7 2.9 %collective-permute-start.23 = (bf16[2,32,1024]{2,1,0:T(8,128)(2,1)S(1)}, bf16[2,32,1024]{2,1,0:T(8,128)(2,1)S(1)}, u32[]{:S(2)}, u32[]{:S(2)}) collective-permute-start(bf16[2,32,1024]{2,1,0:T(8,128)(2,1)S(1)} %get-tuple-element.52), channel_id=1, source_target_pairs={{0,3},{1,0},{2,1},{3,2},{4,7},{5,4},{6,5},{7,6},{8,11},{9,8},{10,9... | collective-permute-start | bytes 393224 | tf_op jit(solution)/shard_map/ppermute | solution.py:185
  130.6 0.9 copy.40.refs_4_
  131.5 0.8 copy-done.6
  132.3 4.9 %shard_map.86 = bf16[256,1024]{1,0:T(8,128)(2,1)} custom-call(s32[2]{0:T(128)} %pad_add_fusion.2.place_ref, bf16[256,1024]{1,0:T(8,128)(2,1)} %get-tuple-element.27.refs_0_, bf16[256,1024]{1,0:T(8,128)(2,1)} %copy-done.6, bf16[2,1024,1024]{2,1,0:T(8,128)(2,1)} %refs_2_.1, bf16[256,1024]{1,0:T(8,128)(2,1)} %refs_3_.1, f32[2,256,1]{2,1,0:T(8,128)} %copy.40.refs_4_), custom_call_target="tpu_custom_call" | custom-call | flops 1073741824 | bytes 5769216 | tf_op jit(solution)/shard_map/pallas_call | solution.py:33
  137.9 2.7 %shard_map.87 = f32[32,2,2048]{2,1,0:T(2,128)} custom-call(s32[2]{0:T(128)} %pad_add_fusion.2.place_ref, bf16[2,32,1024]{2,1,0:T(8,128)(2,1)} %get-tuple-element.55.refs_0_, bf16[2,32,1024]{2,1,0:T(8,128)(2,1)} %copy-done.10, bf16[2,32,1024]{2,1,0:T(8,128)(2,1)} %copy-done.11, bf16[2,32,1024]{2,1,0:T(8,128)(2,1)} %copy-done.12), custom_call_target="tpu_custom_call" | custom-call | flops 262144 | bytes 524288 | tf_op jit(solution)/shard_map/pallas_call | solution.py:33
  140.6 6.5 %all-to-all-done.1 = bf16[8,128,1024]{2,1,0:T(8,128)(2,1)S(1)} async-done(((bf16[8,128,1024]{2,1,0:T(8,128)(2,1)}), bf16[8,128,1024]{2,1,0:T(8,128)(2,1)S(1)}, u32[]{:S(2)}, u32[]{:S(2)}) %all-to-all-start.1) | async-done | bytes 2097184 | tf_op jit(solution)/shard_map/all_to_all | solution.py:314
  147.5 1.3 copy.41
  (124 shorter events, 9.0 us)
Async XLA Ops:
  0.6 9.5 %copy-start = (f32[2,1024]{1,0:T(2,128)S(1)}, f32[2,1024]{1,0:T(2,128)}, u32[]{:S(2)}) copy-start(f32[2,1024]{1,0:T(2,128)} %param.9) | copy-start | bytes 24580
  0.6 9.5 %copy-start.1 = (bf16[256,1024]{1,0:T(8,128)(2,1)S(1)}, bf16[256,1024]{1,0:T(8,128)(2,1)}, u32[]{:S(2)}) copy-start(bf16[256,1024]{1,0:T(8,128)(2,1)} %refs_3_.1) | copy-start | bytes 1572868
  0.7 9.5 %collective-permute-start.1 = (bf16[256,1024]{1,0:T(8,128)(2,1)}, bf16[256,1024]{1,0:T(8,128)(2,1)S(1)}, u32[]{:S(2)}, u32[]{:S(2)}) collective-permute-start(bf16[256,1024]{1,0:T(8,128)(2,1)} %refs_3_.1), channel_id=1, source_target_pairs={{0,4},{4,0},{8,12},{12,8},{16,20},{20,16},{24,28},{28,24},{1,5},{5... | collective-permute-start | bytes 1572872 | tf_op jit(solution)/shard_map/ppermute | solution.py:195
  4.4 11.0 %collective-permute-start.3 = (bf16[72,1024]{1,0:T(8,128)(2,1)S(1)}, bf16[72,1024]{1,0:T(8,128)(2,1)S(1)}, u32[]{:S(2)}, u32[]{:S(2)}) collective-permute-start(bf16[72,1024]{1,0:T(8,128)(2,1)S(1)} %get-tuple-element.59), channel_id=1, source_target_pairs={{0,3},{1,0},{2,1},{3,2},{4,7},{5,4},{6,5},{7,6},{8,11},{9,8},{10,9... | collective-permute-start | bytes 442376 | tf_op jit(solution)/shard_map/ppermute | solution.py:185
  9.1 13.1 %collective-permute-start = (bf16[72,1024]{1,0:T(8,128)(2,1)S(1)}, bf16[72,1024]{1,0:T(8,128)(2,1)S(1)}, u32[]{:S(2)}, u32[]{:S(2)}) collective-permute-start(bf16[72,1024]{1,0:T(8,128)(2,1)S(1)} %get-tuple-element.59), channel_id=1, source_target_pairs={{0,1},{1,2},{2,3},{3,0},{4,5},{5,6},{6,7},{7,4},{8,9},{9,10},{10,1... | collective-permute-start | bytes 442376 | tf_op jit(solution)/shard_map/ppermute | solution.py:185
  9.1 13.1 %collective-permute-start.2 = (bf16[72,1024]{1,0:T(8,128)(2,1)S(1)}, bf16[72,1024]{1,0:T(8,128)(2,1)S(1)}, u32[]{:S(2)}, u32[]{:S(2)}) collective-permute-start(bf16[72,1024]{1,0:T(8,128)(2,1)S(1)} %get-tuple-element.58), channel_id=1, source_target_pairs={{0,2},{1,3},{2,0},{3,1},{4,6},{5,7},{6,4},{7,5},{8,10},{9,11},{10,... | collective-permute-start | bytes 442376 | tf_op jit(solution)/shard_map/ppermute | solution.py:185
  10.1 3.1 %copy-start.5 = (bf16[256,1024]{1,0:T(8,128)(2,1)}, bf16[256,1024]{1,0:T(8,128)(2,1)S(1)}, u32[]{:S(2)}) copy-start(bf16[256,1024]{1,0:T(8,128)(2,1)S(1)} %collective-permute-done.1.refs_5_) | copy-start | bytes 1572868
  13.2 1.3 copy-start.4
  24.1 4.5 %copy-start.13 = (s32[2,64]{1,0:T(2,128)S(1)}, s32[2,64]{1,0:T(2,128)}, u32[]{:S(2)}) copy-start(s32[2,64]{1,0:T(2,128)} %param.11) | copy-start | bytes 1540
  24.1 39.4 %all-to-all-start = ((bf16[8,128,1024]{2,1,0:T(8,128)(2,1)}), bf16[8,128,1024]{2,1,0:T(8,128)(2,1)S(1)}, u32[]{:S(2)}, u32[]{:S(2)}) async-start(bf16[8,128,1024]{2,1,0:T(8,128)(2,1)} %bitcast.112), calls=%async_computation | async-start | bytes 4194304 | tf_op jit(solution)/shard_map/all_to_all | solution.py:246
  28.0 8.9 %collective-permute-start.4 = (f32[256]{0:T(256)S(1)}, f32[256]{0:T(256)S(1)}, u32[]{:S(2)}, u32[]{:S(2)}) collective-permute-start(f32[256]{0:T(256)S(1)} %slice_reduce_fusion), channel_id=1, source_target_pairs={{0,4},{4,0},{8,12},{12,8},{16,20},{20,16},{24,28},{28,24},{1,5},{5... | collective-permute-start | bytes 3080 | tf_op jit(solution)/shard_map/ppermute | solution.py:195
  28.6 4.4 %collective-permute-start.8 = (s32[2,64]{1,0:T(2,128)S(1)}, s32[2,64]{1,0:T(2,128)S(1)}, u32[]{:S(2)}, u32[]{:S(2)}) collective-permute-start(s32[2,64]{1,0:T(2,128)S(1)} %copy-done.13), channel_id=1, source_target_pairs={{0,4},{4,0},{8,12},{12,8},{16,20},{20,16},{24,28},{28,24},{1,5},{5... | collective-permute-start | bytes 1544 | tf_op jit(solution)/shard_map/ppermute | solution.py:195
  28.7 10.6 %collective-permute-start.7 = (bf16[128,1024]{1,0:T(8,128)(2,1)}, bf16[128,1024]{1,0:T(8,128)(2,1)}, u32[]{:S(2)}, u32[]{:S(2)}) collective-permute-start(bf16[128,1024]{1,0:T(8,128)(2,1)} %bitcast.10), channel_id=1, source_target_pairs={{0,3},{1,0},{2,1},{3,2},{4,7},{5,4},{6,5},{7,6},{8,11},{9,8},{10,9... | collective-permute-start | bytes 786440 | tf_op jit(solution)/shard_map/ppermute | solution.py:185
  31.3 22.5 %collective-permute-start.6 = (bf16[128,1024]{1,0:T(8,128)(2,1)S(1)}, bf16[128,1024]{1,0:T(8,128)(2,1)}, u32[]{:S(2)}, u32[]{:S(2)}) collective-permute-start(bf16[128,1024]{1,0:T(8,128)(2,1)S(1)} %bitcast.126), channel_id=1, source_target_pairs={{0,2},{1,3},{2,0},{3,1},{4,6},{5,7},{6,4},{7,5},{8,10},{9,11},{10,... | collective-permute-start | bytes 786440 | tf_op jit(solution)/shard_map/ppermute | solution.py:185
  31.3 22.5 %collective-permute-start.5 = (bf16[128,1024]{1,0:T(8,128)(2,1)S(1)}, bf16[128,1024]{1,0:T(8,128)(2,1)}, u32[]{:S(2)}, u32[]{:S(2)}) collective-permute-start(bf16[128,1024]{1,0:T(8,128)(2,1)S(1)} %bitcast.125), channel_id=1, source_target_pairs={{0,1},{1,2},{2,3},{3,0},{4,5},{5,6},{6,7},{7,4},{8,9},{9,10},{10,1... | collective-permute-start | bytes 786440 | tf_op jit(solution)/shard_map/ppermute | solution.py:185
  55.5 9.2 %copy-start.2 = (bf16[128,1024]{1,0:T(8,128)(2,1)}, bf16[128,1024]{1,0:T(8,128)(2,1)S(1)}, u32[]{:S(2)}) copy-start(bf16[128,1024]{1,0:T(8,128)(2,1)S(1)} %multiply_convert_fusion.1) | copy-start | bytes 786436
  55.5 8.0 %collective-permute-start.9 = (bf16[128,1024]{1,0:T(8,128)(2,1)S(1)}, bf16[128,1024]{1,0:T(8,128)(2,1)S(1)}, u32[]{:S(2)}, u32[]{:S(2)}) collective-permute-start(bf16[128,1024]{1,0:T(8,128)(2,1)S(1)} %multiply_convert_fusion.1), channel_id=1, source_target_pairs={{0,1},{1,0},{2,3},{3,2},{4,5},{5,4},{6,7},{7,6},{8,9},{9,8},{10,11... | collective-permute-start | bytes 786440 | tf_op jit(solution)/shard_map/ppermute | solution.py:188
  56.7 6.8 %collective-permute-start.11 = (s32[2,128]{1,0:T(2,128)S(1)}, s32[2,128]{1,0:T(2,128)S(1)}, u32[]{:S(2)}, u32[]{:S(2)}) collective-permute-start(s32[2,128]{1,0:T(2,128)S(1)} %pad_add_fusion), channel_id=1, source_target_pairs={{0,1},{1,0},{2,3},{3,2},{4,5},{5,4},{6,7},{7,6},{8,9},{9,8},{10,11... | collective-permute-start | bytes 3080 | tf_op jit(solution)/shard_map/ppermute | solution.py:188
  63.5 1.2 copy-start.8
  64.7 3.7 %collective-permute-start.10 = (f32[2,2,128]{2,1,0:T(2,128)S(1)}, f32[2,2,128]{2,1,0:T(2,128)S(1)}, u32[]{:S(2)}, u32[]{:S(2)}) collective-permute-start(f32[2,2,128]{2,1,0:T(2,128)S(1)} %pad_maximum_fusion.6), channel_id=1, source_target_pairs={{0,1},{1,0},{2,3},{3,2},{4,5},{5,4},{6,7},{7,6},{8,9},{9,8},{10,11... | collective-permute-start | bytes 6152 | tf_op jit(solution)/shard_map/ppermute | solution.py:188
  68.4 3.0 %copy-start.3 = (bf16[128,1024]{1,0:T(8,128)(2,1)S(1)}, bf16[128,1024]{1,0:T(8,128)(2,1)}, u32[]{:S(2)}) copy-start(bf16[128,1024]{1,0:T(8,128)(2,1)} %copy-done.2) | copy-start | bytes 786436
  68.4 3.0 %copy-start.9 = (bf16[128,1024]{1,0:T(8,128)(2,1)S(1)}, bf16[128,1024]{1,0:T(8,128)(2,1)}, u32[]{:S(2)}) copy-start(bf16[128,1024]{1,0:T(8,128)(2,1)} %copy-done.8) | copy-start | bytes 786436
  70.3 8.3 %collective-permute-start.12 = (bf16[128,1024]{1,0:T(8,128)(2,1)}, bf16[128,1024]{1,0:T(8,128)(2,1)}, u32[]{:S(2)}, u32[]{:S(2)}) collective-permute-start(bf16[128,1024]{1,0:T(8,128)(2,1)} %convolution_convert_fusion.1), channel_id=1, source_target_pairs={{0,1},{1,0},{2,3},{3,2},{4,5},{5,4},{6,7},{7,6},{8,9},{9,8},{10,11... | collective-permute-start | bytes 786440 | tf_op jit(solution)/shard_map/ppermute | solution.py:188
  73.5 42.9 %all-to-all-start.2 = ((bf16[8,128,1024]{2,1,0:T(8,128)(2,1)}), bf16[8,128,1024]{2,1,0:T(8,128)(2,1)}, u32[]{:S(2)}, u32[]{:S(2)}) async-start(bf16[8,128,1024]{2,1,0:T(8,128)(2,1)} %bitcast.113), calls=%async_computation.2 | async-start | bytes 4194304 | tf_op jit(solution)/shard_map/all_to_all | solution.py:293
  82.1 27.7 %copy-start.7 = (bf16[128,1024]{1,0:T(8,128)(2,1)}, bf16[128,1024]{1,0:T(8,128)(2,1)S(1)}, u32[]{:S(2)}) copy-start(bf16[128,1024]{1,0:T(8,128)(2,1)S(1)} %subtract_convert_fusion.refs_0_) | copy-start | bytes 786436
  82.2 5.6 %collective-permute-start.13 = (f32[64]{0:T(128)S(1)}, f32[64]{0:T(128)S(1)}, u32[]{:S(2)}, u32[]{:S(2)}) collective-permute-start(f32[64]{0:T(128)S(1)} %slice_bitcast_fusion), channel_id=1, source_target_pairs={{0,4},{4,0},{8,12},{12,8},{16,20},{20,16},{24,28},{28,24},{1,5},{5... | collective-permute-start | bytes 776 | tf_op jit(solution)/shard_map/ppermute | solution.py:195
  82.5 27.3 %collective-permute-start.17 = (bf16[128,1024]{1,0:T(8,128)(2,1)S(1)}, bf16[128,1024]{1,0:T(8,128)(2,1)S(1)}, u32[]{:S(2)}, u32[]{:S(2)}) collective-permute-start(bf16[128,1024]{1,0:T(8,128)(2,1)S(1)} %subtract_convert_fusion.refs_0_), channel_id=1, source_target_pairs={{0,1},{1,2},{2,3},{3,0},{4,5},{5,6},{6,7},{7,4},{8,9},{9,10},{10,1... | collective-permute-start | bytes 786440 | tf_op jit(solution)/shard_map/ppermute | solution.py:185
  83.5 26.3 %collective-permute-start.18 = (bf16[128,1024]{1,0:T(8,128)(2,1)S(1)}, bf16[128,1024]{1,0:T(8,128)(2,1)S(1)}, u32[]{:S(2)}, u32[]{:S(2)}) collective-permute-start(bf16[128,1024]{1,0:T(8,128)(2,1)S(1)} %subtract_convert_fusion.refs_0_), channel_id=1, source_target_pairs={{0,2},{1,3},{2,0},{3,1},{4,6},{5,7},{6,4},{7,5},{8,10},{9,11},{10,... | collective-permute-start | bytes 786440 | tf_op jit(solution)/shard_map/ppermute | solution.py:185
  86.6 23.3 %collective-permute-start.19 = (bf16[128,1024]{1,0:T(8,128)(2,1)S(1)}, bf16[128,1024]{1,0:T(8,128)(2,1)S(1)}, u32[]{:S(2)}, u32[]{:S(2)}) collective-permute-start(bf16[128,1024]{1,0:T(8,128)(2,1)S(1)} %subtract_convert_fusion.refs_0_), channel_id=1, source_target_pairs={{0,3},{1,0},{2,1},{3,2},{4,7},{5,4},{6,5},{7,6},{8,11},{9,8},{10,9... | collective-permute-start | bytes 786440 | tf_op jit(solution)/shard_map/ppermute | solution.py:185
  87.8 16.3 %collective-permute-start.14 = (f32[64]{0:T(128)S(1)}, f32[64]{0:T(128)S(1)}, u32[]{:S(2)}, u32[]{:S(2)}) collective-permute-start(f32[64]{0:T(128)S(1)} %bitcast_add_fusion.1), channel_id=1, source_target_pairs={{0,1},{1,2},{2,3},{3,0},{4,5},{5,6},{6,7},{7,4},{8,9},{9,10},{10,1... | collective-permute-start | bytes 776 | tf_op jit(solution)/shard_map/ppermute | solution.py:185
  89.5 20.1 %collective-permute-start.15 = (f32[64]{0:T(128)S(1)}, f32[64]{0:T(128)S(1)}, u32[]{:S(2)}, u32[]{:S(2)}) collective-permute-start(f32[64]{0:T(128)S(1)} %bitcast_add_fusion.1), channel_id=1, source_target_pairs={{0,2},{1,3},{2,0},{3,1},{4,6},{5,7},{6,4},{7,5},{8,10},{9,11},{10,... | collective-permute-start | bytes 776 | tf_op jit(solution)/shard_map/ppermute | solution.py:185
  104.1 5.7 %collective-permute-start.16 = (f32[64]{0:T(128)S(1)}, f32[64]{0:T(128)S(1)}, u32[]{:S(2)}, u32[]{:S(2)}) collective-permute-start(f32[64]{0:T(128)S(1)} %bitcast_add_fusion.1), channel_id=1, source_target_pairs={{0,3},{1,0},{2,1},{3,2},{4,7},{5,4},{6,5},{7,6},{8,11},{9,8},{10,9... | collective-permute-start | bytes 776 | tf_op jit(solution)/shard_map/ppermute | solution.py:185
  109.8 0.7 copy-start.14
  109.8 0.8 copy-start.15
  110.6 0.7 copy-start.16
  116.4 30.7 %all-to-all-start.1 = ((bf16[8,128,1024]{2,1,0:T(8,128)(2,1)}), bf16[8,128,1024]{2,1,0:T(8,128)(2,1)S(1)}, u32[]{:S(2)}, u32[]{:S(2)}) async-start(bf16[8,128,1024]{2,1,0:T(8,128)(2,1)} %bitcast.117), calls=%async_computation.1 | async-start | bytes 4194304 | tf_op jit(solution)/shard_map/all_to_all | solution.py:314
  120.5 11.0 %collective-permute-start.20 = (bf16[256,1024]{1,0:T(8,128)(2,1)}, bf16[256,1024]{1,0:T(8,128)(2,1)S(1)}, u32[]{:S(2)}, u32[]{:S(2)}) collective-permute-start(bf16[256,1024]{1,0:T(8,128)(2,1)} %get-tuple-element.28), channel_id=1, source_target_pairs={{0,4},{4,0},{8,12},{12,8},{16,20},{20,16},{24,28},{28,24},{1,5},{5... | collective-permute-start | bytes 1572872 | tf_op jit(solution)/shard_map/ppermute | solution.py:195
  123.8 13.4 %collective-permute-start.21 = (bf16[2,32,1024]{2,1,0:T(8,128)(2,1)S(1)}, bf16[2,32,1024]{2,1,0:T(8,128)(2,1)S(1)}, u32[]{:S(2)}, u32[]{:S(2)}) collective-permute-start(bf16[2,32,1024]{2,1,0:T(8,128)(2,1)S(1)} %get-tuple-element.54), channel_id=1, source_target_pairs={{0,1},{1,2},{2,3},{3,0},{4,5},{5,6},{6,7},{7,4},{8,9},{9,10},{10,1... | collective-permute-start | bytes 393224 | tf_op jit(solution)/shard_map/ppermute | solution.py:185
  126.2 11.0 %collective-permute-start.22 = (bf16[2,32,1024]{2,1,0:T(8,128)(2,1)S(1)}, bf16[2,32,1024]{2,1,0:T(8,128)(2,1)S(1)}, u32[]{:S(2)}, u32[]{:S(2)}) collective-permute-start(bf16[2,32,1024]{2,1,0:T(8,128)(2,1)S(1)} %get-tuple-element.53), channel_id=1, source_target_pairs={{0,2},{1,3},{2,0},{3,1},{4,6},{5,7},{6,4},{7,5},{8,10},{9,11},{10,... | collective-permute-start | bytes 393224 | tf_op jit(solution)/shard_map/ppermute | solution.py:185
  127.7 9.5 %collective-permute-start.23 = (bf16[2,32,1024]{2,1,0:T(8,128)(2,1)S(1)}, bf16[2,32,1024]{2,1,0:T(8,128)(2,1)S(1)}, u32[]{:S(2)}, u32[]{:S(2)}) collective-permute-start(bf16[2,32,1024]{2,1,0:T(8,128)(2,1)S(1)} %get-tuple-element.52), channel_id=1, source_target_pairs={{0,3},{1,0},{2,1},{3,2},{4,7},{5,4},{6,5},{7,6},{8,11},{9,8},{10,9... | collective-permute-start | bytes 393224 | tf_op jit(solution)/shard_map/ppermute | solution.py:185
  131.5 0.8 copy-start.6
  137.2 0.7 copy-start.10
  137.2 0.7 copy-start.11
  137.2 0.7 copy-start.12

commit v12 on v9

--- a/solution.py
+++ b/solution.py
@@ -87,9 +87,9 @@
 
 def input_gradient(place, pieces, group, ratio, seqs):
     hids, steps = len(pieces), len(group)
-    owned, depth = pieces[0].shape
+    taller, depth = pieces[0].shape
     rows, units = group[0].shape
-    part = owned // steps
+    part = rows // hids
     wide = min(512, depth)
 
     def kernel(place_ref, *refs):
@@ -115,7 +115,7 @@
         kernel,
         place,
         depth // wide,
-        [pl.BlockSpec((owned, wide), lambda n, place: (0, n))] * hids
+        [pl.BlockSpec((taller, wide), lambda n, place: (0, n))] * hids
         + [whole((rows, units))] * steps
         + [whole((steps, rows, 1))],
         [pl.BlockSpec((wide, units), lambda n, place: (n, 0))]
@@ -289,7 +289,7 @@
     d_ratio_part = (scale * gated_proj - back_scale * x_proj).reshape(steps, part)
 
     part_out = matmul(normed_rows, after(d_logit, *away), ((0,), (0,))).astype(BF16)
-    part_out = after(part_out, *received).reshape(seqs, depth // seqs, block)
+    part_out = part_out.reshape(seqs, depth // seqs, block)
     part_out = lax.all_to_all(part_out, "seq", 0, 0)
     part_out = part_out.reshape(groups, steps, hids, head_rows, block).astype(F32).sum(0)
     part_out = part_out.astype(BF16)
@@ -299,21 +299,22 @@
     sums = [along_hid(p, shift) if shift else p for shift, p in enumerate(sums)]
     grad_out = head_gradient(place, sums, halves)
 
-    pieces = [d_round] + [along_hid(d_round, shift) for shift in range(1, hids)]
+    below = jnp.concatenate(parts_of(d_ratio_part.reshape(owned)))
+    below = jnp.pad(below, (0, 8 * depth - below.size)).reshape(8, depth)
+    payload = jnp.concatenate([d_round, below])
+    pieces = [payload] + [along_hid(payload, shift) for shift in range(1, hids)]
     ratio_rows = ratio_group.reshape(steps, rows, 1)
     share, mine, *others = input_gradient(place, pieces, group, ratio_rows, seqs)
     share = lax.all_to_all(share.reshape(seqs, depth // seqs, units), "seq", 0, 0)
     share = share.reshape(groups, steps, depth // seqs, units).astype(F32).sum(0)
     grad_in = share.transpose(0, 2, 1)
 
-    d_ratio = d_ratio_part[0]
+    shares = [p[owned:].reshape(-1)[: EXACT * owned].reshape(EXACT, steps, part) for p in pieces]
+    shares = [jnp.sum(p.astype(F32), axis=0) for p in shares]
+    shares = lax.dynamic_slice_in_dim(jnp.stack(shares[::-1] * 2), hids - 1 - j, hids, 0)
+    d_rows = shares[:, 0]
     for m in relations:
-        d_ratio += flip_seq(d_ratio_part[m], m)
-    d_rows = jnp.broadcast_to(d_ratio, (hids, part))
-    for shift in range(1, hids):
-        d_rows = lax.dynamic_update_index_in_dim(
-            d_rows, along_hid(d_ratio, shift), (j - shift) % hids, 0
-        )
+        d_rows += flip_seq(shares[:, m], m)
     ratio_own = ratio_group[0].reshape(rows)
     correction = ratio_own**3 * d_rows.reshape(rows) / width_in
     factors = jnp.stack([ratio_own, correction])[:, :, None]

time: 150 us -> 154 us (1.027)
  waiting for transfers between devices: 55.1 us -> 68.9 us
  starting transfers between devices: 45.3 us -> 31.9 us
  other arithmetic: 8.24 us -> 9.79 us
    ppermute x15 -> x12, starting transfers between devices: 27.2 us -> 15.2 us  [along_hid(): lax.ppermute(values, 'hid', [(a, (a + shift) % hids) for a in range(hids)])]
    ppermute x15 -> x12, waiting for transfers between devices: 42.6 us -> 53.5 us  [along_hid(): lax.ppermute(values, 'hid', [(a, (a + shift) % hids) for a in range(hids)])]
    all_to_all x1, waiting for transfers between devices: 0.01 us -> 6.24 us  [shards(): lax.all_to_all(share.reshape(seqs, depth // seqs, units), 'seq', 0, 0)]
    ppermute x4, waiting for transfers between devices: 11.7 us -> 8.23 us  [turn_hid(): lax.ppermute(values, 'hid', [(a, a - a % halves + (a % halves + shift) %...]
    ppermute x4, starting transfers between devices: 4.35 us -> 2.71 us  [turn_hid(): lax.ppermute(values, 'hid', [(a, a - a % halves + (a % halves + shift) %...]
    unnamed x44 -> x55, local copies, waits for them, and re-layouts: 5.76 us -> 5.98 us
  transfers between devices with their start and end apart: 27 -> 24, of which waited for: 13 -> 11; matrix products, arithmetic and copies ran while one was open for 17% -> 17% of each run, Pallas kernels for 9% -> 8%
where the time goes in v12:
time: 154 us; the launch traced here: 153 us
  waiting for transfers between devices  68.9 us (45%)
  starting transfers between devices  31.9 us (21%)
  local copies, waits for them, and re-layouts  18.6 us (12%)
  Pallas kernels  12.7 us (8%)
  matrix products  10.1 us (7%)
  other arithmetic  9.79 us (6%)
    ppermute x12, waiting for transfers between devices, along_hid(): lax.ppermute(values, 'hid', [(a, (a + shift) % hids) for a in range(hids)])  53.5 us
    ppermute x12, starting transfers between devices, along_hid(): lax.ppermute(values, 'hid', [(a, (a + shift) % hids) for a in range(hids)])  15.2 us
    pallas_call x3, Pallas kernels, call(): pl.pallas_call(kernel, grid_spec=pltpu.PrefetchScalarGridSpec(num_scalar_...  12.7 us
    dot_general x5, matrix products, matmul(): lax.dot_general(a, b, (contract, ((), ())), preferred_element_type=F32)  10.1 us
    ppermute x4, waiting for transfers between devices, turn_hid(): lax.ppermute(values, 'hid', [(a, a - a % halves + (a % halves + shift) %...  8.23 us
    all_to_all x1, waiting for transfers between devices, shards(): lax.all_to_all(share.reshape(seqs, depth // seqs, units), 'seq', 0, 0)  6.24 us
    unnamed x55, local copies, waits for them, and re-layouts  5.98 us
    all_to_all x1, starting transfers between devices, shards(): part_out = lax.all_to_all(part_out, 'seq', 0, 0)  4.47 us
  transfers between devices with their start and end apart: 24, of which 11 were waited for; matrix products, arithmetic and copies ran while one was open for 17% of the time, Pallas kernels for 8%

profile of v12, /device:TPU:0, one launch (start us, length us, event | category | flops | bytes accessed | tf_op | source)
XLA Modules:
  0.0 153.2 jit_solution(6384070248911667623)
XLA Ops:
  1.2 1.2 multiply_reduce_fusion
  2.4 1.1 reshape.370
  4.3 4.7 %collective-permute-start.3 = (bf16[72,1024]{1,0:T(8,128)(2,1)S(1)}, bf16[72,1024]{1,0:T(8,128)(2,1)S(1)}, u32[]{:S(2)}, u32[]{:S(2)}) collective-permute-start(bf16[72,1024]{1,0:T(8,128)(2,1)S(1)} %get-tuple-element.59), channel_id=1, source_target_pairs={{0,3},{1,0},{2,1},{3,2},{4,7},{5,4},{6,5},{7,6},{8,11},{9,8},{10,9... | collective-permute-start | bytes 442376 | tf_op jit(solution)/shard_map/ppermute | solution.py:185
  9.1 1.0 collective-permute-start.2
  10.1 0.7 pad_add_fusion.2.place_ref
  10.9 3.0 %fusion = f32[2,4,64,1024]{3,2,1,0:T(8,128)S(1)} fusion(bf16[2,4,64,1024]{3,2,1,0:T(8,128)(2,1)S(1)} %bitcast.132, bf16[2,1024,1024]{2,1,0:T(8,128)(2,1)} %refs_2_.1, s32[]{:T(128)S(6)} %select_n.118), kind=kOutput, calls=%fused_computation.2 | convolution fusion | flops 1073741824 | bytes 5242884 | tf_op jit(solution)/shard_map/dot_general | solution.py:17
  13.9 1.3 copy-done.6
  15.2 0.9 dynamic-slice_convert_fusion
  16.1 6.1 %collective-permute-done.2 = bf16[72,1024]{1,0:T(8,128)(2,1)S(1)} collective-permute-done((bf16[72,1024]{1,0:T(8,128)(2,1)S(1)}, bf16[72,1024]{1,0:T(8,128)(2,1)S(1)}, u32[]{:S(2)}, u32[]{:S(2)}) %collective-permute-start.2) | collective-permute-done | bytes 147488 | tf_op jit(solution)/shard_map/ppermute | solution.py:185
  22.5 1.6 %broadcast_in_dim.32 = bf16[4,2,128,1024]{3,2,1,0:T(8,128)(2,1)} broadcast(bf16[2,128,1024]{2,1,0:T(8,128)(2,1)S(1)} %bitcast.125), dimensions={1,2,3} | broadcast | bytes 2621440 | tf_op jit(solution)/shard_map/broadcast_in_dim | solution.py:244
  24.1 3.9 %all-to-all-start = ((bf16[8,128,1024]{2,1,0:T(8,128)(2,1)}), bf16[8,128,1024]{2,1,0:T(8,128)(2,1)S(1)}, u32[]{:S(2)}, u32[]{:S(2)}) async-start(bf16[8,128,1024]{2,1,0:T(8,128)(2,1)} %bitcast.121), calls=%async_computation | async-start | bytes 4194304 | tf_op jit(solution)/shard_map/all_to_all | solution.py:246
  28.6 1.1 constant_dynamic-slice_fusion.8
  29.8 3.8 %collective-permute-start.7 = (bf16[128,1024]{1,0:T(8,128)(2,1)}, bf16[128,1024]{1,0:T(8,128)(2,1)}, u32[]{:S(2)}, u32[]{:S(2)}) collective-permute-start(bf16[128,1024]{1,0:T(8,128)(2,1)} %bitcast.10), channel_id=1, source_target_pairs={{0,3},{1,0},{2,1},{3,2},{4,7},{5,4},{6,5},{7,6},{8,11},{9,8},{10,9... | collective-permute-start | bytes 786440 | tf_op jit(solution)/shard_map/ppermute | solution.py:185
  33.7 3.8 %gather_fusion = bf16[128,1024]{1,0:T(8,128)(2,1)S(1)} fusion(bf16[2048,1024]{1,0:T(8,128)(2,1)} %bitcast.131, s32[1024]{0:T(1024)S(1)} %pad_clamp_fusion), kind=kCustom, calls=%fused_computation | custom fusion | bytes 524800 | tf_op jit(solution)/shard_map/jit(_take)/gather | solution.py:240
  37.7 3.4 %collective-permute-done.5 = bf16[128,1024]{1,0:T(8,128)(2,1)} collective-permute-done((bf16[128,1024]{1,0:T(8,128)(2,1)}, bf16[128,1024]{1,0:T(8,128)(2,1)}, u32[]{:S(2)}, u32[]{:S(2)}) %collective-permute-start.5) | collective-permute-done | bytes 262176 | tf_op jit(solution)/shard_map/ppermute | solution.py:185
  41.1 3.4 %collective-permute-done.7 = bf16[128,1024]{1,0:T(8,128)(2,1)} collective-permute-done((bf16[128,1024]{1,0:T(8,128)(2,1)}, bf16[128,1024]{1,0:T(8,128)(2,1)}, u32[]{:S(2)}, u32[]{:S(2)}) %collective-permute-start.7) | collective-permute-done | bytes 262176 | tf_op jit(solution)/shard_map/ppermute | solution.py:185
  44.4 12.3 %collective-permute-done.6 = bf16[128,1024]{1,0:T(8,128)(2,1)} collective-permute-done((bf16[128,1024]{1,0:T(8,128)(2,1)S(1)}, bf16[128,1024]{1,0:T(8,128)(2,1)}, u32[]{:S(2)}, u32[]{:S(2)}) %collective-permute-start.6) | collective-permute-done | bytes 262176 | tf_op jit(solution)/shard_map/ppermute | solution.py:185
  56.7 1.4 multiply_reduce_fusion.4
  58.5 2.0 %collective-permute-start.11 = (s32[2,128]{1,0:T(2,128)S(1)}, s32[2,128]{1,0:T(2,128)S(1)}, u32[]{:S(2)}, u32[]{:S(2)}) collective-permute-start(s32[2,128]{1,0:T(2,128)S(1)} %pad_add_fusion), channel_id=1, source_target_pairs={{0,1},{1,0},{2,3},{3,2},{4,5},{5,4},{6,7},{7,6},{8,9},{9,8},{10,11... | collective-permute-start | bytes 3080 | tf_op jit(solution)/shard_map/ppermute | solution.py:188
  60.5 0.9 copy.44.refs_6_
  61.4 5.0 %collective-permute-done.11 = s32[2,128]{1,0:T(2,128)S(1)} collective-permute-done((s32[2,128]{1,0:T(2,128)S(1)}, s32[2,128]{1,0:T(2,128)S(1)}, u32[]{:S(2)}, u32[]{:S(2)}) %collective-permute-start.11) | collective-permute-done | bytes 1056 | tf_op jit(solution)/shard_map/ppermute | solution.py:188
  66.4 0.8 fusion.46
  67.3 1.0 copy-done.3
  69.0 3.2 %collective-permute-done.10 = f32[2,2,128]{2,1,0:T(2,128)S(1)} collective-permute-done((f32[2,2,128]{2,1,0:T(2,128)S(1)}, f32[2,2,128]{2,1,0:T(2,128)S(1)}, u32[]{:S(2)}, u32[]{:S(2)}) %collective-permute-start.10) | collective-permute-done | bytes 2080 | tf_op jit(solution)/shard_map/ppermute | solution.py:188
  72.3 1.6 %multiply_convert_fusion = bf16[256,1024]{1,0:T(8,128)(2,1)S(1)} fusion(f32[256,1024]{1,0:T(8,128)} %copy-done.3, s32[1024]{0:T(1024)S(1)} %iota_add_fusion, f32[256]{0:T(256)S(1)} %log_add_fusion, s32[256]{0:T(256)S(1)} %pad_add_fusion.1), kind=kLoop, calls=%fused_computation.8 | loop fusion | flops 1572864 | bytes 1579008 | tf_op jit(solution)/shard_map/convert_element_type | solution.py:275
  74.0 1.5 %convolution_convert_fusion.1 = bf16[128,1024]{1,0:T(8,128)(2,1)} fusion(bf16[1024,1024]{1,0:T(8,128)(2,1)S(1)} %bitcast.119, bf16[256,1024]{1,0:T(8,128)(2,1)S(1)} %multiply_convert_fusion), kind=kOutput, calls=%fused_computation.6 | convolution fusion | flops 268566528 | bytes 2621440 | tf_op jit(solution)/shard_map/dot_general | solution.py:17
  75.8 2.1 %convolution_convert_fusion = bf16[1024,1024]{1,0:T(8,128)(2,1)} fusion(bf16[256,1024]{1,0:T(8,128)(2,1)S(1)} %multiply_convert_fusion, bf16[128,1024]{1,0:T(8,128)(2,1)S(1)} %copy-done.11, bf16[128,1024]{1,0:T(8,128)(2,1)S(1)} %copy-done.5), kind=kOutput, calls=%fused_computation.5 | convolution fusion | flops 538968064 | bytes 3145728 | tf_op jit(solution)/shard_map/dot_general | solution.py:17
  77.9 4.5 %all-to-all-start.2 = ((bf16[8,128,1024]{2,1,0:T(8,128)(2,1)}), bf16[8,128,1024]{2,1,0:T(8,128)(2,1)}, u32[]{:S(2)}, u32[]{:S(2)}) async-start(bf16[8,128,1024]{2,1,0:T(8,128)(2,1)} %bitcast.123), calls=%async_computation.2 | async-start | bytes 4194304 | tf_op jit(solution)/shard_map/all_to_all | solution.py:293
  82.4 2.7 %multiply_reduce_fusion.3 = (f32[128]{0:T(128)S(1)}, f32[128]{0:T(128)S(1)}, f32[128]{0:T(128)S(1)}, f32[128,1024]{1,0:T(8,128)}) fusion(bf16[128,1024]{1,0:T(8,128)(2,1)} %collective-permute-done.12, f32[1024]{0:T(1024)S(1)} %bitcast.136, bf16[128,1024]{1,0:T(8,128)(2,1)S(1)} %gather_fusion, pred[128]{0:T(512)(128)(4,1)S(1)} %compare_and_fusion, ...), kind=kOutput, calls=%fused_computation.18 | convolution fusion | flops 270270080 | bytes 3938433 | tf_op jit(solution)/shard_map/dot_general | solution.py:17
  85.3 1.4 subtract_convert_fusion
  86.7 0.7 collective-permute-start.15
  87.4 2.6 %collective-permute-start.14 = (bf16[136,1024]{1,0:T(8,128)(2,1)S(1)}, bf16[136,1024]{1,0:T(8,128)(2,1)S(1)}, u32[]{:S(2)}, u32[]{:S(2)}) collective-permute-start(bf16[136,1024]{1,0:T(8,128)(2,1)S(1)} %pad_maximum_fusion.4.refs_0_), channel_id=1, source_target_pairs={{0,2},{1,3},{2,0},{3,1},{4,6},{5,7},{6,4},{7,5},{8,10},{9,11},{10,... | collective-permute-start | bytes 835592 | tf_op jit(solution)/shard_map/ppermute | solution.py:185
  90.1 5.6 %collective-permute-done.15.refs_3_ = bf16[136,1024]{1,0:T(8,128)(2,1)S(1)} collective-permute-done((bf16[136,1024]{1,0:T(8,128)(2,1)S(1)}, bf16[136,1024]{1,0:T(8,128)(2,1)S(1)}, u32[]{:S(2)}, u32[]{:S(2)}) %collective-permute-start.15) | collective-permute-done | bytes 278560 | tf_op jit(solution)/shard_map/ppermute | solution.py:185
  95.8 19.0 %collective-permute-done.14.refs_2_ = bf16[136,1024]{1,0:T(8,128)(2,1)S(1)} collective-permute-done((bf16[136,1024]{1,0:T(8,128)(2,1)S(1)}, bf16[136,1024]{1,0:T(8,128)(2,1)S(1)}, u32[]{:S(2)}, u32[]{:S(2)}) %collective-permute-start.14) | collective-permute-done | bytes 278560 | tf_op jit(solution)/shard_map/ppermute | solution.py:185
  115.6 5.1 %shard_map.85 = (bf16[1024,1024]{1,0:T(8,128)(2,1)}, bf16[256,1024]{1,0:T(8,128)(2,1)}, bf16[256,1024]{1,0:T(8,128)(2,1)}) custom-call(s32[2]{0:T(128)} %pad_add_fusion.2.place_ref, bf16[136,1024]{1,0:T(8,128)(2,1)} %copy-done.9, bf16[136,1024]{1,0:T(8,128)(2,1)} %copy-done.18, bf16[136,1024]{1,0:T(8,128)(2,1)} %copy-done.17, bf16[136,1024]{1,0:T(8,128)(2,1)} %copy-done.16, ...), custom_call_target="tpu_custom_call" | custom-call | flops 1073741824 | bytes 2164736 | tf_op jit(solution)/shard_map/pallas_call | solution.py:33
  120.9 4.0 %all-to-all-start.1 = ((bf16[8,128,1024]{2,1,0:T(8,128)(2,1)}), bf16[8,128,1024]{2,1,0:T(8,128)(2,1)S(1)}, u32[]{:S(2)}, u32[]{:S(2)}) async-start(bf16[8,128,1024]{2,1,0:T(8,128)(2,1)} %bitcast.126), calls=%async_computation.1 | async-start | bytes 4194304 | tf_op jit(solution)/shard_map/all_to_all | solution.py:308
  125.5 0.9 collective-permute-done.17
  126.5 2.0 %reduce_sum.148 = bf16[2,4,32,1024]{3,2,1,0:T(8,128)(2,1)S(1)} reduce(bf16[4,2,4,32,1024]{4,3,2,1,0:T(8,128)(2,1)} %bitcast.54, bf16[]{:T(256)} %constant.145.clone.1), dimensions={0}, to_apply=%region_14.15 | reduce | flops 786432 | bytes 2621442 | tf_op jit(solution)/shard_map/reduce_sum | solution.py:294
  128.5 0.7 dynamic-slice_bitcast_fusion
  129.5 2.0 %collective-permute-start.18 = (bf16[2,32,1024]{2,1,0:T(8,128)(2,1)S(1)}, bf16[2,32,1024]{2,1,0:T(8,128)(2,1)S(1)}, u32[]{:S(2)}, u32[]{:S(2)}) collective-permute-start(bf16[2,32,1024]{2,1,0:T(8,128)(2,1)S(1)} %get-tuple-element.54), channel_id=1, source_target_pairs={{0,1},{1,2},{2,3},{3,0},{4,5},{5,6},{6,7},{7,4},{8,9},{9,10},{10,1... | collective-permute-start | bytes 393224 | tf_op jit(solution)/shard_map/ppermute | solution.py:185
  131.5 0.9 copy.46.refs_4_
  132.4 0.8 copy-done.8
  133.2 4.9 %shard_map.86 = bf16[256,1024]{1,0:T(8,128)(2,1)} custom-call(s32[2]{0:T(128)} %pad_add_fusion.2.place_ref, bf16[256,1024]{1,0:T(8,128)(2,1)} %get-tuple-element.23.refs_0_, bf16[256,1024]{1,0:T(8,128)(2,1)} %copy-done.8, bf16[2,1024,1024]{2,1,0:T(8,128)(2,1)} %refs_2_.1, bf16[256,1024]{1,0:T(8,128)(2,1)} %refs_3_.1, f32[2,256,1]{2,1,0:T(8,128)} %copy.46.refs_4_), custom_call_target="tpu_custom_call" | custom-call | flops 1073741824 | bytes 5769216 | tf_op jit(solution)/shard_map/pallas_call | solution.py:33
  138.1 3.8 %collective-permute-done.19.refs_2_ = bf16[2,32,1024]{2,1,0:T(8,128)(2,1)S(1)} collective-permute-done((bf16[2,32,1024]{2,1,0:T(8,128)(2,1)S(1)}, bf16[2,32,1024]{2,1,0:T(8,128)(2,1)S(1)}, u32[]{:S(2)}, u32[]{:S(2)}) %collective-permute-start.19) | collective-permute-done | bytes 131104 | tf_op jit(solution)/shard_map/ppermute | solution.py:185
  141.9 0.6 copy-done.13
  142.6 2.7 %shard_map.87 = f32[32,2,2048]{2,1,0:T(2,128)} custom-call(s32[2]{0:T(128)} %pad_add_fusion.2.place_ref, bf16[2,32,1024]{2,1,0:T(8,128)(2,1)} %get-tuple-element.55.refs_0_, bf16[2,32,1024]{2,1,0:T(8,128)(2,1)} %copy-done.14, bf16[2,32,1024]{2,1,0:T(8,128)(2,1)} %copy-done.13, bf16[2,32,1024]{2,1,0:T(8,128)(2,1)} %copy-done.12), custom_call_target="tpu_custom_call" | custom-call | flops 262144 | bytes 524288 | tf_op jit(solution)/shard_map/pallas_call | solution.py:33
  145.2 6.2 %all-to-all-done.1 = bf16[8,128,1024]{2,1,0:T(8,128)(2,1)S(1)} async-done(((bf16[8,128,1024]{2,1,0:T(8,128)(2,1)}), bf16[8,128,1024]{2,1,0:T(8,128)(2,1)S(1)}, u32[]{:S(2)}, u32[]{:S(2)}) %all-to-all-start.1) | async-done | bytes 2097184 | tf_op jit(solution)/shard_map/all_to_all | solution.py:308
  151.9 1.3 copy.47
  (142 shorter events, 6.9 us)
Async XLA Ops:
  0.6 10.1 %copy-start = (f32[2,1024]{1,0:T(2,128)S(1)}, f32[2,1024]{1,0:T(2,128)}, u32[]{:S(2)}) copy-start(f32[2,1024]{1,0:T(2,128)} %param.9) | copy-start | bytes 24580
  0.6 10.1 %copy-start.2 = (bf16[256,1024]{1,0:T(8,128)(2,1)S(1)}, bf16[256,1024]{1,0:T(8,128)(2,1)}, u32[]{:S(2)}) copy-start(bf16[256,1024]{1,0:T(8,128)(2,1)} %refs_3_.1) | copy-start | bytes 1572868
  0.7 10.1 %collective-permute-start.1 = (bf16[256,1024]{1,0:T(8,128)(2,1)}, bf16[256,1024]{1,0:T(8,128)(2,1)S(1)}, u32[]{:S(2)}, u32[]{:S(2)}) collective-permute-start(bf16[256,1024]{1,0:T(8,128)(2,1)} %refs_3_.1), channel_id=1, source_target_pairs={{0,4},{4,0},{8,12},{12,8},{16,20},{20,16},{24,28},{28,24},{1,5},{5... | collective-permute-start | bytes 1572872 | tf_op jit(solution)/shard_map/ppermute | solution.py:195
  4.3 11.7 %collective-permute-start.3 = (bf16[72,1024]{1,0:T(8,128)(2,1)S(1)}, bf16[72,1024]{1,0:T(8,128)(2,1)S(1)}, u32[]{:S(2)}, u32[]{:S(2)}) collective-permute-start(bf16[72,1024]{1,0:T(8,128)(2,1)S(1)} %get-tuple-element.59), channel_id=1, source_target_pairs={{0,3},{1,0},{2,1},{3,2},{4,7},{5,4},{6,5},{7,6},{8,11},{9,8},{10,9... | collective-permute-start | bytes 442376 | tf_op jit(solution)/shard_map/ppermute | solution.py:185
  9.1 13.1 %collective-permute-start = (bf16[72,1024]{1,0:T(8,128)(2,1)S(1)}, bf16[72,1024]{1,0:T(8,128)(2,1)S(1)}, u32[]{:S(2)}, u32[]{:S(2)}) collective-permute-start(bf16[72,1024]{1,0:T(8,128)(2,1)S(1)} %get-tuple-element.59), channel_id=1, source_target_pairs={{0,1},{1,2},{2,3},{3,0},{4,5},{5,6},{6,7},{7,4},{8,9},{9,10},{10,1... | collective-permute-start | bytes 442376 | tf_op jit(solution)/shard_map/ppermute | solution.py:185
  9.1 13.1 %collective-permute-start.2 = (bf16[72,1024]{1,0:T(8,128)(2,1)S(1)}, bf16[72,1024]{1,0:T(8,128)(2,1)S(1)}, u32[]{:S(2)}, u32[]{:S(2)}) collective-permute-start(bf16[72,1024]{1,0:T(8,128)(2,1)S(1)} %get-tuple-element.58), channel_id=1, source_target_pairs={{0,2},{1,3},{2,0},{3,1},{4,6},{5,7},{6,4},{7,5},{8,10},{9,11},{10,... | collective-permute-start | bytes 442376 | tf_op jit(solution)/shard_map/ppermute | solution.py:185
  10.8 3.1 %copy-start.7 = (bf16[256,1024]{1,0:T(8,128)(2,1)}, bf16[256,1024]{1,0:T(8,128)(2,1)S(1)}, u32[]{:S(2)}) copy-start(bf16[256,1024]{1,0:T(8,128)(2,1)S(1)} %collective-permute-done.1.refs_5_) | copy-start | bytes 1572868
  13.9 1.3 copy-start.6
  24.1 4.5 %copy-start.15 = (s32[2,64]{1,0:T(2,128)S(1)}, s32[2,64]{1,0:T(2,128)}, u32[]{:S(2)}) copy-start(s32[2,64]{1,0:T(2,128)} %param.11) | copy-start | bytes 1540
  24.1 42.3 %all-to-all-start = ((bf16[8,128,1024]{2,1,0:T(8,128)(2,1)}), bf16[8,128,1024]{2,1,0:T(8,128)(2,1)S(1)}, u32[]{:S(2)}, u32[]{:S(2)}) async-start(bf16[8,128,1024]{2,1,0:T(8,128)(2,1)} %bitcast.121), calls=%async_computation | async-start | bytes 4194304 | tf_op jit(solution)/shard_map/all_to_all | solution.py:246
  28.1 9.4 %collective-permute-start.4 = (f32[256]{0:T(256)S(1)}, f32[256]{0:T(256)S(1)}, u32[]{:S(2)}, u32[]{:S(2)}) collective-permute-start(f32[256]{0:T(256)S(1)} %slice_reduce_fusion), channel_id=1, source_target_pairs={{0,4},{4,0},{8,12},{12,8},{16,20},{20,16},{24,28},{28,24},{1,5},{5... | collective-permute-start | bytes 3080 | tf_op jit(solution)/shard_map/ppermute | solution.py:195
  28.6 5.0 %collective-permute-start.8 = (s32[2,64]{1,0:T(2,128)S(1)}, s32[2,64]{1,0:T(2,128)S(1)}, u32[]{:S(2)}, u32[]{:S(2)}) collective-permute-start(s32[2,64]{1,0:T(2,128)S(1)} %copy-done.15), channel_id=1, source_target_pairs={{0,4},{4,0},{8,12},{12,8},{16,20},{20,16},{24,28},{28,24},{1,5},{5... | collective-permute-start | bytes 1544 | tf_op jit(solution)/shard_map/ppermute | solution.py:195
  29.7 11.3 %collective-permute-start.5 = (bf16[128,1024]{1,0:T(8,128)(2,1)}, bf16[128,1024]{1,0:T(8,128)(2,1)}, u32[]{:S(2)}, u32[]{:S(2)}) collective-permute-start(bf16[128,1024]{1,0:T(8,128)(2,1)} %bitcast.8), channel_id=1, source_target_pairs={{0,1},{1,2},{2,3},{3,0},{4,5},{5,6},{6,7},{7,4},{8,9},{9,10},{10,1... | collective-permute-start | bytes 786440 | tf_op jit(solution)/shard_map/ppermute | solution.py:185
  29.8 14.6 %collective-permute-start.7 = (bf16[128,1024]{1,0:T(8,128)(2,1)}, bf16[128,1024]{1,0:T(8,128)(2,1)}, u32[]{:S(2)}, u32[]{:S(2)}) collective-permute-start(bf16[128,1024]{1,0:T(8,128)(2,1)} %bitcast.10), channel_id=1, source_target_pairs={{0,3},{1,0},{2,1},{3,2},{4,7},{5,4},{6,5},{7,6},{8,11},{9,8},{10,9... | collective-permute-start | bytes 786440 | tf_op jit(solution)/shard_map/ppermute | solution.py:185
  33.6 23.1 %collective-permute-start.6 = (bf16[128,1024]{1,0:T(8,128)(2,1)S(1)}, bf16[128,1024]{1,0:T(8,128)(2,1)}, u32[]{:S(2)}, u32[]{:S(2)}) collective-permute-start(bf16[128,1024]{1,0:T(8,128)(2,1)S(1)} %bitcast.134), channel_id=1, source_target_pairs={{0,2},{1,3},{2,0},{3,1},{4,6},{5,7},{6,4},{7,5},{8,10},{9,11},{10,... | collective-permute-start | bytes 786440 | tf_op jit(solution)/shard_map/ppermute | solution.py:185
  58.4 10.1 %copy-start.4 = (bf16[128,1024]{1,0:T(8,128)(2,1)}, bf16[128,1024]{1,0:T(8,128)(2,1)S(1)}, u32[]{:S(2)}) copy-start(bf16[128,1024]{1,0:T(8,128)(2,1)S(1)} %multiply_convert_fusion.1) | copy-start | bytes 786436
  58.4 8.0 %collective-permute-start.9 = (bf16[128,1024]{1,0:T(8,128)(2,1)S(1)}, bf16[128,1024]{1,0:T(8,128)(2,1)S(1)}, u32[]{:S(2)}, u32[]{:S(2)}) collective-permute-start(bf16[128,1024]{1,0:T(8,128)(2,1)S(1)} %multiply_convert_fusion.1), channel_id=1, source_target_pairs={{0,1},{1,0},{2,3},{3,2},{4,5},{5,4},{6,7},{7,6},{8,9},{9,8},{10,11... | collective-permute-start | bytes 786440 | tf_op jit(solution)/shard_map/ppermute | solution.py:188
  58.5 7.9 %collective-permute-start.11 = (s32[2,128]{1,0:T(2,128)S(1)}, s32[2,128]{1,0:T(2,128)S(1)}, u32[]{:S(2)}, u32[]{:S(2)}) collective-permute-start(s32[2,128]{1,0:T(2,128)S(1)} %pad_add_fusion), channel_id=1, source_target_pairs={{0,1},{1,0},{2,3},{3,2},{4,5},{5,4},{6,7},{7,6},{8,9},{9,8},{10,11... | collective-permute-start | bytes 3080 | tf_op jit(solution)/shard_map/ppermute | solution.py:188
  66.4 2.1 %copy-start.10 = (bf16[128,1024]{1,0:T(8,128)(2,1)}, bf16[128,1024]{1,0:T(8,128)(2,1)S(1)}, u32[]{:S(2)}) copy-start(bf16[128,1024]{1,0:T(8,128)(2,1)S(1)} %collective-permute-done.9) | copy-start | bytes 786436
  67.2 1.0 copy-start.3
  68.6 3.7 %collective-permute-start.10 = (f32[2,2,128]{2,1,0:T(2,128)S(1)}, f32[2,2,128]{2,1,0:T(2,128)S(1)}, u32[]{:S(2)}, u32[]{:S(2)}) collective-permute-start(f32[2,2,128]{2,1,0:T(2,128)S(1)} %pad_maximum_fusion.7), channel_id=1, source_target_pairs={{0,1},{1,0},{2,3},{3,2},{4,5},{5,4},{6,7},{7,6},{8,9},{9,8},{10,11... | collective-permute-start | bytes 6152 | tf_op jit(solution)/shard_map/ppermute | solution.py:188
  72.3 3.5 %copy-start.5 = (bf16[128,1024]{1,0:T(8,128)(2,1)S(1)}, bf16[128,1024]{1,0:T(8,128)(2,1)}, u32[]{:S(2)}) copy-start(bf16[128,1024]{1,0:T(8,128)(2,1)} %copy-done.4) | copy-start | bytes 786436
  72.3 3.5 %copy-start.11 = (bf16[128,1024]{1,0:T(8,128)(2,1)S(1)}, bf16[128,1024]{1,0:T(8,128)(2,1)}, u32[]{:S(2)}) copy-start(bf16[128,1024]{1,0:T(8,128)(2,1)} %copy-done.10) | copy-start | bytes 786436
  73.9 4.0 %copy-start.1 = (bf16[256,1024]{1,0:T(8,128)(2,1)}, bf16[256,1024]{1,0:T(8,128)(2,1)S(1)}, u32[]{:S(2)}) copy-start(bf16[256,1024]{1,0:T(8,128)(2,1)S(1)} %multiply_convert_fusion) | copy-start | bytes 1572868
  75.5 6.9 %collective-permute-start.12 = (bf16[128,1024]{1,0:T(8,128)(2,1)}, bf16[128,1024]{1,0:T(8,128)(2,1)}, u32[]{:S(2)}, u32[]{:S(2)}) collective-permute-start(bf16[128,1024]{1,0:T(8,128)(2,1)} %convolution_convert_fusion.1), channel_id=1, source_target_pairs={{0,1},{1,0},{2,3},{3,2},{4,5},{5,4},{6,7},{7,6},{8,9},{9,8},{10,11... | collective-permute-start | bytes 786440 | tf_op jit(solution)/shard_map/ppermute | solution.py:188
  77.9 4.5 %slice-start = ((bf16[256,1024]{1,0:T(8,128)(2,1)}), bf16[128,1024]{1,0:T(8,128)(2,1)S(1)}, s32[]{:S(2)}) async-start(bf16[256,1024]{1,0:T(8,128)(2,1)} %copy-done.1), calls=%async_computation.3 | async-start | bytes 524288 | tf_op jit(solution)/shard_map/slice | solution.py:282
  77.9 43.0 %all-to-all-start.2 = ((bf16[8,128,1024]{2,1,0:T(8,128)(2,1)}), bf16[8,128,1024]{2,1,0:T(8,128)(2,1)}, u32[]{:S(2)}, u32[]{:S(2)}) async-start(bf16[8,128,1024]{2,1,0:T(8,128)(2,1)} %bitcast.123), calls=%async_computation.2 | async-start | bytes 4194304 | tf_op jit(solution)/shard_map/all_to_all | solution.py:293
  86.7 28.3 %copy-start.9 = (bf16[136,1024]{1,0:T(8,128)(2,1)}, bf16[136,1024]{1,0:T(8,128)(2,1)S(1)}, u32[]{:S(2)}) copy-start(bf16[136,1024]{1,0:T(8,128)(2,1)S(1)} %pad_maximum_fusion.4.refs_0_) | copy-start | bytes 835588
  86.7 9.0 %collective-permute-start.15 = (bf16[136,1024]{1,0:T(8,128)(2,1)S(1)}, bf16[136,1024]{1,0:T(8,128)(2,1)S(1)}, u32[]{:S(2)}, u32[]{:S(2)}) collective-permute-start(bf16[136,1024]{1,0:T(8,128)(2,1)S(1)} %pad_maximum_fusion.4.refs_0_), channel_id=1, source_target_pairs={{0,3},{1,0},{2,1},{3,2},{4,7},{5,4},{6,5},{7,6},{8,11},{9,8},{10,9... | collective-permute-start | bytes 835592 | tf_op jit(solution)/shard_map/ppermute | solution.py:185
  87.4 27.4 %collective-permute-start.14 = (bf16[136,1024]{1,0:T(8,128)(2,1)S(1)}, bf16[136,1024]{1,0:T(8,128)(2,1)S(1)}, u32[]{:S(2)}, u32[]{:S(2)}) collective-permute-start(bf16[136,1024]{1,0:T(8,128)(2,1)S(1)} %pad_maximum_fusion.4.refs_0_), channel_id=1, source_target_pairs={{0,2},{1,3},{2,0},{3,1},{4,6},{5,7},{6,4},{7,5},{8,10},{9,11},{10,... | collective-permute-start | bytes 835592 | tf_op jit(solution)/shard_map/ppermute | solution.py:185
  90.0 24.9 %collective-permute-start.13 = (bf16[136,1024]{1,0:T(8,128)(2,1)S(1)}, bf16[136,1024]{1,0:T(8,128)(2,1)S(1)}, u32[]{:S(2)}, u32[]{:S(2)}) collective-permute-start(bf16[136,1024]{1,0:T(8,128)(2,1)S(1)} %pad_maximum_fusion.4.refs_0_), channel_id=1, source_target_pairs={{0,1},{1,2},{2,3},{3,0},{4,5},{5,6},{6,7},{7,4},{8,9},{9,10},{10,1... | collective-permute-start | bytes 835592 | tf_op jit(solution)/shard_map/ppermute | solution.py:185
  95.7 19.3 %copy-start.16 = (bf16[136,1024]{1,0:T(8,128)(2,1)}, bf16[136,1024]{1,0:T(8,128)(2,1)S(1)}, u32[]{:S(2)}) copy-start(bf16[136,1024]{1,0:T(8,128)(2,1)S(1)} %collective-permute-done.15.refs_3_) | copy-start | bytes 835588
  114.8 0.7 copy-start.17
  114.9 0.7 copy-start.18
  120.7 11.7 %collective-permute-start.16 = (bf16[256,1024]{1,0:T(8,128)(2,1)}, bf16[256,1024]{1,0:T(8,128)(2,1)S(1)}, u32[]{:S(2)}, u32[]{:S(2)}) collective-permute-start(bf16[256,1024]{1,0:T(8,128)(2,1)} %get-tuple-element.24), channel_id=1, source_target_pairs={{0,4},{4,0},{8,12},{12,8},{16,20},{20,16},{24,28},{28,24},{1,5},{5... | collective-permute-start | bytes 1572872 | tf_op jit(solution)/shard_map/ppermute | solution.py:195
  120.9 30.6 %all-to-all-start.1 = ((bf16[8,128,1024]{2,1,0:T(8,128)(2,1)}), bf16[8,128,1024]{2,1,0:T(8,128)(2,1)S(1)}, u32[]{:S(2)}, u32[]{:S(2)}) async-start(bf16[8,128,1024]{2,1,0:T(8,128)(2,1)} %bitcast.126), calls=%async_computation.1 | async-start | bytes 4194304 | tf_op jit(solution)/shard_map/all_to_all | solution.py:308
  124.9 1.4 collective-permute-start.17
  129.2 8.9 %collective-permute-start.20 = (bf16[2,32,1024]{2,1,0:T(8,128)(2,1)S(1)}, bf16[2,32,1024]{2,1,0:T(8,128)(2,1)S(1)}, u32[]{:S(2)}, u32[]{:S(2)}) collective-permute-start(bf16[2,32,1024]{2,1,0:T(8,128)(2,1)S(1)} %get-tuple-element.52), channel_id=1, source_target_pairs={{0,3},{1,0},{2,1},{3,2},{4,7},{5,4},{6,5},{7,6},{8,11},{9,8},{10,9... | collective-permute-start | bytes 393224 | tf_op jit(solution)/shard_map/ppermute | solution.py:185
  129.2 12.6 %collective-permute-start.19 = (bf16[2,32,1024]{2,1,0:T(8,128)(2,1)S(1)}, bf16[2,32,1024]{2,1,0:T(8,128)(2,1)S(1)}, u32[]{:S(2)}, u32[]{:S(2)}) collective-permute-start(bf16[2,32,1024]{2,1,0:T(8,128)(2,1)S(1)} %get-tuple-element.53), channel_id=1, source_target_pairs={{0,2},{1,3},{2,0},{3,1},{4,6},{5,7},{6,4},{7,5},{8,10},{9,11},{10,... | collective-permute-start | bytes 393224 | tf_op jit(solution)/shard_map/ppermute | solution.py:185
  129.5 12.4 %collective-permute-start.18 = (bf16[2,32,1024]{2,1,0:T(8,128)(2,1)S(1)}, bf16[2,32,1024]{2,1,0:T(8,128)(2,1)S(1)}, u32[]{:S(2)}, u32[]{:S(2)}) collective-permute-start(bf16[2,32,1024]{2,1,0:T(8,128)(2,1)S(1)} %get-tuple-element.54), channel_id=1, source_target_pairs={{0,1},{1,2},{2,3},{3,0},{4,5},{5,6},{6,7},{7,4},{8,9},{9,10},{10,1... | collective-permute-start | bytes 393224 | tf_op jit(solution)/shard_map/ppermute | solution.py:185
  132.4 0.8 copy-start.8
  138.1 3.8 %copy-start.12 = (bf16[2,32,1024]{2,1,0:T(8,128)(2,1)}, bf16[2,32,1024]{2,1,0:T(8,128)(2,1)S(1)}, u32[]{:S(2)}) copy-start(bf16[2,32,1024]{2,1,0:T(8,128)(2,1)S(1)} %collective-permute-done.20.refs_3_) | copy-start | bytes 393220
  141.9 0.6 copy-start.13
  141.9 0.7 copy-start.14

commit v13 on v9

--- a/solution.py
+++ b/solution.py
@@ -289,7 +289,7 @@
     d_ratio_part = (scale * gated_proj - back_scale * x_proj).reshape(steps, part)
 
     part_out = matmul(normed_rows, after(d_logit, *away), ((0,), (0,))).astype(BF16)
-    part_out = after(part_out, *received).reshape(seqs, depth // seqs, block)
+    part_out = part_out.reshape(seqs, depth // seqs, block)
     part_out = lax.all_to_all(part_out, "seq", 0, 0)
     part_out = part_out.reshape(groups, steps, hids, head_rows, block).astype(F32).sum(0)
     part_out = part_out.astype(BF16)

time: 150 us -> 152 us (1.013)
  waiting for transfers between devices: 55.1 us -> 58.7 us
    ppermute x4, waiting for transfers between devices: 11.7 us -> 16.1 us  [turn_hid(): lax.ppermute(values, 'hid', [(a, a - a % halves + (a % halves + shift) %...]
  transfers between devices with their start and end apart: 27 -> 27, of which waited for: 13 -> 13; matrix products, arithmetic and copies ran while one was open for 17% -> 14% of each run, Pallas kernels for 9% -> 8%
where the time goes in v13:
time: 152 us; the launch traced here: 151 us
  waiting for transfers between devices  58.7 us (39%)
  starting transfers between devices  45.2 us (30%)
  local copies, waits for them, and re-layouts  17.8 us (12%)
  Pallas kernels  12.7 us (8%)
  matrix products  8.48 us (6%)
  other arithmetic  7.3 us (5%)
    ppermute x15, waiting for transfers between devices, along_hid(): lax.ppermute(values, 'hid', [(a, (a + shift) % hids) for a in range(hids)])  41.8 us
    ppermute x15, starting transfers between devices, along_hid(): lax.ppermute(values, 'hid', [(a, (a + shift) % hids) for a in range(hids)])  27.2 us
    ppermute x4, waiting for transfers between devices, turn_hid(): lax.ppermute(values, 'hid', [(a, a - a % halves + (a % halves + shift) %...  16.1 us
    pallas_call x3, Pallas kernels, call(): pl.pallas_call(kernel, grid_spec=pltpu.PrefetchScalarGridSpec(num_scalar_...  12.7 us
    dot_general x5, matrix products, matmul(): lax.dot_general(a, b, (contract, ((), ())), preferred_element_type=F32)  8.48 us
    unnamed x44, local copies, waits for them, and re-layouts  5.76 us
    all_to_all x1, starting transfers between devices, shards(): part_out = lax.all_to_all(part_out, 'seq', 0, 0)  4.35 us
    ppermute x4, starting transfers between devices, turn_hid(): lax.ppermute(values, 'hid', [(a, a - a % halves + (a % halves + shift) %...  4.35 us
  transfers between devices with their start and end apart: 27, of which 13 were waited for; matrix products, arithmetic and copies ran while one was open for 14% of the time, Pallas kernels for 8%

profile of v13, /device:TPU:0, one launch (start us, length us, event | category | flops | bytes accessed | tf_op | source)
XLA Modules:
  0.0 151.3 jit_solution(8680427593802539494)
XLA Ops:
  1.2 1.2 multiply_reduce_fusion
  2.5 1.1 reshape.276
  4.4 4.7 %collective-permute-start.3 = (bf16[72,1024]{1,0:T(8,128)(2,1)S(1)}, bf16[72,1024]{1,0:T(8,128)(2,1)S(1)}, u32[]{:S(2)}, u32[]{:S(2)}) collective-permute-start(bf16[72,1024]{1,0:T(8,128)(2,1)S(1)} %get-tuple-element.55), channel_id=1, source_target_pairs={{0,3},{1,0},{2,1},{3,2},{4,7},{5,4},{6,5},{7,6},{8,11},{9,8},{10,9... | collective-permute-start | bytes 442376 | tf_op jit(solution)/shard_map/ppermute | solution.py:185
  9.1 1.0 collective-permute-start.2
  10.2 3.0 %fusion = f32[2,4,64,1024]{3,2,1,0:T(8,128)S(1)} fusion(bf16[2,4,64,1024]{3,2,1,0:T(8,128)(2,1)S(1)} %bitcast.140, bf16[2,1024,1024]{2,1,0:T(8,128)(2,1)} %refs_2_.1, s32[]{:T(128)S(6)} %select_n.139), kind=kOutput, calls=%fused_computation.2 | convolution fusion | flops 1073741824 | bytes 5242884 | tf_op jit(solution)/shard_map/dot_general | solution.py:17
  13.2 1.3 copy-done.4
  14.5 0.8 dynamic-slice_convert_fusion
  15.3 6.9 %collective-permute-done.2 = bf16[72,1024]{1,0:T(8,128)(2,1)S(1)} collective-permute-done((bf16[72,1024]{1,0:T(8,128)(2,1)S(1)}, bf16[72,1024]{1,0:T(8,128)(2,1)S(1)}, u32[]{:S(2)}, u32[]{:S(2)}) %collective-permute-start.2) | collective-permute-done | bytes 147488 | tf_op jit(solution)/shard_map/ppermute | solution.py:185
  22.5 1.6 %broadcast_in_dim.45 = bf16[4,2,128,1024]{3,2,1,0:T(8,128)(2,1)} broadcast(bf16[2,128,1024]{2,1,0:T(8,128)(2,1)S(1)} %bitcast.133), dimensions={1,2,3} | broadcast | bytes 2621440 | tf_op jit(solution)/shard_map/broadcast_in_dim | solution.py:244
  24.1 3.9 %all-to-all-start = ((bf16[8,128,1024]{2,1,0:T(8,128)(2,1)}), bf16[8,128,1024]{2,1,0:T(8,128)(2,1)S(1)}, u32[]{:S(2)}, u32[]{:S(2)}) async-start(bf16[8,128,1024]{2,1,0:T(8,128)(2,1)} %bitcast.129), calls=%async_computation | async-start | bytes 4194304 | tf_op jit(solution)/shard_map/all_to_all | solution.py:246
  28.7 2.6 %collective-permute-start.7 = (bf16[128,1024]{1,0:T(8,128)(2,1)}, bf16[128,1024]{1,0:T(8,128)(2,1)}, u32[]{:S(2)}, u32[]{:S(2)}) collective-permute-start(bf16[128,1024]{1,0:T(8,128)(2,1)} %bitcast.10), channel_id=1, source_target_pairs={{0,3},{1,0},{2,1},{3,2},{4,7},{5,4},{6,5},{7,6},{8,11},{9,8},{10,9... | collective-permute-start | bytes 786440 | tf_op jit(solution)/shard_map/ppermute | solution.py:185
  32.0 1.1 constant_dynamic-slice_fusion.6
  33.2 3.8 %gather_fusion = bf16[128,1024]{1,0:T(8,128)(2,1)S(1)} fusion(bf16[2048,1024]{1,0:T(8,128)(2,1)} %bitcast.139, s32[1024]{0:T(1024)S(1)} %pad_clamp_fusion), kind=kCustom, calls=%fused_computation | custom fusion | bytes 524800 | tf_op jit(solution)/shard_map/jit(_take)/gather | solution.py:240
  37.1 2.2 %collective-permute-done.7 = bf16[128,1024]{1,0:T(8,128)(2,1)} collective-permute-done((bf16[128,1024]{1,0:T(8,128)(2,1)}, bf16[128,1024]{1,0:T(8,128)(2,1)}, u32[]{:S(2)}, u32[]{:S(2)}) %collective-permute-start.7) | collective-permute-done | bytes 262176 | tf_op jit(solution)/shard_map/ppermute | solution.py:185
  39.3 14.5 %collective-permute-done.6 = bf16[128,1024]{1,0:T(8,128)(2,1)} collective-permute-done((bf16[128,1024]{1,0:T(8,128)(2,1)S(1)}, bf16[128,1024]{1,0:T(8,128)(2,1)}, u32[]{:S(2)}, u32[]{:S(2)}) %collective-permute-start.6) | collective-permute-done | bytes 262176 | tf_op jit(solution)/shard_map/ppermute | solution.py:185
  53.8 1.4 multiply_reduce_fusion.4
  55.5 1.2 collective-permute-start.9
  56.7 0.9 collective-permute-start.11
  57.6 5.9 %collective-permute-done.11 = s32[2,128]{1,0:T(2,128)S(1)} collective-permute-done((s32[2,128]{1,0:T(2,128)S(1)}, s32[2,128]{1,0:T(2,128)S(1)}, u32[]{:S(2)}, u32[]{:S(2)}) %collective-permute-start.11) | collective-permute-done | bytes 1056 | tf_op jit(solution)/shard_map/ppermute | solution.py:188
  64.7 1.1 collective-permute-start.10
  65.8 2.5 %collective-permute-done.10 = f32[2,2,128]{2,1,0:T(2,128)S(1)} collective-permute-done((f32[2,2,128]{2,1,0:T(2,128)S(1)}, f32[2,2,128]{2,1,0:T(2,128)S(1)}, u32[]{:S(2)}, u32[]{:S(2)}) %collective-permute-start.10) | collective-permute-done | bytes 2080 | tf_op jit(solution)/shard_map/ppermute | solution.py:188
  68.8 1.5 %convolution_convert_fusion.1 = bf16[128,1024]{1,0:T(8,128)(2,1)} fusion(bf16[1024,1024]{1,0:T(8,128)(2,1)S(1)} %bitcast.127, bf16[256,1024]{1,0:T(8,128)(2,1)S(1)} %multiply_convert_fusion), kind=kOutput, calls=%fused_computation.6 | convolution fusion | flops 268566528 | bytes 2621440 | tf_op jit(solution)/shard_map/dot_general | solution.py:17
  70.3 2.1 %convolution_convert_fusion = bf16[1024,1024]{1,0:T(8,128)(2,1)} fusion(bf16[256,1024]{1,0:T(8,128)(2,1)S(1)} %multiply_convert_fusion, bf16[128,1024]{1,0:T(8,128)(2,1)S(1)} %copy-done.8, bf16[128,1024]{1,0:T(8,128)(2,1)S(1)} %copy-done.3), kind=kOutput, calls=%fused_computation.5 | convolution fusion | flops 538968064 | bytes 3145728 | tf_op jit(solution)/shard_map/dot_general | solution.py:17
  72.4 4.4 %all-to-all-start.2 = ((bf16[8,128,1024]{2,1,0:T(8,128)(2,1)}), bf16[8,128,1024]{2,1,0:T(8,128)(2,1)}, u32[]{:S(2)}, u32[]{:S(2)}) async-start(bf16[8,128,1024]{2,1,0:T(8,128)(2,1)} %bitcast.131), calls=%async_computation.2 | async-start | bytes 4194304 | tf_op jit(solution)/shard_map/all_to_all | solution.py:293
  76.8 1.1 collective-permute-start.12
  77.9 7.6 %collective-permute-done.12 = bf16[128,1024]{1,0:T(8,128)(2,1)S(1)} collective-permute-done((bf16[128,1024]{1,0:T(8,128)(2,1)}, bf16[128,1024]{1,0:T(8,128)(2,1)S(1)}, u32[]{:S(2)}, u32[]{:S(2)}) %collective-permute-start.12) | collective-permute-done | bytes 262176 | tf_op jit(solution)/shard_map/ppermute | solution.py:188
  85.6 1.1 multiply_reduce_fusion.2
  86.9 1.1 collective-permute-start.13
  88.0 2.3 %collective-permute-start.14 = (bf16[128,1024]{1,0:T(8,128)(2,1)S(1)}, bf16[128,1024]{1,0:T(8,128)(2,1)S(1)}, u32[]{:S(2)}, u32[]{:S(2)}) collective-permute-start(bf16[128,1024]{1,0:T(8,128)(2,1)S(1)} %subtract_convert_fusion.refs_0_), channel_id=1, source_target_pairs={{0,2},{1,3},{2,0},{3,1},{4,6},{5,7},{6,4},{7,5},{8,10},{9,11},{10,... | collective-permute-start | bytes 786440 | tf_op jit(solution)/shard_map/ppermute | solution.py:185
  90.4 2.6 %collective-permute-start.15 = (bf16[128,1024]{1,0:T(8,128)(2,1)S(1)}, bf16[128,1024]{1,0:T(8,128)(2,1)S(1)}, u32[]{:S(2)}, u32[]{:S(2)}) collective-permute-start(bf16[128,1024]{1,0:T(8,128)(2,1)S(1)} %subtract_convert_fusion.refs_0_), channel_id=1, source_target_pairs={{0,3},{1,0},{2,1},{3,2},{4,7},{5,4},{6,5},{7,6},{8,11},{9,8},{10,9... | collective-permute-start | bytes 786440 | tf_op jit(solution)/shard_map/ppermute | solution.py:185
  93.7 0.9 copy.39.refs_6_
  94.5 3.6 %collective-permute-done.13.refs_1_ = bf16[128,1024]{1,0:T(8,128)(2,1)S(1)} collective-permute-done((bf16[128,1024]{1,0:T(8,128)(2,1)S(1)}, bf16[128,1024]{1,0:T(8,128)(2,1)S(1)}, u32[]{:S(2)}, u32[]{:S(2)}) %collective-permute-start.13) | collective-permute-done | bytes 262176 | tf_op jit(solution)/shard_map/ppermute | solution.py:185
  98.1 9.9 %collective-permute-done.14.refs_2_ = bf16[128,1024]{1,0:T(8,128)(2,1)S(1)} collective-permute-done((bf16[128,1024]{1,0:T(8,128)(2,1)S(1)}, bf16[128,1024]{1,0:T(8,128)(2,1)S(1)}, u32[]{:S(2)}, u32[]{:S(2)}) %collective-permute-start.14) | collective-permute-done | bytes 262176 | tf_op jit(solution)/shard_map/ppermute | solution.py:185
  109.4 5.1 %shard_map.85 = (bf16[1024,1024]{1,0:T(8,128)(2,1)}, bf16[256,1024]{1,0:T(8,128)(2,1)}, bf16[256,1024]{1,0:T(8,128)(2,1)}) custom-call(s32[2]{0:T(128)} %pad_add_fusion.2.place_ref, bf16[128,1024]{1,0:T(8,128)(2,1)} %copy-done.9, bf16[128,1024]{1,0:T(8,128)(2,1)} %copy-done.14, bf16[128,1024]{1,0:T(8,128)(2,1)} %copy-done.15, bf16[128,1024]{1,0:T(8,128)(2,1)} %copy-done.16, ...), custom_call_target="tpu_custom_call" | custom-call | flops 1073741824 | bytes 2099200 | tf_op jit(solution)/shard_map/pallas_call | solution.py:33
  114.5 3.7 %all-to-all-start.1 = ((bf16[8,128,1024]{2,1,0:T(8,128)(2,1)}), bf16[8,128,1024]{2,1,0:T(8,128)(2,1)S(1)}, u32[]{:S(2)}, u32[]{:S(2)}) async-start(bf16[8,128,1024]{2,1,0:T(8,128)(2,1)} %bitcast.134), calls=%async_computation.1 | async-start | bytes 4194304 | tf_op jit(solution)/shard_map/all_to_all | solution.py:305
  118.8 0.8 collective-permute-done.17
  119.7 5.3 %collective-permute-start.18 = (f32[64]{0:T(128)S(1)}, f32[64]{0:T(128)S(1)}, u32[]{:S(2)}, u32[]{:S(2)}) collective-permute-start(f32[64]{0:T(128)S(1)} %bitcast_add_fusion.1), channel_id=1, source_target_pairs={{0,1},{1,2},{2,3},{3,0},{4,5},{5,6},{6,7},{7,4},{8,9},{9,10},{10,1... | collective-permute-start | bytes 776 | tf_op jit(solution)/shard_map/ppermute | solution.py:185
  125.0 2.9 %collective-permute-start.19 = (f32[64]{0:T(128)S(1)}, f32[64]{0:T(128)S(1)}, u32[]{:S(2)}, u32[]{:S(2)}) collective-permute-start(f32[64]{0:T(128)S(1)} %bitcast_add_fusion.1), channel_id=1, source_target_pairs={{0,2},{1,3},{2,0},{3,1},{4,6},{5,7},{6,4},{7,5},{8,10},{9,11},{10,... | collective-permute-start | bytes 776 | tf_op jit(solution)/shard_map/ppermute | solution.py:185
  127.9 0.9 collective-permute-done.18
  129.5 2.0 %collective-permute-done.20 = f32[64]{0:T(128)S(1)} collective-permute-done((f32[64]{0:T(128)S(1)}, f32[64]{0:T(128)S(1)}, u32[]{:S(2)}, u32[]{:S(2)}) %collective-permute-start.20) | collective-permute-done | bytes 288 | tf_op jit(solution)/shard_map/ppermute | solution.py:185
  131.6 2.0 %reduce_sum.108 = bf16[2,4,32,1024]{3,2,1,0:T(8,128)(2,1)S(1)} reduce(bf16[4,2,4,32,1024]{4,3,2,1,0:T(8,128)(2,1)} %bitcast.57, bf16[]{:T(256)} %constant.168.clone.1), dimensions={0}, to_apply=%region_10.11 | reduce | flops 786432 | bytes 2621442 | tf_op jit(solution)/shard_map/reduce_sum | solution.py:294
  134.3 2.4 %collective-permute-start.22 = (bf16[2,32,1024]{2,1,0:T(8,128)(2,1)S(1)}, bf16[2,32,1024]{2,1,0:T(8,128)(2,1)S(1)}, u32[]{:S(2)}, u32[]{:S(2)}) collective-permute-start(bf16[2,32,1024]{2,1,0:T(8,128)(2,1)S(1)} %get-tuple-element.49), channel_id=1, source_target_pairs={{0,2},{1,3},{2,0},{3,1},{4,6},{5,7},{6,4},{7,5},{8,10},{9,11},{10,... | collective-permute-start | bytes 393224 | tf_op jit(solution)/shard_map/ppermute | solution.py:185
  136.7 1.5 collective-permute-start.23
  138.2 0.9 copy.40.refs_4_
  139.9 4.9 %shard_map.86 = bf16[256,1024]{1,0:T(8,128)(2,1)} custom-call(s32[2]{0:T(128)} %pad_add_fusion.2.place_ref, bf16[256,1024]{1,0:T(8,128)(2,1)} %get-tuple-element.23.refs_0_, bf16[256,1024]{1,0:T(8,128)(2,1)} %copy-done.6, bf16[2,1024,1024]{2,1,0:T(8,128)(2,1)} %refs_2_.1, bf16[256,1024]{1,0:T(8,128)(2,1)} %refs_3_.1, f32[2,256,1]{2,1,0:T(8,128)} %copy.40.refs_4_), custom_call_target="tpu_custom_call" | custom-call | flops 1073741824 | bytes 5769216 | tf_op jit(solution)/shard_map/pallas_call | solution.py:33
  144.8 1.4 collective-permute-done.22.refs_2_
  146.9 2.7 %shard_map.87 = f32[32,2,2048]{2,1,0:T(2,128)} custom-call(s32[2]{0:T(128)} %pad_add_fusion.2.place_ref, bf16[2,32,1024]{2,1,0:T(8,128)(2,1)} %get-tuple-element.51.refs_0_, bf16[2,32,1024]{2,1,0:T(8,128)(2,1)} %copy-done.10, bf16[2,32,1024]{2,1,0:T(8,128)(2,1)} %copy-done.11, bf16[2,32,1024]{2,1,0:T(8,128)(2,1)} %copy-done.12), custom_call_target="tpu_custom_call" | custom-call | flops 262144 | bytes 524288 | tf_op jit(solution)/shard_map/pallas_call | solution.py:33
  150.0 1.3 copy.41
  (120 shorter events, 11.4 us)
Async XLA Ops:
  0.6 9.5 %copy-start = (f32[2,1024]{1,0:T(2,128)S(1)}, f32[2,1024]{1,0:T(2,128)}, u32[]{:S(2)}) copy-start(f32[2,1024]{1,0:T(2,128)} %param.9) | copy-start | bytes 24580
  0.6 9.5 %copy-start.1 = (bf16[256,1024]{1,0:T(8,128)(2,1)S(1)}, bf16[256,1024]{1,0:T(8,128)(2,1)}, u32[]{:S(2)}) copy-start(bf16[256,1024]{1,0:T(8,128)(2,1)} %refs_3_.1) | copy-start | bytes 1572868
  0.7 9.5 %collective-permute-start.1 = (bf16[256,1024]{1,0:T(8,128)(2,1)}, bf16[256,1024]{1,0:T(8,128)(2,1)S(1)}, u32[]{:S(2)}, u32[]{:S(2)}) collective-permute-start(bf16[256,1024]{1,0:T(8,128)(2,1)} %refs_3_.1), channel_id=1, source_target_pairs={{0,4},{4,0},{8,12},{12,8},{16,20},{20,16},{24,28},{28,24},{1,5},{5... | collective-permute-start | bytes 1572872 | tf_op jit(solution)/shard_map/ppermute | solution.py:195
  4.4 11.0 %collective-permute-start.3 = (bf16[72,1024]{1,0:T(8,128)(2,1)S(1)}, bf16[72,1024]{1,0:T(8,128)(2,1)S(1)}, u32[]{:S(2)}, u32[]{:S(2)}) collective-permute-start(bf16[72,1024]{1,0:T(8,128)(2,1)S(1)} %get-tuple-element.55), channel_id=1, source_target_pairs={{0,3},{1,0},{2,1},{3,2},{4,7},{5,4},{6,5},{7,6},{8,11},{9,8},{10,9... | collective-permute-start | bytes 442376 | tf_op jit(solution)/shard_map/ppermute | solution.py:185
  9.1 13.1 %collective-permute-start = (bf16[72,1024]{1,0:T(8,128)(2,1)S(1)}, bf16[72,1024]{1,0:T(8,128)(2,1)S(1)}, u32[]{:S(2)}, u32[]{:S(2)}) collective-permute-start(bf16[72,1024]{1,0:T(8,128)(2,1)S(1)} %get-tuple-element.55), channel_id=1, source_target_pairs={{0,1},{1,2},{2,3},{3,0},{4,5},{5,6},{6,7},{7,4},{8,9},{9,10},{10,1... | collective-permute-start | bytes 442376 | tf_op jit(solution)/shard_map/ppermute | solution.py:185
  9.1 13.1 %collective-permute-start.2 = (bf16[72,1024]{1,0:T(8,128)(2,1)S(1)}, bf16[72,1024]{1,0:T(8,128)(2,1)S(1)}, u32[]{:S(2)}, u32[]{:S(2)}) collective-permute-start(bf16[72,1024]{1,0:T(8,128)(2,1)S(1)} %get-tuple-element.54), channel_id=1, source_target_pairs={{0,2},{1,3},{2,0},{3,1},{4,6},{5,7},{6,4},{7,5},{8,10},{9,11},{10,... | collective-permute-start | bytes 442376 | tf_op jit(solution)/shard_map/ppermute | solution.py:185
  10.1 3.1 %copy-start.5 = (bf16[256,1024]{1,0:T(8,128)(2,1)}, bf16[256,1024]{1,0:T(8,128)(2,1)S(1)}, u32[]{:S(2)}) copy-start(bf16[256,1024]{1,0:T(8,128)(2,1)S(1)} %collective-permute-done.1.refs_5_) | copy-start | bytes 1572868
  13.2 1.3 copy-start.4
  24.1 4.5 %copy-start.13 = (s32[2,64]{1,0:T(2,128)S(1)}, s32[2,64]{1,0:T(2,128)}, u32[]{:S(2)}) copy-start(s32[2,64]{1,0:T(2,128)} %param.11) | copy-start | bytes 1540
  24.1 39.4 %all-to-all-start = ((bf16[8,128,1024]{2,1,0:T(8,128)(2,1)}), bf16[8,128,1024]{2,1,0:T(8,128)(2,1)S(1)}, u32[]{:S(2)}, u32[]{:S(2)}) async-start(bf16[8,128,1024]{2,1,0:T(8,128)(2,1)} %bitcast.129), calls=%async_computation | async-start | bytes 4194304 | tf_op jit(solution)/shard_map/all_to_all | solution.py:246
  28.0 8.9 %collective-permute-start.4 = (f32[256]{0:T(256)S(1)}, f32[256]{0:T(256)S(1)}, u32[]{:S(2)}, u32[]{:S(2)}) collective-permute-start(f32[256]{0:T(256)S(1)} %slice_reduce_fusion), channel_id=1, source_target_pairs={{0,4},{4,0},{8,12},{12,8},{16,20},{20,16},{24,28},{28,24},{1,5},{5... | collective-permute-start | bytes 3080 | tf_op jit(solution)/shard_map/ppermute | solution.py:195
  28.6 4.4 %collective-permute-start.8 = (s32[2,64]{1,0:T(2,128)S(1)}, s32[2,64]{1,0:T(2,128)S(1)}, u32[]{:S(2)}, u32[]{:S(2)}) collective-permute-start(s32[2,64]{1,0:T(2,128)S(1)} %copy-done.13), channel_id=1, source_target_pairs={{0,4},{4,0},{8,12},{12,8},{16,20},{20,16},{24,28},{28,24},{1,5},{5... | collective-permute-start | bytes 1544 | tf_op jit(solution)/shard_map/ppermute | solution.py:195
  28.7 10.6 %collective-permute-start.7 = (bf16[128,1024]{1,0:T(8,128)(2,1)}, bf16[128,1024]{1,0:T(8,128)(2,1)}, u32[]{:S(2)}, u32[]{:S(2)}) collective-permute-start(bf16[128,1024]{1,0:T(8,128)(2,1)} %bitcast.10), channel_id=1, source_target_pairs={{0,3},{1,0},{2,1},{3,2},{4,7},{5,4},{6,5},{7,6},{8,11},{9,8},{10,9... | collective-permute-start | bytes 786440 | tf_op jit(solution)/shard_map/ppermute | solution.py:185
  31.3 22.5 %collective-permute-start.6 = (bf16[128,1024]{1,0:T(8,128)(2,1)S(1)}, bf16[128,1024]{1,0:T(8,128)(2,1)}, u32[]{:S(2)}, u32[]{:S(2)}) collective-permute-start(bf16[128,1024]{1,0:T(8,128)(2,1)S(1)} %bitcast.143), channel_id=1, source_target_pairs={{0,2},{1,3},{2,0},{3,1},{4,6},{5,7},{6,4},{7,5},{8,10},{9,11},{10,... | collective-permute-start | bytes 786440 | tf_op jit(solution)/shard_map/ppermute | solution.py:185
  31.3 22.5 %collective-permute-start.5 = (bf16[128,1024]{1,0:T(8,128)(2,1)S(1)}, bf16[128,1024]{1,0:T(8,128)(2,1)}, u32[]{:S(2)}, u32[]{:S(2)}) collective-permute-start(bf16[128,1024]{1,0:T(8,128)(2,1)S(1)} %bitcast.142), channel_id=1, source_target_pairs={{0,1},{1,2},{2,3},{3,0},{4,5},{5,6},{6,7},{7,4},{8,9},{9,10},{10,1... | collective-permute-start | bytes 786440 | tf_op jit(solution)/shard_map/ppermute | solution.py:185
  55.5 9.2 %copy-start.2 = (bf16[128,1024]{1,0:T(8,128)(2,1)}, bf16[128,1024]{1,0:T(8,128)(2,1)S(1)}, u32[]{:S(2)}) copy-start(bf16[128,1024]{1,0:T(8,128)(2,1)S(1)} %multiply_convert_fusion.1) | copy-start | bytes 786436
  55.5 8.0 %collective-permute-start.9 = (bf16[128,1024]{1,0:T(8,128)(2,1)S(1)}, bf16[128,1024]{1,0:T(8,128)(2,1)S(1)}, u32[]{:S(2)}, u32[]{:S(2)}) collective-permute-start(bf16[128,1024]{1,0:T(8,128)(2,1)S(1)} %multiply_convert_fusion.1), channel_id=1, source_target_pairs={{0,1},{1,0},{2,3},{3,2},{4,5},{5,4},{6,7},{7,6},{8,9},{9,8},{10,11... | collective-permute-start | bytes 786440 | tf_op jit(solution)/shard_map/ppermute | solution.py:188
  56.7 6.8 %collective-permute-start.11 = (s32[2,128]{1,0:T(2,128)S(1)}, s32[2,128]{1,0:T(2,128)S(1)}, u32[]{:S(2)}, u32[]{:S(2)}) collective-permute-start(s32[2,128]{1,0:T(2,128)S(1)} %pad_add_fusion), channel_id=1, source_target_pairs={{0,1},{1,0},{2,3},{3,2},{4,5},{5,4},{6,7},{7,6},{8,9},{9,8},{10,11... | collective-permute-start | bytes 3080 | tf_op jit(solution)/shard_map/ppermute | solution.py:188
  63.5 1.2 copy-start.7
  64.7 3.7 %collective-permute-start.10 = (f32[2,2,128]{2,1,0:T(2,128)S(1)}, f32[2,2,128]{2,1,0:T(2,128)S(1)}, u32[]{:S(2)}, u32[]{:S(2)}) collective-permute-start(f32[2,2,128]{2,1,0:T(2,128)S(1)} %pad_maximum_fusion.6), channel_id=1, source_target_pairs={{0,1},{1,0},{2,3},{3,2},{4,5},{5,4},{6,7},{7,6},{8,9},{9,8},{10,11... | collective-permute-start | bytes 6152 | tf_op jit(solution)/shard_map/ppermute | solution.py:188
  68.4 1.9 %copy-start.3 = (bf16[128,1024]{1,0:T(8,128)(2,1)S(1)}, bf16[128,1024]{1,0:T(8,128)(2,1)}, u32[]{:S(2)}) copy-start(bf16[128,1024]{1,0:T(8,128)(2,1)} %copy-done.2) | copy-start | bytes 786436
  68.4 1.9 %copy-start.8 = (bf16[128,1024]{1,0:T(8,128)(2,1)S(1)}, bf16[128,1024]{1,0:T(8,128)(2,1)}, u32[]{:S(2)}) copy-start(bf16[128,1024]{1,0:T(8,128)(2,1)} %copy-done.7) | copy-start | bytes 786436
  72.4 42.0 %all-to-all-start.2 = ((bf16[8,128,1024]{2,1,0:T(8,128)(2,1)}), bf16[8,128,1024]{2,1,0:T(8,128)(2,1)}, u32[]{:S(2)}, u32[]{:S(2)}) async-start(bf16[8,128,1024]{2,1,0:T(8,128)(2,1)} %bitcast.131), calls=%async_computation.2 | async-start | bytes 4194304 | tf_op jit(solution)/shard_map/all_to_all | solution.py:293
  76.8 8.8 %collective-permute-start.12 = (bf16[128,1024]{1,0:T(8,128)(2,1)}, bf16[128,1024]{1,0:T(8,128)(2,1)S(1)}, u32[]{:S(2)}, u32[]{:S(2)}) collective-permute-start(bf16[128,1024]{1,0:T(8,128)(2,1)} %convolution_convert_fusion.1), channel_id=1, source_target_pairs={{0,1},{1,0},{2,3},{3,2},{4,5},{5,4},{6,7},{7,6},{8,9},{9,8},{10,11... | collective-permute-start | bytes 786440 | tf_op jit(solution)/shard_map/ppermute | solution.py:188
  86.9 21.1 %copy-start.9 = (bf16[128,1024]{1,0:T(8,128)(2,1)}, bf16[128,1024]{1,0:T(8,128)(2,1)S(1)}, u32[]{:S(2)}) copy-start(bf16[128,1024]{1,0:T(8,128)(2,1)S(1)} %subtract_convert_fusion.refs_0_) | copy-start | bytes 786436
  86.9 11.2 %collective-permute-start.13 = (bf16[128,1024]{1,0:T(8,128)(2,1)S(1)}, bf16[128,1024]{1,0:T(8,128)(2,1)S(1)}, u32[]{:S(2)}, u32[]{:S(2)}) collective-permute-start(bf16[128,1024]{1,0:T(8,128)(2,1)S(1)} %subtract_convert_fusion.refs_0_), channel_id=1, source_target_pairs={{0,1},{1,2},{2,3},{3,0},{4,5},{5,6},{6,7},{7,4},{8,9},{9,10},{10,1... | collective-permute-start | bytes 786440 | tf_op jit(solution)/shard_map/ppermute | solution.py:185
  88.0 19.9 %collective-permute-start.14 = (bf16[128,1024]{1,0:T(8,128)(2,1)S(1)}, bf16[128,1024]{1,0:T(8,128)(2,1)S(1)}, u32[]{:S(2)}, u32[]{:S(2)}) collective-permute-start(bf16[128,1024]{1,0:T(8,128)(2,1)S(1)} %subtract_convert_fusion.refs_0_), channel_id=1, source_target_pairs={{0,2},{1,3},{2,0},{3,1},{4,6},{5,7},{6,4},{7,5},{8,10},{9,11},{10,... | collective-permute-start | bytes 786440 | tf_op jit(solution)/shard_map/ppermute | solution.py:185
  90.4 17.6 %collective-permute-start.15 = (bf16[128,1024]{1,0:T(8,128)(2,1)S(1)}, bf16[128,1024]{1,0:T(8,128)(2,1)S(1)}, u32[]{:S(2)}, u32[]{:S(2)}) collective-permute-start(bf16[128,1024]{1,0:T(8,128)(2,1)S(1)} %subtract_convert_fusion.refs_0_), channel_id=1, source_target_pairs={{0,3},{1,0},{2,1},{3,2},{4,7},{5,4},{6,5},{7,6},{8,11},{9,8},{10,9... | collective-permute-start | bytes 786440 | tf_op jit(solution)/shard_map/ppermute | solution.py:185
  98.1 9.9 %copy-start.14 = (bf16[128,1024]{1,0:T(8,128)(2,1)}, bf16[128,1024]{1,0:T(8,128)(2,1)S(1)}, u32[]{:S(2)}) copy-start(bf16[128,1024]{1,0:T(8,128)(2,1)S(1)} %collective-permute-done.13.refs_1_) | copy-start | bytes 786436
  108.0 0.7 copy-start.15
  108.7 0.7 copy-start.16
  114.5 35.1 %all-to-all-start.1 = ((bf16[8,128,1024]{2,1,0:T(8,128)(2,1)}), bf16[8,128,1024]{2,1,0:T(8,128)(2,1)S(1)}, u32[]{:S(2)}, u32[]{:S(2)}) async-start(bf16[8,128,1024]{2,1,0:T(8,128)(2,1)} %bitcast.134), calls=%async_computation.1 | async-start | bytes 4194304 | tf_op jit(solution)/shard_map/all_to_all | solution.py:305
  118.2 1.4 collective-permute-start.17
  118.8 20.3 %collective-permute-start.16 = (bf16[256,1024]{1,0:T(8,128)(2,1)}, bf16[256,1024]{1,0:T(8,128)(2,1)S(1)}, u32[]{:S(2)}, u32[]{:S(2)}) collective-permute-start(bf16[256,1024]{1,0:T(8,128)(2,1)} %get-tuple-element.24), channel_id=1, source_target_pairs={{0,4},{4,0},{8,12},{12,8},{16,20},{20,16},{24,28},{28,24},{1,5},{5... | collective-permute-start | bytes 1572872 | tf_op jit(solution)/shard_map/ppermute | solution.py:195
  119.7 9.2 %collective-permute-start.18 = (f32[64]{0:T(128)S(1)}, f32[64]{0:T(128)S(1)}, u32[]{:S(2)}, u32[]{:S(2)}) collective-permute-start(f32[64]{0:T(128)S(1)} %bitcast_add_fusion.1), channel_id=1, source_target_pairs={{0,1},{1,2},{2,3},{3,0},{4,5},{5,6},{6,7},{7,4},{8,9},{9,10},{10,1... | collective-permute-start | bytes 776 | tf_op jit(solution)/shard_map/ppermute | solution.py:185
  125.0 4.5 %collective-permute-start.19 = (f32[64]{0:T(128)S(1)}, f32[64]{0:T(128)S(1)}, u32[]{:S(2)}, u32[]{:S(2)}) collective-permute-start(f32[64]{0:T(128)S(1)} %bitcast_add_fusion.1), channel_id=1, source_target_pairs={{0,2},{1,3},{2,0},{3,1},{4,6},{5,7},{6,4},{7,5},{8,10},{9,11},{10,... | collective-permute-start | bytes 776 | tf_op jit(solution)/shard_map/ppermute | solution.py:185
  127.9 3.5 %collective-permute-start.20 = (f32[64]{0:T(128)S(1)}, f32[64]{0:T(128)S(1)}, u32[]{:S(2)}, u32[]{:S(2)}) collective-permute-start(f32[64]{0:T(128)S(1)} %bitcast_add_fusion.1), channel_id=1, source_target_pairs={{0,3},{1,0},{2,1},{3,2},{4,7},{5,4},{6,5},{7,6},{8,11},{9,8},{10,9... | collective-permute-start | bytes 776 | tf_op jit(solution)/shard_map/ppermute | solution.py:185
  134.3 10.4 %collective-permute-start.21 = (bf16[2,32,1024]{2,1,0:T(8,128)(2,1)S(1)}, bf16[2,32,1024]{2,1,0:T(8,128)(2,1)S(1)}, u32[]{:S(2)}, u32[]{:S(2)}) collective-permute-start(bf16[2,32,1024]{2,1,0:T(8,128)(2,1)S(1)} %get-tuple-element.50), channel_id=1, source_target_pairs={{0,1},{1,2},{2,3},{3,0},{4,5},{5,6},{6,7},{7,4},{8,9},{9,10},{10,1... | collective-permute-start | bytes 393224 | tf_op jit(solution)/shard_map/ppermute | solution.py:185
  134.3 11.8 %collective-permute-start.22 = (bf16[2,32,1024]{2,1,0:T(8,128)(2,1)S(1)}, bf16[2,32,1024]{2,1,0:T(8,128)(2,1)S(1)}, u32[]{:S(2)}, u32[]{:S(2)}) collective-permute-start(bf16[2,32,1024]{2,1,0:T(8,128)(2,1)S(1)} %get-tuple-element.49), channel_id=1, source_target_pairs={{0,2},{1,3},{2,0},{3,1},{4,6},{5,7},{6,4},{7,5},{8,10},{9,11},{10,... | collective-permute-start | bytes 393224 | tf_op jit(solution)/shard_map/ppermute | solution.py:185
  136.7 9.5 %collective-permute-start.23 = (bf16[2,32,1024]{2,1,0:T(8,128)(2,1)S(1)}, bf16[2,32,1024]{2,1,0:T(8,128)(2,1)S(1)}, u32[]{:S(2)}, u32[]{:S(2)}) collective-permute-start(bf16[2,32,1024]{2,1,0:T(8,128)(2,1)S(1)} %get-tuple-element.48), channel_id=1, source_target_pairs={{0,3},{1,0},{2,1},{3,2},{4,7},{5,4},{6,5},{7,6},{8,11},{9,8},{10,9... | collective-permute-start | bytes 393224 | tf_op jit(solution)/shard_map/ppermute | solution.py:185
  139.1 0.8 copy-start.6
  144.8 1.4 copy-start.10
  146.2 0.7 copy-start.11
  146.2 0.7 copy-start.12

commit v14 on v11

--- a/solution.py
+++ b/solution.py
@@ -301,7 +301,7 @@
 
     pieces = [d_round] + [along_hid(d_round, shift) for shift in range(1, hids)]
     ratio_rows = ratio_group.reshape(steps, rows, 1)
-    d_ratio_part = after(d_ratio_part, d_round)
+    d_ratio_part = after(d_ratio_part, *pieces[1:])
     d_ratio = d_ratio_part[0]
     for m in relations:
         d_ratio += flip_seq(d_ratio_part[m], m)
@@ -310,7 +310,7 @@
         d_rows = lax.dynamic_update_index_in_dim(
             d_rows, along_hid(d_ratio, shift), (j - shift) % hids, 0
         )
-    share, mine, *others = input_gradient(after(place, d_rows), pieces, group, ratio_rows, seqs)
+    share, mine, *others = input_gradient(place, pieces, group, ratio_rows, seqs)
     share = lax.all_to_all(share.reshape(seqs, depth // seqs, units), "seq", 0, 0)
     share = share.reshape(groups, steps, depth // seqs, units).astype(F32).sum(0)
     grad_in = share.transpose(0, 2, 1)

time: 150 us -> 152 us (1.013)
  starting transfers between devices: 40.4 us -> 45.2 us
    ppermute x4, waiting for transfers between devices: 8.41 us -> 16.1 us  [turn_hid(): lax.ppermute(values, 'hid', [(a, a - a % halves + (a % halves + shift) %...]
    all_to_all x1, waiting for transfers between devices: 6.53 us -> 0.01 us  [shards(): lax.all_to_all(share.reshape(seqs, depth // seqs, units), 'seq', 0, 0)]
    ppermute x15, starting transfers between devices: 21.9 us -> 27.2 us  [along_hid(): lax.ppermute(values, 'hid', [(a, (a + shift) % hids) for a in range(hids)])]
    ppermute x15, waiting for transfers between devices: 43.8 us -> 41.9 us  [along_hid(): lax.ppermute(values, 'hid', [(a, (a + shift) % hids) for a in range(hids)])]
  transfers between devices with their start and end apart: 27 -> 27, of which waited for: 9 -> 13; matrix products, arithmetic and copies ran while one was open for 17% -> 14% of each run, Pallas kernels for 9% -> 8%
where the time goes in v14:
time: 152 us
  waiting for transfers between devices  58.7 us (39%)
  starting transfers between devices  45.2 us (30%)
  local copies, waits for them, and re-layouts  18 us (12%)
  Pallas kernels  12.7 us (8%)
  matrix products  8.47 us (6%)
  other arithmetic  7.32 us (5%)
    ppermute x15, waiting for transfers between devices, along_hid(): lax.ppermute(values, 'hid', [(a, (a + shift) % hids) for a in range(hids)])  41.9 us
    ppermute x15, starting transfers between devices, along_hid(): lax.ppermute(values, 'hid', [(a, (a + shift) % hids) for a in range(hids)])  27.2 us
    ppermute x4, waiting for transfers between devices, turn_hid(): lax.ppermute(values, 'hid', [(a, a - a % halves + (a % halves + shift) %...  16.1 us
    pallas_call x3, Pallas kernels, call(): pl.pallas_call(kernel, grid_spec=pltpu.PrefetchScalarGridSpec(num_scalar_...  12.7 us
    dot_general x5, matrix products, matmul(): lax.dot_general(a, b, (contract, ((), ())), preferred_element_type=F32)  8.47 us
    unnamed x44, local copies, waits for them, and re-layouts  5.74 us
    ppermute x4, starting transfers between devices, turn_hid(): lax.ppermute(values, 'hid', [(a, a - a % halves + (a % halves + shift) %...  4.36 us
    all_to_all x1, starting transfers between devices, shards(): part_out = lax.all_to_all(part_out, 'seq', 0, 0)  4.34 us
  transfers between devices with their start and end apart: 27, of which 13 were waited for; matrix products, arithmetic and copies ran while one was open for 14% of the time, Pallas kernels for 8%

profile of v14, /device:TPU:0, one launch (start us, length us, event | category | flops | bytes accessed | tf_op | source)
XLA Modules:
  0.0 151.5 jit_solution(2425477200846287145)
XLA Ops:
  1.2 1.2 multiply_reduce_fusion
  2.5 1.1 reshape.241
  4.4 4.7 %collective-permute-start.3 = (bf16[72,1024]{1,0:T(8,128)(2,1)S(1)}, bf16[72,1024]{1,0:T(8,128)(2,1)S(1)}, u32[]{:S(2)}, u32[]{:S(2)}) collective-permute-start(bf16[72,1024]{1,0:T(8,128)(2,1)S(1)} %get-tuple-element.57), channel_id=1, source_target_pairs={{0,3},{1,0},{2,1},{3,2},{4,7},{5,4},{6,5},{7,6},{8,11},{9,8},{10,9... | collective-permute-start | bytes 442376 | tf_op jit(solution)/shard_map/ppermute | solution.py:185
  9.1 1.0 collective-permute-start.2
  10.2 3.0 %fusion = f32[2,4,64,1024]{3,2,1,0:T(8,128)S(1)} fusion(bf16[2,4,64,1024]{3,2,1,0:T(8,128)(2,1)S(1)} %bitcast.123, bf16[2,1024,1024]{2,1,0:T(8,128)(2,1)} %refs_2_.1, s32[]{:T(128)S(6)} %select_n.139), kind=kOutput, calls=%fused_computation.2 | convolution fusion | flops 1073741824 | bytes 5242884 | tf_op jit(solution)/shard_map/dot_general | solution.py:17
  13.2 1.3 copy-done.4
  14.5 0.8 dynamic-slice_convert_fusion
  15.3 6.9 %collective-permute-done.2 = bf16[72,1024]{1,0:T(8,128)(2,1)S(1)} collective-permute-done((bf16[72,1024]{1,0:T(8,128)(2,1)S(1)}, bf16[72,1024]{1,0:T(8,128)(2,1)S(1)}, u32[]{:S(2)}, u32[]{:S(2)}) %collective-permute-start.2) | collective-permute-done | bytes 147488 | tf_op jit(solution)/shard_map/ppermute | solution.py:185
  22.5 1.6 %broadcast_in_dim.45 = bf16[4,2,128,1024]{3,2,1,0:T(8,128)(2,1)} broadcast(bf16[2,128,1024]{2,1,0:T(8,128)(2,1)S(1)} %bitcast.116), dimensions={1,2,3} | broadcast | bytes 2621440 | tf_op jit(solution)/shard_map/broadcast_in_dim | solution.py:244
  24.1 3.9 %all-to-all-start = ((bf16[8,128,1024]{2,1,0:T(8,128)(2,1)}), bf16[8,128,1024]{2,1,0:T(8,128)(2,1)S(1)}, u32[]{:S(2)}, u32[]{:S(2)}) async-start(bf16[8,128,1024]{2,1,0:T(8,128)(2,1)} %bitcast.112), calls=%async_computation | async-start | bytes 4194304 | tf_op jit(solution)/shard_map/all_to_all | solution.py:246
  28.7 2.6 %collective-permute-start.7 = (bf16[128,1024]{1,0:T(8,128)(2,1)}, bf16[128,1024]{1,0:T(8,128)(2,1)}, u32[]{:S(2)}, u32[]{:S(2)}) collective-permute-start(bf16[128,1024]{1,0:T(8,128)(2,1)} %bitcast.10), channel_id=1, source_target_pairs={{0,3},{1,0},{2,1},{3,2},{4,7},{5,4},{6,5},{7,6},{8,11},{9,8},{10,9... | collective-permute-start | bytes 786440 | tf_op jit(solution)/shard_map/ppermute | solution.py:185
  32.0 1.1 constant_dynamic-slice_fusion.6
  33.2 3.8 %gather_fusion = bf16[128,1024]{1,0:T(8,128)(2,1)S(1)} fusion(bf16[2048,1024]{1,0:T(8,128)(2,1)} %bitcast.122, s32[1024]{0:T(1024)S(1)} %pad_clamp_fusion), kind=kCustom, calls=%fused_computation | custom fusion | bytes 524800 | tf_op jit(solution)/shard_map/jit(_take)/gather | solution.py:240
  37.1 2.2 %collective-permute-done.7 = bf16[128,1024]{1,0:T(8,128)(2,1)} collective-permute-done((bf16[128,1024]{1,0:T(8,128)(2,1)}, bf16[128,1024]{1,0:T(8,128)(2,1)}, u32[]{:S(2)}, u32[]{:S(2)}) %collective-permute-start.7) | collective-permute-done | bytes 262176 | tf_op jit(solution)/shard_map/ppermute | solution.py:185
  39.3 14.5 %collective-permute-done.6 = bf16[128,1024]{1,0:T(8,128)(2,1)} collective-permute-done((bf16[128,1024]{1,0:T(8,128)(2,1)S(1)}, bf16[128,1024]{1,0:T(8,128)(2,1)}, u32[]{:S(2)}, u32[]{:S(2)}) %collective-permute-start.6) | collective-permute-done | bytes 262176 | tf_op jit(solution)/shard_map/ppermute | solution.py:185
  53.8 1.4 multiply_reduce_fusion.4
  55.5 1.2 collective-permute-start.9
  56.7 0.9 collective-permute-start.11
  57.6 5.9 %collective-permute-done.11 = s32[2,128]{1,0:T(2,128)S(1)} collective-permute-done((s32[2,128]{1,0:T(2,128)S(1)}, s32[2,128]{1,0:T(2,128)S(1)}, u32[]{:S(2)}, u32[]{:S(2)}) %collective-permute-start.11) | collective-permute-done | bytes 1056 | tf_op jit(solution)/shard_map/ppermute | solution.py:188
  63.5 0.8 fusion.36
  64.7 1.1 collective-permute-start.10
  65.8 2.5 %collective-permute-done.10 = f32[2,2,128]{2,1,0:T(2,128)S(1)} collective-permute-done((f32[2,2,128]{2,1,0:T(2,128)S(1)}, f32[2,2,128]{2,1,0:T(2,128)S(1)}, u32[]{:S(2)}, u32[]{:S(2)}) %collective-permute-start.10) | collective-permute-done | bytes 2080 | tf_op jit(solution)/shard_map/ppermute | solution.py:188
  68.8 1.5 %convolution_convert_fusion.1 = bf16[128,1024]{1,0:T(8,128)(2,1)} fusion(bf16[1024,1024]{1,0:T(8,128)(2,1)S(1)} %bitcast.110, bf16[256,1024]{1,0:T(8,128)(2,1)S(1)} %multiply_convert_fusion), kind=kOutput, calls=%fused_computation.6 | convolution fusion | flops 268566528 | bytes 2621440 | tf_op jit(solution)/shard_map/dot_general | solution.py:17
  70.3 2.1 %convolution_convert_fusion = bf16[1024,1024]{1,0:T(8,128)(2,1)} fusion(bf16[256,1024]{1,0:T(8,128)(2,1)S(1)} %multiply_convert_fusion, bf16[128,1024]{1,0:T(8,128)(2,1)S(1)} %copy-done.8, bf16[128,1024]{1,0:T(8,128)(2,1)S(1)} %copy-done.3), kind=kOutput, calls=%fused_computation.5 | convolution fusion | flops 538968064 | bytes 3145728 | tf_op jit(solution)/shard_map/dot_general | solution.py:17
  72.4 4.3 %all-to-all-start.2 = ((bf16[8,128,1024]{2,1,0:T(8,128)(2,1)}), bf16[8,128,1024]{2,1,0:T(8,128)(2,1)}, u32[]{:S(2)}, u32[]{:S(2)}) async-start(bf16[8,128,1024]{2,1,0:T(8,128)(2,1)} %bitcast.114), calls=%async_computation.2 | async-start | bytes 4194304 | tf_op jit(solution)/shard_map/all_to_all | solution.py:293
  76.8 1.1 collective-permute-start.12
  77.9 7.6 %collective-permute-done.12 = bf16[128,1024]{1,0:T(8,128)(2,1)S(1)} collective-permute-done((bf16[128,1024]{1,0:T(8,128)(2,1)}, bf16[128,1024]{1,0:T(8,128)(2,1)S(1)}, u32[]{:S(2)}, u32[]{:S(2)}) %collective-permute-start.12) | collective-permute-done | bytes 262176 | tf_op jit(solution)/shard_map/ppermute | solution.py:188
  85.5 1.1 multiply_reduce_fusion.2
  86.9 1.1 collective-permute-start.13
  88.0 2.3 %collective-permute-start.14 = (bf16[128,1024]{1,0:T(8,128)(2,1)S(1)}, bf16[128,1024]{1,0:T(8,128)(2,1)S(1)}, u32[]{:S(2)}, u32[]{:S(2)}) collective-permute-start(bf16[128,1024]{1,0:T(8,128)(2,1)S(1)} %subtract_convert_fusion.refs_0_), channel_id=1, source_target_pairs={{0,2},{1,3},{2,0},{3,1},{4,6},{5,7},{6,4},{7,5},{8,10},{9,11},{10,... | collective-permute-start | bytes 786440 | tf_op jit(solution)/shard_map/ppermute | solution.py:185
  90.3 2.6 %collective-permute-start.15 = (bf16[128,1024]{1,0:T(8,128)(2,1)S(1)}, bf16[128,1024]{1,0:T(8,128)(2,1)S(1)}, u32[]{:S(2)}, u32[]{:S(2)}) collective-permute-start(bf16[128,1024]{1,0:T(8,128)(2,1)S(1)} %subtract_convert_fusion.refs_0_), channel_id=1, source_target_pairs={{0,3},{1,0},{2,1},{3,2},{4,7},{5,4},{6,5},{7,6},{8,11},{9,8},{10,9... | collective-permute-start | bytes 786440 | tf_op jit(solution)/shard_map/ppermute | solution.py:185
  93.7 0.9 copy.39.refs_6_
  94.5 3.6 %collective-permute-done.13.refs_1_ = bf16[128,1024]{1,0:T(8,128)(2,1)S(1)} collective-permute-done((bf16[128,1024]{1,0:T(8,128)(2,1)S(1)}, bf16[128,1024]{1,0:T(8,128)(2,1)S(1)}, u32[]{:S(2)}, u32[]{:S(2)}) %collective-permute-start.13) | collective-permute-done | bytes 262176 | tf_op jit(solution)/shard_map/ppermute | solution.py:185
  98.1 9.9 %collective-permute-done.14.refs_2_ = bf16[128,1024]{1,0:T(8,128)(2,1)S(1)} collective-permute-done((bf16[128,1024]{1,0:T(8,128)(2,1)S(1)}, bf16[128,1024]{1,0:T(8,128)(2,1)S(1)}, u32[]{:S(2)}, u32[]{:S(2)}) %collective-permute-start.14) | collective-permute-done | bytes 262176 | tf_op jit(solution)/shard_map/ppermute | solution.py:185
  109.4 5.1 %shard_map.85 = (bf16[1024,1024]{1,0:T(8,128)(2,1)}, bf16[256,1024]{1,0:T(8,128)(2,1)}, bf16[256,1024]{1,0:T(8,128)(2,1)}) custom-call(s32[2]{0:T(128)} %pad_add_fusion.2.place_ref, bf16[128,1024]{1,0:T(8,128)(2,1)} %copy-done.9, bf16[128,1024]{1,0:T(8,128)(2,1)} %copy-done.14, bf16[128,1024]{1,0:T(8,128)(2,1)} %copy-done.15, bf16[128,1024]{1,0:T(8,128)(2,1)} %copy-done.16, ...), custom_call_target="tpu_custom_call" | custom-call | flops 1073741824 | bytes 2099200 | tf_op jit(solution)/shard_map/pallas_call | solution.py:33
  114.4 3.7 %all-to-all-start.1 = ((bf16[8,128,1024]{2,1,0:T(8,128)(2,1)}), bf16[8,128,1024]{2,1,0:T(8,128)(2,1)S(1)}, u32[]{:S(2)}, u32[]{:S(2)}) async-start(bf16[8,128,1024]{2,1,0:T(8,128)(2,1)} %bitcast.117), calls=%async_computation.1 | async-start | bytes 4194304 | tf_op jit(solution)/shard_map/all_to_all | solution.py:314
  119.9 5.3 %collective-permute-start.18 = (f32[64]{0:T(128)S(1)}, f32[64]{0:T(128)S(1)}, u32[]{:S(2)}, u32[]{:S(2)}) collective-permute-start(f32[64]{0:T(128)S(1)} %bitcast_add_fusion.1), channel_id=1, source_target_pairs={{0,1},{1,2},{2,3},{3,0},{4,5},{5,6},{6,7},{7,4},{8,9},{9,10},{10,1... | collective-permute-start | bytes 776 | tf_op jit(solution)/shard_map/ppermute | solution.py:185
  125.2 3.0 %collective-permute-start.19 = (f32[64]{0:T(128)S(1)}, f32[64]{0:T(128)S(1)}, u32[]{:S(2)}, u32[]{:S(2)}) collective-permute-start(f32[64]{0:T(128)S(1)} %bitcast_add_fusion.1), channel_id=1, source_target_pairs={{0,2},{1,3},{2,0},{3,1},{4,6},{5,7},{6,4},{7,5},{8,10},{9,11},{10,... | collective-permute-start | bytes 776 | tf_op jit(solution)/shard_map/ppermute | solution.py:185
  128.1 0.9 collective-permute-done.18
  129.7 2.0 %collective-permute-done.20 = f32[64]{0:T(128)S(1)} collective-permute-done((f32[64]{0:T(128)S(1)}, f32[64]{0:T(128)S(1)}, u32[]{:S(2)}, u32[]{:S(2)}) %collective-permute-start.20) | collective-permute-done | bytes 288 | tf_op jit(solution)/shard_map/ppermute | solution.py:185
  131.8 2.0 %reduce_sum.108 = bf16[2,4,32,1024]{3,2,1,0:T(8,128)(2,1)S(1)} reduce(bf16[4,2,4,32,1024]{4,3,2,1,0:T(8,128)(2,1)} %bitcast.53, bf16[]{:T(256)} %constant.168.clone.1), dimensions={0}, to_apply=%region_10.11 | reduce | flops 786432 | bytes 2621442 | tf_op jit(solution)/shard_map/reduce_sum | solution.py:294
  134.5 2.4 %collective-permute-start.22 = (bf16[2,32,1024]{2,1,0:T(8,128)(2,1)S(1)}, bf16[2,32,1024]{2,1,0:T(8,128)(2,1)S(1)}, u32[]{:S(2)}, u32[]{:S(2)}) collective-permute-start(bf16[2,32,1024]{2,1,0:T(8,128)(2,1)S(1)} %get-tuple-element.51), channel_id=1, source_target_pairs={{0,2},{1,3},{2,0},{3,1},{4,6},{5,7},{6,4},{7,5},{8,10},{9,11},{10,... | collective-permute-start | bytes 393224 | tf_op jit(solution)/shard_map/ppermute | solution.py:185
  136.9 1.5 collective-permute-start.23
  138.4 0.9 copy.40.refs_4_
  140.0 4.9 %shard_map.86 = bf16[256,1024]{1,0:T(8,128)(2,1)} custom-call(s32[2]{0:T(128)} %pad_add_fusion.2.place_ref, bf16[256,1024]{1,0:T(8,128)(2,1)} %get-tuple-element.24.refs_0_, bf16[256,1024]{1,0:T(8,128)(2,1)} %copy-done.6, bf16[2,1024,1024]{2,1,0:T(8,128)(2,1)} %refs_2_.1, bf16[256,1024]{1,0:T(8,128)(2,1)} %refs_3_.1, f32[2,256,1]{2,1,0:T(8,128)} %copy.40.refs_4_), custom_call_target="tpu_custom_call" | custom-call | flops 1073741824 | bytes 5769216 | tf_op jit(solution)/shard_map/pallas_call | solution.py:33
  145.0 1.5 collective-permute-done.22.refs_2_
  147.1 2.7 %shard_map.87 = f32[32,2,2048]{2,1,0:T(2,128)} custom-call(s32[2]{0:T(128)} %pad_add_fusion.2.place_ref, bf16[2,32,1024]{2,1,0:T(8,128)(2,1)} %get-tuple-element.53.refs_0_, bf16[2,32,1024]{2,1,0:T(8,128)(2,1)} %copy-done.10, bf16[2,32,1024]{2,1,0:T(8,128)(2,1)} %copy-done.11, bf16[2,32,1024]{2,1,0:T(8,128)(2,1)} %copy-done.12), custom_call_target="tpu_custom_call" | custom-call | flops 262144 | bytes 524288 | tf_op jit(solution)/shard_map/pallas_call | solution.py:33
  150.2 1.3 copy.41
  (124 shorter events, 11.7 us)
Async XLA Ops:
  0.6 9.5 %copy-start = (f32[2,1024]{1,0:T(2,128)S(1)}, f32[2,1024]{1,0:T(2,128)}, u32[]{:S(2)}) copy-start(f32[2,1024]{1,0:T(2,128)} %param.9) | copy-start | bytes 24580
  0.6 9.5 %copy-start.1 = (bf16[256,1024]{1,0:T(8,128)(2,1)S(1)}, bf16[256,1024]{1,0:T(8,128)(2,1)}, u32[]{:S(2)}) copy-start(bf16[256,1024]{1,0:T(8,128)(2,1)} %refs_3_.1) | copy-start | bytes 1572868
  0.7 9.5 %collective-permute-start.1 = (bf16[256,1024]{1,0:T(8,128)(2,1)}, bf16[256,1024]{1,0:T(8,128)(2,1)S(1)}, u32[]{:S(2)}, u32[]{:S(2)}) collective-permute-start(bf16[256,1024]{1,0:T(8,128)(2,1)} %refs_3_.1), channel_id=1, source_target_pairs={{0,4},{4,0},{8,12},{12,8},{16,20},{20,16},{24,28},{28,24},{1,5},{5... | collective-permute-start | bytes 1572872 | tf_op jit(solution)/shard_map/ppermute | solution.py:195
  4.4 11.0 %collective-permute-start.3 = (bf16[72,1024]{1,0:T(8,128)(2,1)S(1)}, bf16[72,1024]{1,0:T(8,128)(2,1)S(1)}, u32[]{:S(2)}, u32[]{:S(2)}) collective-permute-start(bf16[72,1024]{1,0:T(8,128)(2,1)S(1)} %get-tuple-element.57), channel_id=1, source_target_pairs={{0,3},{1,0},{2,1},{3,2},{4,7},{5,4},{6,5},{7,6},{8,11},{9,8},{10,9... | collective-permute-start | bytes 442376 | tf_op jit(solution)/shard_map/ppermute | solution.py:185
  9.1 13.1 %collective-permute-start = (bf16[72,1024]{1,0:T(8,128)(2,1)S(1)}, bf16[72,1024]{1,0:T(8,128)(2,1)S(1)}, u32[]{:S(2)}, u32[]{:S(2)}) collective-permute-start(bf16[72,1024]{1,0:T(8,128)(2,1)S(1)} %get-tuple-element.57), channel_id=1, source_target_pairs={{0,1},{1,2},{2,3},{3,0},{4,5},{5,6},{6,7},{7,4},{8,9},{9,10},{10,1... | collective-permute-start | bytes 442376 | tf_op jit(solution)/shard_map/ppermute | solution.py:185
  9.1 13.1 %collective-permute-start.2 = (bf16[72,1024]{1,0:T(8,128)(2,1)S(1)}, bf16[72,1024]{1,0:T(8,128)(2,1)S(1)}, u32[]{:S(2)}, u32[]{:S(2)}) collective-permute-start(bf16[72,1024]{1,0:T(8,128)(2,1)S(1)} %get-tuple-element.56), channel_id=1, source_target_pairs={{0,2},{1,3},{2,0},{3,1},{4,6},{5,7},{6,4},{7,5},{8,10},{9,11},{10,... | collective-permute-start | bytes 442376 | tf_op jit(solution)/shard_map/ppermute | solution.py:185
  10.1 3.1 %copy-start.5 = (bf16[256,1024]{1,0:T(8,128)(2,1)}, bf16[256,1024]{1,0:T(8,128)(2,1)S(1)}, u32[]{:S(2)}) copy-start(bf16[256,1024]{1,0:T(8,128)(2,1)S(1)} %collective-permute-done.1.refs_5_) | copy-start | bytes 1572868
  13.2 1.3 copy-start.4
  24.1 4.5 %copy-start.13 = (s32[2,64]{1,0:T(2,128)S(1)}, s32[2,64]{1,0:T(2,128)}, u32[]{:S(2)}) copy-start(s32[2,64]{1,0:T(2,128)} %param.11) | copy-start | bytes 1540
  24.1 39.4 %all-to-all-start = ((bf16[8,128,1024]{2,1,0:T(8,128)(2,1)}), bf16[8,128,1024]{2,1,0:T(8,128)(2,1)S(1)}, u32[]{:S(2)}, u32[]{:S(2)}) async-start(bf16[8,128,1024]{2,1,0:T(8,128)(2,1)} %bitcast.112), calls=%async_computation | async-start | bytes 4194304 | tf_op jit(solution)/shard_map/all_to_all | solution.py:246
  28.0 8.9 %collective-permute-start.4 = (f32[256]{0:T(256)S(1)}, f32[256]{0:T(256)S(1)}, u32[]{:S(2)}, u32[]{:S(2)}) collective-permute-start(f32[256]{0:T(256)S(1)} %slice_reduce_fusion), channel_id=1, source_target_pairs={{0,4},{4,0},{8,12},{12,8},{16,20},{20,16},{24,28},{28,24},{1,5},{5... | collective-permute-start | bytes 3080 | tf_op jit(solution)/shard_map/ppermute | solution.py:195
  28.6 4.4 %collective-permute-start.8 = (s32[2,64]{1,0:T(2,128)S(1)}, s32[2,64]{1,0:T(2,128)S(1)}, u32[]{:S(2)}, u32[]{:S(2)}) collective-permute-start(s32[2,64]{1,0:T(2,128)S(1)} %copy-done.13), channel_id=1, source_target_pairs={{0,4},{4,0},{8,12},{12,8},{16,20},{20,16},{24,28},{28,24},{1,5},{5... | collective-permute-start | bytes 1544 | tf_op jit(solution)/shard_map/ppermute | solution.py:195
  28.7 10.6 %collective-permute-start.7 = (bf16[128,1024]{1,0:T(8,128)(2,1)}, bf16[128,1024]{1,0:T(8,128)(2,1)}, u32[]{:S(2)}, u32[]{:S(2)}) collective-permute-start(bf16[128,1024]{1,0:T(8,128)(2,1)} %bitcast.10), channel_id=1, source_target_pairs={{0,3},{1,0},{2,1},{3,2},{4,7},{5,4},{6,5},{7,6},{8,11},{9,8},{10,9... | collective-permute-start | bytes 786440 | tf_op jit(solution)/shard_map/ppermute | solution.py:185
  31.3 22.5 %collective-permute-start.6 = (bf16[128,1024]{1,0:T(8,128)(2,1)S(1)}, bf16[128,1024]{1,0:T(8,128)(2,1)}, u32[]{:S(2)}, u32[]{:S(2)}) collective-permute-start(bf16[128,1024]{1,0:T(8,128)(2,1)S(1)} %bitcast.126), channel_id=1, source_target_pairs={{0,2},{1,3},{2,0},{3,1},{4,6},{5,7},{6,4},{7,5},{8,10},{9,11},{10,... | collective-permute-start | bytes 786440 | tf_op jit(solution)/shard_map/ppermute | solution.py:185
  31.3 22.5 %collective-permute-start.5 = (bf16[128,1024]{1,0:T(8,128)(2,1)S(1)}, bf16[128,1024]{1,0:T(8,128)(2,1)}, u32[]{:S(2)}, u32[]{:S(2)}) collective-permute-start(bf16[128,1024]{1,0:T(8,128)(2,1)S(1)} %bitcast.125), channel_id=1, source_target_pairs={{0,1},{1,2},{2,3},{3,0},{4,5},{5,6},{6,7},{7,4},{8,9},{9,10},{10,1... | collective-permute-start | bytes 786440 | tf_op jit(solution)/shard_map/ppermute | solution.py:185
  55.5 9.2 %copy-start.2 = (bf16[128,1024]{1,0:T(8,128)(2,1)}, bf16[128,1024]{1,0:T(8,128)(2,1)S(1)}, u32[]{:S(2)}) copy-start(bf16[128,1024]{1,0:T(8,128)(2,1)S(1)} %multiply_convert_fusion.1) | copy-start | bytes 786436
  55.5 8.0 %collective-permute-start.9 = (bf16[128,1024]{1,0:T(8,128)(2,1)S(1)}, bf16[128,1024]{1,0:T(8,128)(2,1)S(1)}, u32[]{:S(2)}, u32[]{:S(2)}) collective-permute-start(bf16[128,1024]{1,0:T(8,128)(2,1)S(1)} %multiply_convert_fusion.1), channel_id=1, source_target_pairs={{0,1},{1,0},{2,3},{3,2},{4,5},{5,4},{6,7},{7,6},{8,9},{9,8},{10,11... | collective-permute-start | bytes 786440 | tf_op jit(solution)/shard_map/ppermute | solution.py:188
  56.7 6.8 %collective-permute-start.11 = (s32[2,128]{1,0:T(2,128)S(1)}, s32[2,128]{1,0:T(2,128)S(1)}, u32[]{:S(2)}, u32[]{:S(2)}) collective-permute-start(s32[2,128]{1,0:T(2,128)S(1)} %pad_add_fusion), channel_id=1, source_target_pairs={{0,1},{1,0},{2,3},{3,2},{4,5},{5,4},{6,7},{7,6},{8,9},{9,8},{10,11... | collective-permute-start | bytes 3080 | tf_op jit(solution)/shard_map/ppermute | solution.py:188
  63.5 1.2 copy-start.7
  64.7 3.7 %collective-permute-start.10 = (f32[2,2,128]{2,1,0:T(2,128)S(1)}, f32[2,2,128]{2,1,0:T(2,128)S(1)}, u32[]{:S(2)}, u32[]{:S(2)}) collective-permute-start(f32[2,2,128]{2,1,0:T(2,128)S(1)} %pad_maximum_fusion.6), channel_id=1, source_target_pairs={{0,1},{1,0},{2,3},{3,2},{4,5},{5,4},{6,7},{7,6},{8,9},{9,8},{10,11... | collective-permute-start | bytes 6152 | tf_op jit(solution)/shard_map/ppermute | solution.py:188
  68.4 1.9 %copy-start.3 = (bf16[128,1024]{1,0:T(8,128)(2,1)S(1)}, bf16[128,1024]{1,0:T(8,128)(2,1)}, u32[]{:S(2)}) copy-start(bf16[128,1024]{1,0:T(8,128)(2,1)} %copy-done.2) | copy-start | bytes 786436
  68.4 1.9 %copy-start.8 = (bf16[128,1024]{1,0:T(8,128)(2,1)S(1)}, bf16[128,1024]{1,0:T(8,128)(2,1)}, u32[]{:S(2)}) copy-start(bf16[128,1024]{1,0:T(8,128)(2,1)} %copy-done.7) | copy-start | bytes 786436
  72.4 42.0 %all-to-all-start.2 = ((bf16[8,128,1024]{2,1,0:T(8,128)(2,1)}), bf16[8,128,1024]{2,1,0:T(8,128)(2,1)}, u32[]{:S(2)}, u32[]{:S(2)}) async-start(bf16[8,128,1024]{2,1,0:T(8,128)(2,1)} %bitcast.114), calls=%async_computation.2 | async-start | bytes 4194304 | tf_op jit(solution)/shard_map/all_to_all | solution.py:293
  76.8 8.8 %collective-permute-start.12 = (bf16[128,1024]{1,0:T(8,128)(2,1)}, bf16[128,1024]{1,0:T(8,128)(2,1)S(1)}, u32[]{:S(2)}, u32[]{:S(2)}) collective-permute-start(bf16[128,1024]{1,0:T(8,128)(2,1)} %convolution_convert_fusion.1), channel_id=1, source_target_pairs={{0,1},{1,0},{2,3},{3,2},{4,5},{5,4},{6,7},{7,6},{8,9},{9,8},{10,11... | collective-permute-start | bytes 786440 | tf_op jit(solution)/shard_map/ppermute | solution.py:188
  86.9 21.1 %copy-start.9 = (bf16[128,1024]{1,0:T(8,128)(2,1)}, bf16[128,1024]{1,0:T(8,128)(2,1)S(1)}, u32[]{:S(2)}) copy-start(bf16[128,1024]{1,0:T(8,128)(2,1)S(1)} %subtract_convert_fusion.refs_0_) | copy-start | bytes 786436
  86.9 11.2 %collective-permute-start.13 = (bf16[128,1024]{1,0:T(8,128)(2,1)S(1)}, bf16[128,1024]{1,0:T(8,128)(2,1)S(1)}, u32[]{:S(2)}, u32[]{:S(2)}) collective-permute-start(bf16[128,1024]{1,0:T(8,128)(2,1)S(1)} %subtract_convert_fusion.refs_0_), channel_id=1, source_target_pairs={{0,1},{1,2},{2,3},{3,0},{4,5},{5,6},{6,7},{7,4},{8,9},{9,10},{10,1... | collective-permute-start | bytes 786440 | tf_op jit(solution)/shard_map/ppermute | solution.py:185
  88.0 19.9 %collective-permute-start.14 = (bf16[128,1024]{1,0:T(8,128)(2,1)S(1)}, bf16[128,1024]{1,0:T(8,128)(2,1)S(1)}, u32[]{:S(2)}, u32[]{:S(2)}) collective-permute-start(bf16[128,1024]{1,0:T(8,128)(2,1)S(1)} %subtract_convert_fusion.refs_0_), channel_id=1, source_target_pairs={{0,2},{1,3},{2,0},{3,1},{4,6},{5,7},{6,4},{7,5},{8,10},{9,11},{10,... | collective-permute-start | bytes 786440 | tf_op jit(solution)/shard_map/ppermute | solution.py:185
  90.3 17.6 %collective-permute-start.15 = (bf16[128,1024]{1,0:T(8,128)(2,1)S(1)}, bf16[128,1024]{1,0:T(8,128)(2,1)S(1)}, u32[]{:S(2)}, u32[]{:S(2)}) collective-permute-start(bf16[128,1024]{1,0:T(8,128)(2,1)S(1)} %subtract_convert_fusion.refs_0_), channel_id=1, source_target_pairs={{0,3},{1,0},{2,1},{3,2},{4,7},{5,4},{6,5},{7,6},{8,11},{9,8},{10,9... | collective-permute-start | bytes 786440 | tf_op jit(solution)/shard_map/ppermute | solution.py:185
  98.1 9.9 %copy-start.14 = (bf16[128,1024]{1,0:T(8,128)(2,1)}, bf16[128,1024]{1,0:T(8,128)(2,1)S(1)}, u32[]{:S(2)}) copy-start(bf16[128,1024]{1,0:T(8,128)(2,1)S(1)} %collective-permute-done.13.refs_1_) | copy-start | bytes 786436
  108.0 0.7 copy-start.15
  108.7 0.7 copy-start.16
  114.4 35.4 %all-to-all-start.1 = ((bf16[8,128,1024]{2,1,0:T(8,128)(2,1)}), bf16[8,128,1024]{2,1,0:T(8,128)(2,1)S(1)}, u32[]{:S(2)}, u32[]{:S(2)}) async-start(bf16[8,128,1024]{2,1,0:T(8,128)(2,1)} %bitcast.117), calls=%async_computation.1 | async-start | bytes 4194304 | tf_op jit(solution)/shard_map/all_to_all | solution.py:314
  118.5 1.4 collective-permute-start.17
  119.0 20.2 %collective-permute-start.16 = (bf16[256,1024]{1,0:T(8,128)(2,1)}, bf16[256,1024]{1,0:T(8,128)(2,1)S(1)}, u32[]{:S(2)}, u32[]{:S(2)}) collective-permute-start(bf16[256,1024]{1,0:T(8,128)(2,1)} %get-tuple-element.25), channel_id=1, source_target_pairs={{0,4},{4,0},{8,12},{12,8},{16,20},{20,16},{24,28},{28,24},{1,5},{5... | collective-permute-start | bytes 1572872 | tf_op jit(solution)/shard_map/ppermute | solution.py:195
  119.9 9.2 %collective-permute-start.18 = (f32[64]{0:T(128)S(1)}, f32[64]{0:T(128)S(1)}, u32[]{:S(2)}, u32[]{:S(2)}) collective-permute-start(f32[64]{0:T(128)S(1)} %bitcast_add_fusion.1), channel_id=1, source_target_pairs={{0,1},{1,2},{2,3},{3,0},{4,5},{5,6},{6,7},{7,4},{8,9},{9,10},{10,1... | collective-permute-start | bytes 776 | tf_op jit(solution)/shard_map/ppermute | solution.py:185
  125.2 4.5 %collective-permute-start.19 = (f32[64]{0:T(128)S(1)}, f32[64]{0:T(128)S(1)}, u32[]{:S(2)}, u32[]{:S(2)}) collective-permute-start(f32[64]{0:T(128)S(1)} %bitcast_add_fusion.1), channel_id=1, source_target_pairs={{0,2},{1,3},{2,0},{3,1},{4,6},{5,7},{6,4},{7,5},{8,10},{9,11},{10,... | collective-permute-start | bytes 776 | tf_op jit(solution)/shard_map/ppermute | solution.py:185
  128.1 3.5 %collective-permute-start.20 = (f32[64]{0:T(128)S(1)}, f32[64]{0:T(128)S(1)}, u32[]{:S(2)}, u32[]{:S(2)}) collective-permute-start(f32[64]{0:T(128)S(1)} %bitcast_add_fusion.1), channel_id=1, source_target_pairs={{0,3},{1,0},{2,1},{3,2},{4,7},{5,4},{6,5},{7,6},{8,11},{9,8},{10,9... | collective-permute-start | bytes 776 | tf_op jit(solution)/shard_map/ppermute | solution.py:185
  134.5 10.4 %collective-permute-start.21 = (bf16[2,32,1024]{2,1,0:T(8,128)(2,1)S(1)}, bf16[2,32,1024]{2,1,0:T(8,128)(2,1)S(1)}, u32[]{:S(2)}, u32[]{:S(2)}) collective-permute-start(bf16[2,32,1024]{2,1,0:T(8,128)(2,1)S(1)} %get-tuple-element.52), channel_id=1, source_target_pairs={{0,1},{1,2},{2,3},{3,0},{4,5},{5,6},{6,7},{7,4},{8,9},{9,10},{10,1... | collective-permute-start | bytes 393224 | tf_op jit(solution)/shard_map/ppermute | solution.py:185
  134.5 11.9 %collective-permute-start.22 = (bf16[2,32,1024]{2,1,0:T(8,128)(2,1)S(1)}, bf16[2,32,1024]{2,1,0:T(8,128)(2,1)S(1)}, u32[]{:S(2)}, u32[]{:S(2)}) collective-permute-start(bf16[2,32,1024]{2,1,0:T(8,128)(2,1)S(1)} %get-tuple-element.51), channel_id=1, source_target_pairs={{0,2},{1,3},{2,0},{3,1},{4,6},{5,7},{6,4},{7,5},{8,10},{9,11},{10,... | collective-permute-start | bytes 393224 | tf_op jit(solution)/shard_map/ppermute | solution.py:185
  136.9 9.6 %collective-permute-start.23 = (bf16[2,32,1024]{2,1,0:T(8,128)(2,1)S(1)}, bf16[2,32,1024]{2,1,0:T(8,128)(2,1)S(1)}, u32[]{:S(2)}, u32[]{:S(2)}) collective-permute-start(bf16[2,32,1024]{2,1,0:T(8,128)(2,1)S(1)} %get-tuple-element.50), channel_id=1, source_target_pairs={{0,3},{1,0},{2,1},{3,2},{4,7},{5,4},{6,5},{7,6},{8,11},{9,8},{10,9... | collective-permute-start | bytes 393224 | tf_op jit(solution)/shard_map/ppermute | solution.py:185
  139.3 0.8 copy-start.6
  145.0 1.5 copy-start.10
  146.4 0.6 copy-start.11
  146.4 0.7 copy-start.12

commit v15 on v9

--- a/solution.py
+++ b/solution.py
@@ -296,6 +296,7 @@
     sums = [
         lax.dynamic_index_in_dim(part_out, (j + shift) % hids, 1, False) for shift in range(hids)
     ]
+    cut = sums
     sums = [along_hid(p, shift) if shift else p for shift, p in enumerate(sums)]
     grad_out = head_gradient(place, sums, halves)
 
@@ -306,6 +307,7 @@
     share = share.reshape(groups, steps, depth // seqs, units).astype(F32).sum(0)
     grad_in = share.transpose(0, 2, 1)
 
+    d_ratio_part = after(d_ratio_part, *cut)
     d_ratio = d_ratio_part[0]
     for m in relations:
         d_ratio += flip_seq(d_ratio_part[m], m)

time: 150 us -> 153 us (1.020)
  waiting for transfers between devices: 55.1 us -> 67.3 us
  starting transfers between devices: 45.3 us -> 35.3 us
    ppermute x15, waiting for transfers between devices: 42.6 us -> 53.2 us  [along_hid(): lax.ppermute(values, 'hid', [(a, (a + shift) % hids) for a in range(hids)])]
    ppermute x15, starting transfers between devices: 27.2 us -> 18.8 us  [along_hid(): lax.ppermute(values, 'hid', [(a, (a + shift) % hids) for a in range(hids)])]
    ppermute x4, starting transfers between devices: 4.35 us -> 2.78 us  [turn_hid(): lax.ppermute(values, 'hid', [(a, a - a % halves + (a % halves + shift) %...]
    ppermute x4, waiting for transfers between devices: 11.7 us -> 13.2 us  [turn_hid(): lax.ppermute(values, 'hid', [(a, a - a % halves + (a % halves + shift) %...]
  transfers between devices with their start and end apart: 27 -> 27, of which waited for: 13 -> 11; matrix products, arithmetic and copies ran while one was open for 17% -> 16% of each run, Pallas kernels for 9% -> 8%
where the time goes in v15:
time: 153 us; the launch traced here: 152 us
  waiting for transfers between devices  67.3 us (44%)
  starting transfers between devices  35.3 us (23%)
  local copies, waits for them, and re-layouts  18.7 us (12%)
  Pallas kernels  12.7 us (8%)
  matrix products  8.7 us (6%)
  other arithmetic  8.26 us (5%)
    ppermute x15, waiting for transfers between devices, along_hid(): lax.ppermute(values, 'hid', [(a, (a + shift) % hids) for a in range(hids)])  53.2 us
    ppermute x15, starting transfers between devices, along_hid(): lax.ppermute(values, 'hid', [(a, (a + shift) % hids) for a in range(hids)])  18.8 us
    ppermute x4, waiting for transfers between devices, turn_hid(): lax.ppermute(values, 'hid', [(a, a - a % halves + (a % halves + shift) %...  13.2 us
    pallas_call x3, Pallas kernels, call(): pl.pallas_call(kernel, grid_spec=pltpu.PrefetchScalarGridSpec(num_scalar_...  12.7 us
    dot_general x5, matrix products, matmul(): lax.dot_general(a, b, (contract, ((), ())), preferred_element_type=F32)  8.7 us
    unnamed x44, local copies, waits for them, and re-layouts  6.39 us
    all_to_all x1, starting transfers between devices, shards(): part_out = lax.all_to_all(part_out, 'seq', 0, 0)  4.34 us
    all_to_all x1, starting transfers between devices, shards(): lax.all_to_all(share.reshape(seqs, depth // seqs, units), 'seq', 0, 0)  3.89 us
  transfers between devices with their start and end apart: 27, of which 11 were waited for; matrix products, arithmetic and copies ran while one was open for 16% of the time, Pallas kernels for 8%

profile of v15, /device:TPU:0, one launch (start us, length us, event | category | flops | bytes accessed | tf_op | source)
XLA Modules:
  0.0 152.0 jit_solution(15759884686858448496)
XLA Ops:
  1.2 1.2 multiply_reduce_fusion
  2.5 1.1 reshape.241
  4.4 4.7 %collective-permute-start.3 = (bf16[72,1024]{1,0:T(8,128)(2,1)S(1)}, bf16[72,1024]{1,0:T(8,128)(2,1)S(1)}, u32[]{:S(2)}, u32[]{:S(2)}) collective-permute-start(bf16[72,1024]{1,0:T(8,128)(2,1)S(1)} %get-tuple-element.59), channel_id=1, source_target_pairs={{0,3},{1,0},{2,1},{3,2},{4,7},{5,4},{6,5},{7,6},{8,11},{9,8},{10,9... | collective-permute-start | bytes 442376 | tf_op jit(solution)/shard_map/ppermute | solution.py:185
  9.1 1.0 collective-permute-start.2
  10.2 3.0 %fusion = f32[2,4,64,1024]{3,2,1,0:T(8,128)S(1)} fusion(bf16[2,4,64,1024]{3,2,1,0:T(8,128)(2,1)S(1)} %bitcast.123, bf16[2,1024,1024]{2,1,0:T(8,128)(2,1)} %refs_2_.1, s32[]{:T(128)S(6)} %select_n.139), kind=kOutput, calls=%fused_computation.2 | convolution fusion | flops 1073741824 | bytes 5242884 | tf_op jit(solution)/shard_map/dot_general | solution.py:17
  13.2 1.3 copy-done.4
  14.5 0.8 dynamic-slice_convert_fusion
  15.3 6.9 %collective-permute-done.2 = bf16[72,1024]{1,0:T(8,128)(2,1)S(1)} collective-permute-done((bf16[72,1024]{1,0:T(8,128)(2,1)S(1)}, bf16[72,1024]{1,0:T(8,128)(2,1)S(1)}, u32[]{:S(2)}, u32[]{:S(2)}) %collective-permute-start.2) | collective-permute-done | bytes 147488 | tf_op jit(solution)/shard_map/ppermute | solution.py:185
  22.5 1.6 %broadcast_in_dim.45 = bf16[4,2,128,1024]{3,2,1,0:T(8,128)(2,1)} broadcast(bf16[2,128,1024]{2,1,0:T(8,128)(2,1)S(1)} %bitcast.116), dimensions={1,2,3} | broadcast | bytes 2621440 | tf_op jit(solution)/shard_map/broadcast_in_dim | solution.py:244
  24.1 3.9 %all-to-all-start = ((bf16[8,128,1024]{2,1,0:T(8,128)(2,1)}), bf16[8,128,1024]{2,1,0:T(8,128)(2,1)S(1)}, u32[]{:S(2)}, u32[]{:S(2)}) async-start(bf16[8,128,1024]{2,1,0:T(8,128)(2,1)} %bitcast.112), calls=%async_computation | async-start | bytes 4194304 | tf_op jit(solution)/shard_map/all_to_all | solution.py:246
  28.7 1.1 constant_dynamic-slice_fusion.6
  29.8 3.8 %collective-permute-start.7 = (bf16[128,1024]{1,0:T(8,128)(2,1)S(1)}, bf16[128,1024]{1,0:T(8,128)(2,1)}, u32[]{:S(2)}, u32[]{:S(2)}) collective-permute-start(bf16[128,1024]{1,0:T(8,128)(2,1)S(1)} %bitcast.126), channel_id=1, source_target_pairs={{0,3},{1,0},{2,1},{3,2},{4,7},{5,4},{6,5},{7,6},{8,11},{9,8},{10,9... | collective-permute-start | bytes 786440 | tf_op jit(solution)/shard_map/ppermute | solution.py:185
  33.7 3.8 %gather_fusion = bf16[128,1024]{1,0:T(8,128)(2,1)S(1)} fusion(bf16[2048,1024]{1,0:T(8,128)(2,1)} %bitcast.122, s32[1024]{0:T(1024)S(1)} %pad_clamp_fusion), kind=kCustom, calls=%fused_computation | custom fusion | bytes 524800 | tf_op jit(solution)/shard_map/jit(_take)/gather | solution.py:240
  37.7 3.4 %collective-permute-done.5 = bf16[128,1024]{1,0:T(8,128)(2,1)} collective-permute-done((bf16[128,1024]{1,0:T(8,128)(2,1)}, bf16[128,1024]{1,0:T(8,128)(2,1)}, u32[]{:S(2)}, u32[]{:S(2)}) %collective-permute-start.5) | collective-permute-done | bytes 262176 | tf_op jit(solution)/shard_map/ppermute | solution.py:185
  41.1 3.2 %collective-permute-done.7 = bf16[128,1024]{1,0:T(8,128)(2,1)} collective-permute-done((bf16[128,1024]{1,0:T(8,128)(2,1)S(1)}, bf16[128,1024]{1,0:T(8,128)(2,1)}, u32[]{:S(2)}, u32[]{:S(2)}) %collective-permute-start.7) | collective-permute-done | bytes 262176 | tf_op jit(solution)/shard_map/ppermute | solution.py:185
  44.2 12.3 %collective-permute-done.6 = bf16[128,1024]{1,0:T(8,128)(2,1)} collective-permute-done((bf16[128,1024]{1,0:T(8,128)(2,1)S(1)}, bf16[128,1024]{1,0:T(8,128)(2,1)}, u32[]{:S(2)}, u32[]{:S(2)}) %collective-permute-start.6) | collective-permute-done | bytes 262176 | tf_op jit(solution)/shard_map/ppermute | solution.py:185
  56.5 1.4 multiply_reduce_fusion.4
  58.3 2.0 %collective-permute-start.11 = (s32[2,128]{1,0:T(2,128)S(1)}, s32[2,128]{1,0:T(2,128)S(1)}, u32[]{:S(2)}, u32[]{:S(2)}) collective-permute-start(s32[2,128]{1,0:T(2,128)S(1)} %pad_add_fusion), channel_id=1, source_target_pairs={{0,1},{1,0},{2,3},{3,2},{4,5},{5,4},{6,7},{7,6},{8,9},{9,8},{10,11... | collective-permute-start | bytes 3080 | tf_op jit(solution)/shard_map/ppermute | solution.py:188
  60.3 5.9 %collective-permute-done.11 = s32[2,128]{1,0:T(2,128)S(1)} collective-permute-done((s32[2,128]{1,0:T(2,128)S(1)}, s32[2,128]{1,0:T(2,128)S(1)}, u32[]{:S(2)}, u32[]{:S(2)}) %collective-permute-start.11) | collective-permute-done | bytes 1056 | tf_op jit(solution)/shard_map/ppermute | solution.py:188
  66.3 0.8 fusion.36
  67.8 3.3 %collective-permute-done.10 = f32[2,2,128]{2,1,0:T(2,128)S(1)} collective-permute-done((f32[2,2,128]{2,1,0:T(2,128)S(1)}, f32[2,2,128]{2,1,0:T(2,128)S(1)}, u32[]{:S(2)}, u32[]{:S(2)}) %collective-permute-start.10) | collective-permute-done | bytes 2080 | tf_op jit(solution)/shard_map/ppermute | solution.py:188
  71.5 0.8 convolution_convert_fusion.1
  72.7 2.1 %convolution_convert_fusion = bf16[1024,1024]{1,0:T(8,128)(2,1)} fusion(bf16[256,1024]{1,0:T(8,128)(2,1)S(1)} %multiply_convert_fusion, bf16[128,1024]{1,0:T(8,128)(2,1)S(1)} %copy-done.8, bf16[128,1024]{1,0:T(8,128)(2,1)S(1)} %copy-done.3), kind=kOutput, calls=%fused_computation.5 | convolution fusion | flops 538968064 | bytes 3145728 | tf_op jit(solution)/shard_map/dot_general | solution.py:17
  74.8 4.1 %collective-permute-done.12 = bf16[128,1024]{1,0:T(8,128)(2,1)} collective-permute-done((bf16[128,1024]{1,0:T(8,128)(2,1)S(1)}, bf16[128,1024]{1,0:T(8,128)(2,1)}, u32[]{:S(2)}, u32[]{:S(2)}) %collective-permute-start.12) | collective-permute-done | bytes 262176 | tf_op jit(solution)/shard_map/ppermute | solution.py:188
  78.9 4.3 %all-to-all-start.1 = ((bf16[8,128,1024]{2,1,0:T(8,128)(2,1)}), bf16[8,128,1024]{2,1,0:T(8,128)(2,1)}, u32[]{:S(2)}, u32[]{:S(2)}) async-start(bf16[8,128,1024]{2,1,0:T(8,128)(2,1)} %bitcast.114), calls=%async_computation.1 | async-start | bytes 4194304 | tf_op jit(solution)/shard_map/all_to_all | solution.py:293
  83.3 2.0 %multiply_reduce_fusion.2 = (f32[128]{0:T(128)S(1)}, f32[128]{0:T(128)S(1)}, f32[128]{0:T(128)S(1)}, f32[128,1024]{1,0:T(8,128)S(1)}) fusion(f32[128,1024]{1,0:T(8,128)S(1)} %get-tuple-element.48, bf16[128,1024]{1,0:T(8,128)(2,1)} %collective-permute-done.12, f32[1024]{0:T(1024)S(1)} %bitcast.128, bf16[128,1024]{1,0:T(8,128)(2,1)S(1)} %gather_fusion, ...), kind=kOutput, calls=%fused_computation.16 | convolution fusion | flops 270270080 | bytes 3938433 | tf_op jit(solution)/shard_map/dot_general | solution.py:17
  85.3 1.2 subtract_convert_fusion.refs_0_
  87.0 1.3 collective-permute-start.14
  88.6 0.7 pad_add_fusion.2.place_ref
  89.3 0.9 copy.39.refs_6_
  90.2 5.0 %collective-permute-done.15.refs_3_ = bf16[128,1024]{1,0:T(8,128)(2,1)S(1)} collective-permute-done((bf16[128,1024]{1,0:T(8,128)(2,1)S(1)}, bf16[128,1024]{1,0:T(8,128)(2,1)S(1)}, u32[]{:S(2)}, u32[]{:S(2)}) %collective-permute-start.15) | collective-permute-done | bytes 262176 | tf_op jit(solution)/shard_map/ppermute | solution.py:185
  95.1 16.6 %collective-permute-done.14.refs_2_ = bf16[128,1024]{1,0:T(8,128)(2,1)S(1)} collective-permute-done((bf16[128,1024]{1,0:T(8,128)(2,1)S(1)}, bf16[128,1024]{1,0:T(8,128)(2,1)S(1)}, u32[]{:S(2)}, u32[]{:S(2)}) %collective-permute-start.14) | collective-permute-done | bytes 262176 | tf_op jit(solution)/shard_map/ppermute | solution.py:185
  111.7 0.7 copy-done.15
  112.4 0.7 copy-done.16
  113.1 5.1 %shard_map.85 = (bf16[1024,1024]{1,0:T(8,128)(2,1)}, bf16[256,1024]{1,0:T(8,128)(2,1)}, bf16[256,1024]{1,0:T(8,128)(2,1)}) custom-call(s32[2]{0:T(128)} %pad_add_fusion.2.place_ref, bf16[128,1024]{1,0:T(8,128)(2,1)} %copy-done.9, bf16[128,1024]{1,0:T(8,128)(2,1)} %copy-done.16, bf16[128,1024]{1,0:T(8,128)(2,1)} %copy-done.15, bf16[128,1024]{1,0:T(8,128)(2,1)} %copy-done.14, ...), custom_call_target="tpu_custom_call" | custom-call | flops 1073741824 | bytes 2099200 | tf_op jit(solution)/shard_map/pallas_call | solution.py:33
  118.2 3.9 %all-to-all-start.2 = ((bf16[8,128,1024]{2,1,0:T(8,128)(2,1)}), bf16[8,128,1024]{2,1,0:T(8,128)(2,1)S(1)}, u32[]{:S(2)}, u32[]{:S(2)}) async-start(bf16[8,128,1024]{2,1,0:T(8,128)(2,1)} %bitcast.117), calls=%async_computation.2 | async-start | bytes 4194304 | tf_op jit(solution)/shard_map/all_to_all | solution.py:306
  122.4 2.0 %reduce_sum.107 = bf16[2,4,32,1024]{3,2,1,0:T(8,128)(2,1)S(1)} reduce(bf16[4,2,4,32,1024]{4,3,2,1,0:T(8,128)(2,1)} %bitcast.44, bf16[]{:T(256)} %constant.168.clone.1), dimensions={0}, to_apply=%region_9.10 | reduce | flops 786432 | bytes 2621442 | tf_op jit(solution)/shard_map/reduce_sum | solution.py:294
  124.5 0.7 dynamic-slice_bitcast_fusion
  125.7 0.8 collective-permute-done.17
  126.5 3.8 %collective-permute-start.23 = (bf16[2,32,1024]{2,1,0:T(8,128)(2,1)S(1)}, bf16[2,32,1024]{2,1,0:T(8,128)(2,1)S(1)}, u32[]{:S(2)}, u32[]{:S(2)}) collective-permute-start(bf16[2,32,1024]{2,1,0:T(8,128)(2,1)S(1)} %get-tuple-element.52), channel_id=1, source_target_pairs={{0,3},{1,0},{2,1},{3,2},{4,7},{5,4},{6,5},{7,6},{8,11},{9,8},{10,9... | collective-permute-start | bytes 393224 | tf_op jit(solution)/shard_map/ppermute | solution.py:185
  130.3 2.9 %collective-permute-start.19 = (f32[64]{0:T(128)S(1)}, f32[64]{0:T(128)S(1)}, u32[]{:S(2)}, u32[]{:S(2)}) collective-permute-start(f32[64]{0:T(128)S(1)} %bitcast_add_fusion.1), channel_id=1, source_target_pairs={{0,2},{1,3},{2,0},{3,1},{4,6},{5,7},{6,4},{7,5},{8,10},{9,11},{10,... | collective-permute-start | bytes 776 | tf_op jit(solution)/shard_map/ppermute | solution.py:185
  133.3 5.9 %collective-permute-done.19 = f32[64]{0:T(128)S(1)} collective-permute-done((f32[64]{0:T(128)S(1)}, f32[64]{0:T(128)S(1)}, u32[]{:S(2)}, u32[]{:S(2)}) %collective-permute-start.19) | collective-permute-done | bytes 288 | tf_op jit(solution)/shard_map/ppermute | solution.py:185
  139.7 0.9 copy.40.refs_4_
  140.6 0.8 copy-done.6
  141.4 4.9 %shard_map.86 = bf16[256,1024]{1,0:T(8,128)(2,1)} custom-call(s32[2]{0:T(128)} %pad_add_fusion.2.place_ref, bf16[256,1024]{1,0:T(8,128)(2,1)} %get-tuple-element.25.refs_0_, bf16[256,1024]{1,0:T(8,128)(2,1)} %copy-done.6, bf16[2,1024,1024]{2,1,0:T(8,128)(2,1)} %refs_2_.1, bf16[256,1024]{1,0:T(8,128)(2,1)} %refs_3_.1, f32[2,256,1]{2,1,0:T(8,128)} %copy.40.refs_4_), custom_call_target="tpu_custom_call" | custom-call | flops 1073741824 | bytes 5769216 | tf_op jit(solution)/shard_map/pallas_call | solution.py:33
  147.0 0.7 copy-done.12
  147.6 2.7 %shard_map.87 = f32[32,2,2048]{2,1,0:T(2,128)} custom-call(s32[2]{0:T(128)} %pad_add_fusion.2.place_ref, bf16[2,32,1024]{2,1,0:T(8,128)(2,1)} %get-tuple-element.55.refs_0_, bf16[2,32,1024]{2,1,0:T(8,128)(2,1)} %copy-done.12, bf16[2,32,1024]{2,1,0:T(8,128)(2,1)} %copy-done.11, bf16[2,32,1024]{2,1,0:T(8,128)(2,1)} %copy-done.10), custom_call_target="tpu_custom_call" | custom-call | flops 262144 | bytes 524288 | tf_op jit(solution)/shard_map/pallas_call | solution.py:33
  150.7 1.3 copy.41
  (124 shorter events, 7.8 us)
Async XLA Ops:
  0.6 9.5 %copy-start = (f32[2,1024]{1,0:T(2,128)S(1)}, f32[2,1024]{1,0:T(2,128)}, u32[]{:S(2)}) copy-start(f32[2,1024]{1,0:T(2,128)} %param.9) | copy-start | bytes 24580
  0.6 9.5 %copy-start.1 = (bf16[256,1024]{1,0:T(8,128)(2,1)S(1)}, bf16[256,1024]{1,0:T(8,128)(2,1)}, u32[]{:S(2)}) copy-start(bf16[256,1024]{1,0:T(8,128)(2,1)} %refs_3_.1) | copy-start | bytes 1572868
  0.7 9.5 %collective-permute-start.1 = (bf16[256,1024]{1,0:T(8,128)(2,1)}, bf16[256,1024]{1,0:T(8,128)(2,1)S(1)}, u32[]{:S(2)}, u32[]{:S(2)}) collective-permute-start(bf16[256,1024]{1,0:T(8,128)(2,1)} %refs_3_.1), channel_id=1, source_target_pairs={{0,4},{4,0},{8,12},{12,8},{16,20},{20,16},{24,28},{28,24},{1,5},{5... | collective-permute-start | bytes 1572872 | tf_op jit(solution)/shard_map/ppermute | solution.py:195
  4.4 11.0 %collective-permute-start.3 = (bf16[72,1024]{1,0:T(8,128)(2,1)S(1)}, bf16[72,1024]{1,0:T(8,128)(2,1)S(1)}, u32[]{:S(2)}, u32[]{:S(2)}) collective-permute-start(bf16[72,1024]{1,0:T(8,128)(2,1)S(1)} %get-tuple-element.59), channel_id=1, source_target_pairs={{0,3},{1,0},{2,1},{3,2},{4,7},{5,4},{6,5},{7,6},{8,11},{9,8},{10,9... | collective-permute-start | bytes 442376 | tf_op jit(solution)/shard_map/ppermute | solution.py:185
  9.1 13.1 %collective-permute-start = (bf16[72,1024]{1,0:T(8,128)(2,1)S(1)}, bf16[72,1024]{1,0:T(8,128)(2,1)S(1)}, u32[]{:S(2)}, u32[]{:S(2)}) collective-permute-start(bf16[72,1024]{1,0:T(8,128)(2,1)S(1)} %get-tuple-element.59), channel_id=1, source_target_pairs={{0,1},{1,2},{2,3},{3,0},{4,5},{5,6},{6,7},{7,4},{8,9},{9,10},{10,1... | collective-permute-start | bytes 442376 | tf_op jit(solution)/shard_map/ppermute | solution.py:185
  9.1 13.1 %collective-permute-start.2 = (bf16[72,1024]{1,0:T(8,128)(2,1)S(1)}, bf16[72,1024]{1,0:T(8,128)(2,1)S(1)}, u32[]{:S(2)}, u32[]{:S(2)}) collective-permute-start(bf16[72,1024]{1,0:T(8,128)(2,1)S(1)} %get-tuple-element.58), channel_id=1, source_target_pairs={{0,2},{1,3},{2,0},{3,1},{4,6},{5,7},{6,4},{7,5},{8,10},{9,11},{10,... | collective-permute-start | bytes 442376 | tf_op jit(solution)/shard_map/ppermute | solution.py:185
  10.1 3.1 %copy-start.5 = (bf16[256,1024]{1,0:T(8,128)(2,1)}, bf16[256,1024]{1,0:T(8,128)(2,1)S(1)}, u32[]{:S(2)}) copy-start(bf16[256,1024]{1,0:T(8,128)(2,1)S(1)} %collective-permute-done.1.refs_5_) | copy-start | bytes 1572868
  13.2 1.3 copy-start.4
  24.1 4.5 %copy-start.13 = (s32[2,64]{1,0:T(2,128)S(1)}, s32[2,64]{1,0:T(2,128)}, u32[]{:S(2)}) copy-start(s32[2,64]{1,0:T(2,128)} %param.11) | copy-start | bytes 1540
  24.1 42.1 %all-to-all-start = ((bf16[8,128,1024]{2,1,0:T(8,128)(2,1)}), bf16[8,128,1024]{2,1,0:T(8,128)(2,1)S(1)}, u32[]{:S(2)}, u32[]{:S(2)}) async-start(bf16[8,128,1024]{2,1,0:T(8,128)(2,1)} %bitcast.112), calls=%async_computation | async-start | bytes 4194304 | tf_op jit(solution)/shard_map/all_to_all | solution.py:246
  28.1 9.4 %collective-permute-start.4 = (f32[256]{0:T(256)S(1)}, f32[256]{0:T(256)S(1)}, u32[]{:S(2)}, u32[]{:S(2)}) collective-permute-start(f32[256]{0:T(256)S(1)} %slice_reduce_fusion), channel_id=1, source_target_pairs={{0,4},{4,0},{8,12},{12,8},{16,20},{20,16},{24,28},{28,24},{1,5},{5... | collective-permute-start | bytes 3080 | tf_op jit(solution)/shard_map/ppermute | solution.py:195
  28.6 5.0 %collective-permute-start.8 = (s32[2,64]{1,0:T(2,128)S(1)}, s32[2,64]{1,0:T(2,128)S(1)}, u32[]{:S(2)}, u32[]{:S(2)}) collective-permute-start(s32[2,64]{1,0:T(2,128)S(1)} %copy-done.13), channel_id=1, source_target_pairs={{0,4},{4,0},{8,12},{12,8},{16,20},{20,16},{24,28},{28,24},{1,5},{5... | collective-permute-start | bytes 1544 | tf_op jit(solution)/shard_map/ppermute | solution.py:195
  29.7 11.3 %collective-permute-start.5 = (bf16[128,1024]{1,0:T(8,128)(2,1)}, bf16[128,1024]{1,0:T(8,128)(2,1)}, u32[]{:S(2)}, u32[]{:S(2)}) collective-permute-start(bf16[128,1024]{1,0:T(8,128)(2,1)} %bitcast.8), channel_id=1, source_target_pairs={{0,1},{1,2},{2,3},{3,0},{4,5},{5,6},{6,7},{7,4},{8,9},{9,10},{10,1... | collective-permute-start | bytes 786440 | tf_op jit(solution)/shard_map/ppermute | solution.py:185
  29.8 14.4 %collective-permute-start.7 = (bf16[128,1024]{1,0:T(8,128)(2,1)S(1)}, bf16[128,1024]{1,0:T(8,128)(2,1)}, u32[]{:S(2)}, u32[]{:S(2)}) collective-permute-start(bf16[128,1024]{1,0:T(8,128)(2,1)S(1)} %bitcast.126), channel_id=1, source_target_pairs={{0,3},{1,0},{2,1},{3,2},{4,7},{5,4},{6,5},{7,6},{8,11},{9,8},{10,9... | collective-permute-start | bytes 786440 | tf_op jit(solution)/shard_map/ppermute | solution.py:185
  33.6 22.9 %collective-permute-start.6 = (bf16[128,1024]{1,0:T(8,128)(2,1)S(1)}, bf16[128,1024]{1,0:T(8,128)(2,1)}, u32[]{:S(2)}, u32[]{:S(2)}) collective-permute-start(bf16[128,1024]{1,0:T(8,128)(2,1)S(1)} %bitcast.125), channel_id=1, source_target_pairs={{0,2},{1,3},{2,0},{3,1},{4,6},{5,7},{6,4},{7,5},{8,10},{9,11},{10,... | collective-permute-start | bytes 786440 | tf_op jit(solution)/shard_map/ppermute | solution.py:185
  58.2 9.1 %copy-start.2 = (bf16[128,1024]{1,0:T(8,128)(2,1)}, bf16[128,1024]{1,0:T(8,128)(2,1)S(1)}, u32[]{:S(2)}) copy-start(bf16[128,1024]{1,0:T(8,128)(2,1)S(1)} %multiply_convert_fusion.1) | copy-start | bytes 786436
  58.2 8.0 %collective-permute-start.9 = (bf16[128,1024]{1,0:T(8,128)(2,1)S(1)}, bf16[128,1024]{1,0:T(8,128)(2,1)S(1)}, u32[]{:S(2)}, u32[]{:S(2)}) collective-permute-start(bf16[128,1024]{1,0:T(8,128)(2,1)S(1)} %multiply_convert_fusion.1), channel_id=1, source_target_pairs={{0,1},{1,0},{2,3},{3,2},{4,5},{5,4},{6,7},{7,6},{8,9},{9,8},{10,11... | collective-permute-start | bytes 786440 | tf_op jit(solution)/shard_map/ppermute | solution.py:188
  58.3 7.9 %collective-permute-start.11 = (s32[2,128]{1,0:T(2,128)S(1)}, s32[2,128]{1,0:T(2,128)S(1)}, u32[]{:S(2)}, u32[]{:S(2)}) collective-permute-start(s32[2,128]{1,0:T(2,128)S(1)} %pad_add_fusion), channel_id=1, source_target_pairs={{0,1},{1,0},{2,3},{3,2},{4,5},{5,4},{6,7},{7,6},{8,9},{9,8},{10,11... | collective-permute-start | bytes 3080 | tf_op jit(solution)/shard_map/ppermute | solution.py:188
  66.2 1.2 copy-start.7
  67.4 3.7 %collective-permute-start.10 = (f32[2,2,128]{2,1,0:T(2,128)S(1)}, f32[2,2,128]{2,1,0:T(2,128)S(1)}, u32[]{:S(2)}, u32[]{:S(2)}) collective-permute-start(f32[2,2,128]{2,1,0:T(2,128)S(1)} %pad_maximum_fusion.6), channel_id=1, source_target_pairs={{0,1},{1,0},{2,3},{3,2},{4,5},{5,4},{6,7},{7,6},{8,9},{9,8},{10,11... | collective-permute-start | bytes 6152 | tf_op jit(solution)/shard_map/ppermute | solution.py:188
  71.1 1.6 %copy-start.3 = (bf16[128,1024]{1,0:T(8,128)(2,1)S(1)}, bf16[128,1024]{1,0:T(8,128)(2,1)}, u32[]{:S(2)}) copy-start(bf16[128,1024]{1,0:T(8,128)(2,1)} %copy-done.2) | copy-start | bytes 786436
  71.1 1.6 %copy-start.8 = (bf16[128,1024]{1,0:T(8,128)(2,1)S(1)}, bf16[128,1024]{1,0:T(8,128)(2,1)}, u32[]{:S(2)}) copy-start(bf16[128,1024]{1,0:T(8,128)(2,1)} %copy-done.7) | copy-start | bytes 786436
  72.3 6.5 %collective-permute-start.12 = (bf16[128,1024]{1,0:T(8,128)(2,1)S(1)}, bf16[128,1024]{1,0:T(8,128)(2,1)}, u32[]{:S(2)}, u32[]{:S(2)}) collective-permute-start(bf16[128,1024]{1,0:T(8,128)(2,1)S(1)} %convolution_convert_fusion.1), channel_id=1, source_target_pairs={{0,1},{1,0},{2,3},{3,2},{4,5},{5,4},{6,7},{7,6},{8,9},{9,8},{10,11... | collective-permute-start | bytes 786440 | tf_op jit(solution)/shard_map/ppermute | solution.py:188
  78.9 39.3 %all-to-all-start.1 = ((bf16[8,128,1024]{2,1,0:T(8,128)(2,1)}), bf16[8,128,1024]{2,1,0:T(8,128)(2,1)}, u32[]{:S(2)}, u32[]{:S(2)}) async-start(bf16[8,128,1024]{2,1,0:T(8,128)(2,1)} %bitcast.114), calls=%async_computation.1 | async-start | bytes 4194304 | tf_op jit(solution)/shard_map/all_to_all | solution.py:293
  86.5 25.2 %copy-start.9 = (bf16[128,1024]{1,0:T(8,128)(2,1)}, bf16[128,1024]{1,0:T(8,128)(2,1)S(1)}, u32[]{:S(2)}) copy-start(bf16[128,1024]{1,0:T(8,128)(2,1)S(1)} %subtract_convert_fusion.refs_0_) | copy-start | bytes 786436
  86.5 8.6 %collective-permute-start.15 = (bf16[128,1024]{1,0:T(8,128)(2,1)S(1)}, bf16[128,1024]{1,0:T(8,128)(2,1)S(1)}, u32[]{:S(2)}, u32[]{:S(2)}) collective-permute-start(bf16[128,1024]{1,0:T(8,128)(2,1)S(1)} %subtract_convert_fusion.refs_0_), channel_id=1, source_target_pairs={{0,3},{1,0},{2,1},{3,2},{4,7},{5,4},{6,5},{7,6},{8,11},{9,8},{10,9... | collective-permute-start | bytes 786440 | tf_op jit(solution)/shard_map/ppermute | solution.py:185
  87.0 24.7 %collective-permute-start.14 = (bf16[128,1024]{1,0:T(8,128)(2,1)S(1)}, bf16[128,1024]{1,0:T(8,128)(2,1)S(1)}, u32[]{:S(2)}, u32[]{:S(2)}) collective-permute-start(bf16[128,1024]{1,0:T(8,128)(2,1)S(1)} %subtract_convert_fusion.refs_0_), channel_id=1, source_target_pairs={{0,2},{1,3},{2,0},{3,1},{4,6},{5,7},{6,4},{7,5},{8,10},{9,11},{10,... | collective-permute-start | bytes 786440 | tf_op jit(solution)/shard_map/ppermute | solution.py:185
  88.3 23.4 %collective-permute-start.13 = (bf16[128,1024]{1,0:T(8,128)(2,1)S(1)}, bf16[128,1024]{1,0:T(8,128)(2,1)S(1)}, u32[]{:S(2)}, u32[]{:S(2)}) collective-permute-start(bf16[128,1024]{1,0:T(8,128)(2,1)S(1)} %subtract_convert_fusion.refs_0_), channel_id=1, source_target_pairs={{0,1},{1,2},{2,3},{3,0},{4,5},{5,6},{6,7},{7,4},{8,9},{9,10},{10,1... | collective-permute-start | bytes 786440 | tf_op jit(solution)/shard_map/ppermute | solution.py:185
  95.1 16.6 %copy-start.14 = (bf16[128,1024]{1,0:T(8,128)(2,1)}, bf16[128,1024]{1,0:T(8,128)(2,1)S(1)}, u32[]{:S(2)}) copy-start(bf16[128,1024]{1,0:T(8,128)(2,1)S(1)} %collective-permute-done.15.refs_3_) | copy-start | bytes 786436
  111.7 0.7 copy-start.15
  112.4 0.7 copy-start.16
  118.2 32.1 %all-to-all-start.2 = ((bf16[8,128,1024]{2,1,0:T(8,128)(2,1)}), bf16[8,128,1024]{2,1,0:T(8,128)(2,1)S(1)}, u32[]{:S(2)}, u32[]{:S(2)}) async-start(bf16[8,128,1024]{2,1,0:T(8,128)(2,1)} %bitcast.117), calls=%async_computation.2 | async-start | bytes 4194304 | tf_op jit(solution)/shard_map/all_to_all | solution.py:306
  125.2 1.3 collective-permute-start.17
  125.7 14.9 %collective-permute-start.16 = (bf16[256,1024]{1,0:T(8,128)(2,1)}, bf16[256,1024]{1,0:T(8,128)(2,1)S(1)}, u32[]{:S(2)}, u32[]{:S(2)}) collective-permute-start(bf16[256,1024]{1,0:T(8,128)(2,1)} %get-tuple-element.26), channel_id=1, source_target_pairs={{0,4},{4,0},{8,12},{12,8},{16,20},{20,16},{24,28},{28,24},{1,5},{5... | collective-permute-start | bytes 1572872 | tf_op jit(solution)/shard_map/ppermute | solution.py:195
  126.5 6.8 %collective-permute-start.18 = (f32[64]{0:T(128)S(1)}, f32[64]{0:T(128)S(1)}, u32[]{:S(2)}, u32[]{:S(2)}) collective-permute-start(f32[64]{0:T(128)S(1)} %bitcast_add_fusion.1), channel_id=1, source_target_pairs={{0,1},{1,2},{2,3},{3,0},{4,5},{5,6},{6,7},{7,4},{8,9},{9,10},{10,1... | collective-permute-start | bytes 776 | tf_op jit(solution)/shard_map/ppermute | solution.py:185
  126.5 19.8 %collective-permute-start.23 = (bf16[2,32,1024]{2,1,0:T(8,128)(2,1)S(1)}, bf16[2,32,1024]{2,1,0:T(8,128)(2,1)S(1)}, u32[]{:S(2)}, u32[]{:S(2)}) collective-permute-start(bf16[2,32,1024]{2,1,0:T(8,128)(2,1)S(1)} %get-tuple-element.52), channel_id=1, source_target_pairs={{0,3},{1,0},{2,1},{3,2},{4,7},{5,4},{6,5},{7,6},{8,11},{9,8},{10,9... | collective-permute-start | bytes 393224 | tf_op jit(solution)/shard_map/ppermute | solution.py:185
  130.3 16.0 %collective-permute-start.22 = (bf16[2,32,1024]{2,1,0:T(8,128)(2,1)S(1)}, bf16[2,32,1024]{2,1,0:T(8,128)(2,1)S(1)}, u32[]{:S(2)}, u32[]{:S(2)}) collective-permute-start(bf16[2,32,1024]{2,1,0:T(8,128)(2,1)S(1)} %get-tuple-element.53), channel_id=1, source_target_pairs={{0,2},{1,3},{2,0},{3,1},{4,6},{5,7},{6,4},{7,5},{8,10},{9,11},{10,... | collective-permute-start | bytes 393224 | tf_op jit(solution)/shard_map/ppermute | solution.py:185
  130.3 8.8 %collective-permute-start.19 = (f32[64]{0:T(128)S(1)}, f32[64]{0:T(128)S(1)}, u32[]{:S(2)}, u32[]{:S(2)}) collective-permute-start(f32[64]{0:T(128)S(1)} %bitcast_add_fusion.1), channel_id=1, source_target_pairs={{0,2},{1,3},{2,0},{3,1},{4,6},{5,7},{6,4},{7,5},{8,10},{9,11},{10,... | collective-permute-start | bytes 776 | tf_op jit(solution)/shard_map/ppermute | solution.py:185
  133.3 6.3 %collective-permute-start.20 = (f32[64]{0:T(128)S(1)}, f32[64]{0:T(128)S(1)}, u32[]{:S(2)}, u32[]{:S(2)}) collective-permute-start(f32[64]{0:T(128)S(1)} %bitcast_add_fusion.1), channel_id=1, source_target_pairs={{0,3},{1,0},{2,1},{3,2},{4,7},{5,4},{6,5},{7,6},{8,11},{9,8},{10,9... | collective-permute-start | bytes 776 | tf_op jit(solution)/shard_map/ppermute | solution.py:185
  139.2 7.1 %collective-permute-start.21 = (bf16[2,32,1024]{2,1,0:T(8,128)(2,1)S(1)}, bf16[2,32,1024]{2,1,0:T(8,128)(2,1)S(1)}, u32[]{:S(2)}, u32[]{:S(2)}) collective-permute-start(bf16[2,32,1024]{2,1,0:T(8,128)(2,1)S(1)} %get-tuple-element.54), channel_id=1, source_target_pairs={{0,1},{1,2},{2,3},{3,0},{4,5},{5,6},{6,7},{7,4},{8,9},{9,10},{10,1... | collective-permute-start | bytes 393224 | tf_op jit(solution)/shard_map/ppermute | solution.py:185
  140.6 0.8 copy-start.6
  146.3 0.6 copy-start.10
  146.3 0.7 copy-start.11
  147.0 0.7 copy-start.12

commit v16 on v11

--- a/solution.py
+++ b/solution.py
@@ -310,7 +310,7 @@
         d_rows = lax.dynamic_update_index_in_dim(
             d_rows, along_hid(d_ratio, shift), (j - shift) % hids, 0
         )
-    share, mine, *others = input_gradient(after(place, d_rows), pieces, group, ratio_rows, seqs)
+    share, mine, *others = input_gradient(after(place, d_ratio), pieces, group, ratio_rows, seqs)
     share = lax.all_to_all(share.reshape(seqs, depth // seqs, units), "seq", 0, 0)
     share = share.reshape(groups, steps, depth // seqs, units).astype(F32).sum(0)
     grad_in = share.transpose(0, 2, 1)

time: 150 us -> 146 us (0.973)
  waiting for transfers between devices: 58.7 us -> 51.6 us
  starting transfers between devices: 40.4 us -> 44 us
    all_to_all x1, waiting for transfers between devices: 6.53 us -> 0.01 us  [shards(): lax.all_to_all(share.reshape(seqs, depth // seqs, units), 'seq', 0, 0)]
    ppermute x15, starting transfers between devices: 21.9 us -> 26 us  [along_hid(): lax.ppermute(values, 'hid', [(a, (a + shift) % hids) for a in range(hids)])]
  transfers between devices with their start and end apart: 27 -> 27, of which waited for: 9 -> 12; matrix products, arithmetic and copies ran while one was open for 17% -> 17% of each run, Pallas kernels for 9% -> 9%
where the time goes in v16:
time: 146 us; the launch traced here: 145 us
  waiting for transfers between devices  51.6 us (35%)
  starting transfers between devices  44 us (30%)
  local copies, waits for them, and re-layouts  18 us (12%)
  Pallas kernels  12.7 us (9%)
  matrix products  9.41 us (6%)
  other arithmetic  8.26 us (6%)
    ppermute x15, waiting for transfers between devices, along_hid(): lax.ppermute(values, 'hid', [(a, (a + shift) % hids) for a in range(hids)])  42.9 us
    ppermute x15, starting transfers between devices, along_hid(): lax.ppermute(values, 'hid', [(a, (a + shift) % hids) for a in range(hids)])  26 us
    pallas_call x3, Pallas kernels, call(): pl.pallas_call(kernel, grid_spec=pltpu.PrefetchScalarGridSpec(num_scalar_...  12.7 us
    dot_general x5, matrix products, matmul(): lax.dot_general(a, b, (contract, ((), ())), preferred_element_type=F32)  9.41 us
    ppermute x4, waiting for transfers between devices, turn_hid(): lax.ppermute(values, 'hid', [(a, a - a % halves + (a % halves + shift) %...  8.42 us
    unnamed x44, local copies, waits for them, and re-layouts  5.74 us
    all_to_all x1, starting transfers between devices, shards(): part_out = lax.all_to_all(part_out, 'seq', 0, 0)  4.34 us
    ppermute x4, starting transfers between devices, turn_hid(): lax.ppermute(values, 'hid', [(a, a - a % halves + (a % halves + shift) %...  4.29 us
  transfers between devices with their start and end apart: 27, of which 12 were waited for; matrix products, arithmetic and copies ran while one was open for 17% of the time, Pallas kernels for 9%

profile of v16, /device:TPU:0, one launch (start us, length us, event | category | flops | bytes accessed | tf_op | source)
XLA Modules:
  0.0 145.1 jit_solution(5984636069163304222)
XLA Ops:
  1.2 1.2 multiply_reduce_fusion
  2.5 1.1 reshape.241
  4.4 4.7 %collective-permute-start.3 = (bf16[72,1024]{1,0:T(8,128)(2,1)S(1)}, bf16[72,1024]{1,0:T(8,128)(2,1)S(1)}, u32[]{:S(2)}, u32[]{:S(2)}) collective-permute-start(bf16[72,1024]{1,0:T(8,128)(2,1)S(1)} %get-tuple-element.59), channel_id=1, source_target_pairs={{0,3},{1,0},{2,1},{3,2},{4,7},{5,4},{6,5},{7,6},{8,11},{9,8},{10,9... | collective-permute-start | bytes 442376 | tf_op jit(solution)/shard_map/ppermute | solution.py:185
  9.1 1.0 collective-permute-start.2
  10.2 3.0 %fusion = f32[2,4,64,1024]{3,2,1,0:T(8,128)S(1)} fusion(bf16[2,4,64,1024]{3,2,1,0:T(8,128)(2,1)S(1)} %bitcast.123, bf16[2,1024,1024]{2,1,0:T(8,128)(2,1)} %refs_2_.1, s32[]{:T(128)S(6)} %select_n.139), kind=kOutput, calls=%fused_computation.2 | convolution fusion | flops 1073741824 | bytes 5242884 | tf_op jit(solution)/shard_map/dot_general | solution.py:17
  13.2 1.3 copy-done.4
  14.5 0.8 dynamic-slice_convert_fusion
  15.3 6.9 %collective-permute-done.2 = bf16[72,1024]{1,0:T(8,128)(2,1)S(1)} collective-permute-done((bf16[72,1024]{1,0:T(8,128)(2,1)S(1)}, bf16[72,1024]{1,0:T(8,128)(2,1)S(1)}, u32[]{:S(2)}, u32[]{:S(2)}) %collective-permute-start.2) | collective-permute-done | bytes 147488 | tf_op jit(solution)/shard_map/ppermute | solution.py:185
  22.5 1.6 %broadcast_in_dim.45 = bf16[4,2,128,1024]{3,2,1,0:T(8,128)(2,1)} broadcast(bf16[2,128,1024]{2,1,0:T(8,128)(2,1)S(1)} %bitcast.116), dimensions={1,2,3} | broadcast | bytes 2621440 | tf_op jit(solution)/shard_map/broadcast_in_dim | solution.py:244
  24.1 3.9 %all-to-all-start = ((bf16[8,128,1024]{2,1,0:T(8,128)(2,1)}), bf16[8,128,1024]{2,1,0:T(8,128)(2,1)S(1)}, u32[]{:S(2)}, u32[]{:S(2)}) async-start(bf16[8,128,1024]{2,1,0:T(8,128)(2,1)} %bitcast.112), calls=%async_computation | async-start | bytes 4194304 | tf_op jit(solution)/shard_map/all_to_all | solution.py:246
  28.7 2.6 %collective-permute-start.7 = (bf16[128,1024]{1,0:T(8,128)(2,1)}, bf16[128,1024]{1,0:T(8,128)(2,1)}, u32[]{:S(2)}, u32[]{:S(2)}) collective-permute-start(bf16[128,1024]{1,0:T(8,128)(2,1)} %bitcast.10), channel_id=1, source_target_pairs={{0,3},{1,0},{2,1},{3,2},{4,7},{5,4},{6,5},{7,6},{8,11},{9,8},{10,9... | collective-permute-start | bytes 786440 | tf_op jit(solution)/shard_map/ppermute | solution.py:185
  32.0 1.1 constant_dynamic-slice_fusion.6
  33.2 3.8 %gather_fusion = bf16[128,1024]{1,0:T(8,128)(2,1)S(1)} fusion(bf16[2048,1024]{1,0:T(8,128)(2,1)} %bitcast.122, s32[1024]{0:T(1024)S(1)} %pad_clamp_fusion), kind=kCustom, calls=%fused_computation | custom fusion | bytes 524800 | tf_op jit(solution)/shard_map/jit(_take)/gather | solution.py:240
  37.1 2.2 %collective-permute-done.7 = bf16[128,1024]{1,0:T(8,128)(2,1)} collective-permute-done((bf16[128,1024]{1,0:T(8,128)(2,1)}, bf16[128,1024]{1,0:T(8,128)(2,1)}, u32[]{:S(2)}, u32[]{:S(2)}) %collective-permute-start.7) | collective-permute-done | bytes 262176 | tf_op jit(solution)/shard_map/ppermute | solution.py:185
  39.3 14.5 %collective-permute-done.6 = bf16[128,1024]{1,0:T(8,128)(2,1)} collective-permute-done((bf16[128,1024]{1,0:T(8,128)(2,1)S(1)}, bf16[128,1024]{1,0:T(8,128)(2,1)}, u32[]{:S(2)}, u32[]{:S(2)}) %collective-permute-start.6) | collective-permute-done | bytes 262176 | tf_op jit(solution)/shard_map/ppermute | solution.py:185
  53.8 1.4 multiply_reduce_fusion.4
  55.5 1.2 collective-permute-start.9
  56.7 0.9 collective-permute-start.11
  57.6 5.9 %collective-permute-done.11 = s32[2,128]{1,0:T(2,128)S(1)} collective-permute-done((s32[2,128]{1,0:T(2,128)S(1)}, s32[2,128]{1,0:T(2,128)S(1)}, u32[]{:S(2)}, u32[]{:S(2)}) %collective-permute-start.11) | collective-permute-done | bytes 1056 | tf_op jit(solution)/shard_map/ppermute | solution.py:188
  63.5 0.8 fusion.36
  64.7 1.1 collective-permute-start.10
  65.8 2.5 %collective-permute-done.10 = f32[2,2,128]{2,1,0:T(2,128)S(1)} collective-permute-done((f32[2,2,128]{2,1,0:T(2,128)S(1)}, f32[2,2,128]{2,1,0:T(2,128)S(1)}, u32[]{:S(2)}, u32[]{:S(2)}) %collective-permute-start.10) | collective-permute-done | bytes 2080 | tf_op jit(solution)/shard_map/ppermute | solution.py:188
  68.8 1.5 %convolution_convert_fusion.1 = bf16[128,1024]{1,0:T(8,128)(2,1)} fusion(bf16[1024,1024]{1,0:T(8,128)(2,1)S(1)} %bitcast.110, bf16[256,1024]{1,0:T(8,128)(2,1)S(1)} %multiply_convert_fusion), kind=kOutput, calls=%fused_computation.6 | convolution fusion | flops 268566528 | bytes 2621440 | tf_op jit(solution)/shard_map/dot_general | solution.py:17
  70.3 1.1 collective-permute-start.12
  71.4 2.1 %convolution_convert_fusion = bf16[1024,1024]{1,0:T(8,128)(2,1)} fusion(bf16[256,1024]{1,0:T(8,128)(2,1)S(1)} %multiply_convert_fusion, bf16[128,1024]{1,0:T(8,128)(2,1)S(1)} %copy-done.8, bf16[128,1024]{1,0:T(8,128)(2,1)S(1)} %copy-done.3), kind=kOutput, calls=%fused_computation.5 | convolution fusion | flops 538968064 | bytes 3145728 | tf_op jit(solution)/shard_map/dot_general | solution.py:17
  73.5 4.3 %all-to-all-start.2 = ((bf16[8,128,1024]{2,1,0:T(8,128)(2,1)}), bf16[8,128,1024]{2,1,0:T(8,128)(2,1)}, u32[]{:S(2)}, u32[]{:S(2)}) async-start(bf16[8,128,1024]{2,1,0:T(8,128)(2,1)} %bitcast.114), calls=%async_computation.2 | async-start | bytes 4194304 | tf_op jit(solution)/shard_map/all_to_all | solution.py:293
  78.6 2.0 %multiply_reduce_fusion.3 = (f32[128]{0:T(128)S(1)}, f32[128]{0:T(128)S(1)}, f32[128]{0:T(128)S(1)}, f32[128,1024]{1,0:T(8,128)S(1)}) fusion(f32[128,1024]{1,0:T(8,128)S(1)} %get-tuple-element.48, bf16[128,1024]{1,0:T(8,128)(2,1)} %collective-permute-done.12, f32[1024]{0:T(1024)S(1)} %bitcast.128, bf16[128,1024]{1,0:T(8,128)(2,1)S(1)} %gather_fusion, ...), kind=kOutput, calls=%fused_computation.18 | convolution fusion | flops 270270080 | bytes 3938433 | tf_op jit(solution)/shard_map/dot_general | solution.py:17
  80.6 1.2 subtract_convert_fusion.refs_0_
  81.8 1.0 collective-permute-start.14
  82.9 3.1 %collective-permute-start.15 = (bf16[128,1024]{1,0:T(8,128)(2,1)S(1)}, bf16[128,1024]{1,0:T(8,128)(2,1)S(1)}, u32[]{:S(2)}, u32[]{:S(2)}) collective-permute-start(bf16[128,1024]{1,0:T(8,128)(2,1)S(1)} %subtract_convert_fusion.refs_0_), channel_id=1, source_target_pairs={{0,2},{1,3},{2,0},{3,1},{4,6},{5,7},{6,4},{7,5},{8,10},{9,11},{10,... | collective-permute-start | bytes 786440 | tf_op jit(solution)/shard_map/ppermute | solution.py:185
  86.0 1.2 collective-permute-start.16
  87.5 0.9 copy.39.refs_6_
  88.6 4.4 %collective-permute-done.14.refs_1_ = bf16[128,1024]{1,0:T(8,128)(2,1)S(1)} collective-permute-done((bf16[128,1024]{1,0:T(8,128)(2,1)S(1)}, bf16[128,1024]{1,0:T(8,128)(2,1)S(1)}, u32[]{:S(2)}, u32[]{:S(2)}) %collective-permute-start.14) | collective-permute-done | bytes 262176 | tf_op jit(solution)/shard_map/ppermute | solution.py:185
  93.0 10.6 %collective-permute-done.15.refs_2_ = bf16[128,1024]{1,0:T(8,128)(2,1)S(1)} collective-permute-done((bf16[128,1024]{1,0:T(8,128)(2,1)S(1)}, bf16[128,1024]{1,0:T(8,128)(2,1)S(1)}, u32[]{:S(2)}, u32[]{:S(2)}) %collective-permute-start.15) | collective-permute-done | bytes 262176 | tf_op jit(solution)/shard_map/ppermute | solution.py:185
  105.0 5.1 %shard_map.85 = (bf16[1024,1024]{1,0:T(8,128)(2,1)}, bf16[256,1024]{1,0:T(8,128)(2,1)}, bf16[256,1024]{1,0:T(8,128)(2,1)}) custom-call(s32[2]{0:T(128)} %pad_add_fusion.2.place_ref, bf16[128,1024]{1,0:T(8,128)(2,1)} %copy-done.9, bf16[128,1024]{1,0:T(8,128)(2,1)} %copy-done.14, bf16[128,1024]{1,0:T(8,128)(2,1)} %copy-done.15, bf16[128,1024]{1,0:T(8,128)(2,1)} %copy-done.16, ...), custom_call_target="tpu_custom_call" | custom-call | flops 1073741824 | bytes 2099200 | tf_op jit(solution)/shard_map/pallas_call | solution.py:33
  110.1 3.9 %all-to-all-start.1 = ((bf16[8,128,1024]{2,1,0:T(8,128)(2,1)}), bf16[8,128,1024]{2,1,0:T(8,128)(2,1)S(1)}, u32[]{:S(2)}, u32[]{:S(2)}) async-start(bf16[8,128,1024]{2,1,0:T(8,128)(2,1)} %bitcast.117), calls=%async_computation.1 | async-start | bytes 4194304 | tf_op jit(solution)/shard_map/all_to_all | solution.py:314
  114.5 5.4 %collective-permute-start.18 = (f32[64]{0:T(128)S(1)}, f32[64]{0:T(128)S(1)}, u32[]{:S(2)}, u32[]{:S(2)}) collective-permute-start(f32[64]{0:T(128)S(1)} %bitcast_add_fusion.1), channel_id=1, source_target_pairs={{0,1},{1,2},{2,3},{3,0},{4,5},{5,6},{6,7},{7,4},{8,9},{9,10},{10,1... | collective-permute-start | bytes 776 | tf_op jit(solution)/shard_map/ppermute | solution.py:185
  119.9 2.1 %collective-permute-start.19 = (f32[64]{0:T(128)S(1)}, f32[64]{0:T(128)S(1)}, u32[]{:S(2)}, u32[]{:S(2)}) collective-permute-start(f32[64]{0:T(128)S(1)} %bitcast_add_fusion.1), channel_id=1, source_target_pairs={{0,2},{1,3},{2,0},{3,1},{4,6},{5,7},{6,4},{7,5},{8,10},{9,11},{10,... | collective-permute-start | bytes 776 | tf_op jit(solution)/shard_map/ppermute | solution.py:185
  123.0 1.4 collective-permute-done.19
  124.4 1.1 collective-permute-done.20
  125.7 2.0 %reduce_sum.108 = bf16[2,4,32,1024]{3,2,1,0:T(8,128)(2,1)S(1)} reduce(bf16[4,2,4,32,1024]{4,3,2,1,0:T(8,128)(2,1)} %bitcast.53, bf16[]{:T(256)} %constant.168.clone.1), dimensions={0}, to_apply=%region_10.11 | reduce | flops 786432 | bytes 2621442 | tf_op jit(solution)/shard_map/reduce_sum | solution.py:294
  128.4 2.7 %collective-permute-start.22 = (bf16[2,32,1024]{2,1,0:T(8,128)(2,1)S(1)}, bf16[2,32,1024]{2,1,0:T(8,128)(2,1)S(1)}, u32[]{:S(2)}, u32[]{:S(2)}) collective-permute-start(bf16[2,32,1024]{2,1,0:T(8,128)(2,1)S(1)} %get-tuple-element.53), channel_id=1, source_target_pairs={{0,2},{1,3},{2,0},{3,1},{4,6},{5,7},{6,4},{7,5},{8,10},{9,11},{10,... | collective-permute-start | bytes 393224 | tf_op jit(solution)/shard_map/ppermute | solution.py:185
  131.1 1.2 collective-permute-start.23
  132.3 0.9 copy.40.refs_4_
  133.9 4.9 %shard_map.86 = bf16[256,1024]{1,0:T(8,128)(2,1)} custom-call(s32[2]{0:T(128)} %pad_add_fusion.2.place_ref, bf16[256,1024]{1,0:T(8,128)(2,1)} %get-tuple-element.27.refs_0_, bf16[256,1024]{1,0:T(8,128)(2,1)} %copy-done.6, bf16[2,1024,1024]{2,1,0:T(8,128)(2,1)} %refs_2_.1, bf16[256,1024]{1,0:T(8,128)(2,1)} %refs_3_.1, f32[2,256,1]{2,1,0:T(8,128)} %copy.40.refs_4_), custom_call_target="tpu_custom_call" | custom-call | flops 1073741824 | bytes 5769216 | tf_op jit(solution)/shard_map/pallas_call | solution.py:33
  138.8 1.2 collective-permute-done.22.refs_2_
  140.7 2.7 %shard_map.87 = f32[32,2,2048]{2,1,0:T(2,128)} custom-call(s32[2]{0:T(128)} %pad_add_fusion.2.place_ref, bf16[2,32,1024]{2,1,0:T(8,128)(2,1)} %get-tuple-element.55.refs_0_, bf16[2,32,1024]{2,1,0:T(8,128)(2,1)} %copy-done.10, bf16[2,32,1024]{2,1,0:T(8,128)(2,1)} %copy-done.11, bf16[2,32,1024]{2,1,0:T(8,128)(2,1)} %copy-done.12), custom_call_target="tpu_custom_call" | custom-call | flops 262144 | bytes 524288 | tf_op jit(solution)/shard_map/pallas_call | solution.py:33
  143.8 1.3 copy.41
  (124 shorter events, 11.2 us)
Async XLA Ops:
  0.6 9.5 %copy-start = (f32[2,1024]{1,0:T(2,128)S(1)}, f32[2,1024]{1,0:T(2,128)}, u32[]{:S(2)}) copy-start(f32[2,1024]{1,0:T(2,128)} %param.9) | copy-start | bytes 24580
  0.6 9.5 %copy-start.1 = (bf16[256,1024]{1,0:T(8,128)(2,1)S(1)}, bf16[256,1024]{1,0:T(8,128)(2,1)}, u32[]{:S(2)}) copy-start(bf16[256,1024]{1,0:T(8,128)(2,1)} %refs_3_.1) | copy-start | bytes 1572868
  0.7 9.5 %collective-permute-start.1 = (bf16[256,1024]{1,0:T(8,128)(2,1)}, bf16[256,1024]{1,0:T(8,128)(2,1)S(1)}, u32[]{:S(2)}, u32[]{:S(2)}) collective-permute-start(bf16[256,1024]{1,0:T(8,128)(2,1)} %refs_3_.1), channel_id=1, source_target_pairs={{0,4},{4,0},{8,12},{12,8},{16,20},{20,16},{24,28},{28,24},{1,5},{5... | collective-permute-start | bytes 1572872 | tf_op jit(solution)/shard_map/ppermute | solution.py:195
  4.4 11.0 %collective-permute-start.3 = (bf16[72,1024]{1,0:T(8,128)(2,1)S(1)}, bf16[72,1024]{1,0:T(8,128)(2,1)S(1)}, u32[]{:S(2)}, u32[]{:S(2)}) collective-permute-start(bf16[72,1024]{1,0:T(8,128)(2,1)S(1)} %get-tuple-element.59), channel_id=1, source_target_pairs={{0,3},{1,0},{2,1},{3,2},{4,7},{5,4},{6,5},{7,6},{8,11},{9,8},{10,9... | collective-permute-start | bytes 442376 | tf_op jit(solution)/shard_map/ppermute | solution.py:185
  9.1 13.1 %collective-permute-start = (bf16[72,1024]{1,0:T(8,128)(2,1)S(1)}, bf16[72,1024]{1,0:T(8,128)(2,1)S(1)}, u32[]{:S(2)}, u32[]{:S(2)}) collective-permute-start(bf16[72,1024]{1,0:T(8,128)(2,1)S(1)} %get-tuple-element.59), channel_id=1, source_target_pairs={{0,1},{1,2},{2,3},{3,0},{4,5},{5,6},{6,7},{7,4},{8,9},{9,10},{10,1... | collective-permute-start | bytes 442376 | tf_op jit(solution)/shard_map/ppermute | solution.py:185
  9.1 13.1 %collective-permute-start.2 = (bf16[72,1024]{1,0:T(8,128)(2,1)S(1)}, bf16[72,1024]{1,0:T(8,128)(2,1)S(1)}, u32[]{:S(2)}, u32[]{:S(2)}) collective-permute-start(bf16[72,1024]{1,0:T(8,128)(2,1)S(1)} %get-tuple-element.58), channel_id=1, source_target_pairs={{0,2},{1,3},{2,0},{3,1},{4,6},{5,7},{6,4},{7,5},{8,10},{9,11},{10,... | collective-permute-start | bytes 442376 | tf_op jit(solution)/shard_map/ppermute | solution.py:185
  10.1 3.1 %copy-start.5 = (bf16[256,1024]{1,0:T(8,128)(2,1)}, bf16[256,1024]{1,0:T(8,128)(2,1)S(1)}, u32[]{:S(2)}) copy-start(bf16[256,1024]{1,0:T(8,128)(2,1)S(1)} %collective-permute-done.1.refs_5_) | copy-start | bytes 1572868
  13.2 1.3 copy-start.4
  24.1 4.5 %copy-start.13 = (s32[2,64]{1,0:T(2,128)S(1)}, s32[2,64]{1,0:T(2,128)}, u32[]{:S(2)}) copy-start(s32[2,64]{1,0:T(2,128)} %param.11) | copy-start | bytes 1540
  24.1 39.4 %all-to-all-start = ((bf16[8,128,1024]{2,1,0:T(8,128)(2,1)}), bf16[8,128,1024]{2,1,0:T(8,128)(2,1)S(1)}, u32[]{:S(2)}, u32[]{:S(2)}) async-start(bf16[8,128,1024]{2,1,0:T(8,128)(2,1)} %bitcast.112), calls=%async_computation | async-start | bytes 4194304 | tf_op jit(solution)/shard_map/all_to_all | solution.py:246
  28.0 8.9 %collective-permute-start.4 = (f32[256]{0:T(256)S(1)}, f32[256]{0:T(256)S(1)}, u32[]{:S(2)}, u32[]{:S(2)}) collective-permute-start(f32[256]{0:T(256)S(1)} %slice_reduce_fusion), channel_id=1, source_target_pairs={{0,4},{4,0},{8,12},{12,8},{16,20},{20,16},{24,28},{28,24},{1,5},{5... | collective-permute-start | bytes 3080 | tf_op jit(solution)/shard_map/ppermute | solution.py:195
  28.6 4.4 %collective-permute-start.8 = (s32[2,64]{1,0:T(2,128)S(1)}, s32[2,64]{1,0:T(2,128)S(1)}, u32[]{:S(2)}, u32[]{:S(2)}) collective-permute-start(s32[2,64]{1,0:T(2,128)S(1)} %copy-done.13), channel_id=1, source_target_pairs={{0,4},{4,0},{8,12},{12,8},{16,20},{20,16},{24,28},{28,24},{1,5},{5... | collective-permute-start | bytes 1544 | tf_op jit(solution)/shard_map/ppermute | solution.py:195
  28.7 10.6 %collective-permute-start.7 = (bf16[128,1024]{1,0:T(8,128)(2,1)}, bf16[128,1024]{1,0:T(8,128)(2,1)}, u32[]{:S(2)}, u32[]{:S(2)}) collective-permute-start(bf16[128,1024]{1,0:T(8,128)(2,1)} %bitcast.10), channel_id=1, source_target_pairs={{0,3},{1,0},{2,1},{3,2},{4,7},{5,4},{6,5},{7,6},{8,11},{9,8},{10,9... | collective-permute-start | bytes 786440 | tf_op jit(solution)/shard_map/ppermute | solution.py:185
  31.3 22.5 %collective-permute-start.6 = (bf16[128,1024]{1,0:T(8,128)(2,1)S(1)}, bf16[128,1024]{1,0:T(8,128)(2,1)}, u32[]{:S(2)}, u32[]{:S(2)}) collective-permute-start(bf16[128,1024]{1,0:T(8,128)(2,1)S(1)} %bitcast.126), channel_id=1, source_target_pairs={{0,2},{1,3},{2,0},{3,1},{4,6},{5,7},{6,4},{7,5},{8,10},{9,11},{10,... | collective-permute-start | bytes 786440 | tf_op jit(solution)/shard_map/ppermute | solution.py:185
  31.3 22.5 %collective-permute-start.5 = (bf16[128,1024]{1,0:T(8,128)(2,1)S(1)}, bf16[128,1024]{1,0:T(8,128)(2,1)}, u32[]{:S(2)}, u32[]{:S(2)}) collective-permute-start(bf16[128,1024]{1,0:T(8,128)(2,1)S(1)} %bitcast.125), channel_id=1, source_target_pairs={{0,1},{1,2},{2,3},{3,0},{4,5},{5,6},{6,7},{7,4},{8,9},{9,10},{10,1... | collective-permute-start | bytes 786440 | tf_op jit(solution)/shard_map/ppermute | solution.py:185
  55.5 9.2 %copy-start.2 = (bf16[128,1024]{1,0:T(8,128)(2,1)}, bf16[128,1024]{1,0:T(8,128)(2,1)S(1)}, u32[]{:S(2)}) copy-start(bf16[128,1024]{1,0:T(8,128)(2,1)S(1)} %multiply_convert_fusion.1) | copy-start | bytes 786436
  55.5 8.0 %collective-permute-start.9 = (bf16[128,1024]{1,0:T(8,128)(2,1)S(1)}, bf16[128,1024]{1,0:T(8,128)(2,1)S(1)}, u32[]{:S(2)}, u32[]{:S(2)}) collective-permute-start(bf16[128,1024]{1,0:T(8,128)(2,1)S(1)} %multiply_convert_fusion.1), channel_id=1, source_target_pairs={{0,1},{1,0},{2,3},{3,2},{4,5},{5,4},{6,7},{7,6},{8,9},{9,8},{10,11... | collective-permute-start | bytes 786440 | tf_op jit(solution)/shard_map/ppermute | solution.py:188
  56.7 6.8 %collective-permute-start.11 = (s32[2,128]{1,0:T(2,128)S(1)}, s32[2,128]{1,0:T(2,128)S(1)}, u32[]{:S(2)}, u32[]{:S(2)}) collective-permute-start(s32[2,128]{1,0:T(2,128)S(1)} %pad_add_fusion), channel_id=1, source_target_pairs={{0,1},{1,0},{2,3},{3,2},{4,5},{5,4},{6,7},{7,6},{8,9},{9,8},{10,11... | collective-permute-start | bytes 3080 | tf_op jit(solution)/shard_map/ppermute | solution.py:188
  63.5 1.2 copy-start.7
  64.7 3.7 %collective-permute-start.10 = (f32[2,2,128]{2,1,0:T(2,128)S(1)}, f32[2,2,128]{2,1,0:T(2,128)S(1)}, u32[]{:S(2)}, u32[]{:S(2)}) collective-permute-start(f32[2,2,128]{2,1,0:T(2,128)S(1)} %pad_maximum_fusion.6), channel_id=1, source_target_pairs={{0,1},{1,0},{2,3},{3,2},{4,5},{5,4},{6,7},{7,6},{8,9},{9,8},{10,11... | collective-permute-start | bytes 6152 | tf_op jit(solution)/shard_map/ppermute | solution.py:188
  68.4 3.0 %copy-start.3 = (bf16[128,1024]{1,0:T(8,128)(2,1)S(1)}, bf16[128,1024]{1,0:T(8,128)(2,1)}, u32[]{:S(2)}) copy-start(bf16[128,1024]{1,0:T(8,128)(2,1)} %copy-done.2) | copy-start | bytes 786436
  68.4 3.0 %copy-start.8 = (bf16[128,1024]{1,0:T(8,128)(2,1)S(1)}, bf16[128,1024]{1,0:T(8,128)(2,1)}, u32[]{:S(2)}) copy-start(bf16[128,1024]{1,0:T(8,128)(2,1)} %copy-done.7) | copy-start | bytes 786436
  70.3 8.3 %collective-permute-start.12 = (bf16[128,1024]{1,0:T(8,128)(2,1)}, bf16[128,1024]{1,0:T(8,128)(2,1)}, u32[]{:S(2)}, u32[]{:S(2)}) collective-permute-start(bf16[128,1024]{1,0:T(8,128)(2,1)} %convolution_convert_fusion.1), channel_id=1, source_target_pairs={{0,1},{1,0},{2,3},{3,2},{4,5},{5,4},{6,7},{7,6},{8,9},{9,8},{10,11... | collective-permute-start | bytes 786440 | tf_op jit(solution)/shard_map/ppermute | solution.py:188
  73.5 36.6 %all-to-all-start.2 = ((bf16[8,128,1024]{2,1,0:T(8,128)(2,1)}), bf16[8,128,1024]{2,1,0:T(8,128)(2,1)}, u32[]{:S(2)}, u32[]{:S(2)}) async-start(bf16[8,128,1024]{2,1,0:T(8,128)(2,1)} %bitcast.114), calls=%async_computation.2 | async-start | bytes 4194304 | tf_op jit(solution)/shard_map/all_to_all | solution.py:293
  81.8 21.8 %copy-start.9 = (bf16[128,1024]{1,0:T(8,128)(2,1)}, bf16[128,1024]{1,0:T(8,128)(2,1)S(1)}, u32[]{:S(2)}) copy-start(bf16[128,1024]{1,0:T(8,128)(2,1)S(1)} %subtract_convert_fusion.refs_0_) | copy-start | bytes 786436
  81.8 11.1 %collective-permute-start.14 = (bf16[128,1024]{1,0:T(8,128)(2,1)S(1)}, bf16[128,1024]{1,0:T(8,128)(2,1)S(1)}, u32[]{:S(2)}, u32[]{:S(2)}) collective-permute-start(bf16[128,1024]{1,0:T(8,128)(2,1)S(1)} %subtract_convert_fusion.refs_0_), channel_id=1, source_target_pairs={{0,1},{1,2},{2,3},{3,0},{4,5},{5,6},{6,7},{7,4},{8,9},{9,10},{10,1... | collective-permute-start | bytes 786440 | tf_op jit(solution)/shard_map/ppermute | solution.py:185
  82.9 20.7 %collective-permute-start.15 = (bf16[128,1024]{1,0:T(8,128)(2,1)S(1)}, bf16[128,1024]{1,0:T(8,128)(2,1)S(1)}, u32[]{:S(2)}, u32[]{:S(2)}) collective-permute-start(bf16[128,1024]{1,0:T(8,128)(2,1)S(1)} %subtract_convert_fusion.refs_0_), channel_id=1, source_target_pairs={{0,2},{1,3},{2,0},{3,1},{4,6},{5,7},{6,4},{7,5},{8,10},{9,11},{10,... | collective-permute-start | bytes 786440 | tf_op jit(solution)/shard_map/ppermute | solution.py:185
  86.0 17.7 %collective-permute-start.16 = (bf16[128,1024]{1,0:T(8,128)(2,1)S(1)}, bf16[128,1024]{1,0:T(8,128)(2,1)S(1)}, u32[]{:S(2)}, u32[]{:S(2)}) collective-permute-start(bf16[128,1024]{1,0:T(8,128)(2,1)S(1)} %subtract_convert_fusion.refs_0_), channel_id=1, source_target_pairs={{0,3},{1,0},{2,1},{3,2},{4,7},{5,4},{6,5},{7,6},{8,11},{9,8},{10,9... | collective-permute-start | bytes 786440 | tf_op jit(solution)/shard_map/ppermute | solution.py:185
  87.4 1.2 collective-permute-start.13
  93.0 10.7 %copy-start.14 = (bf16[128,1024]{1,0:T(8,128)(2,1)}, bf16[128,1024]{1,0:T(8,128)(2,1)S(1)}, u32[]{:S(2)}) copy-start(bf16[128,1024]{1,0:T(8,128)(2,1)S(1)} %collective-permute-done.14.refs_1_) | copy-start | bytes 786436
  103.6 0.7 copy-start.15
  104.3 0.7 copy-start.16
  110.1 33.3 %all-to-all-start.1 = ((bf16[8,128,1024]{2,1,0:T(8,128)(2,1)}), bf16[8,128,1024]{2,1,0:T(8,128)(2,1)S(1)}, u32[]{:S(2)}, u32[]{:S(2)}) async-start(bf16[8,128,1024]{2,1,0:T(8,128)(2,1)} %bitcast.117), calls=%async_computation.1 | async-start | bytes 4194304 | tf_op jit(solution)/shard_map/all_to_all | solution.py:314
  114.0 19.1 %collective-permute-start.17 = (bf16[256,1024]{1,0:T(8,128)(2,1)}, bf16[256,1024]{1,0:T(8,128)(2,1)S(1)}, u32[]{:S(2)}, u32[]{:S(2)}) collective-permute-start(bf16[256,1024]{1,0:T(8,128)(2,1)} %get-tuple-element.28), channel_id=1, source_target_pairs={{0,4},{4,0},{8,12},{12,8},{16,20},{20,16},{24,28},{28,24},{1,5},{5... | collective-permute-start | bytes 1572872 | tf_op jit(solution)/shard_map/ppermute | solution.py:195
  114.5 8.4 %collective-permute-start.18 = (f32[64]{0:T(128)S(1)}, f32[64]{0:T(128)S(1)}, u32[]{:S(2)}, u32[]{:S(2)}) collective-permute-start(f32[64]{0:T(128)S(1)} %bitcast_add_fusion.1), channel_id=1, source_target_pairs={{0,1},{1,2},{2,3},{3,0},{4,5},{5,6},{6,7},{7,4},{8,9},{9,10},{10,1... | collective-permute-start | bytes 776 | tf_op jit(solution)/shard_map/ppermute | solution.py:185
  119.9 4.4 %collective-permute-start.19 = (f32[64]{0:T(128)S(1)}, f32[64]{0:T(128)S(1)}, u32[]{:S(2)}, u32[]{:S(2)}) collective-permute-start(f32[64]{0:T(128)S(1)} %bitcast_add_fusion.1), channel_id=1, source_target_pairs={{0,2},{1,3},{2,0},{3,1},{4,6},{5,7},{6,4},{7,5},{8,10},{9,11},{10,... | collective-permute-start | bytes 776 | tf_op jit(solution)/shard_map/ppermute | solution.py:185
  122.0 3.5 %collective-permute-start.20 = (f32[64]{0:T(128)S(1)}, f32[64]{0:T(128)S(1)}, u32[]{:S(2)}, u32[]{:S(2)}) collective-permute-start(f32[64]{0:T(128)S(1)} %bitcast_add_fusion.1), channel_id=1, source_target_pairs={{0,3},{1,0},{2,1},{3,2},{4,7},{5,4},{6,5},{7,6},{8,11},{9,8},{10,9... | collective-permute-start | bytes 776 | tf_op jit(solution)/shard_map/ppermute | solution.py:185
  128.4 10.4 %collective-permute-start.21 = (bf16[2,32,1024]{2,1,0:T(8,128)(2,1)S(1)}, bf16[2,32,1024]{2,1,0:T(8,128)(2,1)S(1)}, u32[]{:S(2)}, u32[]{:S(2)}) collective-permute-start(bf16[2,32,1024]{2,1,0:T(8,128)(2,1)S(1)} %get-tuple-element.54), channel_id=1, source_target_pairs={{0,1},{1,2},{2,3},{3,0},{4,5},{5,6},{6,7},{7,4},{8,9},{9,10},{10,1... | collective-permute-start | bytes 393224 | tf_op jit(solution)/shard_map/ppermute | solution.py:185
  128.4 11.6 %collective-permute-start.22 = (bf16[2,32,1024]{2,1,0:T(8,128)(2,1)S(1)}, bf16[2,32,1024]{2,1,0:T(8,128)(2,1)S(1)}, u32[]{:S(2)}, u32[]{:S(2)}) collective-permute-start(bf16[2,32,1024]{2,1,0:T(8,128)(2,1)S(1)} %get-tuple-element.53), channel_id=1, source_target_pairs={{0,2},{1,3},{2,0},{3,1},{4,6},{5,7},{6,4},{7,5},{8,10},{9,11},{10,... | collective-permute-start | bytes 393224 | tf_op jit(solution)/shard_map/ppermute | solution.py:185
  131.1 9.0 %collective-permute-start.23 = (bf16[2,32,1024]{2,1,0:T(8,128)(2,1)S(1)}, bf16[2,32,1024]{2,1,0:T(8,128)(2,1)S(1)}, u32[]{:S(2)}, u32[]{:S(2)}) collective-permute-start(bf16[2,32,1024]{2,1,0:T(8,128)(2,1)S(1)} %get-tuple-element.52), channel_id=1, source_target_pairs={{0,3},{1,0},{2,1},{3,2},{4,7},{5,4},{6,5},{7,6},{8,11},{9,8},{10,9... | collective-permute-start | bytes 393224 | tf_op jit(solution)/shard_map/ppermute | solution.py:185
  133.1 0.8 copy-start.6
  138.8 1.2 copy-start.10
  140.0 0.6 copy-start.11
  140.0 0.7 copy-start.12

commit v17 on v16

--- a/solution.py
+++ b/solution.py
@@ -90,7 +90,7 @@
     owned, depth = pieces[0].shape
     rows, units = group[0].shape
     part = owned // steps
-    wide = min(512, depth)
+    wide = depth
 
     def kernel(place_ref, *refs):
         chunks, group, ratio = refs[:hids], refs[hids : hids + steps], refs[hids + steps]

time: 146 us -> 146 us (level)
  no operation moved by 1% of the time
where the time goes in v17:
time: 146 us; the launch traced here: 145 us
  waiting for transfers between devices  51.6 us (35%)
  starting transfers between devices  44 us (30%)
  local copies, waits for them, and re-layouts  18 us (12%)
  Pallas kernels  12.7 us (9%)
  matrix products  9.42 us (6%)
  other arithmetic  8.26 us (6%)
    ppermute x15, waiting for transfers between devices, along_hid(): lax.ppermute(values, 'hid', [(a, (a + shift) % hids) for a in range(hids)])  43 us
    ppermute x15, starting transfers between devices, along_hid(): lax.ppermute(values, 'hid', [(a, (a + shift) % hids) for a in range(hids)])  25.9 us
    pallas_call x3, Pallas kernels, call(): pl.pallas_call(kernel, grid_spec=pltpu.PrefetchScalarGridSpec(num_scalar_...  12.7 us
    dot_general x5, matrix products, matmul(): lax.dot_general(a, b, (contract, ((), ())), preferred_element_type=F32)  9.42 us
    ppermute x4, waiting for transfers between devices, turn_hid(): lax.ppermute(values, 'hid', [(a, a - a % halves + (a % halves + shift) %...  8.41 us
    unnamed x44, local copies, waits for them, and re-layouts  5.74 us
    all_to_all x1, starting transfers between devices, shards(): part_out = lax.all_to_all(part_out, 'seq', 0, 0)  4.34 us
    ppermute x4, starting transfers between devices, turn_hid(): lax.ppermute(values, 'hid', [(a, a - a % halves + (a % halves + shift) %...  4.29 us
  transfers between devices with their start and end apart: 27, of which 12 were waited for; matrix products, arithmetic and copies ran while one was open for 17% of the time, Pallas kernels for 9%

profile of v17, /device:TPU:0, one launch (start us, length us, event | category | flops | bytes accessed | tf_op | source)
XLA Modules:
  0.0 145.2 jit_solution(8577170775361626116)
XLA Ops:
  1.2 1.2 multiply_reduce_fusion
  2.5 1.1 reshape.241
  4.4 4.7 %collective-permute-start.3 = (bf16[72,1024]{1,0:T(8,128)(2,1)S(1)}, bf16[72,1024]{1,0:T(8,128)(2,1)S(1)}, u32[]{:S(2)}, u32[]{:S(2)}) collective-permute-start(bf16[72,1024]{1,0:T(8,128)(2,1)S(1)} %get-tuple-element.59), channel_id=1, source_target_pairs={{0,3},{1,0},{2,1},{3,2},{4,7},{5,4},{6,5},{7,6},{8,11},{9,8},{10,9... | collective-permute-start | bytes 442376 | tf_op jit(solution)/shard_map/ppermute | solution.py:185
  9.1 1.0 collective-permute-start.2
  10.2 3.0 %fusion = f32[2,4,64,1024]{3,2,1,0:T(8,128)S(1)} fusion(bf16[2,4,64,1024]{3,2,1,0:T(8,128)(2,1)S(1)} %bitcast.123, bf16[2,1024,1024]{2,1,0:T(8,128)(2,1)} %refs_2_.1, s32[]{:T(128)S(6)} %select_n.139), kind=kOutput, calls=%fused_computation.2 | convolution fusion | flops 1073741824 | bytes 5242884 | tf_op jit(solution)/shard_map/dot_general | solution.py:17
  13.2 1.3 copy-done.4
  14.5 0.8 dynamic-slice_convert_fusion
  15.3 6.9 %collective-permute-done.2 = bf16[72,1024]{1,0:T(8,128)(2,1)S(1)} collective-permute-done((bf16[72,1024]{1,0:T(8,128)(2,1)S(1)}, bf16[72,1024]{1,0:T(8,128)(2,1)S(1)}, u32[]{:S(2)}, u32[]{:S(2)}) %collective-permute-start.2) | collective-permute-done | bytes 147488 | tf_op jit(solution)/shard_map/ppermute | solution.py:185
  22.5 1.6 %broadcast_in_dim.45 = bf16[4,2,128,1024]{3,2,1,0:T(8,128)(2,1)} broadcast(bf16[2,128,1024]{2,1,0:T(8,128)(2,1)S(1)} %bitcast.116), dimensions={1,2,3} | broadcast | bytes 2621440 | tf_op jit(solution)/shard_map/broadcast_in_dim | solution.py:244
  24.1 3.9 %all-to-all-start = ((bf16[8,128,1024]{2,1,0:T(8,128)(2,1)}), bf16[8,128,1024]{2,1,0:T(8,128)(2,1)S(1)}, u32[]{:S(2)}, u32[]{:S(2)}) async-start(bf16[8,128,1024]{2,1,0:T(8,128)(2,1)} %bitcast.112), calls=%async_computation | async-start | bytes 4194304 | tf_op jit(solution)/shard_map/all_to_all | solution.py:246
  28.7 2.6 %collective-permute-start.7 = (bf16[128,1024]{1,0:T(8,128)(2,1)}, bf16[128,1024]{1,0:T(8,128)(2,1)}, u32[]{:S(2)}, u32[]{:S(2)}) collective-permute-start(bf16[128,1024]{1,0:T(8,128)(2,1)} %bitcast.10), channel_id=1, source_target_pairs={{0,3},{1,0},{2,1},{3,2},{4,7},{5,4},{6,5},{7,6},{8,11},{9,8},{10,9... | collective-permute-start | bytes 786440 | tf_op jit(solution)/shard_map/ppermute | solution.py:185
  32.0 1.1 constant_dynamic-slice_fusion.6
  33.2 3.8 %gather_fusion = bf16[128,1024]{1,0:T(8,128)(2,1)S(1)} fusion(bf16[2048,1024]{1,0:T(8,128)(2,1)} %bitcast.122, s32[1024]{0:T(1024)S(1)} %pad_clamp_fusion), kind=kCustom, calls=%fused_computation | custom fusion | bytes 524800 | tf_op jit(solution)/shard_map/jit(_take)/gather | solution.py:240
  37.1 2.2 %collective-permute-done.7 = bf16[128,1024]{1,0:T(8,128)(2,1)} collective-permute-done((bf16[128,1024]{1,0:T(8,128)(2,1)}, bf16[128,1024]{1,0:T(8,128)(2,1)}, u32[]{:S(2)}, u32[]{:S(2)}) %collective-permute-start.7) | collective-permute-done | bytes 262176 | tf_op jit(solution)/shard_map/ppermute | solution.py:185
  39.3 14.5 %collective-permute-done.6 = bf16[128,1024]{1,0:T(8,128)(2,1)} collective-permute-done((bf16[128,1024]{1,0:T(8,128)(2,1)S(1)}, bf16[128,1024]{1,0:T(8,128)(2,1)}, u32[]{:S(2)}, u32[]{:S(2)}) %collective-permute-start.6) | collective-permute-done | bytes 262176 | tf_op jit(solution)/shard_map/ppermute | solution.py:185
  53.8 1.4 multiply_reduce_fusion.4
  55.5 1.2 collective-permute-start.9
  56.7 0.9 collective-permute-start.11
  57.6 5.9 %collective-permute-done.11 = s32[2,128]{1,0:T(2,128)S(1)} collective-permute-done((s32[2,128]{1,0:T(2,128)S(1)}, s32[2,128]{1,0:T(2,128)S(1)}, u32[]{:S(2)}, u32[]{:S(2)}) %collective-permute-start.11) | collective-permute-done | bytes 1056 | tf_op jit(solution)/shard_map/ppermute | solution.py:188
  63.5 0.8 fusion.36
  64.7 1.1 collective-permute-start.10
  65.8 2.5 %collective-permute-done.10 = f32[2,2,128]{2,1,0:T(2,128)S(1)} collective-permute-done((f32[2,2,128]{2,1,0:T(2,128)S(1)}, f32[2,2,128]{2,1,0:T(2,128)S(1)}, u32[]{:S(2)}, u32[]{:S(2)}) %collective-permute-start.10) | collective-permute-done | bytes 2080 | tf_op jit(solution)/shard_map/ppermute | solution.py:188
  68.8 1.5 %convolution_convert_fusion.1 = bf16[128,1024]{1,0:T(8,128)(2,1)} fusion(bf16[1024,1024]{1,0:T(8,128)(2,1)S(1)} %bitcast.110, bf16[256,1024]{1,0:T(8,128)(2,1)S(1)} %multiply_convert_fusion), kind=kOutput, calls=%fused_computation.6 | convolution fusion | flops 268566528 | bytes 2621440 | tf_op jit(solution)/shard_map/dot_general | solution.py:17
  70.3 1.1 collective-permute-start.12
  71.4 2.1 %convolution_convert_fusion = bf16[1024,1024]{1,0:T(8,128)(2,1)} fusion(bf16[256,1024]{1,0:T(8,128)(2,1)S(1)} %multiply_convert_fusion, bf16[128,1024]{1,0:T(8,128)(2,1)S(1)} %copy-done.8, bf16[128,1024]{1,0:T(8,128)(2,1)S(1)} %copy-done.3), kind=kOutput, calls=%fused_computation.5 | convolution fusion | flops 538968064 | bytes 3145728 | tf_op jit(solution)/shard_map/dot_general | solution.py:17
  73.5 4.3 %all-to-all-start.2 = ((bf16[8,128,1024]{2,1,0:T(8,128)(2,1)}), bf16[8,128,1024]{2,1,0:T(8,128)(2,1)}, u32[]{:S(2)}, u32[]{:S(2)}) async-start(bf16[8,128,1024]{2,1,0:T(8,128)(2,1)} %bitcast.114), calls=%async_computation.2 | async-start | bytes 4194304 | tf_op jit(solution)/shard_map/all_to_all | solution.py:293
  78.6 2.0 %multiply_reduce_fusion.3 = (f32[128]{0:T(128)S(1)}, f32[128]{0:T(128)S(1)}, f32[128]{0:T(128)S(1)}, f32[128,1024]{1,0:T(8,128)S(1)}) fusion(f32[128,1024]{1,0:T(8,128)S(1)} %get-tuple-element.48, bf16[128,1024]{1,0:T(8,128)(2,1)} %collective-permute-done.12, f32[1024]{0:T(1024)S(1)} %bitcast.128, bf16[128,1024]{1,0:T(8,128)(2,1)S(1)} %gather_fusion, ...), kind=kOutput, calls=%fused_computation.18 | convolution fusion | flops 270270080 | bytes 3938433 | tf_op jit(solution)/shard_map/dot_general | solution.py:17
  80.6 1.2 subtract_convert_fusion.refs_0_
  81.9 1.0 collective-permute-start.14
  82.9 3.1 %collective-permute-start.15 = (bf16[128,1024]{1,0:T(8,128)(2,1)S(1)}, bf16[128,1024]{1,0:T(8,128)(2,1)S(1)}, u32[]{:S(2)}, u32[]{:S(2)}) collective-permute-start(bf16[128,1024]{1,0:T(8,128)(2,1)S(1)} %subtract_convert_fusion.refs_0_), channel_id=1, source_target_pairs={{0,2},{1,3},{2,0},{3,1},{4,6},{5,7},{6,4},{7,5},{8,10},{9,11},{10,... | collective-permute-start | bytes 786440 | tf_op jit(solution)/shard_map/ppermute | solution.py:185
  86.0 1.2 collective-permute-start.16
  87.5 0.9 copy.39.refs_6_
  88.6 4.4 %collective-permute-done.14.refs_1_ = bf16[128,1024]{1,0:T(8,128)(2,1)S(1)} collective-permute-done((bf16[128,1024]{1,0:T(8,128)(2,1)S(1)}, bf16[128,1024]{1,0:T(8,128)(2,1)S(1)}, u32[]{:S(2)}, u32[]{:S(2)}) %collective-permute-start.14) | collective-permute-done | bytes 262176 | tf_op jit(solution)/shard_map/ppermute | solution.py:185
  93.0 10.6 %collective-permute-done.15.refs_2_ = bf16[128,1024]{1,0:T(8,128)(2,1)S(1)} collective-permute-done((bf16[128,1024]{1,0:T(8,128)(2,1)S(1)}, bf16[128,1024]{1,0:T(8,128)(2,1)S(1)}, u32[]{:S(2)}, u32[]{:S(2)}) %collective-permute-start.15) | collective-permute-done | bytes 262176 | tf_op jit(solution)/shard_map/ppermute | solution.py:185
  105.0 5.1 %shard_map.85 = (bf16[1024,1024]{1,0:T(8,128)(2,1)}, bf16[256,1024]{1,0:T(8,128)(2,1)}, bf16[256,1024]{1,0:T(8,128)(2,1)}) custom-call(s32[2]{0:T(128)} %pad_add_fusion.2.place_ref, bf16[128,1024]{1,0:T(8,128)(2,1)} %copy-done.9, bf16[128,1024]{1,0:T(8,128)(2,1)} %copy-done.14, bf16[128,1024]{1,0:T(8,128)(2,1)} %copy-done.15, bf16[128,1024]{1,0:T(8,128)(2,1)} %copy-done.16, ...), custom_call_target="tpu_custom_call" | custom-call | flops 1073741824 | bytes 2099200 | tf_op jit(solution)/shard_map/pallas_call | solution.py:33
  110.2 3.9 %all-to-all-start.1 = ((bf16[8,128,1024]{2,1,0:T(8,128)(2,1)}), bf16[8,128,1024]{2,1,0:T(8,128)(2,1)S(1)}, u32[]{:S(2)}, u32[]{:S(2)}) async-start(bf16[8,128,1024]{2,1,0:T(8,128)(2,1)} %bitcast.117), calls=%async_computation.1 | async-start | bytes 4194304 | tf_op jit(solution)/shard_map/all_to_all | solution.py:314
  114.6 5.4 %collective-permute-start.18 = (f32[64]{0:T(128)S(1)}, f32[64]{0:T(128)S(1)}, u32[]{:S(2)}, u32[]{:S(2)}) collective-permute-start(f32[64]{0:T(128)S(1)} %bitcast_add_fusion.1), channel_id=1, source_target_pairs={{0,1},{1,2},{2,3},{3,0},{4,5},{5,6},{6,7},{7,4},{8,9},{9,10},{10,1... | collective-permute-start | bytes 776 | tf_op jit(solution)/shard_map/ppermute | solution.py:185
  120.0 2.1 %collective-permute-start.19 = (f32[64]{0:T(128)S(1)}, f32[64]{0:T(128)S(1)}, u32[]{:S(2)}, u32[]{:S(2)}) collective-permute-start(f32[64]{0:T(128)S(1)} %bitcast_add_fusion.1), channel_id=1, source_target_pairs={{0,2},{1,3},{2,0},{3,1},{4,6},{5,7},{6,4},{7,5},{8,10},{9,11},{10,... | collective-permute-start | bytes 776 | tf_op jit(solution)/shard_map/ppermute | solution.py:185
  123.0 1.4 collective-permute-done.19
  124.4 1.1 collective-permute-done.20
  125.7 2.0 %reduce_sum.108 = bf16[2,4,32,1024]{3,2,1,0:T(8,128)(2,1)S(1)} reduce(bf16[4,2,4,32,1024]{4,3,2,1,0:T(8,128)(2,1)} %bitcast.53, bf16[]{:T(256)} %constant.168.clone.1), dimensions={0}, to_apply=%region_10.11 | reduce | flops 786432 | bytes 2621442 | tf_op jit(solution)/shard_map/reduce_sum | solution.py:294
  128.4 2.7 %collective-permute-start.22 = (bf16[2,32,1024]{2,1,0:T(8,128)(2,1)S(1)}, bf16[2,32,1024]{2,1,0:T(8,128)(2,1)S(1)}, u32[]{:S(2)}, u32[]{:S(2)}) collective-permute-start(bf16[2,32,1024]{2,1,0:T(8,128)(2,1)S(1)} %get-tuple-element.53), channel_id=1, source_target_pairs={{0,2},{1,3},{2,0},{3,1},{4,6},{5,7},{6,4},{7,5},{8,10},{9,11},{10,... | collective-permute-start | bytes 393224 | tf_op jit(solution)/shard_map/ppermute | solution.py:185
  131.1 1.2 collective-permute-start.23
  132.3 0.9 copy.40.refs_4_
  134.0 4.9 %shard_map.86 = bf16[256,1024]{1,0:T(8,128)(2,1)} custom-call(s32[2]{0:T(128)} %pad_add_fusion.2.place_ref, bf16[256,1024]{1,0:T(8,128)(2,1)} %get-tuple-element.27.refs_0_, bf16[256,1024]{1,0:T(8,128)(2,1)} %copy-done.6, bf16[2,1024,1024]{2,1,0:T(8,128)(2,1)} %refs_2_.1, bf16[256,1024]{1,0:T(8,128)(2,1)} %refs_3_.1, f32[2,256,1]{2,1,0:T(8,128)} %copy.40.refs_4_), custom_call_target="tpu_custom_call" | custom-call | flops 1073741824 | bytes 5769216 | tf_op jit(solution)/shard_map/pallas_call | solution.py:33
  138.9 1.2 collective-permute-done.22.refs_2_
  140.8 2.7 %shard_map.87 = f32[32,2,2048]{2,1,0:T(2,128)} custom-call(s32[2]{0:T(128)} %pad_add_fusion.2.place_ref, bf16[2,32,1024]{2,1,0:T(8,128)(2,1)} %get-tuple-element.55.refs_0_, bf16[2,32,1024]{2,1,0:T(8,128)(2,1)} %copy-done.10, bf16[2,32,1024]{2,1,0:T(8,128)(2,1)} %copy-done.11, bf16[2,32,1024]{2,1,0:T(8,128)(2,1)} %copy-done.12), custom_call_target="tpu_custom_call" | custom-call | flops 262144 | bytes 524288 | tf_op jit(solution)/shard_map/pallas_call | solution.py:33
  143.9 1.3 copy.41
  (124 shorter events, 11.2 us)
Async XLA Ops:
  0.6 9.5 %copy-start = (f32[2,1024]{1,0:T(2,128)S(1)}, f32[2,1024]{1,0:T(2,128)}, u32[]{:S(2)}) copy-start(f32[2,1024]{1,0:T(2,128)} %param.9) | copy-start | bytes 24580
  0.6 9.5 %copy-start.1 = (bf16[256,1024]{1,0:T(8,128)(2,1)S(1)}, bf16[256,1024]{1,0:T(8,128)(2,1)}, u32[]{:S(2)}) copy-start(bf16[256,1024]{1,0:T(8,128)(2,1)} %refs_3_.1) | copy-start | bytes 1572868
  0.7 9.5 %collective-permute-start.1 = (bf16[256,1024]{1,0:T(8,128)(2,1)}, bf16[256,1024]{1,0:T(8,128)(2,1)S(1)}, u32[]{:S(2)}, u32[]{:S(2)}) collective-permute-start(bf16[256,1024]{1,0:T(8,128)(2,1)} %refs_3_.1), channel_id=1, source_target_pairs={{0,4},{4,0},{8,12},{12,8},{16,20},{20,16},{24,28},{28,24},{1,5},{5... | collective-permute-start | bytes 1572872 | tf_op jit(solution)/shard_map/ppermute | solution.py:195
  4.4 11.0 %collective-permute-start.3 = (bf16[72,1024]{1,0:T(8,128)(2,1)S(1)}, bf16[72,1024]{1,0:T(8,128)(2,1)S(1)}, u32[]{:S(2)}, u32[]{:S(2)}) collective-permute-start(bf16[72,1024]{1,0:T(8,128)(2,1)S(1)} %get-tuple-element.59), channel_id=1, source_target_pairs={{0,3},{1,0},{2,1},{3,2},{4,7},{5,4},{6,5},{7,6},{8,11},{9,8},{10,9... | collective-permute-start | bytes 442376 | tf_op jit(solution)/shard_map/ppermute | solution.py:185
  9.1 13.1 %collective-permute-start = (bf16[72,1024]{1,0:T(8,128)(2,1)S(1)}, bf16[72,1024]{1,0:T(8,128)(2,1)S(1)}, u32[]{:S(2)}, u32[]{:S(2)}) collective-permute-start(bf16[72,1024]{1,0:T(8,128)(2,1)S(1)} %get-tuple-element.59), channel_id=1, source_target_pairs={{0,1},{1,2},{2,3},{3,0},{4,5},{5,6},{6,7},{7,4},{8,9},{9,10},{10,1... | collective-permute-start | bytes 442376 | tf_op jit(solution)/shard_map/ppermute | solution.py:185
  9.1 13.1 %collective-permute-start.2 = (bf16[72,1024]{1,0:T(8,128)(2,1)S(1)}, bf16[72,1024]{1,0:T(8,128)(2,1)S(1)}, u32[]{:S(2)}, u32[]{:S(2)}) collective-permute-start(bf16[72,1024]{1,0:T(8,128)(2,1)S(1)} %get-tuple-element.58), channel_id=1, source_target_pairs={{0,2},{1,3},{2,0},{3,1},{4,6},{5,7},{6,4},{7,5},{8,10},{9,11},{10,... | collective-permute-start | bytes 442376 | tf_op jit(solution)/shard_map/ppermute | solution.py:185
  10.1 3.1 %copy-start.5 = (bf16[256,1024]{1,0:T(8,128)(2,1)}, bf16[256,1024]{1,0:T(8,128)(2,1)S(1)}, u32[]{:S(2)}) copy-start(bf16[256,1024]{1,0:T(8,128)(2,1)S(1)} %collective-permute-done.1.refs_5_) | copy-start | bytes 1572868
  13.2 1.3 copy-start.4
  24.1 4.5 %copy-start.13 = (s32[2,64]{1,0:T(2,128)S(1)}, s32[2,64]{1,0:T(2,128)}, u32[]{:S(2)}) copy-start(s32[2,64]{1,0:T(2,128)} %param.11) | copy-start | bytes 1540
  24.1 39.4 %all-to-all-start = ((bf16[8,128,1024]{2,1,0:T(8,128)(2,1)}), bf16[8,128,1024]{2,1,0:T(8,128)(2,1)S(1)}, u32[]{:S(2)}, u32[]{:S(2)}) async-start(bf16[8,128,1024]{2,1,0:T(8,128)(2,1)} %bitcast.112), calls=%async_computation | async-start | bytes 4194304 | tf_op jit(solution)/shard_map/all_to_all | solution.py:246
  28.0 8.9 %collective-permute-start.4 = (f32[256]{0:T(256)S(1)}, f32[256]{0:T(256)S(1)}, u32[]{:S(2)}, u32[]{:S(2)}) collective-permute-start(f32[256]{0:T(256)S(1)} %slice_reduce_fusion), channel_id=1, source_target_pairs={{0,4},{4,0},{8,12},{12,8},{16,20},{20,16},{24,28},{28,24},{1,5},{5... | collective-permute-start | bytes 3080 | tf_op jit(solution)/shard_map/ppermute | solution.py:195
  28.6 4.4 %collective-permute-start.8 = (s32[2,64]{1,0:T(2,128)S(1)}, s32[2,64]{1,0:T(2,128)S(1)}, u32[]{:S(2)}, u32[]{:S(2)}) collective-permute-start(s32[2,64]{1,0:T(2,128)S(1)} %copy-done.13), channel_id=1, source_target_pairs={{0,4},{4,0},{8,12},{12,8},{16,20},{20,16},{24,28},{28,24},{1,5},{5... | collective-permute-start | bytes 1544 | tf_op jit(solution)/shard_map/ppermute | solution.py:195
  28.7 10.6 %collective-permute-start.7 = (bf16[128,1024]{1,0:T(8,128)(2,1)}, bf16[128,1024]{1,0:T(8,128)(2,1)}, u32[]{:S(2)}, u32[]{:S(2)}) collective-permute-start(bf16[128,1024]{1,0:T(8,128)(2,1)} %bitcast.10), channel_id=1, source_target_pairs={{0,3},{1,0},{2,1},{3,2},{4,7},{5,4},{6,5},{7,6},{8,11},{9,8},{10,9... | collective-permute-start | bytes 786440 | tf_op jit(solution)/shard_map/ppermute | solution.py:185
  31.3 22.5 %collective-permute-start.6 = (bf16[128,1024]{1,0:T(8,128)(2,1)S(1)}, bf16[128,1024]{1,0:T(8,128)(2,1)}, u32[]{:S(2)}, u32[]{:S(2)}) collective-permute-start(bf16[128,1024]{1,0:T(8,128)(2,1)S(1)} %bitcast.126), channel_id=1, source_target_pairs={{0,2},{1,3},{2,0},{3,1},{4,6},{5,7},{6,4},{7,5},{8,10},{9,11},{10,... | collective-permute-start | bytes 786440 | tf_op jit(solution)/shard_map/ppermute | solution.py:185
  31.3 22.5 %collective-permute-start.5 = (bf16[128,1024]{1,0:T(8,128)(2,1)S(1)}, bf16[128,1024]{1,0:T(8,128)(2,1)}, u32[]{:S(2)}, u32[]{:S(2)}) collective-permute-start(bf16[128,1024]{1,0:T(8,128)(2,1)S(1)} %bitcast.125), channel_id=1, source_target_pairs={{0,1},{1,2},{2,3},{3,0},{4,5},{5,6},{6,7},{7,4},{8,9},{9,10},{10,1... | collective-permute-start | bytes 786440 | tf_op jit(solution)/shard_map/ppermute | solution.py:185
  55.5 9.2 %copy-start.2 = (bf16[128,1024]{1,0:T(8,128)(2,1)}, bf16[128,1024]{1,0:T(8,128)(2,1)S(1)}, u32[]{:S(2)}) copy-start(bf16[128,1024]{1,0:T(8,128)(2,1)S(1)} %multiply_convert_fusion.1) | copy-start | bytes 786436
  55.5 8.0 %collective-permute-start.9 = (bf16[128,1024]{1,0:T(8,128)(2,1)S(1)}, bf16[128,1024]{1,0:T(8,128)(2,1)S(1)}, u32[]{:S(2)}, u32[]{:S(2)}) collective-permute-start(bf16[128,1024]{1,0:T(8,128)(2,1)S(1)} %multiply_convert_fusion.1), channel_id=1, source_target_pairs={{0,1},{1,0},{2,3},{3,2},{4,5},{5,4},{6,7},{7,6},{8,9},{9,8},{10,11... | collective-permute-start | bytes 786440 | tf_op jit(solution)/shard_map/ppermute | solution.py:188
  56.7 6.8 %collective-permute-start.11 = (s32[2,128]{1,0:T(2,128)S(1)}, s32[2,128]{1,0:T(2,128)S(1)}, u32[]{:S(2)}, u32[]{:S(2)}) collective-permute-start(s32[2,128]{1,0:T(2,128)S(1)} %pad_add_fusion), channel_id=1, source_target_pairs={{0,1},{1,0},{2,3},{3,2},{4,5},{5,4},{6,7},{7,6},{8,9},{9,8},{10,11... | collective-permute-start | bytes 3080 | tf_op jit(solution)/shard_map/ppermute | solution.py:188
  63.5 1.2 copy-start.7
  64.7 3.7 %collective-permute-start.10 = (f32[2,2,128]{2,1,0:T(2,128)S(1)}, f32[2,2,128]{2,1,0:T(2,128)S(1)}, u32[]{:S(2)}, u32[]{:S(2)}) collective-permute-start(f32[2,2,128]{2,1,0:T(2,128)S(1)} %pad_maximum_fusion.6), channel_id=1, source_target_pairs={{0,1},{1,0},{2,3},{3,2},{4,5},{5,4},{6,7},{7,6},{8,9},{9,8},{10,11... | collective-permute-start | bytes 6152 | tf_op jit(solution)/shard_map/ppermute | solution.py:188
  68.4 3.0 %copy-start.3 = (bf16[128,1024]{1,0:T(8,128)(2,1)S(1)}, bf16[128,1024]{1,0:T(8,128)(2,1)}, u32[]{:S(2)}) copy-start(bf16[128,1024]{1,0:T(8,128)(2,1)} %copy-done.2) | copy-start | bytes 786436
  68.4 3.0 %copy-start.8 = (bf16[128,1024]{1,0:T(8,128)(2,1)S(1)}, bf16[128,1024]{1,0:T(8,128)(2,1)}, u32[]{:S(2)}) copy-start(bf16[128,1024]{1,0:T(8,128)(2,1)} %copy-done.7) | copy-start | bytes 786436
  70.3 8.3 %collective-permute-start.12 = (bf16[128,1024]{1,0:T(8,128)(2,1)}, bf16[128,1024]{1,0:T(8,128)(2,1)}, u32[]{:S(2)}, u32[]{:S(2)}) collective-permute-start(bf16[128,1024]{1,0:T(8,128)(2,1)} %convolution_convert_fusion.1), channel_id=1, source_target_pairs={{0,1},{1,0},{2,3},{3,2},{4,5},{5,4},{6,7},{7,6},{8,9},{9,8},{10,11... | collective-permute-start | bytes 786440 | tf_op jit(solution)/shard_map/ppermute | solution.py:188
  73.5 36.7 %all-to-all-start.2 = ((bf16[8,128,1024]{2,1,0:T(8,128)(2,1)}), bf16[8,128,1024]{2,1,0:T(8,128)(2,1)}, u32[]{:S(2)}, u32[]{:S(2)}) async-start(bf16[8,128,1024]{2,1,0:T(8,128)(2,1)} %bitcast.114), calls=%async_computation.2 | async-start | bytes 4194304 | tf_op jit(solution)/shard_map/all_to_all | solution.py:293
  81.8 21.8 %copy-start.9 = (bf16[128,1024]{1,0:T(8,128)(2,1)}, bf16[128,1024]{1,0:T(8,128)(2,1)S(1)}, u32[]{:S(2)}) copy-start(bf16[128,1024]{1,0:T(8,128)(2,1)S(1)} %subtract_convert_fusion.refs_0_) | copy-start | bytes 786436
  81.9 11.1 %collective-permute-start.14 = (bf16[128,1024]{1,0:T(8,128)(2,1)S(1)}, bf16[128,1024]{1,0:T(8,128)(2,1)S(1)}, u32[]{:S(2)}, u32[]{:S(2)}) collective-permute-start(bf16[128,1024]{1,0:T(8,128)(2,1)S(1)} %subtract_convert_fusion.refs_0_), channel_id=1, source_target_pairs={{0,1},{1,2},{2,3},{3,0},{4,5},{5,6},{6,7},{7,4},{8,9},{9,10},{10,1... | collective-permute-start | bytes 786440 | tf_op jit(solution)/shard_map/ppermute | solution.py:185
  82.9 20.7 %collective-permute-start.15 = (bf16[128,1024]{1,0:T(8,128)(2,1)S(1)}, bf16[128,1024]{1,0:T(8,128)(2,1)S(1)}, u32[]{:S(2)}, u32[]{:S(2)}) collective-permute-start(bf16[128,1024]{1,0:T(8,128)(2,1)S(1)} %subtract_convert_fusion.refs_0_), channel_id=1, source_target_pairs={{0,2},{1,3},{2,0},{3,1},{4,6},{5,7},{6,4},{7,5},{8,10},{9,11},{10,... | collective-permute-start | bytes 786440 | tf_op jit(solution)/shard_map/ppermute | solution.py:185
  86.0 17.7 %collective-permute-start.16 = (bf16[128,1024]{1,0:T(8,128)(2,1)S(1)}, bf16[128,1024]{1,0:T(8,128)(2,1)S(1)}, u32[]{:S(2)}, u32[]{:S(2)}) collective-permute-start(bf16[128,1024]{1,0:T(8,128)(2,1)S(1)} %subtract_convert_fusion.refs_0_), channel_id=1, source_target_pairs={{0,3},{1,0},{2,1},{3,2},{4,7},{5,4},{6,5},{7,6},{8,11},{9,8},{10,9... | collective-permute-start | bytes 786440 | tf_op jit(solution)/shard_map/ppermute | solution.py:185
  87.4 1.2 collective-permute-start.13
  93.0 10.6 %copy-start.14 = (bf16[128,1024]{1,0:T(8,128)(2,1)}, bf16[128,1024]{1,0:T(8,128)(2,1)S(1)}, u32[]{:S(2)}) copy-start(bf16[128,1024]{1,0:T(8,128)(2,1)S(1)} %collective-permute-done.14.refs_1_) | copy-start | bytes 786436
  103.6 0.7 copy-start.15
  104.3 0.7 copy-start.16
  110.2 33.3 %all-to-all-start.1 = ((bf16[8,128,1024]{2,1,0:T(8,128)(2,1)}), bf16[8,128,1024]{2,1,0:T(8,128)(2,1)S(1)}, u32[]{:S(2)}, u32[]{:S(2)}) async-start(bf16[8,128,1024]{2,1,0:T(8,128)(2,1)} %bitcast.117), calls=%async_computation.1 | async-start | bytes 4194304 | tf_op jit(solution)/shard_map/all_to_all | solution.py:314
  114.0 19.1 %collective-permute-start.17 = (bf16[256,1024]{1,0:T(8,128)(2,1)}, bf16[256,1024]{1,0:T(8,128)(2,1)S(1)}, u32[]{:S(2)}, u32[]{:S(2)}) collective-permute-start(bf16[256,1024]{1,0:T(8,128)(2,1)} %get-tuple-element.28), channel_id=1, source_target_pairs={{0,4},{4,0},{8,12},{12,8},{16,20},{20,16},{24,28},{28,24},{1,5},{5... | collective-permute-start | bytes 1572872 | tf_op jit(solution)/shard_map/ppermute | solution.py:195
  114.6 8.4 %collective-permute-start.18 = (f32[64]{0:T(128)S(1)}, f32[64]{0:T(128)S(1)}, u32[]{:S(2)}, u32[]{:S(2)}) collective-permute-start(f32[64]{0:T(128)S(1)} %bitcast_add_fusion.1), channel_id=1, source_target_pairs={{0,1},{1,2},{2,3},{3,0},{4,5},{5,6},{6,7},{7,4},{8,9},{9,10},{10,1... | collective-permute-start | bytes 776 | tf_op jit(solution)/shard_map/ppermute | solution.py:185
  120.0 4.4 %collective-permute-start.19 = (f32[64]{0:T(128)S(1)}, f32[64]{0:T(128)S(1)}, u32[]{:S(2)}, u32[]{:S(2)}) collective-permute-start(f32[64]{0:T(128)S(1)} %bitcast_add_fusion.1), channel_id=1, source_target_pairs={{0,2},{1,3},{2,0},{3,1},{4,6},{5,7},{6,4},{7,5},{8,10},{9,11},{10,... | collective-permute-start | bytes 776 | tf_op jit(solution)/shard_map/ppermute | solution.py:185
  122.0 3.5 %collective-permute-start.20 = (f32[64]{0:T(128)S(1)}, f32[64]{0:T(128)S(1)}, u32[]{:S(2)}, u32[]{:S(2)}) collective-permute-start(f32[64]{0:T(128)S(1)} %bitcast_add_fusion.1), channel_id=1, source_target_pairs={{0,3},{1,0},{2,1},{3,2},{4,7},{5,4},{6,5},{7,6},{8,11},{9,8},{10,9... | collective-permute-start | bytes 776 | tf_op jit(solution)/shard_map/ppermute | solution.py:185
  128.4 10.4 %collective-permute-start.21 = (bf16[2,32,1024]{2,1,0:T(8,128)(2,1)S(1)}, bf16[2,32,1024]{2,1,0:T(8,128)(2,1)S(1)}, u32[]{:S(2)}, u32[]{:S(2)}) collective-permute-start(bf16[2,32,1024]{2,1,0:T(8,128)(2,1)S(1)} %get-tuple-element.54), channel_id=1, source_target_pairs={{0,1},{1,2},{2,3},{3,0},{4,5},{5,6},{6,7},{7,4},{8,9},{9,10},{10,1... | collective-permute-start | bytes 393224 | tf_op jit(solution)/shard_map/ppermute | solution.py:185
  128.4 11.6 %collective-permute-start.22 = (bf16[2,32,1024]{2,1,0:T(8,128)(2,1)S(1)}, bf16[2,32,1024]{2,1,0:T(8,128)(2,1)S(1)}, u32[]{:S(2)}, u32[]{:S(2)}) collective-permute-start(bf16[2,32,1024]{2,1,0:T(8,128)(2,1)S(1)} %get-tuple-element.53), channel_id=1, source_target_pairs={{0,2},{1,3},{2,0},{3,1},{4,6},{5,7},{6,4},{7,5},{8,10},{9,11},{10,... | collective-permute-start | bytes 393224 | tf_op jit(solution)/shard_map/ppermute | solution.py:185
  131.1 9.0 %collective-permute-start.23 = (bf16[2,32,1024]{2,1,0:T(8,128)(2,1)S(1)}, bf16[2,32,1024]{2,1,0:T(8,128)(2,1)S(1)}, u32[]{:S(2)}, u32[]{:S(2)}) collective-permute-start(bf16[2,32,1024]{2,1,0:T(8,128)(2,1)S(1)} %get-tuple-element.52), channel_id=1, source_target_pairs={{0,3},{1,0},{2,1},{3,2},{4,7},{5,4},{6,5},{7,6},{8,11},{9,8},{10,9... | collective-permute-start | bytes 393224 | tf_op jit(solution)/shard_map/ppermute | solution.py:185
  133.2 0.8 copy-start.6
  138.9 1.2 copy-start.10
  140.1 0.6 copy-start.11
  140.1 0.7 copy-start.12

commit v18 on v17

--- a/solution.py
+++ b/solution.py
@@ -207,10 +207,9 @@
     tail = 8 * block
     small = jnp.concatenate(parts_of(squares_part))
     small = jnp.pad(small, (0, tail - small.size)).reshape(8, block)
-    head_parts = w_out.reshape(head_rows, steps, halves, block)
     head_send = []
     for k in range(halves):
-        piece = lax.dynamic_index_in_dim(head_parts, (half + k) % halves, 2, False)
+        piece = lax.dynamic_slice_in_dim(w_out, (half + k) % halves * block, block, 2)
         piece = piece.transpose(1, 0, 2).reshape(steps * head_rows, block)
         head_send.append(jnp.concatenate([piece, small]))
     head_got = [head_send[0]]

time: 146 us -> 145 us (level)
  no operation moved by 1% of the time
where the time goes in v18:
time: 145 us
  waiting for transfers between devices  51.6 us (36%)
  starting transfers between devices  44 us (30%)
  local copies, waits for them, and re-layouts  17.4 us (12%)
  Pallas kernels  12.7 us (9%)
  matrix products  9.41 us (6%)
  other arithmetic  8.26 us (6%)
    ppermute x15, waiting for transfers between devices, along_hid(): lax.ppermute(values, 'hid', [(a, (a + shift) % hids) for a in range(hids)])  42.9 us
    ppermute x15, starting transfers between devices, along_hid(): lax.ppermute(values, 'hid', [(a, (a + shift) % hids) for a in range(hids)])  25.9 us
    pallas_call x3, Pallas kernels, call(): pl.pallas_call(kernel, grid_spec=pltpu.PrefetchScalarGridSpec(num_scalar_...  12.7 us
    dot_general x5, matrix products, matmul(): lax.dot_general(a, b, (contract, ((), ())), preferred_element_type=F32)  9.41 us
    ppermute x4, waiting for transfers between devices, turn_hid(): lax.ppermute(values, 'hid', [(a, a - a % halves + (a % halves + shift) %...  8.41 us
    unnamed x44, local copies, waits for them, and re-layouts  5.64 us
    all_to_all x1, starting transfers between devices, shards(): part_out = lax.all_to_all(part_out, 'seq', 0, 0)  4.34 us
    ppermute x4, starting transfers between devices, turn_hid(): lax.ppermute(values, 'hid', [(a, a - a % halves + (a % halves + shift) %...  4.29 us
  transfers between devices with their start and end apart: 27, of which 12 were waited for; matrix products, arithmetic and copies ran while one was open for 17% of the time, Pallas kernels for 9%

profile of v18, /device:TPU:0, one launch (start us, length us, event | category | flops | bytes accessed | tf_op | source)
XLA Modules:
  0.0 144.5 jit_solution(10672267478717938528)
XLA Ops:
  1.2 1.2 multiply_reduce_fusion
  2.5 1.2 constant_dynamic-slice_fusion.8
  3.8 4.7 %collective-permute-start.3 = (bf16[72,1024]{1,0:T(8,128)(2,1)S(1)}, bf16[72,1024]{1,0:T(8,128)(2,1)S(1)}, u32[]{:S(2)}, u32[]{:S(2)}) collective-permute-start(bf16[72,1024]{1,0:T(8,128)(2,1)S(1)} %get-tuple-element.59), channel_id=1, source_target_pairs={{0,3},{1,0},{2,1},{3,2},{4,7},{5,4},{6,5},{7,6},{8,11},{9,8},{10,9... | collective-permute-start | bytes 442376 | tf_op jit(solution)/shard_map/ppermute | solution.py:185
  8.5 1.0 collective-permute-start.2
  9.6 3.0 %fusion = f32[2,4,64,1024]{3,2,1,0:T(8,128)S(1)} fusion(bf16[2,4,64,1024]{3,2,1,0:T(8,128)(2,1)S(1)} %bitcast.116, bf16[2,1024,1024]{2,1,0:T(8,128)(2,1)} %refs_2_.1, s32[]{:T(128)S(6)} %select_n.138), kind=kOutput, calls=%fused_computation.2 | convolution fusion | flops 1073741824 | bytes 5242884 | tf_op jit(solution)/shard_map/dot_general | solution.py:17
  12.6 1.3 copy-done.4
  13.9 0.8 dynamic-slice_convert_fusion
  14.7 6.9 %collective-permute-done.2 = bf16[72,1024]{1,0:T(8,128)(2,1)S(1)} collective-permute-done((bf16[72,1024]{1,0:T(8,128)(2,1)S(1)}, bf16[72,1024]{1,0:T(8,128)(2,1)S(1)}, u32[]{:S(2)}, u32[]{:S(2)}) %collective-permute-start.2) | collective-permute-done | bytes 147488 | tf_op jit(solution)/shard_map/ppermute | solution.py:185
  21.9 1.6 %broadcast_in_dim.45 = bf16[4,2,128,1024]{3,2,1,0:T(8,128)(2,1)} broadcast(bf16[2,128,1024]{2,1,0:T(8,128)(2,1)S(1)} %bitcast.109), dimensions={1,2,3} | broadcast | bytes 2621440 | tf_op jit(solution)/shard_map/broadcast_in_dim | solution.py:243
  23.5 3.9 %all-to-all-start = ((bf16[8,128,1024]{2,1,0:T(8,128)(2,1)}), bf16[8,128,1024]{2,1,0:T(8,128)(2,1)S(1)}, u32[]{:S(2)}, u32[]{:S(2)}) async-start(bf16[8,128,1024]{2,1,0:T(8,128)(2,1)} %bitcast.105), calls=%async_computation | async-start | bytes 4194304 | tf_op jit(solution)/shard_map/all_to_all | solution.py:245
  28.0 2.6 %collective-permute-start.7 = (bf16[128,1024]{1,0:T(8,128)(2,1)}, bf16[128,1024]{1,0:T(8,128)(2,1)}, u32[]{:S(2)}, u32[]{:S(2)}) collective-permute-start(bf16[128,1024]{1,0:T(8,128)(2,1)} %bitcast.10), channel_id=1, source_target_pairs={{0,3},{1,0},{2,1},{3,2},{4,7},{5,4},{6,5},{7,6},{8,11},{9,8},{10,9... | collective-permute-start | bytes 786440 | tf_op jit(solution)/shard_map/ppermute | solution.py:185
  31.3 1.1 constant_dynamic-slice_fusion.6
  32.5 3.8 %gather_fusion = bf16[128,1024]{1,0:T(8,128)(2,1)S(1)} fusion(bf16[2048,1024]{1,0:T(8,128)(2,1)} %bitcast.115, s32[1024]{0:T(1024)S(1)} %pad_clamp_fusion), kind=kCustom, calls=%fused_computation | custom fusion | bytes 524800 | tf_op jit(solution)/shard_map/jit(_take)/gather | solution.py:239
  36.5 2.2 %collective-permute-done.7 = bf16[128,1024]{1,0:T(8,128)(2,1)} collective-permute-done((bf16[128,1024]{1,0:T(8,128)(2,1)}, bf16[128,1024]{1,0:T(8,128)(2,1)}, u32[]{:S(2)}, u32[]{:S(2)}) %collective-permute-start.7) | collective-permute-done | bytes 262176 | tf_op jit(solution)/shard_map/ppermute | solution.py:185
  38.7 14.5 %collective-permute-done.6 = bf16[128,1024]{1,0:T(8,128)(2,1)} collective-permute-done((bf16[128,1024]{1,0:T(8,128)(2,1)S(1)}, bf16[128,1024]{1,0:T(8,128)(2,1)}, u32[]{:S(2)}, u32[]{:S(2)}) %collective-permute-start.6) | collective-permute-done | bytes 262176 | tf_op jit(solution)/shard_map/ppermute | solution.py:185
  53.1 1.4 multiply_reduce_fusion.4
  54.8 1.2 collective-permute-start.9
  56.1 0.9 collective-permute-start.11
  56.9 5.9 %collective-permute-done.11 = s32[2,128]{1,0:T(2,128)S(1)} collective-permute-done((s32[2,128]{1,0:T(2,128)S(1)}, s32[2,128]{1,0:T(2,128)S(1)}, u32[]{:S(2)}, u32[]{:S(2)}) %collective-permute-start.11) | collective-permute-done | bytes 1056 | tf_op jit(solution)/shard_map/ppermute | solution.py:188
  62.9 0.8 fusion.36
  64.0 1.1 collective-permute-start.10
  65.2 2.5 %collective-permute-done.10 = f32[2,2,128]{2,1,0:T(2,128)S(1)} collective-permute-done((f32[2,2,128]{2,1,0:T(2,128)S(1)}, f32[2,2,128]{2,1,0:T(2,128)S(1)}, u32[]{:S(2)}, u32[]{:S(2)}) %collective-permute-start.10) | collective-permute-done | bytes 2080 | tf_op jit(solution)/shard_map/ppermute | solution.py:188
  68.1 1.5 %convolution_convert_fusion.1 = bf16[128,1024]{1,0:T(8,128)(2,1)} fusion(bf16[1024,1024]{1,0:T(8,128)(2,1)S(1)} %bitcast.103, bf16[256,1024]{1,0:T(8,128)(2,1)S(1)} %multiply_convert_fusion), kind=kOutput, calls=%fused_computation.6 | convolution fusion | flops 268566528 | bytes 2621440 | tf_op jit(solution)/shard_map/dot_general | solution.py:17
  69.7 1.1 collective-permute-start.12
  70.7 2.1 %convolution_convert_fusion = bf16[1024,1024]{1,0:T(8,128)(2,1)} fusion(bf16[256,1024]{1,0:T(8,128)(2,1)S(1)} %multiply_convert_fusion, bf16[128,1024]{1,0:T(8,128)(2,1)S(1)} %copy-done.8, bf16[128,1024]{1,0:T(8,128)(2,1)S(1)} %copy-done.3), kind=kOutput, calls=%fused_computation.5 | convolution fusion | flops 538968064 | bytes 3145728 | tf_op jit(solution)/shard_map/dot_general | solution.py:17
  72.8 4.3 %all-to-all-start.2 = ((bf16[8,128,1024]{2,1,0:T(8,128)(2,1)}), bf16[8,128,1024]{2,1,0:T(8,128)(2,1)}, u32[]{:S(2)}, u32[]{:S(2)}) async-start(bf16[8,128,1024]{2,1,0:T(8,128)(2,1)} %bitcast.107), calls=%async_computation.2 | async-start | bytes 4194304 | tf_op jit(solution)/shard_map/all_to_all | solution.py:292
  78.0 2.0 %multiply_reduce_fusion.3 = (f32[128]{0:T(128)S(1)}, f32[128]{0:T(128)S(1)}, f32[128]{0:T(128)S(1)}, f32[128,1024]{1,0:T(8,128)S(1)}) fusion(f32[128,1024]{1,0:T(8,128)S(1)} %get-tuple-element.48, bf16[128,1024]{1,0:T(8,128)(2,1)} %collective-permute-done.12, f32[1024]{0:T(1024)S(1)} %bitcast.121, bf16[128,1024]{1,0:T(8,128)(2,1)S(1)} %gather_fusion, ...), kind=kOutput, calls=%fused_computation.18 | convolution fusion | flops 270270080 | bytes 3938433 | tf_op jit(solution)/shard_map/dot_general | solution.py:17
  80.0 1.2 subtract_convert_fusion.refs_0_
  81.2 1.0 collective-permute-start.14
  82.2 3.1 %collective-permute-start.15 = (bf16[128,1024]{1,0:T(8,128)(2,1)S(1)}, bf16[128,1024]{1,0:T(8,128)(2,1)S(1)}, u32[]{:S(2)}, u32[]{:S(2)}) collective-permute-start(bf16[128,1024]{1,0:T(8,128)(2,1)S(1)} %subtract_convert_fusion.refs_0_), channel_id=1, source_target_pairs={{0,2},{1,3},{2,0},{3,1},{4,6},{5,7},{6,4},{7,5},{8,10},{9,11},{10,... | collective-permute-start | bytes 786440 | tf_op jit(solution)/shard_map/ppermute | solution.py:185
  85.3 1.2 collective-permute-start.16
  86.9 0.9 copy.45.refs_6_
  88.0 4.4 %collective-permute-done.14.refs_1_ = bf16[128,1024]{1,0:T(8,128)(2,1)S(1)} collective-permute-done((bf16[128,1024]{1,0:T(8,128)(2,1)S(1)}, bf16[128,1024]{1,0:T(8,128)(2,1)S(1)}, u32[]{:S(2)}, u32[]{:S(2)}) %collective-permute-start.14) | collective-permute-done | bytes 262176 | tf_op jit(solution)/shard_map/ppermute | solution.py:185
  92.4 10.6 %collective-permute-done.15.refs_2_ = bf16[128,1024]{1,0:T(8,128)(2,1)S(1)} collective-permute-done((bf16[128,1024]{1,0:T(8,128)(2,1)S(1)}, bf16[128,1024]{1,0:T(8,128)(2,1)S(1)}, u32[]{:S(2)}, u32[]{:S(2)}) %collective-permute-start.15) | collective-permute-done | bytes 262176 | tf_op jit(solution)/shard_map/ppermute | solution.py:185
  104.4 5.1 %shard_map.85 = (bf16[1024,1024]{1,0:T(8,128)(2,1)}, bf16[256,1024]{1,0:T(8,128)(2,1)}, bf16[256,1024]{1,0:T(8,128)(2,1)}) custom-call(s32[2]{0:T(128)} %pad_add_fusion.2.place_ref, bf16[128,1024]{1,0:T(8,128)(2,1)} %copy-done.9, bf16[128,1024]{1,0:T(8,128)(2,1)} %copy-done.14, bf16[128,1024]{1,0:T(8,128)(2,1)} %copy-done.15, bf16[128,1024]{1,0:T(8,128)(2,1)} %copy-done.16, ...), custom_call_target="tpu_custom_call" | custom-call | flops 1073741824 | bytes 2099200 | tf_op jit(solution)/shard_map/pallas_call | solution.py:33
  109.5 3.9 %all-to-all-start.1 = ((bf16[8,128,1024]{2,1,0:T(8,128)(2,1)}), bf16[8,128,1024]{2,1,0:T(8,128)(2,1)S(1)}, u32[]{:S(2)}, u32[]{:S(2)}) async-start(bf16[8,128,1024]{2,1,0:T(8,128)(2,1)} %bitcast.110), calls=%async_computation.1 | async-start | bytes 4194304 | tf_op jit(solution)/shard_map/all_to_all | solution.py:313
  113.9 5.4 %collective-permute-start.18 = (f32[64]{0:T(128)S(1)}, f32[64]{0:T(128)S(1)}, u32[]{:S(2)}, u32[]{:S(2)}) collective-permute-start(f32[64]{0:T(128)S(1)} %bitcast_add_fusion.1), channel_id=1, source_target_pairs={{0,1},{1,2},{2,3},{3,0},{4,5},{5,6},{6,7},{7,4},{8,9},{9,10},{10,1... | collective-permute-start | bytes 776 | tf_op jit(solution)/shard_map/ppermute | solution.py:185
  119.3 2.1 %collective-permute-start.19 = (f32[64]{0:T(128)S(1)}, f32[64]{0:T(128)S(1)}, u32[]{:S(2)}, u32[]{:S(2)}) collective-permute-start(f32[64]{0:T(128)S(1)} %bitcast_add_fusion.1), channel_id=1, source_target_pairs={{0,2},{1,3},{2,0},{3,1},{4,6},{5,7},{6,4},{7,5},{8,10},{9,11},{10,... | collective-permute-start | bytes 776 | tf_op jit(solution)/shard_map/ppermute | solution.py:185
  122.4 1.4 collective-permute-done.19
  123.8 1.1 collective-permute-done.20
  125.1 2.0 %reduce_sum.108 = bf16[2,4,32,1024]{3,2,1,0:T(8,128)(2,1)S(1)} reduce(bf16[4,2,4,32,1024]{4,3,2,1,0:T(8,128)(2,1)} %bitcast.53, bf16[]{:T(256)} %constant.163.clone.1), dimensions={0}, to_apply=%region_10.11 | reduce | flops 786432 | bytes 2621442 | tf_op jit(solution)/shard_map/reduce_sum | solution.py:293
  127.8 2.7 %collective-permute-start.22 = (bf16[2,32,1024]{2,1,0:T(8,128)(2,1)S(1)}, bf16[2,32,1024]{2,1,0:T(8,128)(2,1)S(1)}, u32[]{:S(2)}, u32[]{:S(2)}) collective-permute-start(bf16[2,32,1024]{2,1,0:T(8,128)(2,1)S(1)} %get-tuple-element.53), channel_id=1, source_target_pairs={{0,2},{1,3},{2,0},{3,1},{4,6},{5,7},{6,4},{7,5},{8,10},{9,11},{10,... | collective-permute-start | bytes 393224 | tf_op jit(solution)/shard_map/ppermute | solution.py:185
  130.5 1.2 collective-permute-start.23
  131.7 0.9 copy.46.refs_4_
  133.3 4.9 %shard_map.86 = bf16[256,1024]{1,0:T(8,128)(2,1)} custom-call(s32[2]{0:T(128)} %pad_add_fusion.2.place_ref, bf16[256,1024]{1,0:T(8,128)(2,1)} %get-tuple-element.27.refs_0_, bf16[256,1024]{1,0:T(8,128)(2,1)} %copy-done.6, bf16[2,1024,1024]{2,1,0:T(8,128)(2,1)} %refs_2_.1, bf16[256,1024]{1,0:T(8,128)(2,1)} %refs_3_.1, f32[2,256,1]{2,1,0:T(8,128)} %copy.46.refs_4_), custom_call_target="tpu_custom_call" | custom-call | flops 1073741824 | bytes 5769216 | tf_op jit(solution)/shard_map/pallas_call | solution.py:33
  138.2 1.2 collective-permute-done.22.refs_2_
  140.1 2.7 %shard_map.87 = f32[32,2,2048]{2,1,0:T(2,128)} custom-call(s32[2]{0:T(128)} %pad_add_fusion.2.place_ref, bf16[2,32,1024]{2,1,0:T(8,128)(2,1)} %get-tuple-element.55.refs_0_, bf16[2,32,1024]{2,1,0:T(8,128)(2,1)} %copy-done.10, bf16[2,32,1024]{2,1,0:T(8,128)(2,1)} %copy-done.11, bf16[2,32,1024]{2,1,0:T(8,128)(2,1)} %copy-done.12), custom_call_target="tpu_custom_call" | custom-call | flops 262144 | bytes 524288 | tf_op jit(solution)/shard_map/pallas_call | solution.py:33
  143.2 1.3 copy.47
  (123 shorter events, 10.6 us)
Async XLA Ops:
  0.6 8.9 %copy-start = (f32[2,1024]{1,0:T(2,128)S(1)}, f32[2,1024]{1,0:T(2,128)}, u32[]{:S(2)}) copy-start(f32[2,1024]{1,0:T(2,128)} %param.9) | copy-start | bytes 24580
  0.6 8.9 %copy-start.1 = (bf16[256,1024]{1,0:T(8,128)(2,1)S(1)}, bf16[256,1024]{1,0:T(8,128)(2,1)}, u32[]{:S(2)}) copy-start(bf16[256,1024]{1,0:T(8,128)(2,1)} %refs_3_.1) | copy-start | bytes 1572868
  0.7 8.8 %collective-permute-start.1 = (bf16[256,1024]{1,0:T(8,128)(2,1)}, bf16[256,1024]{1,0:T(8,128)(2,1)S(1)}, u32[]{:S(2)}, u32[]{:S(2)}) collective-permute-start(bf16[256,1024]{1,0:T(8,128)(2,1)} %refs_3_.1), channel_id=1, source_target_pairs={{0,4},{4,0},{8,12},{12,8},{16,20},{20,16},{24,28},{28,24},{1,5},{5... | collective-permute-start | bytes 1572872 | tf_op jit(solution)/shard_map/ppermute | solution.py:195
  3.8 11.0 %collective-permute-start.3 = (bf16[72,1024]{1,0:T(8,128)(2,1)S(1)}, bf16[72,1024]{1,0:T(8,128)(2,1)S(1)}, u32[]{:S(2)}, u32[]{:S(2)}) collective-permute-start(bf16[72,1024]{1,0:T(8,128)(2,1)S(1)} %get-tuple-element.59), channel_id=1, source_target_pairs={{0,3},{1,0},{2,1},{3,2},{4,7},{5,4},{6,5},{7,6},{8,11},{9,8},{10,9... | collective-permute-start | bytes 442376 | tf_op jit(solution)/shard_map/ppermute | solution.py:185
  8.5 13.1 %collective-permute-start = (bf16[72,1024]{1,0:T(8,128)(2,1)S(1)}, bf16[72,1024]{1,0:T(8,128)(2,1)S(1)}, u32[]{:S(2)}, u32[]{:S(2)}) collective-permute-start(bf16[72,1024]{1,0:T(8,128)(2,1)S(1)} %get-tuple-element.59), channel_id=1, source_target_pairs={{0,1},{1,2},{2,3},{3,0},{4,5},{5,6},{6,7},{7,4},{8,9},{9,10},{10,1... | collective-permute-start | bytes 442376 | tf_op jit(solution)/shard_map/ppermute | solution.py:185
  8.5 13.1 %collective-permute-start.2 = (bf16[72,1024]{1,0:T(8,128)(2,1)S(1)}, bf16[72,1024]{1,0:T(8,128)(2,1)S(1)}, u32[]{:S(2)}, u32[]{:S(2)}) collective-permute-start(bf16[72,1024]{1,0:T(8,128)(2,1)S(1)} %get-tuple-element.58), channel_id=1, source_target_pairs={{0,2},{1,3},{2,0},{3,1},{4,6},{5,7},{6,4},{7,5},{8,10},{9,11},{10,... | collective-permute-start | bytes 442376 | tf_op jit(solution)/shard_map/ppermute | solution.py:185
  9.5 3.1 %copy-start.5 = (bf16[256,1024]{1,0:T(8,128)(2,1)}, bf16[256,1024]{1,0:T(8,128)(2,1)S(1)}, u32[]{:S(2)}) copy-start(bf16[256,1024]{1,0:T(8,128)(2,1)S(1)} %collective-permute-done.1.refs_5_) | copy-start | bytes 1572868
  12.6 1.3 copy-start.4
  23.5 4.5 %copy-start.13 = (s32[2,64]{1,0:T(2,128)S(1)}, s32[2,64]{1,0:T(2,128)}, u32[]{:S(2)}) copy-start(s32[2,64]{1,0:T(2,128)} %param.11) | copy-start | bytes 1540
  23.5 39.4 %all-to-all-start = ((bf16[8,128,1024]{2,1,0:T(8,128)(2,1)}), bf16[8,128,1024]{2,1,0:T(8,128)(2,1)S(1)}, u32[]{:S(2)}, u32[]{:S(2)}) async-start(bf16[8,128,1024]{2,1,0:T(8,128)(2,1)} %bitcast.105), calls=%async_computation | async-start | bytes 4194304 | tf_op jit(solution)/shard_map/all_to_all | solution.py:245
  27.4 8.9 %collective-permute-start.4 = (f32[256]{0:T(256)S(1)}, f32[256]{0:T(256)S(1)}, u32[]{:S(2)}, u32[]{:S(2)}) collective-permute-start(f32[256]{0:T(256)S(1)} %slice_reduce_fusion), channel_id=1, source_target_pairs={{0,4},{4,0},{8,12},{12,8},{16,20},{20,16},{24,28},{28,24},{1,5},{5... | collective-permute-start | bytes 3080 | tf_op jit(solution)/shard_map/ppermute | solution.py:195
  28.0 4.4 %collective-permute-start.8 = (s32[2,64]{1,0:T(2,128)S(1)}, s32[2,64]{1,0:T(2,128)S(1)}, u32[]{:S(2)}, u32[]{:S(2)}) collective-permute-start(s32[2,64]{1,0:T(2,128)S(1)} %copy-done.13), channel_id=1, source_target_pairs={{0,4},{4,0},{8,12},{12,8},{16,20},{20,16},{24,28},{28,24},{1,5},{5... | collective-permute-start | bytes 1544 | tf_op jit(solution)/shard_map/ppermute | solution.py:195
  28.0 10.6 %collective-permute-start.7 = (bf16[128,1024]{1,0:T(8,128)(2,1)}, bf16[128,1024]{1,0:T(8,128)(2,1)}, u32[]{:S(2)}, u32[]{:S(2)}) collective-permute-start(bf16[128,1024]{1,0:T(8,128)(2,1)} %bitcast.10), channel_id=1, source_target_pairs={{0,3},{1,0},{2,1},{3,2},{4,7},{5,4},{6,5},{7,6},{8,11},{9,8},{10,9... | collective-permute-start | bytes 786440 | tf_op jit(solution)/shard_map/ppermute | solution.py:185
  30.7 22.5 %collective-permute-start.6 = (bf16[128,1024]{1,0:T(8,128)(2,1)S(1)}, bf16[128,1024]{1,0:T(8,128)(2,1)}, u32[]{:S(2)}, u32[]{:S(2)}) collective-permute-start(bf16[128,1024]{1,0:T(8,128)(2,1)S(1)} %bitcast.119), channel_id=1, source_target_pairs={{0,2},{1,3},{2,0},{3,1},{4,6},{5,7},{6,4},{7,5},{8,10},{9,11},{10,... | collective-permute-start | bytes 786440 | tf_op jit(solution)/shard_map/ppermute | solution.py:185
  30.7 22.5 %collective-permute-start.5 = (bf16[128,1024]{1,0:T(8,128)(2,1)S(1)}, bf16[128,1024]{1,0:T(8,128)(2,1)}, u32[]{:S(2)}, u32[]{:S(2)}) collective-permute-start(bf16[128,1024]{1,0:T(8,128)(2,1)S(1)} %bitcast.118), channel_id=1, source_target_pairs={{0,1},{1,2},{2,3},{3,0},{4,5},{5,6},{6,7},{7,4},{8,9},{9,10},{10,1... | collective-permute-start | bytes 786440 | tf_op jit(solution)/shard_map/ppermute | solution.py:185
  54.8 9.2 %copy-start.2 = (bf16[128,1024]{1,0:T(8,128)(2,1)}, bf16[128,1024]{1,0:T(8,128)(2,1)S(1)}, u32[]{:S(2)}) copy-start(bf16[128,1024]{1,0:T(8,128)(2,1)S(1)} %multiply_convert_fusion.1) | copy-start | bytes 786436
  54.8 8.0 %collective-permute-start.9 = (bf16[128,1024]{1,0:T(8,128)(2,1)S(1)}, bf16[128,1024]{1,0:T(8,128)(2,1)S(1)}, u32[]{:S(2)}, u32[]{:S(2)}) collective-permute-start(bf16[128,1024]{1,0:T(8,128)(2,1)S(1)} %multiply_convert_fusion.1), channel_id=1, source_target_pairs={{0,1},{1,0},{2,3},{3,2},{4,5},{5,4},{6,7},{7,6},{8,9},{9,8},{10,11... | collective-permute-start | bytes 786440 | tf_op jit(solution)/shard_map/ppermute | solution.py:188
  56.1 6.8 %collective-permute-start.11 = (s32[2,128]{1,0:T(2,128)S(1)}, s32[2,128]{1,0:T(2,128)S(1)}, u32[]{:S(2)}, u32[]{:S(2)}) collective-permute-start(s32[2,128]{1,0:T(2,128)S(1)} %pad_add_fusion), channel_id=1, source_target_pairs={{0,1},{1,0},{2,3},{3,2},{4,5},{5,4},{6,7},{7,6},{8,9},{9,8},{10,11... | collective-permute-start | bytes 3080 | tf_op jit(solution)/shard_map/ppermute | solution.py:188
  62.9 1.2 copy-start.7
  64.0 3.7 %collective-permute-start.10 = (f32[2,2,128]{2,1,0:T(2,128)S(1)}, f32[2,2,128]{2,1,0:T(2,128)S(1)}, u32[]{:S(2)}, u32[]{:S(2)}) collective-permute-start(f32[2,2,128]{2,1,0:T(2,128)S(1)} %pad_maximum_fusion.6), channel_id=1, source_target_pairs={{0,1},{1,0},{2,3},{3,2},{4,5},{5,4},{6,7},{7,6},{8,9},{9,8},{10,11... | collective-permute-start | bytes 6152 | tf_op jit(solution)/shard_map/ppermute | solution.py:188
  67.8 3.0 %copy-start.3 = (bf16[128,1024]{1,0:T(8,128)(2,1)S(1)}, bf16[128,1024]{1,0:T(8,128)(2,1)}, u32[]{:S(2)}) copy-start(bf16[128,1024]{1,0:T(8,128)(2,1)} %copy-done.2) | copy-start | bytes 786436
  67.8 3.0 %copy-start.8 = (bf16[128,1024]{1,0:T(8,128)(2,1)S(1)}, bf16[128,1024]{1,0:T(8,128)(2,1)}, u32[]{:S(2)}) copy-start(bf16[128,1024]{1,0:T(8,128)(2,1)} %copy-done.7) | copy-start | bytes 786436
  69.7 8.3 %collective-permute-start.12 = (bf16[128,1024]{1,0:T(8,128)(2,1)}, bf16[128,1024]{1,0:T(8,128)(2,1)}, u32[]{:S(2)}, u32[]{:S(2)}) collective-permute-start(bf16[128,1024]{1,0:T(8,128)(2,1)} %convolution_convert_fusion.1), channel_id=1, source_target_pairs={{0,1},{1,0},{2,3},{3,2},{4,5},{5,4},{6,7},{7,6},{8,9},{9,8},{10,11... | collective-permute-start | bytes 786440 | tf_op jit(solution)/shard_map/ppermute | solution.py:188
  72.8 36.7 %all-to-all-start.2 = ((bf16[8,128,1024]{2,1,0:T(8,128)(2,1)}), bf16[8,128,1024]{2,1,0:T(8,128)(2,1)}, u32[]{:S(2)}, u32[]{:S(2)}) async-start(bf16[8,128,1024]{2,1,0:T(8,128)(2,1)} %bitcast.107), calls=%async_computation.2 | async-start | bytes 4194304 | tf_op jit(solution)/shard_map/all_to_all | solution.py:292
  81.2 21.8 %copy-start.9 = (bf16[128,1024]{1,0:T(8,128)(2,1)}, bf16[128,1024]{1,0:T(8,128)(2,1)S(1)}, u32[]{:S(2)}) copy-start(bf16[128,1024]{1,0:T(8,128)(2,1)S(1)} %subtract_convert_fusion.refs_0_) | copy-start | bytes 786436
  81.2 11.1 %collective-permute-start.14 = (bf16[128,1024]{1,0:T(8,128)(2,1)S(1)}, bf16[128,1024]{1,0:T(8,128)(2,1)S(1)}, u32[]{:S(2)}, u32[]{:S(2)}) collective-permute-start(bf16[128,1024]{1,0:T(8,128)(2,1)S(1)} %subtract_convert_fusion.refs_0_), channel_id=1, source_target_pairs={{0,1},{1,2},{2,3},{3,0},{4,5},{5,6},{6,7},{7,4},{8,9},{9,10},{10,1... | collective-permute-start | bytes 786440 | tf_op jit(solution)/shard_map/ppermute | solution.py:185
  82.2 20.7 %collective-permute-start.15 = (bf16[128,1024]{1,0:T(8,128)(2,1)S(1)}, bf16[128,1024]{1,0:T(8,128)(2,1)S(1)}, u32[]{:S(2)}, u32[]{:S(2)}) collective-permute-start(bf16[128,1024]{1,0:T(8,128)(2,1)S(1)} %subtract_convert_fusion.refs_0_), channel_id=1, source_target_pairs={{0,2},{1,3},{2,0},{3,1},{4,6},{5,7},{6,4},{7,5},{8,10},{9,11},{10,... | collective-permute-start | bytes 786440 | tf_op jit(solution)/shard_map/ppermute | solution.py:185
  85.3 17.7 %collective-permute-start.16 = (bf16[128,1024]{1,0:T(8,128)(2,1)S(1)}, bf16[128,1024]{1,0:T(8,128)(2,1)S(1)}, u32[]{:S(2)}, u32[]{:S(2)}) collective-permute-start(bf16[128,1024]{1,0:T(8,128)(2,1)S(1)} %subtract_convert_fusion.refs_0_), channel_id=1, source_target_pairs={{0,3},{1,0},{2,1},{3,2},{4,7},{5,4},{6,5},{7,6},{8,11},{9,8},{10,9... | collective-permute-start | bytes 786440 | tf_op jit(solution)/shard_map/ppermute | solution.py:185
  86.8 1.2 collective-permute-start.13
  92.4 10.6 %copy-start.14 = (bf16[128,1024]{1,0:T(8,128)(2,1)}, bf16[128,1024]{1,0:T(8,128)(2,1)S(1)}, u32[]{:S(2)}) copy-start(bf16[128,1024]{1,0:T(8,128)(2,1)S(1)} %collective-permute-done.14.refs_1_) | copy-start | bytes 786436
  103.0 0.7 copy-start.15
  103.7 0.7 copy-start.16
  109.5 33.3 %all-to-all-start.1 = ((bf16[8,128,1024]{2,1,0:T(8,128)(2,1)}), bf16[8,128,1024]{2,1,0:T(8,128)(2,1)S(1)}, u32[]{:S(2)}, u32[]{:S(2)}) async-start(bf16[8,128,1024]{2,1,0:T(8,128)(2,1)} %bitcast.110), calls=%async_computation.1 | async-start | bytes 4194304 | tf_op jit(solution)/shard_map/all_to_all | solution.py:313
  113.4 19.1 %collective-permute-start.17 = (bf16[256,1024]{1,0:T(8,128)(2,1)}, bf16[256,1024]{1,0:T(8,128)(2,1)S(1)}, u32[]{:S(2)}, u32[]{:S(2)}) collective-permute-start(bf16[256,1024]{1,0:T(8,128)(2,1)} %get-tuple-element.28), channel_id=1, source_target_pairs={{0,4},{4,0},{8,12},{12,8},{16,20},{20,16},{24,28},{28,24},{1,5},{5... | collective-permute-start | bytes 1572872 | tf_op jit(solution)/shard_map/ppermute | solution.py:195
  113.9 8.4 %collective-permute-start.18 = (f32[64]{0:T(128)S(1)}, f32[64]{0:T(128)S(1)}, u32[]{:S(2)}, u32[]{:S(2)}) collective-permute-start(f32[64]{0:T(128)S(1)} %bitcast_add_fusion.1), channel_id=1, source_target_pairs={{0,1},{1,2},{2,3},{3,0},{4,5},{5,6},{6,7},{7,4},{8,9},{9,10},{10,1... | collective-permute-start | bytes 776 | tf_op jit(solution)/shard_map/ppermute | solution.py:185
  119.3 4.4 %collective-permute-start.19 = (f32[64]{0:T(128)S(1)}, f32[64]{0:T(128)S(1)}, u32[]{:S(2)}, u32[]{:S(2)}) collective-permute-start(f32[64]{0:T(128)S(1)} %bitcast_add_fusion.1), channel_id=1, source_target_pairs={{0,2},{1,3},{2,0},{3,1},{4,6},{5,7},{6,4},{7,5},{8,10},{9,11},{10,... | collective-permute-start | bytes 776 | tf_op jit(solution)/shard_map/ppermute | solution.py:185
  121.4 3.5 %collective-permute-start.20 = (f32[64]{0:T(128)S(1)}, f32[64]{0:T(128)S(1)}, u32[]{:S(2)}, u32[]{:S(2)}) collective-permute-start(f32[64]{0:T(128)S(1)} %bitcast_add_fusion.1), channel_id=1, source_target_pairs={{0,3},{1,0},{2,1},{3,2},{4,7},{5,4},{6,5},{7,6},{8,11},{9,8},{10,9... | collective-permute-start | bytes 776 | tf_op jit(solution)/shard_map/ppermute | solution.py:185
  127.8 10.4 %collective-permute-start.21 = (bf16[2,32,1024]{2,1,0:T(8,128)(2,1)S(1)}, bf16[2,32,1024]{2,1,0:T(8,128)(2,1)S(1)}, u32[]{:S(2)}, u32[]{:S(2)}) collective-permute-start(bf16[2,32,1024]{2,1,0:T(8,128)(2,1)S(1)} %get-tuple-element.54), channel_id=1, source_target_pairs={{0,1},{1,2},{2,3},{3,0},{4,5},{5,6},{6,7},{7,4},{8,9},{9,10},{10,1... | collective-permute-start | bytes 393224 | tf_op jit(solution)/shard_map/ppermute | solution.py:185
  127.8 11.6 %collective-permute-start.22 = (bf16[2,32,1024]{2,1,0:T(8,128)(2,1)S(1)}, bf16[2,32,1024]{2,1,0:T(8,128)(2,1)S(1)}, u32[]{:S(2)}, u32[]{:S(2)}) collective-permute-start(bf16[2,32,1024]{2,1,0:T(8,128)(2,1)S(1)} %get-tuple-element.53), channel_id=1, source_target_pairs={{0,2},{1,3},{2,0},{3,1},{4,6},{5,7},{6,4},{7,5},{8,10},{9,11},{10,... | collective-permute-start | bytes 393224 | tf_op jit(solution)/shard_map/ppermute | solution.py:185
  130.5 9.0 %collective-permute-start.23 = (bf16[2,32,1024]{2,1,0:T(8,128)(2,1)S(1)}, bf16[2,32,1024]{2,1,0:T(8,128)(2,1)S(1)}, u32[]{:S(2)}, u32[]{:S(2)}) collective-permute-start(bf16[2,32,1024]{2,1,0:T(8,128)(2,1)S(1)} %get-tuple-element.52), channel_id=1, source_target_pairs={{0,3},{1,0},{2,1},{3,2},{4,7},{5,4},{6,5},{7,6},{8,11},{9,8},{10,9... | collective-permute-start | bytes 393224 | tf_op jit(solution)/shard_map/ppermute | solution.py:185
  132.5 0.8 copy-start.6
  138.2 1.2 copy-start.10
  139.4 0.6 copy-start.11
  139.4 0.7 copy-start.12
